TPU v7x, 128 devices: a whole 4x4x4 slice. The times are simulated.
128 devices in a mesh: pole: 4 (over x), row: 16 (over z, y), col: 2 (over core).
Axes of the slice: x: 4, y: 4, z: 4, core: 2. Of those that a mesh axis runs over, the one named last changes fastest.
Arguments:
- lower_factor: bfloat16 [4, 10, 2, 512, 512], P('pole', None, None, 'row', 'col'), may hold values from -0.125 to 0.125
- upper_factor: bfloat16 [4, 10, 2, 512, 512], P('pole', None, None, 'row', 'col'), may hold values from -0.125 to 0.125
- diag_inverse: bfloat16 [4, 7, 2, 512, 512], P('pole', None, None, 'row', 'col'), may hold values from -6 to 6
- residues: float32 [4, 2], P('pole'), may hold values from -4 to 4
- widths: int32 [7], replicated, may hold values from 192 to 512, as said below
- pattern: int32 [10], replicated, may hold values 0 or 1
Outputs:
- density: float32 [27, 512, 512], P(None, 'row', 'col')
Inputs may be any that keep to these rules, and one draw needn't show every extreme that they name: `widths`: some supernode has exactly 512 columns.
All inputs are finite; a program needn't handle non-finite values.
Results may differ from a plain program's by a relative error of at most 0.014.
Values may be sent and summed in bfloat16 or wider, within the bound.
No kernel may reach another device: no remote copies, remote signals or barrier semaphores. Data moves between devices by JAX's collectives and lax.ppermute only.
A program may use at most 64 MiB of HBM per device.

v0:
```python
import jax
import jax.numpy as jnp
from jax import lax
from jax.sharding import PartitionSpec as P

LEV = 3
NS = 7
NL = 10


def ancestors(member):
    chain_list = []
    current = member
    while current > 0:
        current = (current - 1) // 2
        chain_list.append(current)
    return chain_list


def pair_table(count):
    table = {}
    for member in range(1, count):
        for above in ancestors(member):
            table[member, above] = len(table)
    return table


def complex_product(form, left, right, axis):
    real_left = left[:, :, 0]
    imag_left = left[:, :, 1]
    real_right = right[:, :, 0]
    imag_right = right[:, :, 1]
    real_part = jnp.einsum(
        form, real_left, real_right, preferred_element_type=jnp.float32
    ) - jnp.einsum(form, imag_left, imag_right, preferred_element_type=jnp.float32)
    imag_part = jnp.einsum(
        form, real_left, imag_right, preferred_element_type=jnp.float32
    ) + jnp.einsum(form, imag_left, real_right, preferred_element_type=jnp.float32)
    return jnp.stack([real_part, imag_part], axis=axis)


def body(lower_factor, upper_factor, diag_inverse, residues, widths, pattern):
    lower = lower_factor[0]
    upper = upper_factor[0]
    dinv = diag_inverse[0]
    rows_local = lower.shape[2]
    cols_local = lower.shape[3]
    row_start = lax.axis_index("row") * rows_local
    col_start = lax.axis_index("col") * cols_local
    row_keep = ((row_start + jnp.arange(rows_local))[None, :] < widths[:, None]).astype(
        jnp.bfloat16
    )
    col_keep = ((col_start + jnp.arange(cols_local))[None, :] < widths[:, None]).astype(
        jnp.bfloat16
    )
    pattern_mask = pattern.astype(jnp.bfloat16)
    table = pair_table(NS)

    def lhat(member, above):
        index = table[member, above]
        return lower[index] * (
            pattern_mask[index] * row_keep[above][:, None] * col_keep[member][None, :]
        )

    def uhat(member, above):
        index = table[member, above]
        return upper[index] * (
            pattern_mask[index] * row_keep[member][:, None] * col_keep[above][None, :]
        )

    def dhat(member):
        return dinv[member] * (row_keep[member][:, None] * col_keep[member][None, :])

    blocks = {(0, 0): dhat(0)}

    def solve_group(group):
        chain_list = ancestors(group[0])
        lower_tiles = jnp.stack(
            [jnp.stack([lhat(member, above) for above in chain_list]) for member in group]
        )
        upper_tiles = jnp.stack(
            [jnp.stack([uhat(member, above) for above in chain_list]) for member in group]
        )
        lower_full = lax.all_gather(lower_tiles, "row", axis=3, tiled=True)
        upper_full = lax.all_gather(upper_tiles, "col", axis=4, tiled=True)
        corner = jnp.stack(
            [jnp.stack([blocks[first, second] for second in chain_list]) for first in chain_list]
        )
        below = complex_product(
            "ijrk,gjkc->girc", lax.all_gather(corner, "col", axis=4, tiled=True), lower_full, 2
        )
        below_tiles = (-below).astype(jnp.bfloat16)
        cols_part = upper_full
        beside = complex_product(
            "gjrk,jikc->girc", cols_part, lax.all_gather(corner, "row", axis=3, tiled=True), 2
        )
        beside_tiles = (-beside).astype(jnp.bfloat16)
        cols_part = upper_full
        product = complex_product(
            "gjrk,gjkc->grc", cols_part, lax.all_gather(below_tiles, "row", axis=3, tiled=True), 1
        )
        diag_own = jnp.stack([dhat(member) for member in group]).astype(jnp.float32)
        diag_tiles = (diag_own - product).astype(jnp.bfloat16)
        for slot, member in enumerate(group):
            for place, above in enumerate(chain_list):
                blocks[above, member] = below_tiles[slot, place]
                blocks[member, above] = beside_tiles[slot, place]
            blocks[member, member] = diag_tiles[slot]

    weight_real = residues[0, 0]
    weight_imag = residues[0, 1]

    def density_term(block):
        return weight_real * block[0].astype(jnp.float32) - weight_imag * block[1].astype(
            jnp.float32
        )

    def block_of(index):
        if index < NS:
            return blocks[index, index]
        if index < NS + NL:
            pair = list(table)[index - NS]
            return blocks[pair[1], pair[0]]
        pair = list(table)[index - NS - NL]
        return blocks[pair[0], pair[1]]

    for level in range(1, LEV):
        members = list(range(2**level - 1, 2 ** (level + 1) - 1))
        groups = [[member] for member in members]
        for group in groups:
            solve_group(group)
    stacked = jnp.stack([density_term(block_of(index)) for index in range(NS + 2 * NL)])
    return lax.psum(stacked.astype(jnp.bfloat16), "pole").astype(jnp.float32)


def solution(mesh):
    return jax.shard_map(
        body,
        mesh=mesh,
        in_specs=(
            P("pole", None, None, "row", "col"),
            P("pole", None, None, "row", "col"),
            P("pole", None, None, "row", "col"),
            P("pole", None),
            P(),
            P(),
        ),
        out_specs=P(None, "row", "col"),
        check_vma=False,
    )
```

profile of v0, /device:TPU:0, one launch (start us, length us, event | category | flops | bytes accessed | tf_op | source)
XLA Modules:
  0.0 530.5 jit_solution(13398027393837465595)
XLA Ops:
  9.4 4.4 broadcast_multiply_fusion.29
  13.8 5.1 broadcast_multiply_fusion.30
  23.9 25.8 %all_gather.83 = bf16[1,1,2,512,256]{4,3,2,1,0:T(8,128)(2,1)S(1)} all-gather(bf16[1,1,2,32,256]{4,3,2,1,0:T(8,128)(2,1)S(1)} %get-tuple-element.30), channel_id=1, replica_groups=mesh['pole'=4,'row'=16,'col'=2] {'row'}, dimensions={3}, use_global_device_ids=true | all-gather | bytes 557056 | tf_op jit(solution)/shard_map/all_gather | solution.py:84
  49.8 1.9 all_gather.80
  52.3 23.3 %all_gather.84 = bf16[1,1,2,512,256]{4,3,2,1,0:T(8,128)(2,1)S(1)} all-gather(bf16[1,1,2,32,256]{4,3,2,1,0:T(8,128)(2,1)S(1)} %fusion.76), channel_id=1, replica_groups=mesh['pole'=4,'row'=16,'col'=2] {'row'}, dimensions={3}, use_global_device_ids=true | all-gather | bytes 557056 | tf_op jit(solution)/shard_map/all_gather | solution.py:100
  75.6 1.9 all_gather.82
  77.8 22.1 %all_gather.79 = bf16[1,1,2,512,256]{4,3,2,1,0:T(8,128)(2,1)S(1)} all-gather(bf16[1,1,2,32,256]{4,3,2,1,0:T(8,128)(2,1)S(1)} %get-tuple-element.31), channel_id=1, replica_groups=mesh['pole'=4,'row'=16,'col'=2] {'row'}, dimensions={3}, use_global_device_ids=true | all-gather | bytes 557056 | tf_op jit(solution)/shard_map/all_gather | solution.py:84
  100.1 23.6 %all_gather.87 = bf16[1,1,2,512,256]{4,3,2,1,0:T(8,128)(2,1)S(1)} all-gather(bf16[1,1,2,32,256]{4,3,2,1,0:T(8,128)(2,1)S(1)} %slice_multiply_fusion.4), channel_id=1, replica_groups=mesh['pole'=4,'row'=16,'col'=2] {'row'}, dimensions={3}, use_global_device_ids=true | all-gather | bytes 557056 | tf_op jit(solution)/shard_map/all_gather | solution.py:95
  124.7 22.0 %all_gather.81 = bf16[1,1,2,512,256]{4,3,2,1,0:T(8,128)(2,1)S(1)} all-gather(bf16[1,1,2,32,256]{4,3,2,1,0:T(8,128)(2,1)S(1)} %fusion.74), channel_id=1, replica_groups=mesh['pole'=4,'row'=16,'col'=2] {'row'}, dimensions={3}, use_global_device_ids=true | all-gather | bytes 557056 | tf_op jit(solution)/shard_map/all_gather | solution.py:100
  149.7 2.0 all_gather.95
  157.2 2.0 all_gather.88
  168.8 30.8 %all-gather.35.cloned.1.call-done = bf16[2,2,512,256]{3,2,0,1:T(8,128)(2,1)} async-done(((bf16[2,2,32,256]{3,2,0,1:T(8,128)(2,1)}), bf16[2,2,512,256]{3,2,0,1:T(8,128)(2,1)}) %all-gather.35.cloned.1.call-update) | async-done | bytes 1048592 | tf_op jit(solution)/shard_map/all_gather | solution.py:84
  209.9 1.9 all-gather.6
  211.8 1.9 all-gather.2
  213.7 1.9 all-gather
  215.6 2.1 all-gather.4
  217.7 26.0 %all-gather.25.cloned.1.call-done = bf16[1,2,2,512,256]{4,3,2,1,0:T(8,128)(2,1)} async-done(((bf16[1,2,2,32,256]{4,3,2,1,0:T(8,128)(2,1)}), bf16[1,2,2,512,256]{4,3,2,1,0:T(8,128)(2,1)}) %all-gather.25.cloned.1.call-update) | async-done | bytes 1048592 | tf_op jit(solution)/shard_map/all_gather | solution.py:100
  246.9 41.0 %all-gather.21.cloned.1.call-done = bf16[1,2,2,512,256]{4,3,2,1,0:T(8,128)(2,1)} async-done(((bf16[1,2,2,32,256]{4,3,2,1,0:T(8,128)(2,1)}), bf16[1,2,2,512,256]{4,3,2,1,0:T(8,128)(2,1)}) %all-gather.21.cloned.1.call-update) | async-done | bytes 1048592 | tf_op jit(solution)/shard_map/all_gather | solution.py:100
  291.0 41.1 %all-gather.19.cloned.1.call-done = bf16[1,2,2,512,256]{4,3,2,1,0:T(8,128)(2,1)} async-done(((bf16[1,2,2,32,256]{4,3,2,1,0:T(8,128)(2,1)}), bf16[1,2,2,512,256]{4,3,2,1,0:T(8,128)(2,1)}) %all-gather.19.cloned.1.call-update) | async-done | bytes 1048592 | tf_op jit(solution)/shard_map/all_gather | solution.py:100
  335.8 40.6 %all-gather.23.cloned.1.call-done = bf16[1,2,2,512,256]{4,3,2,1,0:T(8,128)(2,1)} async-done(((bf16[1,2,2,32,256]{4,3,2,1,0:T(8,128)(2,1)}), bf16[1,2,2,512,256]{4,3,2,1,0:T(8,128)(2,1)}) %all-gather.23.cloned.1.call-update) | async-done | bytes 1048592 | tf_op jit(solution)/shard_map/all_gather | solution.py:100
  385.1 38.0 %all-gather.27.cloned.1.call-done = bf16[2,2,2,512,256]{4,3,2,1,0:T(8,128)(2,1)} async-done(((bf16[2,2,2,32,256]{4,3,2,1,0:T(8,128)(2,1)}), bf16[2,2,2,512,256]{4,3,2,1,0:T(8,128)(2,1)}) %all-gather.27.cloned.1.call-update) | async-done | bytes 2097168 | tf_op jit(solution)/shard_map/all_gather | solution.py:95
  448.1 21.5 %all-gather.29.cloned.1.call-done = bf16[2,2,2,512,256]{4,3,2,1,0:T(8,128)(2,1)} async-done(((bf16[2,2,2,32,256]{4,3,2,1,0:T(8,128)(2,1)}), bf16[2,2,2,512,256]{4,3,2,1,0:T(8,128)(2,1)}) %all-gather.29.cloned.1.call-update) | async-done | bytes 2097168 | tf_op jit(solution)/shard_map/all_gather | solution.py:95
  480.1 41.8 %all-reduce.2.cloned.1.call-done = bf16[27,32,256]{2,1,0:T(8,128)(2,1)} async-done(((bf16[27,32,256]{2,1,0:T(8,128)(2,1)}), bf16[27,32,256]{2,1,0:T(8,128)(2,1)}) %all-reduce.2.cloned.1.call-update) | async-done | bytes 442384 | tf_op jit(solution)/shard_map/psum | solution.py:133
  521.9 2.0 convert_element_type.978
  (222 shorter events, 91.7 us)
Async XLA Ops:
  6.5 43.2 %copy-start.13 = (bf16[1,7,2,32,256]{4,3,2,1,0:T(8,128)(2,1)S(1)}, bf16[1,7,2,32,256]{4,3,2,1,0:T(8,128)(2,1)}, u32[]{:S(2)}) copy-start(bf16[1,7,2,32,256]{4,3,2,1,0:T(8,128)(2,1)} %param.8) | copy-start | bytes 688132
  6.5 145.1 %all-gather.37.cloned.1.call-start = ((), (), s32[]{:S(2)}) async-start(), calls=%async_computation.10 | async-start | bytes 1114112 | tf_op jit(solution)/shard_map/all_gather | solution.py:84
  20.1 55.5 %copy-start.14 = (bf16[1,10,2,32,256]{4,3,2,1,0:T(8,128)(2,1)S(1)}, bf16[1,10,2,32,256]{4,3,2,1,0:T(8,128)(2,1)}, u32[]{:S(2)}) copy-start(bf16[1,10,2,32,256]{4,3,2,1,0:T(8,128)(2,1)} %param.7) | copy-start | bytes 983044
  20.7 138.4 %all-gather.33.cloned.1.call-start = ((), (), s32[]{:S(2)}) async-start(), calls=%async_computation.8 | async-start | bytes 1114112 | tf_op jit(solution)/shard_map/all_gather | solution.py:84
  21.5 142.5 %all-gather.31.cloned.1.call-start = ((), (), s32[]{:S(2)}) async-start(), calls=%async_computation.7 | async-start | bytes 1114112 | tf_op jit(solution)/shard_map/all_gather | solution.py:84
  22.2 177.4 %all-gather.35.cloned.1.call-start = ((), (), s32[]{:S(2)}) async-start(), calls=%async_computation.9 | async-start | bytes 1114112 | tf_op jit(solution)/shard_map/all_gather | solution.py:84
  22.9 220.8 %all-gather.25.cloned.1.call-start = ((), (), s32[]{:S(2)}) async-start(), calls=%async_computation.3 | async-start | bytes 1114112 | tf_op jit(solution)/shard_map/all_gather | solution.py:100
  149.7 6.9 %copy-start.2 = (bf16[2,2,2,32,256]{4,3,2,1,0:T(8,128)(2,1)}, bf16[2,2,2,32,256]{4,3,2,1,0:T(8,128)(2,1)S(1)}, u32[]{:S(2)}) copy-start(bf16[2,2,2,32,256]{4,3,2,1,0:T(8,128)(2,1)S(1)} %pad_maximum_fusion.1) | copy-start | bytes 393220
  156.4 131.4 %all-gather.21.cloned.1.call-start = ((), (), s32[]{:S(2)}) async-start(), calls=%async_computation.1 | async-start | bytes 1114112 | tf_op jit(solution)/shard_map/all_gather | solution.py:100
  157.2 8.2 %copy-start.3 = (bf16[2,2,2,32,256]{4,3,2,1,0:T(8,128)(2,1)}, bf16[2,2,2,32,256]{4,3,2,1,0:T(8,128)(2,1)S(1)}, u32[]{:S(2)}) copy-start(bf16[2,2,2,32,256]{4,3,2,1,0:T(8,128)(2,1)S(1)} %pad_maximum_fusion) | copy-start | bytes 393220
  163.9 168.3 %all-gather.19.cloned.1.call-start = ((), (), s32[]{:S(2)}) async-start(), calls=%async_computation | async-start | bytes 1114112 | tf_op jit(solution)/shard_map/all_gather | solution.py:100
  168.7 37.0 %copy-start.18 = (f32[1,2]{1,0:T(1,128)S(1)}, f32[1,2]{1,0:T(1,128)}, u32[]{:S(2)}) copy-start(f32[1,2]{1,0:T(1,128)} %param.9) | copy-start | bytes 28
  168.7 207.7 %all-gather.23.cloned.1.call-start = ((), (), s32[]{:S(2)}) async-start(), calls=%async_computation.2 | async-start | bytes 1114112 | tf_op jit(solution)/shard_map/all_gather | solution.py:100
  204.3 218.8 %all-gather.27.cloned.1.call-start = ((), (), s32[]{:S(2)}) async-start(), calls=%async_computation.4 | async-start | bytes 2228224 | tf_op jit(solution)/shard_map/all_gather | solution.py:95
  205.1 264.6 %all-gather.29.cloned.1.call-start = ((), (), s32[]{:S(2)}) async-start(), calls=%async_computation.5 | async-start | bytes 2228224 | tf_op jit(solution)/shard_map/all_gather | solution.py:95
  205.6 316.3 %all-reduce.2.cloned.1.call-start = ((), (), s32[]{:S(2)}) async-start(), calls=%async_computation.6 | async-start | bytes 884736 | tf_op jit(solution)/shard_map/psum | solution.py:133
  245.6 133.5 %copy-start.4 = (bf16[1,2,2,512,256]{4,3,2,1,0:T(8,128)(2,1)S(1)}, bf16[1,2,2,512,256]{4,3,2,1,0:T(8,128)(2,1)}, u32[]{:S(2)}) copy-start(bf16[1,2,2,512,256]{4,3,2,1,0:T(8,128)(2,1)} %all-gather.25.cloned.1.call-done) | copy-start | bytes 3145732
  289.7 90.6 %copy-start.5 = (bf16[1,2,2,512,256]{4,3,2,1,0:T(8,128)(2,1)S(1)}, bf16[1,2,2,512,256]{4,3,2,1,0:T(8,128)(2,1)}, u32[]{:S(2)}) copy-start(bf16[1,2,2,512,256]{4,3,2,1,0:T(8,128)(2,1)} %all-gather.21.cloned.1.call-done) | copy-start | bytes 3145732
  376.4 4.3 copy-start.6
  376.4 4.3 copy-start.17
  427.2 4.4 copy-start.10
  427.2 6.8 %copy-start.9 = (bf16[1,2,2,32,256]{4,3,2,1,0:T(8,128)(2,1)S(1)}, bf16[1,2,2,32,256]{4,3,2,1,0:T(8,128)(2,1)}, u32[]{:S(2)}) copy-start(bf16[1,2,2,32,256]{4,3,2,1,0:T(8,128)(2,1)} %fusion.65) | copy-start | bytes 196612
  427.2 9.2 %copy-start.11 = (bf16[1,2,2,32,256]{4,3,2,1,0:T(8,128)(2,1)S(1)}, bf16[1,2,2,32,256]{4,3,2,1,0:T(8,128)(2,1)}, u32[]{:S(2)}) copy-start(bf16[1,2,2,32,256]{4,3,2,1,0:T(8,128)(2,1)} %fusion.66) | copy-start | bytes 196612
  427.2 11.5 %copy-start.8 = (bf16[1,2,2,32,256]{4,3,2,1,0:T(8,128)(2,1)S(1)}, bf16[1,2,2,32,256]{4,3,2,1,0:T(8,128)(2,1)}, u32[]{:S(2)}) copy-start(bf16[1,2,2,32,256]{4,3,2,1,0:T(8,128)(2,1)} %fusion.67) | copy-start | bytes 196612
  (10 other events, 31.7 us)
Sparse Core Ops, SparseCore 0:
  20.9 45.7 all-gather.36
  68.8 42.0 all-gather.32
  113.1 42.2 all-gather.30
  157.4 42.1 all-gather.34
  201.6 42.0 all-gather.24
  245.7 42.0 all-gather.20
  290.0 42.0 all-gather.18
  334.3 42.0 all-gather.22
  378.6 44.5 all-gather.26
  425.1 44.5 all-gather.28
  480.2 41.6 all-reduce.1
where the time goes:
time: 532 us; the launch traced here: 530 us
  waiting for transfers between devices  282 us (53%)
  blocking collectives  134 us (25%)
  other arithmetic  52.7 us (10%)
  matrix products  44.6 us (8%)
  between operations  14.2 us (3%)
    all_gather x4, waiting for transfers between devices, solve_group(): lax.all_gather(below_tiles, 'row', axis=3, tiled=True)  149 us
    all_gather x2, waiting for transfers between devices, solve_group(): lax.all_gather(corner, 'row', axis=3, tiled=True)  59.5 us
    all_gather x2, blocking collectives, solve_group(): lower_full = lax.all_gather(lower_tiles, 'row', axis=3, tiled=True)  47.8 us
    all_gather x2, blocking collectives, solve_group(): lax.all_gather(below_tiles, 'row', axis=3, tiled=True)  45.3 us
    psum x1, waiting for transfers between devices, body(): return lax.psum(stacked.astype(jnp.bfloat16), 'pole').astype(jnp.float32)  41.8 us
    all_gather x4, waiting for transfers between devices, solve_group(): lower_full = lax.all_gather(lower_tiles, 'row', axis=3, tiled=True)  30.8 us
    unnamed x26, other arithmetic  30.4 us
    all_gather x1, blocking collectives, solve_group(): lax.all_gather(corner, 'row', axis=3, tiled=True)  23.6 us
  transfers between devices with their start and end apart: 11, of which 8 were waited for; matrix products, arithmetic and copies ran while one was open for 14% of the time, Pallas kernels for 0%

commit v1 on v0

v1 whole, which is shorter than its diff:
```python
import jax
import jax.numpy as jnp
from jax import lax
from jax.experimental import pallas as pl
from jax.experimental.pallas import tpu as pltpu
from jax.sharding import PartitionSpec as P

BF = jnp.bfloat16
F32 = jnp.float32
VMEM_LIMIT = 48 * 1024 * 1024


def ring_y(step):
    return [(z * 4 + y, z * 4 + (y + step) % 4) for z in range(4) for y in range(4)]


def ring_z(step):
    return [(z * 4 + y, ((z + step) % 4) * 4 + y) for z in range(4) for y in range(4)]


def ring_x(step):
    return [(x, (x + step) % 4) for x in range(4)]


SWAP = [(0, 1), (1, 0)]


def place():
    row = lax.axis_index("row")
    return lax.axis_index("pole"), lax.div(row, 4), lax.rem(row, 4), lax.axis_index("col")


def node_of(y):
    return 3 + 2 * lax.rem(y, 2) + lax.div(y, 2)


def vm():
    return pl.BlockSpec(memory_space=pltpu.VMEM)


def sm():
    return pl.BlockSpec(memory_space=pltpu.SMEM)


def hbm():
    return pl.BlockSpec(memory_space=pl.ANY)


def call(kernel, outs, in_specs, out_specs, scratch=(), flops=0, nbytes=0):
    return pl.pallas_call(
        kernel,
        out_shape=outs,
        in_specs=in_specs,
        out_specs=out_specs,
        scratch_shapes=list(scratch),
        compiler_params=pltpu.CompilerParams(vmem_limit_bytes=VMEM_LIMIT),
        cost_estimate=pl.CostEstimate(flops=flops, bytes_accessed=nbytes, transcendentals=0),
    )


def shape(*dims, dtype=BF):
    return jax.ShapeDtypeStruct(dims, dtype)


def pack_kernel(low, up, dia, widths, pattern, zbuf, y0, y1, y2, y3):
    x, z, y, c = place()
    rows = (32 * (4 * z + y)) + lax.broadcasted_iota(jnp.int32, (32, 256), 0)
    cols = (256 * c) + lax.broadcasted_iota(jnp.int32, (32, 256), 1)

    def masked(tile, row_node, col_node, on):
        keep = (rows < widths[row_node]) & (cols < widths[col_node]) & (on != 0)
        return jnp.where(keep[None], tile.astype(F32), 0.0).astype(BF)

    zbuf[0] = masked(dia[0], 0, 0, 1)
    for i in range(2):
        zbuf[1 + 2 * i] = masked(up[i], 1 + i, 0, pattern[i])
        zbuf[2 + 2 * i] = masked(low[i], 0, 1 + i, pattern[i])
    for d, out in enumerate((y0, y1, y2, y3)):
        k = node_of(lax.rem(y + d, 4))
        p = lax.div(k - 1, 2)
        at = 2 * (k - 3) + 2
        out[0] = masked(dia[p], p, p, 1)
        out[1] = masked(low[at], p, k, pattern[at])
        out[2] = masked(low[at + 1], 0, k, pattern[at + 1])
        out[3] = masked(up[at], k, p, pattern[at])
        out[4] = masked(up[at + 1], k, 0, pattern[at + 1])
        out[5] = masked(dia[k], k, k, 1)


def merge_z_kernel(b0, b1, b2, b3, own, other, sems):
    x, z, y, c = place()
    p = lax.rem(y, 2)
    copies = []
    for d, buf in enumerate((b0, b1, b2, b3)):
        at = lax.rem(z + 4 - d, 4)
        copies.append((buf.at[0], own.at[0, :, at]))
        copies.append((buf.at[0], other.at[0, :, at]))
        copies.append((buf.at[pl.ds(1 + 2 * p, 2)], own.at[pl.ds(1, 2), :, at]))
        copies.append((buf.at[pl.ds(3 - 2 * p, 2)], other.at[pl.ds(1, 2), :, at]))
    run_copies(copies, sems)


def run_copies(copies, sems):
    made = [pltpu.make_async_copy(s, t, sems.at[i]) for i, (s, t) in enumerate(copies)]
    for m in made:
        m.start()
    for m in made:
        m.wait()


def merge_y_kernel(b0, b1, b2, b3, zb, uk, dk, sems):
    x, z, y, c = place()
    copies = []
    for d, buf in enumerate((b0, b1, b2, b3)):
        at = lax.rem(y + 4 - d, 4)
        copies.append((buf.at[pl.ds(0, 3)], zb.at[:, :, at]))
        copies.append((buf.at[pl.ds(3, 2)], uk.at[:, :, at]))
        copies.append((buf.at[5], dk.at[:, at]))
    run_copies(copies, sems)


def left_of(pairs):
    real = [jnp.concatenate([r, -i], axis=1) for r, i in pairs]
    imag = [jnp.concatenate([i, r], axis=1) for r, i in pairs]
    return jnp.concatenate(real + imag, axis=0)


def dot(a, b):
    return jnp.dot(a, b, preferred_element_type=F32)


def pairs_of(res, count):
    half = 128 * count
    return [
        (res[128 * i : 128 * i + 128], res[half + 128 * i : half + 128 * i + 128])
        for i in range(count)
    ]


def first_kernel(
    o0, o1, o2, o3, s0, s1, s2, s3, z0, z1, z2, z3, uko, uks, res,
    edge, wide, dens, right, zright, ukf, sems,
):
    x, z, y, c = place()
    copies = []
    for d, (mine, swapped) in enumerate(((o0, s0), (o1, s1), (o2, s2), (o3, s3))):
        at = lax.rem(y + 4 - d, 4)
        copies.append((mine, right.at[c, :, :, :, at]))
        copies.append((swapped, right.at[1 - c, :, :, :, at]))
    for d, buf in enumerate((z0, z1, z2, z3)):
        at = lax.rem(z + 4 - d, 4)
        copies.append((buf.at[pl.ds(0, 1)], zright.at[:, :, at]))
    copies.append((uko, ukf.at[c]))
    copies.append((uks, ukf.at[1 - c]))
    run_copies(copies, sems)

    def operand(half, block):
        return right[half, block].reshape(1024, 256)

    def wide_rows(get):
        return tuple(jnp.concatenate([get(0, part), get(1, part)], axis=1) for part in range(2))

    ukp = wide_rows(lambda h, part: ukf[h, 0, part].reshape(128, 256))
    d0r = wide_rows(lambda h, part: right[h, 0, part, z].reshape(128, 256))
    upr = wide_rows(lambda h, part: right[h, 1, part, z].reshape(128, 256))
    ukp_left = left_of([ukp])
    halves = []
    for h in range(2):
        ((re, im),) = pairs_of(dot(ukp_left, operand(h, 1)), 1)
        halves.append(
            (
                (ukf[h, 1, 0].reshape(128, 256).astype(F32) - re).astype(BF),
                (ukf[h, 1, 1].reshape(128, 256).astype(F32) - im).astype(BF),
            )
        )
    v = tuple(jnp.concatenate([halves[0][i], halves[1][i]], axis=1) for i in range(2))
    left = left_of([v, upr])
    outs = []
    for h in range(2):
        got = pairs_of((-dot(left, operand(h, 0))).astype(BF), 2)
        outs.append(got)
    xk0 = tuple(jnp.concatenate([outs[0][0][i], outs[1][0][i]], axis=1) for i in range(2))
    xp0 = tuple(jnp.concatenate([outs[0][1][i], outs[1][1][i]], axis=1) for i in range(2))
    for i in range(2):
        wide[0, i] = xp0[i]
        wide[1, i] = d0r[i]
        wide[2, i] = xk0[i]
    kl, pl_, dl = pairs_of(dot(left_of([xk0, xp0, d0r]), right[c, 2].reshape(1024, 256)), 3)
    (kd,) = pairs_of(dot(ukp_left, zright[0].reshape(1024, 256)), 1)
    xkp = [-(kd[i] + kl[i]) for i in range(2)]
    xpp = [zright[0, i, z].reshape(128, 256).astype(F32) - pl_[i] for i in range(2)]
    x0p = [-dl[i] for i in range(2)]
    for i in range(2):
        edge[0, i] = xpp[i].astype(BF)
        edge[1, i] = x0p[i].astype(BF)
        edge[2, i] = xkp[i].astype(BF)
    wr, wi = res[0, 0], res[0, 1]

    def density(re, im):
        return wr * re.astype(F32) - wi * im.astype(F32)

    def half_of(block, part):
        return wide[block, part, :, pl.ds(pl.multiple_of(c * 256, 256), 256)]

    dens[0] = density(*xkp)
    dens[1] = density(half_of(2, 0), half_of(2, 1))
    a = density(*xpp)
    b = density(half_of(0, 0), half_of(0, 1))
    e = density(*x0p)
    f = density(half_of(1, 0), half_of(1, 1))
    dens[2] = jnp.where(y < 2, a, b)
    dens[3] = jnp.where(y < 2, f, e)


def second_kernel(
    edge_o, edge_s, wide, dens, z0, z1, z2, z3, dk, res,
    slot0, slot1, slot2, slot3, zright, slots, sems,
):
    x, z, y, c = place()
    copies = []
    for d, buf in enumerate((z0, z1, z2, z3)):
        at = lax.rem(z + 4 - d, 4)
        copies.append((buf.at[pl.ds(1, 2)], zright.at[:, :, at]))
    run_copies(copies, sems)

    first = c == 0

    def full(block):
        out = []
        for i in range(2):
            a, b = edge_o[block, i], edge_s[block, i]
            out.append(
                jnp.concatenate([jnp.where(first, a, b), jnp.where(first, b, a)], axis=1)
            )
        return tuple(out)

    left_p = left_of([full(0), full(1), full(2)])
    left_0 = left_of([(wide[i, 0], wide[i, 1]) for i in range(3)])
    total = dot(left_p, zright[0].reshape(1024, 256)) + dot(left_0, zright[1].reshape(1024, 256))
    pk, ok, kk = pairs_of(total, 3)
    wr, wi = res[0, 0], res[0, 1]
    parts = [
        wr * (dk[0].reshape(128, 256).astype(F32) - kk[0])
        - wi * (dk[1].reshape(128, 256).astype(F32) - kk[1]),
        wi * pk[1] - wr * pk[0],
        wi * ok[1] - wr * ok[0],
    ] + [dens[i] for i in range(4)]
    for s in range(4):
        for t in range(4):
            for b, part in enumerate(parts):
                lo = 32 * t + 8 * s
                slots[s, t, 8 * b : 8 * b + 8] = part[lo : lo + 8]
    for d, out in enumerate((slot0, slot1, slot2, slot3)):
        out[...] = slots[lax.rem(x + d, 4)].astype(BF)


def sum_kernel(a0, a1, a2, a3, t0, t1, t2, t3, acc):
    x, z, y, c = place()
    acc[...] = (
        a0[...].astype(F32) + a1[...].astype(F32) + a2[...].astype(F32) + a3[...].astype(F32)
    )
    for d, out in enumerate((t0, t1, t2, t3)):
        out[...] = acc[lax.rem(y + d, 4)].astype(BF)


def gather_kernel(t0, t1, t2, t3, out):
    x, z, y, c = place()
    for d, t in enumerate((t0, t1, t2, t3)):
        out[lax.rem(y + 4 - d, 4)] = t[...]


NODE = (3, 5, 4, 6)


def out_index(y):
    k = NODE[y]
    p = 1 + y % 2
    pair = 2 * (k - 3) + 2
    first = [k, 7 + pair, 7 + pair + 1, 17 + pair, 17 + pair + 1]
    if y < 2:
        return first + [p, 0 if y == 0 else None]
    return first + [17 + p - 1, 7 + p - 1]


def final_kernel(g0, g1, g2, g3, out):
    x, z, y, c = place()
    for d, g in enumerate((g0, g1, g2, g3)):
        at = pl.multiple_of(8 * lax.rem(x + 4 - d, 4), 8)
        for s in range(4):
            rows = g[s].astype(F32)
            for b, index in enumerate(out_index(s)):
                if index is not None:
                    out[index, pl.ds(at, 8), :] = rows[8 * b : 8 * b + 8]


def body(lower_factor, upper_factor, diag_inverse, residues, widths, pattern):
    lower, upper, diag = lower_factor[0], upper_factor[0], diag_inverse[0]
    tile = (2, 32, 256)
    zbuf, *ybuf = call(
        pack_kernel,
        [shape(5, *tile)] + [shape(6, *tile)] * 4,
        [vm(), vm(), vm(), sm(), sm()],
        [vm()] * 5,
        nbytes=2 << 20,
    )(lower, upper, diag, widths, pattern)
    y_in = [ybuf[0]] + [lax.ppermute(ybuf[d], "row", ring_y(d)) for d in (1, 2, 3)]
    z_in = [zbuf] + [lax.ppermute(zbuf, "row", ring_z(d)) for d in (1, 2, 3)]
    zb, uk, dk = call(
        merge_y_kernel,
        [shape(3, 2, 4, 32, 256), shape(2, 2, 4, 32, 256), shape(2, 4, 32, 256)],
        [hbm()] * 4,
        [hbm()] * 3,
        [pltpu.SemaphoreType.DMA((12,))],
        nbytes=2 << 20,
    )(*y_in)
    own, other = call(
        merge_z_kernel,
        [shape(3, 2, 4, 32, 256)] * 2,
        [hbm()] * 4,
        [hbm()] * 2,
        [pltpu.SemaphoreType.DMA((16,))],
        nbytes=2 << 20,
    )(*z_in)
    zz = [zb] + [lax.ppermute(zb, "row", ring_z(d)) for d in (1, 2, 3)]
    yy = [own] + [lax.ppermute(own if d == 2 else other, "row", ring_y(d)) for d in (1, 2, 3)]
    uks = lax.ppermute(uk, "col", SWAP)
    ss = [lax.ppermute(a, "col", SWAP) for a in yy]
    edge, wide, dens = call(
        first_kernel,
        [shape(3, 2, 128, 256), shape(3, 2, 128, 512), shape(4, 128, 256, dtype=F32)],
        [hbm()] * 14 + [sm()],
        [vm()] * 3,
        [
            pltpu.VMEM((2, 3, 2, 4, 4, 32, 256), BF),
            pltpu.VMEM((1, 2, 4, 4, 32, 256), BF),
            pltpu.VMEM((2, 2, 2, 4, 32, 256), BF),
            pltpu.SemaphoreType.DMA((14,)),
        ],
        flops=1342177280,
        nbytes=4 << 20,
    )(*yy, *ss, *zz, uk, uks, residues)
    edge_s = lax.ppermute(edge, "col", SWAP)
    slots = call(
        second_kernel,
        [shape(4, 56, 256)] * 4,
        [vm()] * 4 + [hbm()] * 4 + [vm(), sm()],
        [vm()] * 4,
        [
            pltpu.VMEM((2, 2, 4, 4, 32, 256), BF),
            pltpu.VMEM((4, 4, 56, 256), F32),
            pltpu.SemaphoreType.DMA((4,)),
        ],
        flops=805306368,
        nbytes=4 << 20,
    )(edge, edge_s, wide, dens, *zz, dk, residues)
    at_x = [slots[0]] + [lax.ppermute(slots[d], "pole", ring_x(d)) for d in (1, 2, 3)]
    sums = call(
        sum_kernel,
        [shape(56, 256)] * 4,
        [vm()] * 4,
        [vm()] * 4,
        [pltpu.VMEM((4, 56, 256), F32)],
        nbytes=1 << 20,
    )(*at_x)
    at_y = [sums[0]] + [lax.ppermute(sums[d], "row", ring_y(d)) for d in (1, 2, 3)]
    mine = call(
        gather_kernel, [shape(4, 56, 256)], [vm()] * 4, [vm()], nbytes=1 << 18
    )(*at_y)[0]
    full = [mine] + [lax.ppermute(mine, "pole", ring_x(d)) for d in (1, 2, 3)]
    return call(
        final_kernel, [shape(27, 32, 256, dtype=F32)], [vm()] * 4, [vm()], nbytes=2 << 20
    )(*full)[0]


def solution(mesh):
    return jax.shard_map(
        body,
        mesh=mesh,
        in_specs=(
            P("pole", None, None, "row", "col"),
            P("pole", None, None, "row", "col"),
            P("pole", None, None, "row", "col"),
            P("pole", None),
            P(),
            P(),
        ),
        out_specs=P(None, "row", "col"),
        check_vma=False,
    )
```

time: 532 us -> 105 us (0.20)
  waiting for transfers between devices: 282 us -> 58.1 us
  blocking collectives: 134 us -> 0 us
  other arithmetic: 52.7 us -> 0 us
  matrix products: 44.6 us -> 0 us
  starting transfers between devices: 0.41 us -> 33.6 us
  between operations: 14.2 us -> 0.13 us
  Pallas kernels: 0 us -> 8.49 us
    all_gather x10 -> x0, waiting for transfers between devices: 239 us -> none  [the longest x4 149 us: solve_group(): lax.all_gather(below_tiles, 'row', axis=3, tiled=True)]
    all_gather x14 -> x0, blocking collectives: 134 us -> none  [the longest x2 47.8 us: solve_group(): lower_full = lax.all_gather(lower_tiles, 'row', axis=3, tiled=True)]
    ppermute x0 -> x27, waiting for transfers between devices: none -> 58.1 us  [the longest x3 15.9 us: body(): lax.ppermute(own if d == 2 else other, 'row', ring_y(d))]
    dot_general x72 -> x0, matrix products: 44.6 us -> none  [the longest x18 16.9 us: complex_product(): jnp.einsum(form, real_left, imag_right, preferred_element_type=jnp.float32)]
    psum x1 -> x0, waiting for transfers between devices: 41.8 us -> none  [body(): return lax.psum(stacked.astype(jnp.bfloat16), 'pole').astype(jnp.float32)]
    ppermute x0 -> x27, starting transfers between devices: none -> 33.6 us  [the longest x3 5.98 us: body(): lax.ppermute(ybuf[d], 'row', ring_y(d))]
    unnamed x26 -> x0, other arithmetic: 30.4 us -> none
    mul x13 -> x0, other arithmetic: 11.6 us -> none  [the longest x3 5.33 us: uhat(): pattern_mask[index] * row_keep[member][:, None] * col_keep[above][None, :]]
  transfers between devices with their start and end apart: 11 -> 27, of which waited for: 8 -> 18; matrix products, arithmetic and copies ran while one was open for 14% -> 0% of each run, Pallas kernels for 0% -> 0%
where the time goes in v1:
time: 105 us
  waiting for transfers between devices  58.1 us (55%)
  starting transfers between devices  33.6 us (32%)
  Pallas kernels  8.49 us (8%)
  local copies, waits for them, and re-layouts  4.69 us (4%)
    ppermute x3, waiting for transfers between devices, body(): lax.ppermute(own if d == 2 else other, 'row', ring_y(d))  15.9 us
    ppermute x3, waiting for transfers between devices, body(): z_in = [zbuf] + [lax.ppermute(zbuf, 'row', ring_z(d)) for d in (1, 2, 3)]  9.73 us
    ppermute x3, waiting for transfers between devices, body(): zz = [zb] + [lax.ppermute(zb, 'row', ring_z(d)) for d in (1, 2, 3)]  9.5 us
    ppermute x3, waiting for transfers between devices, body(): lax.ppermute(ybuf[d], 'row', ring_y(d))  7.48 us
    ppermute x3, starting transfers between devices, body(): lax.ppermute(ybuf[d], 'row', ring_y(d))  5.98 us
    ppermute x3, starting transfers between devices, body(): lax.ppermute(slots[d], 'pole', ring_x(d))  5.73 us
    ppermute x3, waiting for transfers between devices, body(): full = [mine] + [lax.ppermute(mine, 'pole', ring_x(d)) for d in (1, 2, 3)]  5.69 us
    ppermute x3, starting transfers between devices, body(): z_in = [zbuf] + [lax.ppermute(zbuf, 'row', ring_z(d)) for d in (1, 2, 3)]  5.37 us
  transfers between devices with their start and end apart: 27, of which 18 were waited for; matrix products, arithmetic and copies ran while one was open for 0% of the time, Pallas kernels for 0%

profile of v1, /device:TPU:0, one launch (start us, length us, event | category | flops | bytes accessed | tf_op | source)
XLA Modules:
  0.0 105.0 jit_solution(14693421801985392146)
XLA Ops:
  4.4 1.7 %collective-permute-start.10 = (bf16[6,2,32,256]{3,2,1,0:T(8,128)(2,1)S(1)}, bf16[6,2,32,256]{3,2,1,0:T(8,128)(2,1)S(1)}, u32[]{:S(2)}, u32[]{:S(2)}) collective-permute-start(bf16[6,2,32,256]{3,2,1,0:T(8,128)(2,1)S(1)} %get-tuple-element.30), channel_id=1, source_target_pairs={{0,2},{2,4},{4,6},{6,0},{8,10},{10,12},{12,14},{14,8},{16,18},{18,... | collective-permute-start | bytes 589832 | tf_op jit(solution)/shard_map/ppermute | solution.py:306
  6.1 2.9 %collective-permute-start.11 = (bf16[6,2,32,256]{3,2,1,0:T(8,128)(2,1)S(1)}, bf16[6,2,32,256]{3,2,1,0:T(8,128)(2,1)S(1)}, u32[]{:S(2)}, u32[]{:S(2)}) collective-permute-start(bf16[6,2,32,256]{3,2,1,0:T(8,128)(2,1)S(1)} %get-tuple-element.31), channel_id=1, source_target_pairs={{0,4},{2,6},{4,0},{6,2},{8,12},{10,14},{12,8},{14,10},{16,20},{18,... | collective-permute-start | bytes 589832 | tf_op jit(solution)/shard_map/ppermute | solution.py:306
  10.4 2.1 %collective-permute-done.10.b1 = bf16[6,2,32,256]{3,2,1,0:T(8,128)(2,1)S(1)} collective-permute-done((bf16[6,2,32,256]{3,2,1,0:T(8,128)(2,1)S(1)}, bf16[6,2,32,256]{3,2,1,0:T(8,128)(2,1)S(1)}, u32[]{:S(2)}, u32[]{:S(2)}) %collective-permute-start.10) | collective-permute-done | bytes 196640 | tf_op jit(solution)/shard_map/ppermute | solution.py:306
  12.5 5.4 %collective-permute-done.11.b2 = bf16[6,2,32,256]{3,2,1,0:T(8,128)(2,1)S(1)} collective-permute-done((bf16[6,2,32,256]{3,2,1,0:T(8,128)(2,1)S(1)}, bf16[6,2,32,256]{3,2,1,0:T(8,128)(2,1)S(1)}, u32[]{:S(2)}, u32[]{:S(2)}) %collective-permute-start.11) | collective-permute-done | bytes 196640 | tf_op jit(solution)/shard_map/ppermute | solution.py:306
  18.3 4.1 %collective-permute-start.2 = (bf16[5,2,32,256]{3,2,1,0:T(8,128)(2,1)S(1)}, bf16[5,2,32,256]{3,2,1,0:T(8,128)(2,1)S(1)}, u32[]{:S(2)}, u32[]{:S(2)}) collective-permute-start(bf16[5,2,32,256]{3,2,1,0:T(8,128)(2,1)S(1)} %get-tuple-element.26.b0), channel_id=1, source_target_pairs={{0,24},{2,26},{4,28},{6,30},{8,0},{10,2},{12,4},{14,6},{16,8},{18,... | collective-permute-start | bytes 491528 | tf_op jit(solution)/shard_map/ppermute | solution.py:307
  23.7 6.3 %collective-permute-done.2.b3 = bf16[5,2,32,256]{3,2,1,0:T(8,128)(2,1)S(1)} collective-permute-done((bf16[5,2,32,256]{3,2,1,0:T(8,128)(2,1)S(1)}, bf16[5,2,32,256]{3,2,1,0:T(8,128)(2,1)S(1)}, u32[]{:S(2)}, u32[]{:S(2)}) %collective-permute-start.2) | collective-permute-done | bytes 163872 | tf_op jit(solution)/shard_map/ppermute | solution.py:307
  31.0 2.4 %collective-permute-done.b1 = bf16[5,2,32,256]{3,2,1,0:T(8,128)(2,1)S(1)} collective-permute-done((bf16[5,2,32,256]{3,2,1,0:T(8,128)(2,1)S(1)}, bf16[5,2,32,256]{3,2,1,0:T(8,128)(2,1)S(1)}, u32[]{:S(2)}, u32[]{:S(2)}) %collective-permute-start) | collective-permute-done | bytes 163872 | tf_op jit(solution)/shard_map/ppermute | solution.py:307
  33.9 2.2 %collective-permute-start.5 = (bf16[3,2,4,32,256]{4,3,2,1,0:T(8,128)(2,1)S(1)}, bf16[3,2,4,32,256]{4,3,2,1,0:T(8,128)(2,1)S(1)}, u32[]{:S(2)}, u32[]{:S(2)}) collective-permute-start(bf16[3,2,4,32,256]{4,3,2,1,0:T(8,128)(2,1)S(1)} %get-tuple-element.28), channel_id=1, source_target_pairs={{0,6},{2,0},{4,2},{6,4},{8,14},{10,8},{12,10},{14,12},{16,22},{18,... | collective-permute-start | bytes 1179656 | tf_op jit(solution)/shard_map/ppermute | solution.py:325
  36.2 2.4 %collective-permute-start.4 = (bf16[3,2,4,32,256]{4,3,2,1,0:T(8,128)(2,1)S(1)}, bf16[3,2,4,32,256]{4,3,2,1,0:T(8,128)(2,1)S(1)}, u32[]{:S(2)}, u32[]{:S(2)}) collective-permute-start(bf16[3,2,4,32,256]{4,3,2,1,0:T(8,128)(2,1)S(1)} %get-tuple-element.27.o0), channel_id=1, source_target_pairs={{0,4},{2,6},{4,0},{6,2},{8,12},{10,14},{12,8},{14,10},{16,20},{18,... | collective-permute-start | bytes 1179656 | tf_op jit(solution)/shard_map/ppermute | solution.py:325
  39.5 13.4 %collective-permute-done.5.o3 = bf16[3,2,4,32,256]{4,3,2,1,0:T(8,128)(2,1)S(1)} collective-permute-done((bf16[3,2,4,32,256]{4,3,2,1,0:T(8,128)(2,1)S(1)}, bf16[3,2,4,32,256]{4,3,2,1,0:T(8,128)(2,1)S(1)}, u32[]{:S(2)}, u32[]{:S(2)}) %collective-permute-start.5) | collective-permute-done | bytes 393248 | tf_op jit(solution)/shard_map/ppermute | solution.py:325
  53.7 2.5 %collective-permute-done.3.o1 = bf16[3,2,4,32,256]{4,3,2,1,0:T(8,128)(2,1)S(1)} collective-permute-done((bf16[3,2,4,32,256]{4,3,2,1,0:T(8,128)(2,1)S(1)}, bf16[3,2,4,32,256]{4,3,2,1,0:T(8,128)(2,1)S(1)}, u32[]{:S(2)}, u32[]{:S(2)}) %collective-permute-start.3) | collective-permute-done | bytes 393248 | tf_op jit(solution)/shard_map/ppermute | solution.py:325
  56.9 5.4 %collective-permute-done.14.z2 = bf16[3,2,4,32,256]{4,3,2,1,0:T(8,128)(2,1)S(1)} collective-permute-done((bf16[3,2,4,32,256]{4,3,2,1,0:T(8,128)(2,1)S(1)}, bf16[3,2,4,32,256]{4,3,2,1,0:T(8,128)(2,1)S(1)}, u32[]{:S(2)}, u32[]{:S(2)}) %collective-permute-start.14) | collective-permute-done | bytes 393248 | tf_op jit(solution)/shard_map/ppermute | solution.py:324
  62.3 4.1 %collective-permute-done.13.z1 = bf16[3,2,4,32,256]{4,3,2,1,0:T(8,128)(2,1)S(1)} collective-permute-done((bf16[3,2,4,32,256]{4,3,2,1,0:T(8,128)(2,1)S(1)}, bf16[3,2,4,32,256]{4,3,2,1,0:T(8,128)(2,1)S(1)}, u32[]{:S(2)}, u32[]{:S(2)}) %collective-permute-start.13) | collective-permute-done | bytes 393248 | tf_op jit(solution)/shard_map/ppermute | solution.py:324
  66.4 4.0 %shard_map.67 = (bf16[3,2,128,256]{3,2,1,0:T(8,128)(2,1)S(1)}, bf16[3,2,128,512]{3,2,1,0:T(8,128)(2,1)}, f32[4,128,256]{2,1,0:T(8,128)S(1)}) custom-call(bf16[3,2,4,32,256]{4,3,2,1,0:T(8,128)(2,1)S(1)} %get-tuple-element.27.o0, bf16[3,2,4,32,256]{4,3,2,1,0:T(8,128)(2,1)S(1)} %collective-permute-done.3.o1, ...), custom_call_target="tpu_custom_call" | custom-call | flops 1342177280 | bytes 4194304 | tf_op jit(solution)/shard_map/pallas_call | solution.py:328
  70.5 1.7 %collective-permute-done.17.edge_s = bf16[3,2,128,256]{3,2,1,0:T(8,128)(2,1)S(1)} collective-permute-done((bf16[3,2,128,256]{3,2,1,0:T(8,128)(2,1)S(1)}, bf16[3,2,128,256]{3,2,1,0:T(8,128)(2,1)S(1)}, u32[]{:S(2)}, u32[]{:S(2)}) %collective-permute-start.17) | collective-permute-done | bytes 393248 | tf_op jit(solution)/shard_map/ppermute | solution.py:342
  73.3 1.7 %shard_map.68 = (bf16[4,56,256]{2,1,0:T(8,128)(2,1)S(1)}, bf16[4,56,256]{2,1,0:T(8,128)(2,1)S(1)}, bf16[4,56,256]{2,1,0:T(8,128)(2,1)S(1)}, bf16[4,56,256]{2,1,0:T(8,128)(2,1)S(1)}) custom-call(bf16[3,2,128,256]{3,2,1,0:T(8,128)(2,1)S(1)} %get-tuple-element.35.edge_o, bf16[3,2,128,256]{3,2,1,0:T(8,128)(2,1)S(1)} %collective-permute-done.17.edge_s, ...), custom_call_target="tpu_custom_call" | custom-call | flops 805306368 | bytes 4194304 | tf_op jit(solution)/shard_map/pallas_call | solution.py:343
  75.1 1.6 %collective-permute-start.18 = (bf16[4,56,256]{2,1,0:T(8,128)(2,1)S(1)}, bf16[4,56,256]{2,1,0:T(8,128)(2,1)S(1)}, u32[]{:S(2)}, u32[]{:S(2)}) collective-permute-start(bf16[4,56,256]{2,1,0:T(8,128)(2,1)S(1)} %get-tuple-element.40), channel_id=1, source_target_pairs={{0,32},{32,64},{64,96},{96,0},{1,33},{33,65},{65,97},{97,1},{2,34}... | collective-permute-start | bytes 344072 | tf_op jit(solution)/shard_map/ppermute | solution.py:356
  76.7 2.7 %collective-permute-start.19 = (bf16[4,56,256]{2,1,0:T(8,128)(2,1)S(1)}, bf16[4,56,256]{2,1,0:T(8,128)(2,1)S(1)}, u32[]{:S(2)}, u32[]{:S(2)}) collective-permute-start(bf16[4,56,256]{2,1,0:T(8,128)(2,1)S(1)} %get-tuple-element.41), channel_id=1, source_target_pairs={{0,64},{32,96},{64,0},{96,32},{1,65},{33,97},{65,1},{97,33},{2,66}... | collective-permute-start | bytes 344072 | tf_op jit(solution)/shard_map/ppermute | solution.py:356
  81.6 3.5 %collective-permute-done.19.a2 = bf16[4,56,256]{2,1,0:T(8,128)(2,1)S(1)} collective-permute-done((bf16[4,56,256]{2,1,0:T(8,128)(2,1)S(1)}, bf16[4,56,256]{2,1,0:T(8,128)(2,1)S(1)}, u32[]{:S(2)}, u32[]{:S(2)}) %collective-permute-start.19) | collective-permute-done | bytes 114720 | tf_op jit(solution)/shard_map/ppermute | solution.py:356
  85.2 5.1 %collective-permute-start.22 = (bf16[56,256]{1,0:T(8,128)(2,1)S(1)}, bf16[56,256]{1,0:T(8,128)(2,1)S(1)}, u32[]{:S(2)}, u32[]{:S(2)}) collective-permute-start(bf16[56,256]{1,0:T(8,128)(2,1)S(1)} %get-tuple-element.45), channel_id=1, source_target_pairs={{0,4},{2,6},{4,0},{6,2},{8,12},{10,14},{12,8},{14,10},{16,20},{18,... | collective-permute-start | bytes 86024 | tf_op jit(solution)/shard_map/ppermute | solution.py:365
  91.0 1.5 %collective-permute-done.22.t2 = bf16[56,256]{1,0:T(8,128)(2,1)S(1)} collective-permute-done((bf16[56,256]{1,0:T(8,128)(2,1)S(1)}, bf16[56,256]{1,0:T(8,128)(2,1)S(1)}, u32[]{:S(2)}, u32[]{:S(2)}) %collective-permute-start.22) | collective-permute-done | bytes 28704 | tf_op jit(solution)/shard_map/ppermute | solution.py:365
  92.4 1.7 %collective-permute-done.23.t3 = bf16[56,256]{1,0:T(8,128)(2,1)S(1)} collective-permute-done((bf16[56,256]{1,0:T(8,128)(2,1)S(1)}, bf16[56,256]{1,0:T(8,128)(2,1)S(1)}, u32[]{:S(2)}, u32[]{:S(2)}) %collective-permute-start.23) | collective-permute-done | bytes 28704 | tf_op jit(solution)/shard_map/ppermute | solution.py:365
  94.2 2.3 %collective-permute-start.26 = (bf16[4,56,256]{2,1,0:T(8,128)(2,1)S(1)}, bf16[4,56,256]{2,1,0:T(8,128)(2,1)S(1)}, u32[]{:S(2)}, u32[]{:S(2)}) collective-permute-start(bf16[4,56,256]{2,1,0:T(8,128)(2,1)S(1)} %shard_map.70.g0), channel_id=1, source_target_pairs={{0,96},{32,0},{64,32},{96,64},{1,97},{33,1},{65,33},{97,65},{2,98}... | collective-permute-start | bytes 344072 | tf_op jit(solution)/shard_map/ppermute | solution.py:369
  99.0 3.8 %collective-permute-done.25.g2 = bf16[4,56,256]{2,1,0:T(8,128)(2,1)S(1)} collective-permute-done((bf16[4,56,256]{2,1,0:T(8,128)(2,1)S(1)}, bf16[4,56,256]{2,1,0:T(8,128)(2,1)S(1)}, u32[]{:S(2)}, u32[]{:S(2)}) %collective-permute-start.25) | collective-permute-done | bytes 114720 | tf_op jit(solution)/shard_map/ppermute | solution.py:369
  (52 shorter events, 20.3 us)
Async XLA Ops:
  4.4 8.1 %collective-permute-start.10 = (bf16[6,2,32,256]{3,2,1,0:T(8,128)(2,1)S(1)}, bf16[6,2,32,256]{3,2,1,0:T(8,128)(2,1)S(1)}, u32[]{:S(2)}, u32[]{:S(2)}) collective-permute-start(bf16[6,2,32,256]{3,2,1,0:T(8,128)(2,1)S(1)} %get-tuple-element.30), channel_id=1, source_target_pairs={{0,2},{2,4},{4,6},{6,0},{8,10},{10,12},{12,14},{14,8},{16,18},{18,... | collective-permute-start | bytes 589832 | tf_op jit(solution)/shard_map/ppermute | solution.py:306
  6.1 11.7 %collective-permute-start.11 = (bf16[6,2,32,256]{3,2,1,0:T(8,128)(2,1)S(1)}, bf16[6,2,32,256]{3,2,1,0:T(8,128)(2,1)S(1)}, u32[]{:S(2)}, u32[]{:S(2)}) collective-permute-start(bf16[6,2,32,256]{3,2,1,0:T(8,128)(2,1)S(1)} %get-tuple-element.31), channel_id=1, source_target_pairs={{0,4},{2,6},{4,0},{6,2},{8,12},{10,14},{12,8},{14,10},{16,20},{18,... | collective-permute-start | bytes 589832 | tf_op jit(solution)/shard_map/ppermute | solution.py:306
  9.0 8.8 %collective-permute-start.12 = (bf16[6,2,32,256]{3,2,1,0:T(8,128)(2,1)S(1)}, bf16[6,2,32,256]{3,2,1,0:T(8,128)(2,1)S(1)}, u32[]{:S(2)}, u32[]{:S(2)}) collective-permute-start(bf16[6,2,32,256]{3,2,1,0:T(8,128)(2,1)S(1)} %get-tuple-element.32), channel_id=1, source_target_pairs={{0,6},{2,0},{4,2},{6,4},{8,14},{10,8},{12,10},{14,12},{16,22},{18,... | collective-permute-start | bytes 589832 | tf_op jit(solution)/shard_map/ppermute | solution.py:306
  18.2 20.4 %collective-permute-start.16 = (bf16[2,2,4,32,256]{4,3,2,1,0:T(8,128)(2,1)S(1)}, bf16[2,2,4,32,256]{4,3,2,1,0:T(8,128)(2,1)S(1)}, u32[]{:S(2)}, u32[]{:S(2)}) collective-permute-start(bf16[2,2,4,32,256]{4,3,2,1,0:T(8,128)(2,1)S(1)} %get-tuple-element.34.uko), channel_id=1, source_target_pairs={{0,1},{1,0},{2,3},{3,2},{4,5},{5,4},{6,7},{7,6},{8,9},{9,8},{10,11... | collective-permute-start | bytes 786440 | tf_op jit(solution)/shard_map/ppermute | solution.py:326
  18.3 11.7 %collective-permute-start.2 = (bf16[5,2,32,256]{3,2,1,0:T(8,128)(2,1)S(1)}, bf16[5,2,32,256]{3,2,1,0:T(8,128)(2,1)S(1)}, u32[]{:S(2)}, u32[]{:S(2)}) collective-permute-start(bf16[5,2,32,256]{3,2,1,0:T(8,128)(2,1)S(1)} %get-tuple-element.26.b0), channel_id=1, source_target_pairs={{0,24},{2,26},{4,28},{6,30},{8,0},{10,2},{12,4},{14,6},{16,8},{18,... | collective-permute-start | bytes 491528 | tf_op jit(solution)/shard_map/ppermute | solution.py:307
  22.4 8.6 %collective-permute-start.1 = (bf16[5,2,32,256]{3,2,1,0:T(8,128)(2,1)S(1)}, bf16[5,2,32,256]{3,2,1,0:T(8,128)(2,1)S(1)}, u32[]{:S(2)}, u32[]{:S(2)}) collective-permute-start(bf16[5,2,32,256]{3,2,1,0:T(8,128)(2,1)S(1)} %get-tuple-element.26.b0), channel_id=1, source_target_pairs={{0,16},{2,18},{4,20},{6,22},{8,24},{10,26},{12,28},{14,30},{16,0},... | collective-permute-start | bytes 491528 | tf_op jit(solution)/shard_map/ppermute | solution.py:307
  22.4 11.0 %collective-permute-start = (bf16[5,2,32,256]{3,2,1,0:T(8,128)(2,1)S(1)}, bf16[5,2,32,256]{3,2,1,0:T(8,128)(2,1)S(1)}, u32[]{:S(2)}, u32[]{:S(2)}) collective-permute-start(bf16[5,2,32,256]{3,2,1,0:T(8,128)(2,1)S(1)} %get-tuple-element.26.b0), channel_id=1, source_target_pairs={{0,8},{2,10},{4,12},{6,14},{8,16},{10,18},{12,20},{14,22},{16,24},... | collective-permute-start | bytes 491528 | tf_op jit(solution)/shard_map/ppermute | solution.py:307
  33.9 19.0 %collective-permute-start.5 = (bf16[3,2,4,32,256]{4,3,2,1,0:T(8,128)(2,1)S(1)}, bf16[3,2,4,32,256]{4,3,2,1,0:T(8,128)(2,1)S(1)}, u32[]{:S(2)}, u32[]{:S(2)}) collective-permute-start(bf16[3,2,4,32,256]{4,3,2,1,0:T(8,128)(2,1)S(1)} %get-tuple-element.28), channel_id=1, source_target_pairs={{0,6},{2,0},{4,2},{6,4},{8,14},{10,8},{12,10},{14,12},{16,22},{18,... | collective-permute-start | bytes 1179656 | tf_op jit(solution)/shard_map/ppermute | solution.py:325
  36.2 20.1 %collective-permute-start.3 = (bf16[3,2,4,32,256]{4,3,2,1,0:T(8,128)(2,1)S(1)}, bf16[3,2,4,32,256]{4,3,2,1,0:T(8,128)(2,1)S(1)}, u32[]{:S(2)}, u32[]{:S(2)}) collective-permute-start(bf16[3,2,4,32,256]{4,3,2,1,0:T(8,128)(2,1)S(1)} %get-tuple-element.28), channel_id=1, source_target_pairs={{0,2},{2,4},{4,6},{6,0},{8,10},{10,12},{12,14},{14,8},{16,18},{18,... | collective-permute-start | bytes 1179656 | tf_op jit(solution)/shard_map/ppermute | solution.py:325
  36.2 20.1 %collective-permute-start.6 = (bf16[3,2,4,32,256]{4,3,2,1,0:T(8,128)(2,1)S(1)}, bf16[3,2,4,32,256]{4,3,2,1,0:T(8,128)(2,1)S(1)}, u32[]{:S(2)}, u32[]{:S(2)}) collective-permute-start(bf16[3,2,4,32,256]{4,3,2,1,0:T(8,128)(2,1)S(1)} %get-tuple-element.27.o0), channel_id=1, source_target_pairs={{0,1},{1,0},{2,3},{3,2},{4,5},{5,4},{6,7},{7,6},{8,9},{9,8},{10,11... | collective-permute-start | bytes 1179656 | tf_op jit(solution)/shard_map/ppermute | solution.py:327
  36.2 20.1 %collective-permute-start.4 = (bf16[3,2,4,32,256]{4,3,2,1,0:T(8,128)(2,1)S(1)}, bf16[3,2,4,32,256]{4,3,2,1,0:T(8,128)(2,1)S(1)}, u32[]{:S(2)}, u32[]{:S(2)}) collective-permute-start(bf16[3,2,4,32,256]{4,3,2,1,0:T(8,128)(2,1)S(1)} %get-tuple-element.27.o0), channel_id=1, source_target_pairs={{0,4},{2,6},{4,0},{6,2},{8,12},{10,14},{12,8},{14,10},{16,20},{18,... | collective-permute-start | bytes 1179656 | tf_op jit(solution)/shard_map/ppermute | solution.py:325
  38.6 18.2 %collective-permute-start.15 = (bf16[3,2,4,32,256]{4,3,2,1,0:T(8,128)(2,1)S(1)}, bf16[3,2,4,32,256]{4,3,2,1,0:T(8,128)(2,1)S(1)}, u32[]{:S(2)}, u32[]{:S(2)}) collective-permute-start(bf16[3,2,4,32,256]{4,3,2,1,0:T(8,128)(2,1)S(1)} %get-tuple-element.33.z0), channel_id=1, source_target_pairs={{0,24},{2,26},{4,28},{6,30},{8,0},{10,2},{12,4},{14,6},{16,8},{18,... | collective-permute-start | bytes 1179656 | tf_op jit(solution)/shard_map/ppermute | solution.py:324
  52.9 9.4 %collective-permute-start.14 = (bf16[3,2,4,32,256]{4,3,2,1,0:T(8,128)(2,1)S(1)}, bf16[3,2,4,32,256]{4,3,2,1,0:T(8,128)(2,1)S(1)}, u32[]{:S(2)}, u32[]{:S(2)}) collective-permute-start(bf16[3,2,4,32,256]{4,3,2,1,0:T(8,128)(2,1)S(1)} %get-tuple-element.33.z0), channel_id=1, source_target_pairs={{0,16},{2,18},{4,20},{6,22},{8,24},{10,26},{12,28},{14,30},{16,0},... | collective-permute-start | bytes 1179656 | tf_op jit(solution)/shard_map/ppermute | solution.py:324
  56.3 10.1 %collective-permute-start.13 = (bf16[3,2,4,32,256]{4,3,2,1,0:T(8,128)(2,1)S(1)}, bf16[3,2,4,32,256]{4,3,2,1,0:T(8,128)(2,1)S(1)}, u32[]{:S(2)}, u32[]{:S(2)}) collective-permute-start(bf16[3,2,4,32,256]{4,3,2,1,0:T(8,128)(2,1)S(1)} %get-tuple-element.33.z0), channel_id=1, source_target_pairs={{0,8},{2,10},{4,12},{6,14},{8,16},{10,18},{12,20},{14,22},{16,24},... | collective-permute-start | bytes 1179656 | tf_op jit(solution)/shard_map/ppermute | solution.py:324
  56.3 10.1 %collective-permute-start.9 = (bf16[3,2,4,32,256]{4,3,2,1,0:T(8,128)(2,1)S(1)}, bf16[3,2,4,32,256]{4,3,2,1,0:T(8,128)(2,1)S(1)}, u32[]{:S(2)}, u32[]{:S(2)}) collective-permute-start(bf16[3,2,4,32,256]{4,3,2,1,0:T(8,128)(2,1)S(1)} %collective-permute-done.5.o3), channel_id=1, source_target_pairs={{0,1},{1,0},{2,3},{3,2},{4,5},{5,4},{6,7},{7,6},{8,9},{9,8},{10,11... | collective-permute-start | bytes 1179656 | tf_op jit(solution)/shard_map/ppermute | solution.py:327
  56.3 10.1 %collective-permute-start.7 = (bf16[3,2,4,32,256]{4,3,2,1,0:T(8,128)(2,1)S(1)}, bf16[3,2,4,32,256]{4,3,2,1,0:T(8,128)(2,1)S(1)}, u32[]{:S(2)}, u32[]{:S(2)}) collective-permute-start(bf16[3,2,4,32,256]{4,3,2,1,0:T(8,128)(2,1)S(1)} %collective-permute-done.3.o1), channel_id=1, source_target_pairs={{0,1},{1,0},{2,3},{3,2},{4,5},{5,4},{6,7},{7,6},{8,9},{9,8},{10,11... | collective-permute-start | bytes 1179656 | tf_op jit(solution)/shard_map/ppermute | solution.py:327
  56.8 9.6 %collective-permute-start.8 = (bf16[3,2,4,32,256]{4,3,2,1,0:T(8,128)(2,1)S(1)}, bf16[3,2,4,32,256]{4,3,2,1,0:T(8,128)(2,1)S(1)}, u32[]{:S(2)}, u32[]{:S(2)}) collective-permute-start(bf16[3,2,4,32,256]{4,3,2,1,0:T(8,128)(2,1)S(1)} %collective-permute-done.4.o2), channel_id=1, source_target_pairs={{0,1},{1,0},{2,3},{3,2},{4,5},{5,4},{6,7},{7,6},{8,9},{9,8},{10,11... | collective-permute-start | bytes 1179656 | tf_op jit(solution)/shard_map/ppermute | solution.py:327
  75.1 6.5 %collective-permute-start.18 = (bf16[4,56,256]{2,1,0:T(8,128)(2,1)S(1)}, bf16[4,56,256]{2,1,0:T(8,128)(2,1)S(1)}, u32[]{:S(2)}, u32[]{:S(2)}) collective-permute-start(bf16[4,56,256]{2,1,0:T(8,128)(2,1)S(1)} %get-tuple-element.40), channel_id=1, source_target_pairs={{0,32},{32,64},{64,96},{96,0},{1,33},{33,65},{65,97},{97,1},{2,34}... | collective-permute-start | bytes 344072 | tf_op jit(solution)/shard_map/ppermute | solution.py:356
  76.7 8.4 %collective-permute-start.19 = (bf16[4,56,256]{2,1,0:T(8,128)(2,1)S(1)}, bf16[4,56,256]{2,1,0:T(8,128)(2,1)S(1)}, u32[]{:S(2)}, u32[]{:S(2)}) collective-permute-start(bf16[4,56,256]{2,1,0:T(8,128)(2,1)S(1)} %get-tuple-element.41), channel_id=1, source_target_pairs={{0,64},{32,96},{64,0},{96,32},{1,65},{33,97},{65,1},{97,33},{2,66}... | collective-permute-start | bytes 344072 | tf_op jit(solution)/shard_map/ppermute | solution.py:356
  79.4 5.6 %collective-permute-start.20 = (bf16[4,56,256]{2,1,0:T(8,128)(2,1)S(1)}, bf16[4,56,256]{2,1,0:T(8,128)(2,1)S(1)}, u32[]{:S(2)}, u32[]{:S(2)}) collective-permute-start(bf16[4,56,256]{2,1,0:T(8,128)(2,1)S(1)} %get-tuple-element.42), channel_id=1, source_target_pairs={{0,96},{32,0},{64,32},{96,64},{1,97},{33,1},{65,33},{97,65},{2,98}... | collective-permute-start | bytes 344072 | tf_op jit(solution)/shard_map/ppermute | solution.py:356
  85.1 5.9 %collective-permute-start.21 = (bf16[56,256]{1,0:T(8,128)(2,1)S(1)}, bf16[56,256]{1,0:T(8,128)(2,1)S(1)}, u32[]{:S(2)}, u32[]{:S(2)}) collective-permute-start(bf16[56,256]{1,0:T(8,128)(2,1)S(1)} %get-tuple-element.44), channel_id=1, source_target_pairs={{0,2},{2,4},{4,6},{6,0},{8,10},{10,12},{12,14},{14,8},{16,18},{18,... | collective-permute-start | bytes 86024 | tf_op jit(solution)/shard_map/ppermute | solution.py:365
  85.2 7.3 %collective-permute-start.22 = (bf16[56,256]{1,0:T(8,128)(2,1)S(1)}, bf16[56,256]{1,0:T(8,128)(2,1)S(1)}, u32[]{:S(2)}, u32[]{:S(2)}) collective-permute-start(bf16[56,256]{1,0:T(8,128)(2,1)S(1)} %get-tuple-element.45), channel_id=1, source_target_pairs={{0,4},{2,6},{4,0},{6,2},{8,12},{10,14},{12,8},{14,10},{16,20},{18,... | collective-permute-start | bytes 86024 | tf_op jit(solution)/shard_map/ppermute | solution.py:365
  96.5 6.3 %collective-permute-start.25 = (bf16[4,56,256]{2,1,0:T(8,128)(2,1)S(1)}, bf16[4,56,256]{2,1,0:T(8,128)(2,1)S(1)}, u32[]{:S(2)}, u32[]{:S(2)}) collective-permute-start(bf16[4,56,256]{2,1,0:T(8,128)(2,1)S(1)} %shard_map.70.g0), channel_id=1, source_target_pairs={{0,64},{32,96},{64,0},{96,32},{1,65},{33,97},{65,1},{97,33},{2,66}... | collective-permute-start | bytes 344072 | tf_op jit(solution)/shard_map/ppermute | solution.py:369
  97.6 6.4 %collective-permute-start.24 = (bf16[4,56,256]{2,1,0:T(8,128)(2,1)S(1)}, bf16[4,56,256]{2,1,0:T(8,128)(2,1)S(1)}, u32[]{:S(2)}, u32[]{:S(2)}) collective-permute-start(bf16[4,56,256]{2,1,0:T(8,128)(2,1)S(1)} %shard_map.70.g0), channel_id=1, source_target_pairs={{0,32},{32,64},{64,96},{96,0},{1,33},{33,65},{65,97},{97,1},{2,34}... | collective-permute-start | bytes 344072 | tf_op jit(solution)/shard_map/ppermute | solution.py:369
  (10 other events, 46.1 us)

commit v2 on v0

v2 whole, which is shorter than its diff:
```python
import jax
import jax.numpy as jnp
from jax import lax
from jax.experimental import pallas as pl
from jax.experimental.pallas import tpu as pltpu
from jax.sharding import PartitionSpec as P

BF = jnp.bfloat16
F32 = jnp.float32
VMEM_LIMIT = 24 * 1024 * 1024


def ring_both(step):
    pairs = []
    for z in range(4):
        for y in range(4):
            here = (z * 4 + y) * 2
            pairs.append((here, (z * 4 + (y + step) % 4) * 2))
            pairs.append((here + 1, (((z + step) % 4) * 4 + y) * 2 + 1))
    return pairs


def ring_other(step):
    pairs = []
    for z in range(4):
        for y in range(4):
            here = (z * 4 + y) * 2
            pairs.append((here, (((z + step) % 4) * 4 + y) * 2))
            pairs.append((here + 1, (z * 4 + (y + step) % 4) * 2 + 1))
    return pairs


def ring_x(step):
    return [(x, (x + step) % 4) for x in range(4)]


SWAP = [(0, 1), (1, 0)]


def place():
    row = lax.axis_index("row")
    return lax.axis_index("pole"), lax.div(row, 4), lax.rem(row, 4), lax.axis_index("col")


def node_of(y):
    return 3 + 2 * lax.rem(y, 2) + lax.div(y, 2)


def vm():
    return pl.BlockSpec(memory_space=pltpu.VMEM)


def sm():
    return pl.BlockSpec(memory_space=pltpu.SMEM)


def far():
    return pl.BlockSpec(memory_space=pltpu.HBM)


def hbm():
    return pl.BlockSpec(memory_space=pl.ANY)


def call(kernel, outs, in_specs, out_specs, scratch=(), flops=0, nbytes=0, vmem=VMEM_LIMIT):
    return pl.pallas_call(
        kernel,
        out_shape=outs,
        in_specs=in_specs,
        out_specs=out_specs,
        scratch_shapes=list(scratch),
        compiler_params=pltpu.CompilerParams(vmem_limit_bytes=vmem),
        cost_estimate=pl.CostEstimate(flops=flops, bytes_accessed=nbytes, transcendentals=0),
    )


def shape(*dims, dtype=BF):
    return jax.ShapeDtypeStruct(dims, dtype)


def pack_kernel(
    low, up, dia, low_s, up_s, dia_s, widths, pattern, out0, out1, out2, out3
):
    x, z, y, c = place()
    rows = (32 * (4 * z + y)) + lax.broadcasted_iota(jnp.int32, (32, 256), 0)
    cols = lax.broadcasted_iota(jnp.int32, (32, 256), 1)

    def mask(row_node, col_node, on, half):
        keep = (rows < widths[row_node]) & (cols + 256 * half < widths[col_node]) & (on != 0)
        return jnp.where(keep, 1.0, 0.0).astype(BF)[None]

    @pl.when(c == 0)
    def _():
        for d, out in enumerate((out0, out1, out2, out3)):
            k = node_of(lax.rem(y + d, 4))
            p = lax.div(k - 1, 2)
            at = 2 * (k - 3) + 2
            for h, (lo, u, di) in enumerate(((low, up, dia), (low_s, up_s, dia_s))):
                out[0, h] = di[p] * mask(p, p, 1, h)
                out[1, h] = lo[at] * mask(p, k, pattern[at], h)
                out[2, h] = lo[at + 1] * mask(0, k, pattern[at + 1], h)
                out[3, h] = u[at] * mask(k, p, pattern[at], h)
                out[4, h] = u[at + 1] * mask(k, 0, pattern[at + 1], h)
                out[5, h] = di[k] * mask(k, k, 1, h)

    @pl.when(c == 1)
    def _():
        for h, (lo, u, di) in enumerate(((low_s, up_s, dia_s), (low, up, dia))):
            tiles = [di[0] * mask(0, 0, 1, h)]
            for i in range(2):
                tiles.append(u[i] * mask(1 + i, 0, pattern[i], h))
                tiles.append(lo[i] * mask(0, 1 + i, pattern[i], h))
            for out in (out0, out1, out2, out3):
                for t in range(5):
                    out[t, h] = tiles[t]


def run_copies(copies, sems):
    made = [pltpu.make_async_copy(s, t, sems.at[i]) for i, (s, t) in enumerate(copies)]
    for m in made:
        m.start()
    for m in made:
        m.wait()


def merge_kernel(b0, b1, b2, b3, near, far, uk, sems):
    x, z, y, c = place()
    p = lax.rem(y, 2)

    @pl.when(c == 0)
    def _():
        copies = []
        for d, buf in enumerate((b0, b1, b2, b3)):
            at = lax.rem(y + 4 - d, 4)
            copies.append((buf.at[pl.ds(0, 3)], near.at[:, :, :, at]))
            copies.append((buf.at[pl.ds(0, 3)], far.at[:, :, :, at]))
            copies.append((buf.at[pl.ds(3, 3)], uk.at[:, :, :, at]))
        run_copies(copies, sems)

    @pl.when(c == 1)
    def _():
        copies = []
        for d, buf in enumerate((b0, b1, b2, b3)):
            at = lax.rem(z + 4 - d, 4)
            copies.append((buf.at[0], near.at[0, :, :, at]))
            copies.append((buf.at[0], far.at[0, :, :, at]))
            copies.append((buf.at[pl.ds(1 + 2 * p, 2)], far.at[pl.ds(1, 2), :, :, at]))
            copies.append((buf.at[pl.ds(3 - 2 * p, 2)], near.at[pl.ds(1, 2), :, :, at]))
        run_copies(copies, sems)


def left_of(pairs):
    real = [jnp.concatenate([r, -i], axis=1) for r, i in pairs]
    imag = [jnp.concatenate([i, r], axis=1) for r, i in pairs]
    return jnp.concatenate(real + imag, axis=0)


def dot(a, b):
    return jnp.dot(a, b, preferred_element_type=F32)


def pairs_of(res, count):
    half = 128 * count
    return [
        (res[128 * i : 128 * i + 128], res[half + 128 * i : half + 128 * i + 128])
        for i in range(count)
    ]


def split_kernel(r0, r1, r2, r3, first, second, sems):
    x, z, y, c = place()

    @pl.when(c == 0)
    def _():
        copies = []
        for d, buf in enumerate((r0, r1, r2, r3)):
            at = lax.rem(z + 4 - d, 4)
            copies.append((buf.at[pl.ds(1, 2), 0], first.at[:, :, at]))
            copies.append((buf.at[pl.ds(1, 2), 1], second.at[:, :, at]))
        run_copies(copies, sems)


def first_kernel(r0, r1, r2, r3, uk, uks, out, right, sems):
    x, z, y, c = place()

    def wide_rows(get):
        return tuple(jnp.concatenate([get(0, part), get(1, part)], axis=1) for part in range(2))

    def times(left, count, block):
        got = [pairs_of(dot(left, right[block, h].reshape(1024, 256)), count) for h in range(2)]
        return [
            tuple(jnp.concatenate([got[0][n][i], got[1][n][i]], axis=1) for i in range(2))
            for n in range(count)
        ]

    def rows_of(block):
        return wide_rows(lambda h, part: right[block, h, part, z].reshape(128, 256))

    def put(slot, pair, sign=1):
        for i in range(2):
            out[slot, i] = (pair[i] if sign > 0 else -pair[i]).astype(BF)

    @pl.when(c == 0)
    def _():
        copies = []
        for d, buf in enumerate((r0, r1, r2, r3)):
            copies.append((buf.at[0], right.at[0, :, :, lax.rem(z + 4 - d, 4)]))
        run_copies(copies, sems)
        ukp = wide_rows(lambda h, part: uk[0, h, part].reshape(128, 256))
        (kd,) = times(left_of([ukp]), 1, 0)
        put(0, kd)
        put(1, rows_of(0))

    @pl.when(c == 1)
    def _():
        copies = []
        for d, buf in enumerate((r0, r1, r2, r3)):
            copies.append((buf, right.at[:, :, :, :, lax.rem(y + 4 - d, 4)]))
        run_copies(copies, sems)
        ukp = wide_rows(lambda h, part: uks[0, h, part].reshape(128, 256))
        uk0 = wide_rows(lambda h, part: uks[1, h, part].reshape(128, 256))
        (kv,) = times(left_of([ukp]), 1, 1)
        v = tuple((uk0[i].astype(F32) - kv[i]).astype(BF) for i in range(2))
        xk0, xp0 = [
            tuple((-part).astype(BF) for part in pair)
            for pair in times(left_of([v, rows_of(1)]), 2, 0)
        ]
        d0r = rows_of(0)
        kl, pl_, dl = times(left_of([xk0, xp0, d0r]), 3, 2)
        put(0, pl_)
        put(1, dl, -1)
        put(2, kl)
        put(3, xp0)
        put(4, d0r)
        put(5, xk0)


def second_kernel(
    edge, edge_s, half0, half1, uk, uks, res, slot0, slot1, slot2, slot3, parts
):
    x, z, y, c = place()
    wr, wi = res[0, 0], res[0, 1]

    def density(re, im):
        return wr * re.astype(F32) - wi * im.astype(F32)

    def work(e0, e1, right, dk, half):
        own = slice(256 * half, 256 * half + 256)
        xpp = [e0[1, i].astype(F32) - e1[0, i].astype(F32) for i in range(2)]
        xkp = [-(e0[0, i].astype(F32) + e1[2, i].astype(F32)) for i in range(2)]
        left_p = left_of(
            [
                tuple(v.astype(BF) for v in xpp),
                (e1[1, 0], e1[1, 1]),
                tuple(v.astype(BF) for v in xkp),
            ]
        )
        left_0 = left_of([(e1[i, 0], e1[i, 1]) for i in (3, 4, 5)])
        total = dot(left_p, right[0].reshape(1024, 256)) + dot(
            left_0, right[1].reshape(1024, 256)
        )
        pk, ok, kk = pairs_of(total, 3)
        parts[0] = density(
            dk[2, half, 0].reshape(128, 256).astype(F32) - kk[0],
            dk[2, half, 1].reshape(128, 256).astype(F32) - kk[1],
        )
        parts[1] = density(-pk[0], -pk[1])
        parts[2] = density(-ok[0], -ok[1])
        parts[3] = density(xkp[0][:, own], xkp[1][:, own])
        parts[4] = density(e1[5, 0, :, own], e1[5, 1, :, own])

        @pl.when(y < 2)
        def _():
            parts[5] = density(xpp[0][:, own], xpp[1][:, own])
            parts[6] = density(e1[4, 0, :, own], e1[4, 1, :, own])

        @pl.when(y >= 2)
        def _():
            parts[5] = density(e1[3, 0, :, own], e1[3, 1, :, own])
            parts[6] = density(e1[1, 0, :, own], e1[1, 1, :, own])

    @pl.when(c == 0)
    def _():
        work(edge, edge_s, half0, uk, 0)

    @pl.when(c == 1)
    def _():
        work(edge_s, edge, half1, uks, 1)

    for d, out in enumerate((slot0, slot1, slot2, slot3)):
        at = pl.multiple_of(32 * lax.rem(x + d, 4), 32)
        for b in range(7):
            out[b] = parts[b, pl.ds(at, 32), :].astype(BF)


def sum_kernel(a0, a1, a2, a3, out):
    total = a0[...].astype(F32) + a1[...].astype(F32)
    out[...] = (total + (a2[...].astype(F32) + a3[...].astype(F32))).astype(BF)


def spread(step):
    return [
        (x * 16 + z * 4 + y, ((y + step) % 4) * 16 + z * 4 + x)
        for x in range(4)
        for z in range(4)
        for y in range(4)
    ]


def final_kernel(g0, g1, g2, g3, out):
    x, z, y, c = place()
    for d, g in enumerate((g0, g1, g2, g3)):
        b = lax.rem(x + 4 - d, 4)
        k = node_of(b)
        p = 1 + lax.rem(b, 2)
        pair = 2 * (k - 3) + 2
        low = b < 2
        out[k] = g[0].astype(F32)
        out[7 + pair] = g[1].astype(F32)
        out[8 + pair] = g[2].astype(F32)
        out[17 + pair] = g[3].astype(F32)
        out[18 + pair] = g[4].astype(F32)
        out[jnp.where(low, p, 16 + p)] = g[5].astype(F32)

        @pl.when(b != 1)
        def _():
            out[jnp.where(low, 0, 6 + p)] = g[6].astype(F32)


def body(lower_factor, upper_factor, diag_inverse, residues, widths, pattern):
    mine = (lower_factor[0], upper_factor[0], diag_inverse[0])
    swapped = [lax.ppermute(a, "col", SWAP) for a in mine]
    grid = ("row", "col")
    bufs = call(
        pack_kernel,
        [shape(6, 2, 2, 32, 256)] * 4,
        [vm()] * 6 + [sm()] * 2,
        [vm()] * 4,
        nbytes=4 << 20,
    )(*mine, *swapped, widths, pattern)
    came = {d: lax.ppermute(bufs[d], grid, ring_both(d)) for d in (1, 3, 2)}
    near, far, uk = call(
        merge_kernel,
        [shape(3, 2, 2, 4, 32, 256)] * 3,
        [hbm()] * 4,
        [hbm()] * 3,
        [pltpu.SemaphoreType.DMA((16,))],
        nbytes=4 << 20,
    )(bufs[0], came[1], came[2], came[3])
    came = {d: lax.ppermute(near, grid, ring_other(d)) for d in (1, 3)}
    came[2] = lax.ppermute(far, grid, ring_other(2))
    uks = lax.ppermute(uk, "col", SWAP)
    blocks = (far, came[1], came[2], came[3])
    half0, half1 = call(
        split_kernel,
        [shape(2, 2, 4, 4, 32, 256)] * 2,
        [hbm()] * 4,
        [hbm()] * 2,
        [pltpu.SemaphoreType.DMA((8,))],
        nbytes=4 << 20,
    )(*blocks)
    half1 = lax.ppermute(half1, "col", SWAP)
    edge = call(
        first_kernel,
        [shape(6, 2, 128, 512)],
        [hbm()] * 4 + [vm()] * 2,
        [vm()],
        [pltpu.VMEM((3, 2, 2, 4, 4, 32, 256), BF), pltpu.SemaphoreType.DMA((4,))],
        flops=1610612736,
        nbytes=4 << 20,
    )(*blocks, uk, uks)[0]
    edge_s = lax.ppermute(edge, "col", SWAP)
    slots = call(
        second_kernel,
        [shape(7, 32, 256)] * 4,
        [vm()] * 6 + [sm()],
        [vm()] * 4,
        [pltpu.VMEM((7, 128, 256), F32)],
        flops=805306368,
        nbytes=4 << 20,
    )(edge, edge_s, half0, half1, uk, uks, residues)
    at_x = [slots[0]] + [lax.ppermute(slots[d], "pole", ring_x(d)) for d in (1, 3, 2)]
    total = call(sum_kernel, [shape(7, 32, 256)], [vm()] * 4, [vm()], nbytes=1 << 20)(*at_x)[0]
    full = [lax.ppermute(total, ("pole", "row"), spread(d)) for d in range(4)]
    return call(
        final_kernel, [shape(27, 32, 256, dtype=F32)], [vm()] * 4, [vm()], nbytes=2 << 20
    )(*full)[0]


def solution(mesh):
    return jax.shard_map(
        body,
        mesh=mesh,
        in_specs=(
            P("pole", None, None, "row", "col"),
            P("pole", None, None, "row", "col"),
            P("pole", None, None, "row", "col"),
            P("pole", None),
            P(),
            P(),
        ),
        out_specs=P(None, "row", "col"),
        check_vma=False,
    )
```

time: 532 us -> 79.9 us (0.15)
  waiting for transfers between devices: 282 us -> 40.4 us
  blocking collectives: 134 us -> 0 us
  other arithmetic: 52.7 us -> 0 us
  matrix products: 44.6 us -> 0 us
  starting transfers between devices: 0.41 us -> 30 us
  between operations: 14.2 us -> 0.09 us
    all_gather x10 -> x0, waiting for transfers between devices: 239 us -> none  [the longest x4 149 us: solve_group(): lax.all_gather(below_tiles, 'row', axis=3, tiled=True)]
    all_gather x14 -> x0, blocking collectives: 134 us -> none  [the longest x2 47.8 us: solve_group(): lower_full = lax.all_gather(lower_tiles, 'row', axis=3, tiled=True)]
    dot_general x72 -> x0, matrix products: 44.6 us -> none  [the longest x18 16.9 us: complex_product(): jnp.einsum(form, real_left, imag_right, preferred_element_type=jnp.float32)]
    psum x1 -> x0, waiting for transfers between devices: 41.8 us -> none  [body(): return lax.psum(stacked.astype(jnp.bfloat16), 'pole').astype(jnp.float32)]
    ppermute x0 -> x19, waiting for transfers between devices: none -> 40.4 us  [the longest x2 9.38 us: body(): came = {d: lax.ppermute(near, grid, ring_other(d)) for d in (1, 3)}]
    unnamed x26 -> x0, other arithmetic: 30.4 us -> none
    ppermute x0 -> x19, starting transfers between devices: none -> 30 us  [the longest x4 10.7 us: body(): full = [lax.ppermute(total, ('pole', 'row'), spread(d)) for d in range(4)]]
    mul x13 -> x0, other arithmetic: 11.6 us -> none  [the longest x3 5.33 us: uhat(): pattern_mask[index] * row_keep[member][:, None] * col_keep[above][None, :]]
  transfers between devices with their start and end apart: 11 -> 19, of which waited for: 8 -> 12; matrix products, arithmetic and copies ran while one was open for 14% -> 0% of each run, Pallas kernels for 0% -> 0%
where the time goes in v2:
time: 79.9 us; the launch traced here: 79.5 us
  waiting for transfers between devices  40.4 us (51%)
  starting transfers between devices  30 us (38%)
  Pallas kernels  4.85 us (6%)
  local copies, waits for them, and re-layouts  4.2 us (5%)
    ppermute x4, starting transfers between devices, body(): full = [lax.ppermute(total, ('pole', 'row'), spread(d)) for d in range(4)]  10.7 us
    ppermute x2, waiting for transfers between devices, body(): came = {d: lax.ppermute(near, grid, ring_other(d)) for d in (1, 3)}  9.38 us
    ppermute x3, waiting for transfers between devices, body(): came = {d: lax.ppermute(bufs[d], grid, ring_both(d)) for d in (1, 3, 2)}  8.62 us
    ppermute x1, waiting for transfers between devices, body(): came[2] = lax.ppermute(far, grid, ring_other(2))  6.83 us
    ppermute x3, starting transfers between devices, body(): came = {d: lax.ppermute(bufs[d], grid, ring_both(d)) for d in (1, 3, 2)}  5.98 us
    ppermute x3, starting transfers between devices, body(): lax.ppermute(slots[d], 'pole', ring_x(d))  5.12 us
    ppermute x3, waiting for transfers between devices, body(): lax.ppermute(slots[d], 'pole', ring_x(d))  4.79 us
    ppermute x4, waiting for transfers between devices, body(): full = [lax.ppermute(total, ('pole', 'row'), spread(d)) for d in range(4)]  4.44 us
  transfers between devices with their start and end apart: 19, of which 12 were waited for; matrix products, arithmetic and copies ran while one was open for 0% of the time, Pallas kernels for 0%

profile of v2, /device:TPU:0, one launch (start us, length us, event | category | flops | bytes accessed | tf_op | source)
XLA Modules:
  0.0 79.5 jit_solution(17372469123065640636)
XLA Ops:
  0.5 2.1 %collective-permute-done.2.dia_s = bf16[7,2,32,256]{3,2,1,0:T(8,128)(2,1)S(1)} collective-permute-done((bf16[7,2,32,256]{3,2,1,0:T(8,128)(2,1)}, bf16[7,2,32,256]{3,2,1,0:T(8,128)(2,1)S(1)}, u32[]{:S(2)}, u32[]{:S(2)}) %collective-permute-start.2) | collective-permute-done | bytes 229408 | tf_op jit(solution)/shard_map/ppermute | solution.py:332
  7.7 1.7 %collective-permute-start.3 = (bf16[6,2,2,32,256]{4,3,2,1,0:T(8,128)(2,1)S(1)}, bf16[6,2,2,32,256]{4,3,2,1,0:T(8,128)(2,1)S(1)}, u32[]{:S(2)}, u32[]{:S(2)}) collective-permute-start(bf16[6,2,2,32,256]{4,3,2,1,0:T(8,128)(2,1)S(1)} %get-tuple-element.19), channel_id=1, source_target_pairs={{0,2},{1,9},{2,4},{3,11},{4,6},{5,13},{6,0},{7,15},{8,10},{9,17},{... | collective-permute-start | bytes 1179656 | tf_op jit(solution)/shard_map/ppermute | solution.py:341
  9.4 2.9 %collective-permute-start.4 = (bf16[6,2,2,32,256]{4,3,2,1,0:T(8,128)(2,1)S(1)}, bf16[6,2,2,32,256]{4,3,2,1,0:T(8,128)(2,1)S(1)}, u32[]{:S(2)}, u32[]{:S(2)}) collective-permute-start(bf16[6,2,2,32,256]{4,3,2,1,0:T(8,128)(2,1)S(1)} %get-tuple-element.20), channel_id=1, source_target_pairs={{0,4},{1,17},{2,6},{3,19},{4,0},{5,21},{6,2},{7,23},{8,12},{9,25},... | collective-permute-start | bytes 1179656 | tf_op jit(solution)/shard_map/ppermute | solution.py:341
  12.3 1.3 %collective-permute-start.5 = (bf16[6,2,2,32,256]{4,3,2,1,0:T(8,128)(2,1)S(1)}, bf16[6,2,2,32,256]{4,3,2,1,0:T(8,128)(2,1)S(1)}, u32[]{:S(2)}, u32[]{:S(2)}) collective-permute-start(bf16[6,2,2,32,256]{4,3,2,1,0:T(8,128)(2,1)S(1)} %get-tuple-element.21), channel_id=1, source_target_pairs={{0,6},{1,25},{2,0},{3,27},{4,2},{5,29},{6,4},{7,31},{8,14},{9,1},{... | collective-permute-start | bytes 1179656 | tf_op jit(solution)/shard_map/ppermute | solution.py:341
  13.6 3.1 %collective-permute-done.3.b1 = bf16[6,2,2,32,256]{4,3,2,1,0:T(8,128)(2,1)S(1)} collective-permute-done((bf16[6,2,2,32,256]{4,3,2,1,0:T(8,128)(2,1)S(1)}, bf16[6,2,2,32,256]{4,3,2,1,0:T(8,128)(2,1)S(1)}, u32[]{:S(2)}, u32[]{:S(2)}) %collective-permute-start.3) | collective-permute-done | bytes 393248 | tf_op jit(solution)/shard_map/ppermute | solution.py:341
  16.7 5.5 %collective-permute-done.4.b2 = bf16[6,2,2,32,256]{4,3,2,1,0:T(8,128)(2,1)S(1)} collective-permute-done((bf16[6,2,2,32,256]{4,3,2,1,0:T(8,128)(2,1)S(1)}, bf16[6,2,2,32,256]{4,3,2,1,0:T(8,128)(2,1)S(1)}, u32[]{:S(2)}, u32[]{:S(2)}) %collective-permute-start.4) | collective-permute-done | bytes 393248 | tf_op jit(solution)/shard_map/ppermute | solution.py:341
  22.8 4.0 %collective-permute-start.7 = (bf16[3,2,2,4,32,256]{5,4,3,2,1,0:T(8,128)(2,1)S(1)}, bf16[3,2,2,4,32,256]{5,4,3,2,1,0:T(8,128)(2,1)S(1)}, u32[]{:S(2)}, u32[]{:S(2)}) collective-permute-start(bf16[3,2,2,4,32,256]{5,4,3,2,1,0:T(8,128)(2,1)S(1)} %get-tuple-element.22.r0), channel_id=1, source_target_pairs={{0,16},{1,5},{2,18},{3,7},{4,20},{5,1},{6,22},{7,3},{8,24},{9,13},... | collective-permute-start | bytes 2359304 | tf_op jit(solution)/shard_map/ppermute | solution.py:351
  27.7 2.2 %collective-permute-start.8 = (bf16[3,2,2,4,32,256]{5,4,3,2,1,0:T(8,128)(2,1)S(1)}, bf16[3,2,2,4,32,256]{5,4,3,2,1,0:T(8,128)(2,1)S(1)}, u32[]{:S(2)}, u32[]{:S(2)}) collective-permute-start(bf16[3,2,2,4,32,256]{5,4,3,2,1,0:T(8,128)(2,1)S(1)} %get-tuple-element.23), channel_id=1, source_target_pairs={{0,24},{1,7},{2,26},{3,1},{4,28},{5,3},{6,30},{7,5},{8,0},{9,15},{... | collective-permute-start | bytes 2359304 | tf_op jit(solution)/shard_map/ppermute | solution.py:350
  30.0 6.8 %collective-permute-done.7.r2 = bf16[3,2,2,4,32,256]{5,4,3,2,1,0:T(8,128)(2,1)S(1)} collective-permute-done((bf16[3,2,2,4,32,256]{5,4,3,2,1,0:T(8,128)(2,1)S(1)}, bf16[3,2,2,4,32,256]{5,4,3,2,1,0:T(8,128)(2,1)S(1)}, u32[]{:S(2)}, u32[]{:S(2)}) %collective-permute-start.7) | collective-permute-done | bytes 786464 | tf_op jit(solution)/shard_map/ppermute | solution.py:351
  36.8 8.3 %collective-permute-done.6.r1 = bf16[3,2,2,4,32,256]{5,4,3,2,1,0:T(8,128)(2,1)S(1)} collective-permute-done((bf16[3,2,2,4,32,256]{5,4,3,2,1,0:T(8,128)(2,1)S(1)}, bf16[3,2,2,4,32,256]{5,4,3,2,1,0:T(8,128)(2,1)S(1)}, u32[]{:S(2)}, u32[]{:S(2)}) %collective-permute-start.6) | collective-permute-done | bytes 786464 | tf_op jit(solution)/shard_map/ppermute | solution.py:350
  45.1 1.1 %collective-permute-done.8.r3 = bf16[3,2,2,4,32,256]{5,4,3,2,1,0:T(8,128)(2,1)S(1)} collective-permute-done((bf16[3,2,2,4,32,256]{5,4,3,2,1,0:T(8,128)(2,1)S(1)}, bf16[3,2,2,4,32,256]{5,4,3,2,1,0:T(8,128)(2,1)S(1)}, u32[]{:S(2)}, u32[]{:S(2)}) %collective-permute-start.8) | collective-permute-done | bytes 786464 | tf_op jit(solution)/shard_map/ppermute | solution.py:350
  47.5 4.2 %collective-permute-done.11.half1 = bf16[2,2,4,4,32,256]{5,4,3,2,1,0:T(8,128)(2,1)S(1)} collective-permute-done((bf16[2,2,4,4,32,256]{5,4,3,2,1,0:T(8,128)(2,1)S(1)}, bf16[2,2,4,4,32,256]{5,4,3,2,1,0:T(8,128)(2,1)S(1)}, u32[]{:S(2)}, u32[]{:S(2)}) %collective-permute-start.11) | collective-permute-done | bytes 1048608 | tf_op jit(solution)/shard_map/ppermute | solution.py:362
  51.8 1.6 %shard_map.68 = (bf16[7,32,256]{2,1,0:T(8,128)(2,1)S(1)}, bf16[7,32,256]{2,1,0:T(8,128)(2,1)S(1)}, bf16[7,32,256]{2,1,0:T(8,128)(2,1)S(1)}, bf16[7,32,256]{2,1,0:T(8,128)(2,1)S(1)}) custom-call(bf16[6,2,128,512]{3,2,1,0:T(8,128)(2,1)S(1)} %shard_map.66.edge, bf16[6,2,128,512]{3,2,1,0:T(8,128)(2,1)S(1)} %collective-permute-done.10.edge_s, ...), custom_call_target="tpu_custom_call" | custom-call | flops 805306368 | bytes 4194304 | tf_op jit(solution)/shard_map/pallas_call | solution.py:373
  53.4 1.6 %collective-permute-start.12 = (bf16[7,32,256]{2,1,0:T(8,128)(2,1)S(1)}, bf16[7,32,256]{2,1,0:T(8,128)(2,1)S(1)}, u32[]{:S(2)}, u32[]{:S(2)}) collective-permute-start(bf16[7,32,256]{2,1,0:T(8,128)(2,1)S(1)} %get-tuple-element.28), channel_id=1, source_target_pairs={{0,32},{32,64},{64,96},{96,0},{1,33},{33,65},{65,97},{97,1},{2,34}... | collective-permute-start | bytes 344072 | tf_op jit(solution)/shard_map/ppermute | solution.py:382
  55.0 1.7 %collective-permute-start.13 = (bf16[7,32,256]{2,1,0:T(8,128)(2,1)S(1)}, bf16[7,32,256]{2,1,0:T(8,128)(2,1)S(1)}, u32[]{:S(2)}, u32[]{:S(2)}) collective-permute-start(bf16[7,32,256]{2,1,0:T(8,128)(2,1)S(1)} %get-tuple-element.29), channel_id=1, source_target_pairs={{0,96},{32,0},{64,32},{96,64},{1,97},{33,1},{65,33},{97,65},{2,98}... | collective-permute-start | bytes 344072 | tf_op jit(solution)/shard_map/ppermute | solution.py:382
  56.7 1.8 %collective-permute-start.14 = (bf16[7,32,256]{2,1,0:T(8,128)(2,1)S(1)}, bf16[7,32,256]{2,1,0:T(8,128)(2,1)S(1)}, u32[]{:S(2)}, u32[]{:S(2)}) collective-permute-start(bf16[7,32,256]{2,1,0:T(8,128)(2,1)S(1)} %get-tuple-element.30), channel_id=1, source_target_pairs={{0,64},{32,96},{64,0},{96,32},{1,65},{33,97},{65,1},{97,33},{2,66}... | collective-permute-start | bytes 344072 | tf_op jit(solution)/shard_map/ppermute | solution.py:382
  58.5 1.3 %collective-permute-done.12.a1 = bf16[7,32,256]{2,1,0:T(8,128)(2,1)S(1)} collective-permute-done((bf16[7,32,256]{2,1,0:T(8,128)(2,1)S(1)}, bf16[7,32,256]{2,1,0:T(8,128)(2,1)S(1)}, u32[]{:S(2)}, u32[]{:S(2)}) %collective-permute-start.12) | collective-permute-done | bytes 114720 | tf_op jit(solution)/shard_map/ppermute | solution.py:382
  59.9 1.8 %collective-permute-done.13.a2 = bf16[7,32,256]{2,1,0:T(8,128)(2,1)S(1)} collective-permute-done((bf16[7,32,256]{2,1,0:T(8,128)(2,1)S(1)}, bf16[7,32,256]{2,1,0:T(8,128)(2,1)S(1)}, u32[]{:S(2)}, u32[]{:S(2)}) %collective-permute-start.13) | collective-permute-done | bytes 114720 | tf_op jit(solution)/shard_map/ppermute | solution.py:382
  61.6 1.7 %collective-permute-done.14.a3 = bf16[7,32,256]{2,1,0:T(8,128)(2,1)S(1)} collective-permute-done((bf16[7,32,256]{2,1,0:T(8,128)(2,1)S(1)}, bf16[7,32,256]{2,1,0:T(8,128)(2,1)S(1)}, u32[]{:S(2)}, u32[]{:S(2)}) %collective-permute-start.14) | collective-permute-done | bytes 114720 | tf_op jit(solution)/shard_map/ppermute | solution.py:382
  64.1 4.4 %collective-permute-start.16 = (bf16[7,32,256]{2,1,0:T(8,128)(2,1)S(1)}, bf16[7,32,256]{2,1,0:T(8,128)(2,1)S(1)}, u32[]{:S(2)}, u32[]{:S(2)}) collective-permute-start(bf16[7,32,256]{2,1,0:T(8,128)(2,1)S(1)} %shard_map.69), channel_id=1, source_target_pairs={{0,32},{2,64},{4,96},{6,0},{8,40},{10,72},{12,104},{14,8},{16,48},... | collective-permute-start | bytes 344072 | tf_op jit(solution)/shard_map/ppermute | solution.py:384
  68.5 3.0 %collective-permute-start.17 = (bf16[7,32,256]{2,1,0:T(8,128)(2,1)S(1)}, bf16[7,32,256]{2,1,0:T(8,128)(2,1)S(1)}, u32[]{:S(2)}, u32[]{:S(2)}) collective-permute-start(bf16[7,32,256]{2,1,0:T(8,128)(2,1)S(1)} %shard_map.69), channel_id=1, source_target_pairs={{0,64},{2,96},{4,0},{6,32},{8,72},{10,104},{12,8},{14,40},{16,80},... | collective-permute-start | bytes 344072 | tf_op jit(solution)/shard_map/ppermute | solution.py:384
  71.5 2.6 %collective-permute-start.18 = (bf16[7,32,256]{2,1,0:T(8,128)(2,1)S(1)}, bf16[7,32,256]{2,1,0:T(8,128)(2,1)S(1)}, u32[]{:S(2)}, u32[]{:S(2)}) collective-permute-start(bf16[7,32,256]{2,1,0:T(8,128)(2,1)S(1)} %shard_map.69), channel_id=1, source_target_pairs={{0,96},{2,0},{4,32},{6,64},{8,104},{10,8},{12,40},{14,72},{16,112}... | collective-permute-start | bytes 344072 | tf_op jit(solution)/shard_map/ppermute | solution.py:384
  74.1 2.7 %collective-permute-done.17.g2 = bf16[7,32,256]{2,1,0:T(8,128)(2,1)S(1)} collective-permute-done((bf16[7,32,256]{2,1,0:T(8,128)(2,1)S(1)}, bf16[7,32,256]{2,1,0:T(8,128)(2,1)S(1)}, u32[]{:S(2)}, u32[]{:S(2)}) %collective-permute-start.17) | collective-permute-done | bytes 114720 | tf_op jit(solution)/shard_map/ppermute | solution.py:384
  76.7 1.8 %collective-permute-done.18.g3 = bf16[7,32,256]{2,1,0:T(8,128)(2,1)S(1)} collective-permute-done((bf16[7,32,256]{2,1,0:T(8,128)(2,1)S(1)}, bf16[7,32,256]{2,1,0:T(8,128)(2,1)S(1)}, u32[]{:S(2)}, u32[]{:S(2)}) %collective-permute-start.18) | collective-permute-done | bytes 114720 | tf_op jit(solution)/shard_map/ppermute | solution.py:384
  (33 shorter events, 10.1 us)
Async XLA Ops:
  0.0 2.6 %collective-permute-start = (bf16[10,2,32,256]{3,2,1,0:T(8,128)(2,1)}, bf16[10,2,32,256]{3,2,1,0:T(8,128)(2,1)S(1)}, u32[]{:S(2)}, u32[]{:S(2)}) collective-permute-start(bf16[10,2,32,256]{3,2,1,0:T(8,128)(2,1)} %bitcast.3), channel_id=1, source_target_pairs={{0,1},{1,0},{2,3},{3,2},{4,5},{5,4},{6,7},{7,6},{8,9},{9,8},{10,11... | collective-permute-start | bytes 983048 | tf_op jit(solution)/shard_map/ppermute | solution.py:332
  0.0 2.6 %collective-permute-start.1 = (bf16[10,2,32,256]{3,2,1,0:T(8,128)(2,1)}, bf16[10,2,32,256]{3,2,1,0:T(8,128)(2,1)S(1)}, u32[]{:S(2)}, u32[]{:S(2)}) collective-permute-start(bf16[10,2,32,256]{3,2,1,0:T(8,128)(2,1)} %bitcast.5), channel_id=1, source_target_pairs={{0,1},{1,0},{2,3},{3,2},{4,5},{5,4},{6,7},{7,6},{8,9},{9,8},{10,11... | collective-permute-start | bytes 983048 | tf_op jit(solution)/shard_map/ppermute | solution.py:332
  0.5 2.1 %collective-permute-start.2 = (bf16[7,2,32,256]{3,2,1,0:T(8,128)(2,1)}, bf16[7,2,32,256]{3,2,1,0:T(8,128)(2,1)S(1)}, u32[]{:S(2)}, u32[]{:S(2)}) collective-permute-start(bf16[7,2,32,256]{3,2,1,0:T(8,128)(2,1)} %bitcast.7), channel_id=1, source_target_pairs={{0,1},{1,0},{2,3},{3,2},{4,5},{5,4},{6,7},{7,6},{8,9},{9,8},{10,11... | collective-permute-start | bytes 688136 | tf_op jit(solution)/shard_map/ppermute | solution.py:332
  2.6 1.0 %copy-start = (bf16[1,10,2,32,256]{4,3,2,1,0:T(8,128)(2,1)S(1)}, bf16[1,10,2,32,256]{4,3,2,1,0:T(8,128)(2,1)}, u32[]{:S(2)}) copy-start(bf16[1,10,2,32,256]{4,3,2,1,0:T(8,128)(2,1)} %param.6) | copy-start | bytes 983044
  3.6 1.0 %copy-start.1 = (bf16[1,10,2,32,256]{4,3,2,1,0:T(8,128)(2,1)S(1)}, bf16[1,10,2,32,256]{4,3,2,1,0:T(8,128)(2,1)}, u32[]{:S(2)}) copy-start(bf16[1,10,2,32,256]{4,3,2,1,0:T(8,128)(2,1)} %param.7) | copy-start | bytes 983044
  4.6 0.9 %copy-start.2 = (bf16[1,7,2,32,256]{4,3,2,1,0:T(8,128)(2,1)S(1)}, bf16[1,7,2,32,256]{4,3,2,1,0:T(8,128)(2,1)}, u32[]{:S(2)}) copy-start(bf16[1,7,2,32,256]{4,3,2,1,0:T(8,128)(2,1)} %param.8) | copy-start | bytes 688132
  5.5 0.7 copy-start.3
  7.7 9.1 %collective-permute-start.3 = (bf16[6,2,2,32,256]{4,3,2,1,0:T(8,128)(2,1)S(1)}, bf16[6,2,2,32,256]{4,3,2,1,0:T(8,128)(2,1)S(1)}, u32[]{:S(2)}, u32[]{:S(2)}) collective-permute-start(bf16[6,2,2,32,256]{4,3,2,1,0:T(8,128)(2,1)S(1)} %get-tuple-element.19), channel_id=1, source_target_pairs={{0,2},{1,9},{2,4},{3,11},{4,6},{5,13},{6,0},{7,15},{8,10},{9,17},{... | collective-permute-start | bytes 1179656 | tf_op jit(solution)/shard_map/ppermute | solution.py:341
  9.4 12.9 %collective-permute-start.4 = (bf16[6,2,2,32,256]{4,3,2,1,0:T(8,128)(2,1)S(1)}, bf16[6,2,2,32,256]{4,3,2,1,0:T(8,128)(2,1)S(1)}, u32[]{:S(2)}, u32[]{:S(2)}) collective-permute-start(bf16[6,2,2,32,256]{4,3,2,1,0:T(8,128)(2,1)S(1)} %get-tuple-element.20), channel_id=1, source_target_pairs={{0,4},{1,17},{2,6},{3,19},{4,0},{5,21},{6,2},{7,23},{8,12},{9,25},... | collective-permute-start | bytes 1179656 | tf_op jit(solution)/shard_map/ppermute | solution.py:341
  12.3 10.0 %collective-permute-start.5 = (bf16[6,2,2,32,256]{4,3,2,1,0:T(8,128)(2,1)S(1)}, bf16[6,2,2,32,256]{4,3,2,1,0:T(8,128)(2,1)S(1)}, u32[]{:S(2)}, u32[]{:S(2)}) collective-permute-start(bf16[6,2,2,32,256]{4,3,2,1,0:T(8,128)(2,1)S(1)} %get-tuple-element.21), channel_id=1, source_target_pairs={{0,6},{1,25},{2,0},{3,27},{4,2},{5,29},{6,4},{7,31},{8,14},{9,1},{... | collective-permute-start | bytes 1179656 | tf_op jit(solution)/shard_map/ppermute | solution.py:341
  22.8 14.0 %collective-permute-start.7 = (bf16[3,2,2,4,32,256]{5,4,3,2,1,0:T(8,128)(2,1)S(1)}, bf16[3,2,2,4,32,256]{5,4,3,2,1,0:T(8,128)(2,1)S(1)}, u32[]{:S(2)}, u32[]{:S(2)}) collective-permute-start(bf16[3,2,2,4,32,256]{5,4,3,2,1,0:T(8,128)(2,1)S(1)} %get-tuple-element.22.r0), channel_id=1, source_target_pairs={{0,16},{1,5},{2,18},{3,7},{4,20},{5,1},{6,22},{7,3},{8,24},{9,13},... | collective-permute-start | bytes 2359304 | tf_op jit(solution)/shard_map/ppermute | solution.py:351
  26.7 18.4 %collective-permute-start.6 = (bf16[3,2,2,4,32,256]{5,4,3,2,1,0:T(8,128)(2,1)S(1)}, bf16[3,2,2,4,32,256]{5,4,3,2,1,0:T(8,128)(2,1)S(1)}, u32[]{:S(2)}, u32[]{:S(2)}) collective-permute-start(bf16[3,2,2,4,32,256]{5,4,3,2,1,0:T(8,128)(2,1)S(1)} %get-tuple-element.23), channel_id=1, source_target_pairs={{0,8},{1,3},{2,10},{3,5},{4,12},{5,7},{6,14},{7,1},{8,16},{9,11},{... | collective-permute-start | bytes 2359304 | tf_op jit(solution)/shard_map/ppermute | solution.py:350
  27.7 18.4 %collective-permute-start.8 = (bf16[3,2,2,4,32,256]{5,4,3,2,1,0:T(8,128)(2,1)S(1)}, bf16[3,2,2,4,32,256]{5,4,3,2,1,0:T(8,128)(2,1)S(1)}, u32[]{:S(2)}, u32[]{:S(2)}) collective-permute-start(bf16[3,2,2,4,32,256]{5,4,3,2,1,0:T(8,128)(2,1)S(1)} %get-tuple-element.23), channel_id=1, source_target_pairs={{0,24},{1,7},{2,26},{3,1},{4,28},{5,3},{6,30},{7,5},{8,0},{9,15},{... | collective-permute-start | bytes 2359304 | tf_op jit(solution)/shard_map/ppermute | solution.py:350
  30.0 16.2 %collective-permute-start.9 = (bf16[3,2,2,4,32,256]{5,4,3,2,1,0:T(8,128)(2,1)S(1)}, bf16[3,2,2,4,32,256]{5,4,3,2,1,0:T(8,128)(2,1)S(1)}, u32[]{:S(2)}, u32[]{:S(2)}) collective-permute-start(bf16[3,2,2,4,32,256]{5,4,3,2,1,0:T(8,128)(2,1)S(1)} %get-tuple-element.24.uk), channel_id=1, source_target_pairs={{0,1},{1,0},{2,3},{3,2},{4,5},{5,4},{6,7},{7,6},{8,9},{9,8},{10,11... | collective-permute-start | bytes 2359304 | tf_op jit(solution)/shard_map/ppermute | solution.py:352
  46.8 5.0 %copy-start.5 = (f32[1,2]{1,0:T(1,128)S(1)}, f32[1,2]{1,0:T(1,128)}, u32[]{:S(2)}) copy-start(f32[1,2]{1,0:T(1,128)} %res.1) | copy-start | bytes 28
  46.8 5.0 %collective-permute-start.10 = (bf16[6,2,128,512]{3,2,1,0:T(8,128)(2,1)S(1)}, bf16[6,2,128,512]{3,2,1,0:T(8,128)(2,1)S(1)}, u32[]{:S(2)}, u32[]{:S(2)}) collective-permute-start(bf16[6,2,128,512]{3,2,1,0:T(8,128)(2,1)S(1)} %shard_map.66.edge), channel_id=1, source_target_pairs={{0,1},{1,0},{2,3},{3,2},{4,5},{5,4},{6,7},{7,6},{8,9},{9,8},{10,11... | collective-permute-start | bytes 4718600 | tf_op jit(solution)/shard_map/ppermute | solution.py:372
  47.1 4.6 %collective-permute-start.11 = (bf16[2,2,4,4,32,256]{5,4,3,2,1,0:T(8,128)(2,1)S(1)}, bf16[2,2,4,4,32,256]{5,4,3,2,1,0:T(8,128)(2,1)S(1)}, u32[]{:S(2)}, u32[]{:S(2)}) collective-permute-start(bf16[2,2,4,4,32,256]{5,4,3,2,1,0:T(8,128)(2,1)S(1)} %get-tuple-element.26), channel_id=1, source_target_pairs={{0,1},{1,0},{2,3},{3,2},{4,5},{5,4},{6,7},{7,6},{8,9},{9,8},{10,11... | collective-permute-start | bytes 3145736 | tf_op jit(solution)/shard_map/ppermute | solution.py:362
  53.4 6.5 %collective-permute-start.12 = (bf16[7,32,256]{2,1,0:T(8,128)(2,1)S(1)}, bf16[7,32,256]{2,1,0:T(8,128)(2,1)S(1)}, u32[]{:S(2)}, u32[]{:S(2)}) collective-permute-start(bf16[7,32,256]{2,1,0:T(8,128)(2,1)S(1)} %get-tuple-element.28), channel_id=1, source_target_pairs={{0,32},{32,64},{64,96},{96,0},{1,33},{33,65},{65,97},{97,1},{2,34}... | collective-permute-start | bytes 344072 | tf_op jit(solution)/shard_map/ppermute | solution.py:382
  55.0 6.7 %collective-permute-start.13 = (bf16[7,32,256]{2,1,0:T(8,128)(2,1)S(1)}, bf16[7,32,256]{2,1,0:T(8,128)(2,1)S(1)}, u32[]{:S(2)}, u32[]{:S(2)}) collective-permute-start(bf16[7,32,256]{2,1,0:T(8,128)(2,1)S(1)} %get-tuple-element.29), channel_id=1, source_target_pairs={{0,96},{32,0},{64,32},{96,64},{1,97},{33,1},{65,33},{97,65},{2,98}... | collective-permute-start | bytes 344072 | tf_op jit(solution)/shard_map/ppermute | solution.py:382
  56.7 6.6 %collective-permute-start.14 = (bf16[7,32,256]{2,1,0:T(8,128)(2,1)S(1)}, bf16[7,32,256]{2,1,0:T(8,128)(2,1)S(1)}, u32[]{:S(2)}, u32[]{:S(2)}) collective-permute-start(bf16[7,32,256]{2,1,0:T(8,128)(2,1)S(1)} %get-tuple-element.30), channel_id=1, source_target_pairs={{0,64},{32,96},{64,0},{96,32},{1,65},{33,97},{65,1},{97,33},{2,66}... | collective-permute-start | bytes 344072 | tf_op jit(solution)/shard_map/ppermute | solution.py:382
  63.4 10.7 %collective-permute-start.15 = (bf16[7,32,256]{2,1,0:T(8,128)(2,1)S(1)}, bf16[7,32,256]{2,1,0:T(8,128)(2,1)S(1)}, u32[]{:S(2)}, u32[]{:S(2)}) collective-permute-start(bf16[7,32,256]{2,1,0:T(8,128)(2,1)S(1)} %shard_map.69), channel_id=1, source_target_pairs={{0,0},{2,32},{4,64},{6,96},{8,8},{10,40},{12,72},{14,104},{16,16},... | collective-permute-start | bytes 344072 | tf_op jit(solution)/shard_map/ppermute | solution.py:384
  64.1 10.0 %collective-permute-start.16 = (bf16[7,32,256]{2,1,0:T(8,128)(2,1)S(1)}, bf16[7,32,256]{2,1,0:T(8,128)(2,1)S(1)}, u32[]{:S(2)}, u32[]{:S(2)}) collective-permute-start(bf16[7,32,256]{2,1,0:T(8,128)(2,1)S(1)} %shard_map.69), channel_id=1, source_target_pairs={{0,32},{2,64},{4,96},{6,0},{8,40},{10,72},{12,104},{14,8},{16,48},... | collective-permute-start | bytes 344072 | tf_op jit(solution)/shard_map/ppermute | solution.py:384
  68.5 8.3 %collective-permute-start.17 = (bf16[7,32,256]{2,1,0:T(8,128)(2,1)S(1)}, bf16[7,32,256]{2,1,0:T(8,128)(2,1)S(1)}, u32[]{:S(2)}, u32[]{:S(2)}) collective-permute-start(bf16[7,32,256]{2,1,0:T(8,128)(2,1)S(1)} %shard_map.69), channel_id=1, source_target_pairs={{0,64},{2,96},{4,0},{6,32},{8,72},{10,104},{12,8},{14,40},{16,80},... | collective-permute-start | bytes 344072 | tf_op jit(solution)/shard_map/ppermute | solution.py:384
  71.5 7.0 %collective-permute-start.18 = (bf16[7,32,256]{2,1,0:T(8,128)(2,1)S(1)}, bf16[7,32,256]{2,1,0:T(8,128)(2,1)S(1)}, u32[]{:S(2)}, u32[]{:S(2)}) collective-permute-start(bf16[7,32,256]{2,1,0:T(8,128)(2,1)S(1)} %shard_map.69), channel_id=1, source_target_pairs={{0,96},{2,0},{4,32},{6,64},{8,104},{10,8},{12,40},{14,72},{16,112}... | collective-permute-start | bytes 344072 | tf_op jit(solution)/shard_map/ppermute | solution.py:384
  (1 other events, 0.7 us)

commit v3 on v2

v3 whole, which is shorter than its diff:
```python
import jax
import jax.numpy as jnp
from jax import lax
from jax.experimental import pallas as pl
from jax.experimental.pallas import tpu as pltpu
from jax.sharding import PartitionSpec as P

BF = jnp.bfloat16
F32 = jnp.float32
VMEM_LIMIT = 24 * 1024 * 1024


def ring_both(step):
    pairs = []
    for z in range(4):
        for y in range(4):
            here = (z * 4 + y) * 2
            pairs.append((here, (z * 4 + (y + step) % 4) * 2))
            pairs.append((here + 1, (((z + step) % 4) * 4 + y) * 2 + 1))
    return pairs


def ring_other(step):
    pairs = []
    for z in range(4):
        for y in range(4):
            here = (z * 4 + y) * 2
            pairs.append((here, (((z + step) % 4) * 4 + y) * 2))
            pairs.append((here + 1, (z * 4 + (y + step) % 4) * 2 + 1))
    return pairs


def pairs_x(step):
    return [(x, x ^ step) for x in range(4)]


SWAP = [(0, 1), (1, 0)]


def place():
    row = lax.axis_index("row")
    return lax.axis_index("pole"), lax.div(row, 4), lax.rem(row, 4), lax.axis_index("col")


def node_of(y):
    return 3 + 2 * lax.rem(y, 2) + lax.div(y, 2)


def vm():
    return pl.BlockSpec(memory_space=pltpu.VMEM)


def sm():
    return pl.BlockSpec(memory_space=pltpu.SMEM)


def in_hbm():
    return pl.BlockSpec(memory_space=pltpu.HBM)


def hbm():
    return pl.BlockSpec(memory_space=pl.ANY)


def call(kernel, outs, in_specs, out_specs, scratch=(), flops=0, nbytes=0, aliases={}):
    return pl.pallas_call(
        kernel,
        out_shape=outs,
        in_specs=in_specs,
        out_specs=out_specs,
        scratch_shapes=list(scratch),
        input_output_aliases=aliases,
        compiler_params=pltpu.CompilerParams(vmem_limit_bytes=VMEM_LIMIT),
        cost_estimate=pl.CostEstimate(flops=flops, bytes_accessed=nbytes, transcendentals=0),
    )


def shape(*dims, dtype=BF):
    return jax.ShapeDtypeStruct(dims, dtype)


def pack(low, up, dia, widths, pattern, outs, own):
    x, z, y, c = place()
    rows = (32 * (4 * z + y)) + lax.broadcasted_iota(jnp.int32, (32, 256), 0)
    cols = lax.broadcasted_iota(jnp.int32, (32, 256), 1)

    def mask(row_node, col_node, on, half):
        keep = (rows < widths[row_node]) & (cols + 256 * half < widths[col_node]) & (on != 0)
        return jnp.where(keep, 1.0, 0.0).astype(BF)[None]

    @pl.when(c == 0)
    def _():
        h = 0 if own else 1
        for d, out in enumerate(outs):
            k = node_of(lax.rem(y + d, 4))
            p = lax.div(k - 1, 2)
            at = 2 * (k - 3) + 2
            out[0, h] = dia[p] * mask(p, p, 1, h)
            out[1, h] = low[at] * mask(p, k, pattern[at], h)
            out[2, h] = low[at + 1] * mask(0, k, pattern[at + 1], h)
            out[3, h] = up[at] * mask(k, p, pattern[at], h)
            out[4, h] = up[at + 1] * mask(k, 0, pattern[at + 1], h)
            out[5, h] = dia[k] * mask(k, k, 1, h)

    @pl.when(c == 1)
    def _():
        h = 1 if own else 0
        tiles = [dia[0] * mask(0, 0, 1, h)]
        for i in range(2):
            tiles.append(up[i] * mask(1 + i, 0, pattern[i], h))
            tiles.append(low[i] * mask(0, 1 + i, pattern[i], h))
        for out in outs:
            for t in range(5):
                out[t, h] = tiles[t]


def pack_own_kernel(
    low_in, up_in, dia_in, widths_in, pattern_in, o0, o1, o2, o3, widths, pattern, low, up, dia, sems
):
    run_copies(
        [(low_in, low), (up_in, up), (dia_in, dia), (widths_in, widths), (pattern_in, pattern)],
        sems,
    )
    pack(low, up, dia, widths, pattern, (o0, o1, o2, o3), True)


def pack_other_kernel(low, up, dia, widths, pattern, i0, i1, i2, i3, *outs):
    pack(low, up, dia, widths, pattern, outs, False)


def run_copies(copies, sems):
    made = [pltpu.make_async_copy(s, t, sems.at[i]) for i, (s, t) in enumerate(copies)]
    for m in made:
        m.start()
    for m in made:
        m.wait()


def merge_kernel(b0, b2, b3, b1, near, far, uk, sems):
    x, z, y, c = place()
    p = lax.rem(y, 2)

    @pl.when(c == 0)
    def _():
        copies = []
        for d, buf in enumerate((b0, b1, b2, b3)):
            at = lax.rem(y + 4 - d, 4)
            copies.append((buf.at[pl.ds(0, 3)], near.at[:, :, :, at]))
            copies.append((buf.at[pl.ds(0, 3)], far.at[:, :, :, at]))
            copies.append((buf.at[pl.ds(3, 3)], uk.at[:, :, :, at]))
        run_copies(copies, sems)

    @pl.when(c == 1)
    def _():
        copies = []
        for d, buf in enumerate((b0, b1, b2, b3)):
            at = lax.rem(z + 4 - d, 4)
            copies.append((buf.at[0], near.at[0, :, :, at]))
            copies.append((buf.at[0], far.at[0, :, :, at]))
            copies.append((buf.at[pl.ds(1 + 2 * p, 2)], far.at[pl.ds(1, 2), :, :, at]))
            copies.append((buf.at[pl.ds(3 - 2 * p, 2)], near.at[pl.ds(1, 2), :, :, at]))
        run_copies(copies, sems)


def left_of(pairs):
    real = [jnp.concatenate([r, -i], axis=1) for r, i in pairs]
    imag = [jnp.concatenate([i, r], axis=1) for r, i in pairs]
    return jnp.concatenate(real + imag, axis=0)


def dot(a, b):
    return jnp.dot(a, b, preferred_element_type=F32)


def pairs_of(res, count):
    half = 128 * count
    return [
        (res[128 * i : 128 * i + 128], res[half + 128 * i : half + 128 * i + 128])
        for i in range(count)
    ]


def split_kernel(r0, r3, r2, r1, after, first, second, sems):
    x, z, y, c = place()

    @pl.when(c == 0)
    def _():
        copies = []
        for d, buf in enumerate((r0, r1, r2, r3)):
            at = lax.rem(z + 4 - d, 4)
            copies.append((buf.at[pl.ds(1, 2), 0], first.at[:, :, at]))
            copies.append((buf.at[pl.ds(1, 2), 1], second.at[:, :, at]))
        run_copies(copies, sems)


def wide_rows(get):
    return tuple(jnp.concatenate([get(0, part), get(1, part)], axis=1) for part in range(2))


def times(left, count, right):
    got = [pairs_of(dot(left, right[h].reshape(1024, 256)), count) for h in range(2)]
    return [
        tuple(jnp.concatenate([got[0][n][i], got[1][n][i]], axis=1) for i in range(2))
        for n in range(count)
    ]


def put(out, slot, pair, sign=1):
    for i in range(2):
        out[slot, i] = (pair[i] if sign > 0 else -pair[i]).astype(BF)


def first_kernel(r0, r3, r2, r1, uk, uks, after, out, last, right, sems):
    x, z, y, c = place()

    def rows_of(block):
        return wide_rows(lambda h, part: right[block, h, part, z].reshape(128, 256))

    @pl.when(c == 0)
    def _():
        copies = []
        for d, buf in enumerate((r0, r1, r2, r3)):
            copies.append((buf.at[0], right.at[0, :, :, lax.rem(z + 4 - d, 4)]))
        run_copies(copies, sems)
        ukp = wide_rows(lambda h, part: uk[0, h, part].reshape(128, 256))
        (kd,) = times(left_of([ukp]), 1, right[0])
        put(out, 0, kd)
        put(out, 1, rows_of(0))

    @pl.when(c == 1)
    def _():
        copies = []
        for d, buf in enumerate((r0, r1, r2, r3)):
            at = lax.rem(y + 4 - d, 4)
            copies.append((buf.at[pl.ds(0, 2)], right.at[:, :, :, :, at]))
            copies.append((buf.at[2], last.at[:, :, :, at]))
        run_copies(copies, sems)
        ukp = wide_rows(lambda h, part: uks[0, h, part].reshape(128, 256))
        uk0 = wide_rows(lambda h, part: uks[1, h, part].reshape(128, 256))
        (kv,) = times(left_of([ukp]), 1, right[1])
        v = tuple((uk0[i].astype(F32) - kv[i]).astype(BF) for i in range(2))
        xk0, xp0 = times(left_of([v, rows_of(1)]), 2, right[0])
        put(out, 0, xp0, -1)
        put(out, 1, rows_of(0))
        put(out, 2, xk0, -1)


def next_kernel(edge, last, after, out):
    x, z, y, c = place()

    @pl.when(c == 1)
    def _():
        pl_, dl, kl = times(left_of([(edge[n, 0], edge[n, 1]) for n in range(3)]), 3, last)
        put(out, 0, pl_)
        put(out, 1, dl, -1)
        put(out, 2, kl)


def density_of(res):
    wr, wi = res[0, 0], res[0, 1]
    return lambda re, im: wr * re.astype(F32) - wi * im.astype(F32)


def third_kernel(edge, edge_s, half0, half1, res, prod, dens):
    x, z, y, c = place()
    density = density_of(res)

    def work(e, right, half):
        own = slice(256 * half, 256 * half + 256)
        left = left_of([(e[n, 0], e[n, 1]) for n in range(3)])
        prod[...] = dot(left, right[1].reshape(1024, 256))
        dens[0] = density(e[2, 0, :, own], e[2, 1, :, own])

        @pl.when(y < 2)
        def _():
            dens[1] = density(e[1, 0, :, own], e[1, 1, :, own])

        @pl.when(y >= 2)
        def _():
            dens[1] = density(e[0, 0, :, own], e[0, 1, :, own])

    @pl.when(c == 0)
    def _():
        work(edge_s, half0, 0)

    @pl.when(c == 1)
    def _():
        work(edge, half1, 1)


def last_kernel(
    edge, edge_s, more, more_s, half0, half1, prod, dens, uk, uks, res,
    slot0, slot1, slot2, slot3, parts,
):
    x, z, y, c = place()
    density = density_of(res)

    def work(e0, e1, right, dk, half):
        own = slice(256 * half, 256 * half + 256)
        xpp = [e0[1, i].astype(F32) - e1[0, i].astype(F32) for i in range(2)]
        xkp = [-(e0[0, i].astype(F32) + e1[2, i].astype(F32)) for i in range(2)]
        left = left_of(
            [
                tuple(v.astype(BF) for v in xpp),
                (e1[1, 0], e1[1, 1]),
                tuple(v.astype(BF) for v in xkp),
            ]
        )
        pk, ok, kk = pairs_of(prod[...] + dot(left, right[0].reshape(1024, 256)), 3)
        parts[0] = density(
            dk[2, half, 0].reshape(128, 256).astype(F32) - kk[0],
            dk[2, half, 1].reshape(128, 256).astype(F32) - kk[1],
        )
        parts[1] = density(-pk[0], -pk[1])
        parts[2] = density(-ok[0], -ok[1])
        parts[3] = density(xkp[0][:, own], xkp[1][:, own])
        parts[4] = dens[0]
        parts[5] = dens[1]

        @pl.when(y < 2)
        def _():
            parts[6] = density(xpp[0][:, own], xpp[1][:, own])

        @pl.when(y >= 2)
        def _():
            parts[6] = density(e1[1, 0, :, own], e1[1, 1, :, own])

    @pl.when(c == 0)
    def _():
        work(edge, more_s, half0, uk, 0)

    @pl.when(c == 1)
    def _():
        work(edge_s, more, half1, uks, 1)

    for d, out in enumerate((slot0, slot1, slot2, slot3)):
        at = pl.multiple_of(32 * lax.rem((x ^ d) + y, 4), 32)
        for b in range(7):
            out[b] = parts[b, pl.ds(at, 32), :].astype(BF)


def sum_kernel(a0, a1, a2, a3, out):
    total = a0[...].astype(F32) + a1[...].astype(F32)
    out[...] = (total + (a2[...].astype(F32) + a3[...].astype(F32))).astype(BF)


def spread(step):
    return [
        (x * 16 + z * 4 + y, ((x + step) % 4) * 16 + z * 4 + (x + y) % 4)
        for x in range(4)
        for z in range(4)
        for y in range(4)
    ]


def final_kernel(g0, g1, g3, g2, out):
    x, z, y, c = place()
    for d, g in enumerate((g0, g1, g2, g3)):
        b = lax.rem(y + 8 - x + d, 4)
        k = node_of(b)
        p = 1 + lax.rem(b, 2)
        pair = 2 * (k - 3) + 2
        low = b < 2
        out[k] = g[0].astype(F32)
        out[7 + pair] = g[1].astype(F32)
        out[8 + pair] = g[2].astype(F32)
        out[17 + pair] = g[3].astype(F32)
        out[18 + pair] = g[4].astype(F32)
        out[jnp.where(low, p, 6 + p)] = g[6].astype(F32)

        @pl.when(b != 1)
        def _():
            out[jnp.where(low, 0, 16 + p)] = g[5].astype(F32)


def body(lower_factor, upper_factor, diag_inverse, residues, widths, pattern):
    mine = (lower_factor[0], upper_factor[0], diag_inverse[0])
    swapped = [lax.ppermute(a, "col", SWAP) for a in mine]
    grid = ("row", "col")
    *bufs, widths, pattern = call(
        pack_own_kernel,
        [shape(6, 2, 2, 32, 256)] * 4 + [shape(7, dtype=jnp.int32), shape(10, dtype=jnp.int32)],
        [in_hbm()] * 5,
        [vm()] * 4 + [sm()] * 2,
        [
            pltpu.VMEM((10, 2, 32, 256), BF),
            pltpu.VMEM((10, 2, 32, 256), BF),
            pltpu.VMEM((7, 2, 32, 256), BF),
            pltpu.SemaphoreType.DMA((5,)),
        ],
        nbytes=4 << 20,
    )(*[pltpu.with_memory_space_constraint(a, pltpu.HBM) for a in (*mine, widths, pattern)])
    bufs = call(
        pack_other_kernel,
        [shape(6, 2, 2, 32, 256)] * 4,
        [vm()] * 3 + [sm()] * 2 + [hbm()] * 4,
        [vm()] * 4,
        nbytes=4 << 20,
        aliases={5: 0, 6: 1, 7: 2, 8: 3},
    )(*swapped, widths, pattern, *bufs)
    came = {d: lax.ppermute(bufs[d], grid, ring_both(d)) for d in (1, 3, 2)}
    near, far, uk = call(
        merge_kernel,
        [shape(3, 2, 2, 4, 32, 256)] * 3,
        [hbm()] * 4,
        [hbm()] * 3,
        [pltpu.SemaphoreType.DMA((16,))],
        nbytes=4 << 20,
    )(bufs[0], came[2], came[3], came[1])
    came = {d: lax.ppermute(near, grid, ring_other(d)) for d in (1, 3)}
    came[2] = lax.ppermute(far, grid, ring_other(2))
    uks = lax.ppermute(uk, "col", SWAP)
    blocks = (far, came[3], came[2], came[1])
    half0, half1 = call(
        split_kernel,
        [shape(2, 2, 4, 4, 32, 256)] * 2,
        [hbm()] * 5,
        [hbm()] * 2,
        [pltpu.SemaphoreType.DMA((8,))],
        nbytes=4 << 20,
    )(*blocks, uks)
    half1 = lax.ppermute(half1, "col", SWAP)
    edge, last = call(
        first_kernel,
        [shape(3, 2, 128, 512), shape(2, 2, 4, 4, 32, 256)],
        [hbm()] * 4 + [vm()] * 2 + [hbm()],
        [vm(), hbm()],
        [pltpu.VMEM((2, 2, 2, 4, 4, 32, 256), BF), pltpu.SemaphoreType.DMA((8,))],
        flops=805306368,
        nbytes=4 << 20,
    )(*blocks, uk, uks, half0)
    edge_s = lax.ppermute(edge, "col", SWAP)
    more = call(
        next_kernel,
        [shape(3, 2, 128, 512)],
        [vm(), vm(), hbm()],
        [vm()],
        flops=805306368,
        nbytes=2 << 20,
    )(edge, last, half1)[0]
    more_s = lax.ppermute(more, "col", SWAP)
    prod, dens = call(
        third_kernel,
        [shape(768, 256, dtype=F32), shape(2, 128, 256, dtype=F32)],
        [vm()] * 4 + [sm()],
        [vm()] * 2,
        flops=402653184,
        nbytes=2 << 20,
    )(edge, edge_s, half0, half1, residues)
    slots = call(
        last_kernel,
        [shape(7, 32, 256)] * 4,
        [vm()] * 10 + [sm()],
        [vm()] * 4,
        [pltpu.VMEM((7, 128, 256), F32)],
        flops=402653184,
        nbytes=4 << 20,
    )(edge, edge_s, more, more_s, half0, half1, prod, dens, uk, uks, residues)
    at_x = [slots[0]] + [lax.ppermute(slots[d], "pole", pairs_x(d)) for d in (2, 3, 1)]
    total = call(sum_kernel, [shape(7, 32, 256)], [vm()] * 4, [vm()], nbytes=1 << 20)(*at_x)[0]
    sent = {d: lax.ppermute(total, ("pole", "row"), spread(d)) for d in (0, 1, 3, 2)}
    full = [sent[d] for d in (0, 1, 3, 2)]
    return call(
        final_kernel, [shape(27, 32, 256, dtype=F32)], [vm()] * 4, [vm()], nbytes=2 << 20
    )(*full)[0]


def solution(mesh):
    return jax.shard_map(
        body,
        mesh=mesh,
        in_specs=(
            P("pole", None, None, "row", "col"),
            P("pole", None, None, "row", "col"),
            P("pole", None, None, "row", "col"),
            P("pole", None),
            P(),
            P(),
        ),
        out_specs=P(None, "row", "col"),
        check_vma=False,
    )
```

time: 79.9 us -> 74.8 us (0.936)
  the two profiles are of different devices: /device:TPU:0 before, /device:TPU:4 now
where the time goes in v3:
time: 74.8 us; the launch traced here: 74.7 us
  waiting for transfers between devices  36.6 us (49%)
  starting transfers between devices  30.5 us (41%)
  Pallas kernels  7.47 us (10%)
    ppermute x2, waiting for transfers between devices, body(): came = {d: lax.ppermute(near, grid, ring_other(d)) for d in (1, 3)}  16.2 us
    ppermute x4, starting transfers between devices, body(): lax.ppermute(total, ('pole', 'row'), spread(d))  11.3 us
    ppermute x3, waiting for transfers between devices, body(): came = {d: lax.ppermute(bufs[d], grid, ring_both(d)) for d in (1, 3, 2)}  8.66 us
    ppermute x3, starting transfers between devices, body(): came = {d: lax.ppermute(bufs[d], grid, ring_both(d)) for d in (1, 3, 2)}  5.3 us
    ppermute x3, starting transfers between devices, body(): lax.ppermute(slots[d], 'pole', pairs_x(d))  4.79 us
    ppermute x4, waiting for transfers between devices, body(): lax.ppermute(total, ('pole', 'row'), spread(d))  4.58 us
    ppermute x2, starting transfers between devices, body(): came = {d: lax.ppermute(near, grid, ring_other(d)) for d in (1, 3)}  4.19 us
    ppermute x3, waiting for transfers between devices, body(): lax.ppermute(slots[d], 'pole', pairs_x(d))  3.8 us
  transfers between devices with their start and end apart: 20, of which 13 were waited for; matrix products, arithmetic and copies ran while one was open for 0% of the time, Pallas kernels for 5%

profile of v3, /device:TPU:4, one launch (start us, length us, event | category | flops | bytes accessed | tf_op | source)
XLA Modules:
  0.0 74.7 jit_solution(7021448746109589387)
XLA Ops:
  0.5 1.9 %shard_map.64 = (bf16[6,2,2,32,256]{4,3,2,1,0:T(8,128)(2,1)S(1)}, bf16[6,2,2,32,256]{4,3,2,1,0:T(8,128)(2,1)S(1)}, bf16[6,2,2,32,256]{4,3,2,1,0:T(8,128)(2,1)S(1...) custom-call(bf16[10,2,32,256]{3,2,1,0:T(8,128)(2,1)} %bitcast.4, ...), custom_call_target="tpu_custom_call" | custom-call | bytes 4194304 | tf_op jit(solution)/shard_map/pallas_call | solution.py:380
  3.3 3.3 %collective-permute-start.3 = (bf16[6,2,2,32,256]{4,3,2,1,0:T(8,128)(2,1)S(1)}, bf16[6,2,2,32,256]{4,3,2,1,0:T(8,128)(2,1)S(1)}, u32[]{:S(2)}, u32[]{:S(2)}) collective-permute-start(bf16[6,2,2,32,256]{4,3,2,1,0:T(8,128)(2,1)S(1)} %get-tuple-element.35), channel_id=1, source_target_pairs={{0,4},{1,17},{2,6},{3,19},{4,0},{5,21},{6,2},{7,23},{8,12},{9,25},... | collective-permute-start | bytes 1179656 | tf_op jit(solution)/shard_map/ppermute | solution.py:401
  6.6 1.1 %collective-permute-start.4 = (bf16[6,2,2,32,256]{4,3,2,1,0:T(8,128)(2,1)S(1)}, bf16[6,2,2,32,256]{4,3,2,1,0:T(8,128)(2,1)S(1)}, u32[]{:S(2)}, u32[]{:S(2)}) collective-permute-start(bf16[6,2,2,32,256]{4,3,2,1,0:T(8,128)(2,1)S(1)} %get-tuple-element.36), channel_id=1, source_target_pairs={{0,6},{1,25},{2,0},{3,27},{4,2},{5,29},{6,4},{7,31},{8,14},{9,1},{... | collective-permute-start | bytes 1179656 | tf_op jit(solution)/shard_map/ppermute | solution.py:401
  8.6 4.1 %collective-permute-done.3.b2 = bf16[6,2,2,32,256]{4,3,2,1,0:T(8,128)(2,1)S(1)} collective-permute-done((bf16[6,2,2,32,256]{4,3,2,1,0:T(8,128)(2,1)S(1)}, bf16[6,2,2,32,256]{4,3,2,1,0:T(8,128)(2,1)S(1)}, u32[]{:S(2)}, u32[]{:S(2)}) %collective-permute-start.3) | collective-permute-done | bytes 393248 | tf_op jit(solution)/shard_map/ppermute | solution.py:401
  12.7 4.6 %collective-permute-done.4.b3 = bf16[6,2,2,32,256]{4,3,2,1,0:T(8,128)(2,1)S(1)} collective-permute-done((bf16[6,2,2,32,256]{4,3,2,1,0:T(8,128)(2,1)S(1)}, bf16[6,2,2,32,256]{4,3,2,1,0:T(8,128)(2,1)S(1)}, u32[]{:S(2)}, u32[]{:S(2)}) %collective-permute-start.4) | collective-permute-done | bytes 393248 | tf_op jit(solution)/shard_map/ppermute | solution.py:401
  17.8 2.0 %collective-permute-start.8 = (bf16[3,2,2,4,32,256]{5,4,3,2,1,0:T(8,128)(2,1)S(1)}, bf16[3,2,2,4,32,256]{5,4,3,2,1,0:T(8,128)(2,1)S(1)}, u32[]{:S(2)}, u32[]{:S(2)}) collective-permute-start(bf16[3,2,2,4,32,256]{5,4,3,2,1,0:T(8,128)(2,1)S(1)} %get-tuple-element.39), channel_id=1, source_target_pairs={{0,8},{1,3},{2,10},{3,5},{4,12},{5,7},{6,14},{7,1},{8,16},{9,11},{... | collective-permute-start | bytes 2359304 | tf_op jit(solution)/shard_map/ppermute | solution.py:410
  19.8 2.2 %collective-permute-start.6 = (bf16[3,2,2,4,32,256]{5,4,3,2,1,0:T(8,128)(2,1)S(1)}, bf16[3,2,2,4,32,256]{5,4,3,2,1,0:T(8,128)(2,1)S(1)}, u32[]{:S(2)}, u32[]{:S(2)}) collective-permute-start(bf16[3,2,2,4,32,256]{5,4,3,2,1,0:T(8,128)(2,1)S(1)} %get-tuple-element.39), channel_id=1, source_target_pairs={{0,24},{1,7},{2,26},{3,1},{4,28},{5,3},{6,30},{7,5},{8,0},{9,15},{... | collective-permute-start | bytes 2359304 | tf_op jit(solution)/shard_map/ppermute | solution.py:410
  22.0 1.8 %collective-permute-start.7 = (bf16[3,2,2,4,32,256]{5,4,3,2,1,0:T(8,128)(2,1)S(1)}, bf16[3,2,2,4,32,256]{5,4,3,2,1,0:T(8,128)(2,1)S(1)}, u32[]{:S(2)}, u32[]{:S(2)}) collective-permute-start(bf16[3,2,2,4,32,256]{5,4,3,2,1,0:T(8,128)(2,1)S(1)} %get-tuple-element.38.r0), channel_id=1, source_target_pairs={{0,16},{1,5},{2,18},{3,7},{4,20},{5,1},{6,22},{7,3},{8,24},{9,13},... | collective-permute-start | bytes 2359304 | tf_op jit(solution)/shard_map/ppermute | solution.py:411
  23.8 8.1 %collective-permute-done.8.r1 = bf16[3,2,2,4,32,256]{5,4,3,2,1,0:T(8,128)(2,1)S(1)} collective-permute-done((bf16[3,2,2,4,32,256]{5,4,3,2,1,0:T(8,128)(2,1)S(1)}, bf16[3,2,2,4,32,256]{5,4,3,2,1,0:T(8,128)(2,1)S(1)}, u32[]{:S(2)}, u32[]{:S(2)}) %collective-permute-start.8) | collective-permute-done | bytes 786464 | tf_op jit(solution)/shard_map/ppermute | solution.py:410
  31.9 8.1 %collective-permute-done.6.r3 = bf16[3,2,2,4,32,256]{5,4,3,2,1,0:T(8,128)(2,1)S(1)} collective-permute-done((bf16[3,2,2,4,32,256]{5,4,3,2,1,0:T(8,128)(2,1)S(1)}, bf16[3,2,2,4,32,256]{5,4,3,2,1,0:T(8,128)(2,1)S(1)}, u32[]{:S(2)}, u32[]{:S(2)}) %collective-permute-start.6) | collective-permute-done | bytes 786464 | tf_op jit(solution)/shard_map/ppermute | solution.py:410
  40.0 1.8 %collective-permute-done.7.r2 = bf16[3,2,2,4,32,256]{5,4,3,2,1,0:T(8,128)(2,1)S(1)} collective-permute-done((bf16[3,2,2,4,32,256]{5,4,3,2,1,0:T(8,128)(2,1)S(1)}, bf16[3,2,2,4,32,256]{5,4,3,2,1,0:T(8,128)(2,1)S(1)}, u32[]{:S(2)}, u32[]{:S(2)}) %collective-permute-start.7) | collective-permute-done | bytes 786464 | tf_op jit(solution)/shard_map/ppermute | solution.py:411
  42.8 1.4 %collective-permute-start.10 = (bf16[3,2,128,512]{3,2,1,0:T(8,128)(2,1)S(1)}, bf16[3,2,128,512]{3,2,1,0:T(8,128)(2,1)S(1)}, u32[]{:S(2)}, u32[]{:S(2)}) collective-permute-start(bf16[3,2,128,512]{3,2,1,0:T(8,128)(2,1)S(1)} %get-tuple-element.42.edge), channel_id=1, source_target_pairs={{0,1},{1,0},{2,3},{3,2},{4,5},{5,4},{6,7},{7,6},{8,9},{9,8},{10,11... | collective-permute-start | bytes 2359304 | tf_op jit(solution)/shard_map/ppermute | solution.py:432
  44.8 1.2 %collective-permute-start.12 = (bf16[3,2,128,512]{3,2,1,0:T(8,128)(2,1)S(1)}, bf16[3,2,128,512]{3,2,1,0:T(8,128)(2,1)S(1)}, u32[]{:S(2)}, u32[]{:S(2)}) collective-permute-start(bf16[3,2,128,512]{3,2,1,0:T(8,128)(2,1)S(1)} %shard_map.69.more), channel_id=1, source_target_pairs={{0,1},{1,0},{2,3},{3,2},{4,5},{5,4},{6,7},{7,6},{8,9},{9,8},{10,11... | collective-permute-start | bytes 2359304 | tf_op jit(solution)/shard_map/ppermute | solution.py:441
  46.0 1.1 %shard_map.70 = (f32[768,256]{1,0:T(8,128)S(1)}, f32[2,128,256]{2,1,0:T(8,128)S(1)}) custom-call(bf16[3,2,128,512]{3,2,1,0:T(8,128)(2,1)S(1)} %get-tuple-element.42.edge, bf16[3,2,128,512]{3,2,1,0:T(8,128)(2,1)S(1)} %collective-permute-done.10.edge_s, bf16[2,2,4,4,32,256]{5,4,3,2,1,0:T(8,128)(2,1)S(1)} %get-tuple-element.41.after.half0, ...), custom_call_target="tpu_custom_call" | custom-call | flops 402653184 | bytes 2097152 | tf_op jit(solution)/shard_map/pallas_call | solution.py:442
  47.9 1.2 %shard_map.71 = (bf16[7,32,256]{2,1,0:T(8,128)(2,1)S(1)}, bf16[7,32,256]{2,1,0:T(8,128)(2,1)S(1)}, bf16[7,32,256]{2,1,0:T(8,128)(2,1)S(1)}, bf16[7,32,256]{2,1,0:T(8,128)(2,1)S(1)}) custom-call(bf16[3,2,128,512]{3,2,1,0:T(8,128)(2,1)S(1)} %get-tuple-element.42.edge, bf16[3,2,128,512]{3,2,1,0:T(8,128)(2,1)S(1)} %collective-permute-done.10.edge_s, ...), custom_call_target="tpu_custom_call" | custom-call | flops 402653184 | bytes 4194304 | tf_op jit(solution)/shard_map/pallas_call | solution.py:450
  49.7 2.2 %collective-permute-start.14 = (bf16[7,32,256]{2,1,0:T(8,128)(2,1)S(1)}, bf16[7,32,256]{2,1,0:T(8,128)(2,1)S(1)}, u32[]{:S(2)}, u32[]{:S(2)}) collective-permute-start(bf16[7,32,256]{2,1,0:T(8,128)(2,1)S(1)} %get-tuple-element.49), channel_id=1, source_target_pairs={{0,96},{32,64},{64,32},{96,0},{1,97},{33,65},{65,33},{97,1},{2,98}... | collective-permute-start | bytes 344072 | tf_op jit(solution)/shard_map/ppermute | solution.py:459
  51.9 2.0 %collective-permute-start.15 = (bf16[7,32,256]{2,1,0:T(8,128)(2,1)S(1)}, bf16[7,32,256]{2,1,0:T(8,128)(2,1)S(1)}, u32[]{:S(2)}, u32[]{:S(2)}) collective-permute-start(bf16[7,32,256]{2,1,0:T(8,128)(2,1)S(1)} %get-tuple-element.50), channel_id=1, source_target_pairs={{0,32},{32,0},{64,96},{96,64},{1,33},{33,1},{65,97},{97,65},{2,34}... | collective-permute-start | bytes 344072 | tf_op jit(solution)/shard_map/ppermute | solution.py:459
  53.9 2.8 %collective-permute-done.13.a1 = bf16[7,32,256]{2,1,0:T(8,128)(2,1)S(1)} collective-permute-done((bf16[7,32,256]{2,1,0:T(8,128)(2,1)S(1)}, bf16[7,32,256]{2,1,0:T(8,128)(2,1)S(1)}, u32[]{:S(2)}, u32[]{:S(2)}) %collective-permute-start.13) | collective-permute-done | bytes 114720 | tf_op jit(solution)/shard_map/ppermute | solution.py:459
  57.8 3.8 %collective-permute-start.19 = (bf16[7,32,256]{2,1,0:T(8,128)(2,1)S(1)}, bf16[7,32,256]{2,1,0:T(8,128)(2,1)S(1)}, u32[]{:S(2)}, u32[]{:S(2)}) collective-permute-start(bf16[7,32,256]{2,1,0:T(8,128)(2,1)S(1)} %shard_map.72), channel_id=1, source_target_pairs={{0,64},{2,66},{4,68},{6,70},{8,72},{10,74},{12,76},{14,78},{16,80}... | collective-permute-start | bytes 344072 | tf_op jit(solution)/shard_map/ppermute | solution.py:461
  61.5 2.8 %collective-permute-start.18 = (bf16[7,32,256]{2,1,0:T(8,128)(2,1)S(1)}, bf16[7,32,256]{2,1,0:T(8,128)(2,1)S(1)}, u32[]{:S(2)}, u32[]{:S(2)}) collective-permute-start(bf16[7,32,256]{2,1,0:T(8,128)(2,1)S(1)} %shard_map.72), channel_id=1, source_target_pairs={{0,96},{2,98},{4,100},{6,102},{8,104},{10,106},{12,108},{14,110},{... | collective-permute-start | bytes 344072 | tf_op jit(solution)/shard_map/ppermute | solution.py:461
  65.2 3.9 %collective-permute-start.16 = (bf16[7,32,256]{2,1,0:T(8,128)(2,1)S(1)}, bf16[7,32,256]{2,1,0:T(8,128)(2,1)S(1)}, u32[]{:S(2)}, u32[]{:S(2)}) collective-permute-start(bf16[7,32,256]{2,1,0:T(8,128)(2,1)S(1)} %shard_map.72), channel_id=1, source_target_pairs={{0,0},{2,2},{4,4},{6,6},{8,8},{10,10},{12,12},{14,14},{16,16},{18,... | collective-permute-start | bytes 344072 | tf_op jit(solution)/shard_map/ppermute | solution.py:461
  69.1 2.5 %collective-permute-done.17.g1 = bf16[7,32,256]{2,1,0:T(8,128)(2,1)S(1)} collective-permute-done((bf16[7,32,256]{2,1,0:T(8,128)(2,1)S(1)}, bf16[7,32,256]{2,1,0:T(8,128)(2,1)S(1)}, u32[]{:S(2)}, u32[]{:S(2)}) %collective-permute-start.17) | collective-permute-done | bytes 114720 | tf_op jit(solution)/shard_map/ppermute | solution.py:461
  71.7 2.0 %collective-permute-done.16.g0 = bf16[7,32,256]{2,1,0:T(8,128)(2,1)S(1)} collective-permute-done((bf16[7,32,256]{2,1,0:T(8,128)(2,1)S(1)}, bf16[7,32,256]{2,1,0:T(8,128)(2,1)S(1)}, u32[]{:S(2)}, u32[]{:S(2)}) %collective-permute-start.16) | collective-permute-done | bytes 114720 | tf_op jit(solution)/shard_map/ppermute | solution.py:461
  73.7 1.0 %shard_map.73 = f32[27,32,256]{2,1,0:T(8,128)} custom-call(bf16[7,32,256]{2,1,0:T(8,128)(2,1)S(1)} %collective-permute-done.16.g0, bf16[7,32,256]{2,1,0:T(8,128)(2,1)S(1)} %collective-permute-done.17.g1, bf16[7,32,256]{2,1,0:T(8,128)(2,1)S(1)} %collective-permute-done.18.g3, bf16[7,32,256]{2,1,0:T(8,128)(2,1)S(1)} %collective-permute-done.19.g2), custom_call_target="tpu_custom_call" | custom-call | bytes 2097152 | tf_op jit(solution)/shard_map/pallas_call | solution.py:463
  (28 shorter events, 7.7 us)
Async XLA Ops:
  0.0 2.6 %collective-permute-start = (bf16[10,2,32,256]{3,2,1,0:T(8,128)(2,1)}, bf16[10,2,32,256]{3,2,1,0:T(8,128)(2,1)S(1)}, u32[]{:S(2)}, u32[]{:S(2)}) collective-permute-start(bf16[10,2,32,256]{3,2,1,0:T(8,128)(2,1)} %bitcast.3), channel_id=1, source_target_pairs={{0,1},{1,0},{2,3},{3,2},{4,5},{5,4},{6,7},{7,6},{8,9},{9,8},{10,11... | collective-permute-start | bytes 983048 | tf_op jit(solution)/shard_map/ppermute | solution.py:378
  0.0 2.6 %collective-permute-start.1 = (bf16[10,2,32,256]{3,2,1,0:T(8,128)(2,1)}, bf16[10,2,32,256]{3,2,1,0:T(8,128)(2,1)S(1)}, u32[]{:S(2)}, u32[]{:S(2)}) collective-permute-start(bf16[10,2,32,256]{3,2,1,0:T(8,128)(2,1)} %bitcast.5), channel_id=1, source_target_pairs={{0,1},{1,0},{2,3},{3,2},{4,5},{5,4},{6,7},{7,6},{8,9},{9,8},{10,11... | collective-permute-start | bytes 983048 | tf_op jit(solution)/shard_map/ppermute | solution.py:378
  0.5 2.1 %collective-permute-start.2 = (bf16[7,2,32,256]{3,2,1,0:T(8,128)(2,1)}, bf16[7,2,32,256]{3,2,1,0:T(8,128)(2,1)S(1)}, u32[]{:S(2)}, u32[]{:S(2)}) collective-permute-start(bf16[7,2,32,256]{3,2,1,0:T(8,128)(2,1)} %bitcast.7), channel_id=1, source_target_pairs={{0,1},{1,0},{2,3},{3,2},{4,5},{5,4},{6,7},{7,6},{8,9},{9,8},{10,11... | collective-permute-start | bytes 688136 | tf_op jit(solution)/shard_map/ppermute | solution.py:378
  3.3 9.4 %collective-permute-start.3 = (bf16[6,2,2,32,256]{4,3,2,1,0:T(8,128)(2,1)S(1)}, bf16[6,2,2,32,256]{4,3,2,1,0:T(8,128)(2,1)S(1)}, u32[]{:S(2)}, u32[]{:S(2)}) collective-permute-start(bf16[6,2,2,32,256]{4,3,2,1,0:T(8,128)(2,1)S(1)} %get-tuple-element.35), channel_id=1, source_target_pairs={{0,4},{1,17},{2,6},{3,19},{4,0},{5,21},{6,2},{7,23},{8,12},{9,25},... | collective-permute-start | bytes 1179656 | tf_op jit(solution)/shard_map/ppermute | solution.py:401
  6.6 10.7 %collective-permute-start.4 = (bf16[6,2,2,32,256]{4,3,2,1,0:T(8,128)(2,1)S(1)}, bf16[6,2,2,32,256]{4,3,2,1,0:T(8,128)(2,1)S(1)}, u32[]{:S(2)}, u32[]{:S(2)}) collective-permute-start(bf16[6,2,2,32,256]{4,3,2,1,0:T(8,128)(2,1)S(1)} %get-tuple-element.36), channel_id=1, source_target_pairs={{0,6},{1,25},{2,0},{3,27},{4,2},{5,29},{6,4},{7,31},{8,14},{9,1},{... | collective-permute-start | bytes 1179656 | tf_op jit(solution)/shard_map/ppermute | solution.py:401
  7.7 9.6 %collective-permute-start.5 = (bf16[6,2,2,32,256]{4,3,2,1,0:T(8,128)(2,1)S(1)}, bf16[6,2,2,32,256]{4,3,2,1,0:T(8,128)(2,1)S(1)}, u32[]{:S(2)}, u32[]{:S(2)}) collective-permute-start(bf16[6,2,2,32,256]{4,3,2,1,0:T(8,128)(2,1)S(1)} %get-tuple-element.37), channel_id=1, source_target_pairs={{0,2},{1,9},{2,4},{3,11},{4,6},{5,13},{6,0},{7,15},{8,10},{9,17},{... | collective-permute-start | bytes 1179656 | tf_op jit(solution)/shard_map/ppermute | solution.py:401
  17.8 14.1 %collective-permute-start.8 = (bf16[3,2,2,4,32,256]{5,4,3,2,1,0:T(8,128)(2,1)S(1)}, bf16[3,2,2,4,32,256]{5,4,3,2,1,0:T(8,128)(2,1)S(1)}, u32[]{:S(2)}, u32[]{:S(2)}) collective-permute-start(bf16[3,2,2,4,32,256]{5,4,3,2,1,0:T(8,128)(2,1)S(1)} %get-tuple-element.39), channel_id=1, source_target_pairs={{0,8},{1,3},{2,10},{3,5},{4,12},{5,7},{6,14},{7,1},{8,16},{9,11},{... | collective-permute-start | bytes 2359304 | tf_op jit(solution)/shard_map/ppermute | solution.py:410
  19.8 20.2 %collective-permute-start.6 = (bf16[3,2,2,4,32,256]{5,4,3,2,1,0:T(8,128)(2,1)S(1)}, bf16[3,2,2,4,32,256]{5,4,3,2,1,0:T(8,128)(2,1)S(1)}, u32[]{:S(2)}, u32[]{:S(2)}) collective-permute-start(bf16[3,2,2,4,32,256]{5,4,3,2,1,0:T(8,128)(2,1)S(1)} %get-tuple-element.39), channel_id=1, source_target_pairs={{0,24},{1,7},{2,26},{3,1},{4,28},{5,3},{6,30},{7,5},{8,0},{9,15},{... | collective-permute-start | bytes 2359304 | tf_op jit(solution)/shard_map/ppermute | solution.py:410
  22.0 19.8 %collective-permute-start.7 = (bf16[3,2,2,4,32,256]{5,4,3,2,1,0:T(8,128)(2,1)S(1)}, bf16[3,2,2,4,32,256]{5,4,3,2,1,0:T(8,128)(2,1)S(1)}, u32[]{:S(2)}, u32[]{:S(2)}) collective-permute-start(bf16[3,2,2,4,32,256]{5,4,3,2,1,0:T(8,128)(2,1)S(1)} %get-tuple-element.38.r0), channel_id=1, source_target_pairs={{0,16},{1,5},{2,18},{3,7},{4,20},{5,1},{6,22},{7,3},{8,24},{9,13},... | collective-permute-start | bytes 2359304 | tf_op jit(solution)/shard_map/ppermute | solution.py:411
  23.8 18.0 %collective-permute-start.9 = (bf16[3,2,2,4,32,256]{5,4,3,2,1,0:T(8,128)(2,1)S(1)}, bf16[3,2,2,4,32,256]{5,4,3,2,1,0:T(8,128)(2,1)S(1)}, u32[]{:S(2)}, u32[]{:S(2)}) collective-permute-start(bf16[3,2,2,4,32,256]{5,4,3,2,1,0:T(8,128)(2,1)S(1)} %get-tuple-element.40.uk), channel_id=1, source_target_pairs={{0,1},{1,0},{2,3},{3,2},{4,5},{5,4},{6,7},{7,6},{8,9},{9,8},{10,11... | collective-permute-start | bytes 2359304 | tf_op jit(solution)/shard_map/ppermute | solution.py:412
  42.0 2.7 %collective-permute-start.11 = (bf16[2,2,4,4,32,256]{5,4,3,2,1,0:T(8,128)(2,1)S(1)}, bf16[2,2,4,4,32,256]{5,4,3,2,1,0:T(8,128)(2,1)S(1)}, u32[]{:S(2)}, u32[]{:S(2)}) collective-permute-start(bf16[2,2,4,4,32,256]{5,4,3,2,1,0:T(8,128)(2,1)S(1)} %get-tuple-element.44), channel_id=1, source_target_pairs={{0,1},{1,0},{2,3},{3,2},{4,5},{5,4},{6,7},{7,6},{8,9},{9,8},{10,11... | collective-permute-start | bytes 3145736 | tf_op jit(solution)/shard_map/ppermute | solution.py:422
  42.8 3.3 %collective-permute-start.10 = (bf16[3,2,128,512]{3,2,1,0:T(8,128)(2,1)S(1)}, bf16[3,2,128,512]{3,2,1,0:T(8,128)(2,1)S(1)}, u32[]{:S(2)}, u32[]{:S(2)}) collective-permute-start(bf16[3,2,128,512]{3,2,1,0:T(8,128)(2,1)S(1)} %get-tuple-element.42.edge), channel_id=1, source_target_pairs={{0,1},{1,0},{2,3},{3,2},{4,5},{5,4},{6,7},{7,6},{8,9},{9,8},{10,11... | collective-permute-start | bytes 2359304 | tf_op jit(solution)/shard_map/ppermute | solution.py:432
  44.8 1.3 %copy-start = (f32[1,2]{1,0:T(1,128)S(1)}, f32[1,2]{1,0:T(1,128)}, u32[]{:S(2)}) copy-start(f32[1,2]{1,0:T(1,128)} %res.3) | copy-start | bytes 28
  44.8 3.1 %collective-permute-start.12 = (bf16[3,2,128,512]{3,2,1,0:T(8,128)(2,1)S(1)}, bf16[3,2,128,512]{3,2,1,0:T(8,128)(2,1)S(1)}, u32[]{:S(2)}, u32[]{:S(2)}) collective-permute-start(bf16[3,2,128,512]{3,2,1,0:T(8,128)(2,1)S(1)} %shard_map.69.more), channel_id=1, source_target_pairs={{0,1},{1,0},{2,3},{3,2},{4,5},{5,4},{6,7},{7,6},{8,9},{9,8},{10,11... | collective-permute-start | bytes 2359304 | tf_op jit(solution)/shard_map/ppermute | solution.py:441
  49.1 7.6 %collective-permute-start.13 = (bf16[7,32,256]{2,1,0:T(8,128)(2,1)S(1)}, bf16[7,32,256]{2,1,0:T(8,128)(2,1)S(1)}, u32[]{:S(2)}, u32[]{:S(2)}) collective-permute-start(bf16[7,32,256]{2,1,0:T(8,128)(2,1)S(1)} %get-tuple-element.48), channel_id=1, source_target_pairs={{0,64},{32,96},{64,0},{96,32},{1,65},{33,97},{65,1},{97,33},{2,66}... | collective-permute-start | bytes 344072 | tf_op jit(solution)/shard_map/ppermute | solution.py:459
  49.7 8.0 %collective-permute-start.14 = (bf16[7,32,256]{2,1,0:T(8,128)(2,1)S(1)}, bf16[7,32,256]{2,1,0:T(8,128)(2,1)S(1)}, u32[]{:S(2)}, u32[]{:S(2)}) collective-permute-start(bf16[7,32,256]{2,1,0:T(8,128)(2,1)S(1)} %get-tuple-element.49), channel_id=1, source_target_pairs={{0,96},{32,64},{64,32},{96,0},{1,97},{33,65},{65,33},{97,1},{2,98}... | collective-permute-start | bytes 344072 | tf_op jit(solution)/shard_map/ppermute | solution.py:459
  51.9 5.8 %collective-permute-start.15 = (bf16[7,32,256]{2,1,0:T(8,128)(2,1)S(1)}, bf16[7,32,256]{2,1,0:T(8,128)(2,1)S(1)}, u32[]{:S(2)}, u32[]{:S(2)}) collective-permute-start(bf16[7,32,256]{2,1,0:T(8,128)(2,1)S(1)} %get-tuple-element.50), channel_id=1, source_target_pairs={{0,32},{32,0},{64,96},{96,64},{1,33},{33,1},{65,97},{97,65},{2,34}... | collective-permute-start | bytes 344072 | tf_op jit(solution)/shard_map/ppermute | solution.py:459
  57.8 11.3 %collective-permute-start.19 = (bf16[7,32,256]{2,1,0:T(8,128)(2,1)S(1)}, bf16[7,32,256]{2,1,0:T(8,128)(2,1)S(1)}, u32[]{:S(2)}, u32[]{:S(2)}) collective-permute-start(bf16[7,32,256]{2,1,0:T(8,128)(2,1)S(1)} %shard_map.72), channel_id=1, source_target_pairs={{0,64},{2,66},{4,68},{6,70},{8,72},{10,74},{12,76},{14,78},{16,80}... | collective-permute-start | bytes 344072 | tf_op jit(solution)/shard_map/ppermute | solution.py:461
  61.5 7.6 %collective-permute-start.18 = (bf16[7,32,256]{2,1,0:T(8,128)(2,1)S(1)}, bf16[7,32,256]{2,1,0:T(8,128)(2,1)S(1)}, u32[]{:S(2)}, u32[]{:S(2)}) collective-permute-start(bf16[7,32,256]{2,1,0:T(8,128)(2,1)S(1)} %shard_map.72), channel_id=1, source_target_pairs={{0,96},{2,98},{4,100},{6,102},{8,104},{10,106},{12,108},{14,110},{... | collective-permute-start | bytes 344072 | tf_op jit(solution)/shard_map/ppermute | solution.py:461
  64.3 7.3 %collective-permute-start.17 = (bf16[7,32,256]{2,1,0:T(8,128)(2,1)S(1)}, bf16[7,32,256]{2,1,0:T(8,128)(2,1)S(1)}, u32[]{:S(2)}, u32[]{:S(2)}) collective-permute-start(bf16[7,32,256]{2,1,0:T(8,128)(2,1)S(1)} %shard_map.72), channel_id=1, source_target_pairs={{0,32},{2,34},{4,36},{6,38},{8,40},{10,42},{12,44},{14,46},{16,48}... | collective-permute-start | bytes 344072 | tf_op jit(solution)/shard_map/ppermute | solution.py:461
  65.2 8.5 %collective-permute-start.16 = (bf16[7,32,256]{2,1,0:T(8,128)(2,1)S(1)}, bf16[7,32,256]{2,1,0:T(8,128)(2,1)S(1)}, u32[]{:S(2)}, u32[]{:S(2)}) collective-permute-start(bf16[7,32,256]{2,1,0:T(8,128)(2,1)S(1)} %shard_map.72), channel_id=1, source_target_pairs={{0,0},{2,2},{4,4},{6,6},{8,8},{10,10},{12,12},{14,14},{16,16},{18,... | collective-permute-start | bytes 344072 | tf_op jit(solution)/shard_map/ppermute | solution.py:461

commit v4 on v3

--- a/solution.py
+++ b/solution.py
@@ -180,7 +180,7 @@
     ]
 
 
-def split_kernel(r0, r3, r2, r1, after, first, second, sems):
+def split_kernel(r0, r3, r2, r1, after, stay, go, sems):
     x, z, y, c = place()
 
     @pl.when(c == 0)
@@ -188,8 +188,15 @@
         copies = []
         for d, buf in enumerate((r0, r1, r2, r3)):
             at = lax.rem(z + 4 - d, 4)
-            copies.append((buf.at[pl.ds(1, 2), 0], first.at[:, :, at]))
-            copies.append((buf.at[pl.ds(1, 2), 1], second.at[:, :, at]))
+            copies.append((buf.at[pl.ds(1, 2), 0], stay.at[:, :, at]))
+            copies.append((buf.at[pl.ds(1, 2), 1], go.at[:, :, at]))
+        run_copies(copies, sems)
+
+    @pl.when(c == 1)
+    def _():
+        copies = []
+        for d, buf in enumerate((r0, r1, r2, r3)):
+            copies.append((buf.at[2], go.at[:, :, :, lax.rem(y + 4 - d, 4)]))
         run_copies(copies, sems)
 
 
@@ -210,7 +217,7 @@
         out[slot, i] = (pair[i] if sign > 0 else -pair[i]).astype(BF)
 
 
-def first_kernel(r0, r3, r2, r1, uk, uks, after, out, last, right, sems):
+def first_kernel(r0, r3, r2, r1, uk, uks, after, out, right, sems):
     x, z, y, c = place()
 
     def rows_of(block):
@@ -233,7 +240,6 @@
         for d, buf in enumerate((r0, r1, r2, r3)):
             at = lax.rem(y + 4 - d, 4)
             copies.append((buf.at[pl.ds(0, 2)], right.at[:, :, :, :, at]))
-            copies.append((buf.at[2], last.at[:, :, :, at]))
         run_copies(copies, sems)
         ukp = wide_rows(lambda h, part: uks[0, h, part].reshape(128, 256))
         uk0 = wide_rows(lambda h, part: uks[1, h, part].reshape(128, 256))
@@ -245,93 +251,64 @@
         put(out, 2, xk0, -1)
 
 
-def next_kernel(edge, last, after, out):
-    x, z, y, c = place()
-
-    @pl.when(c == 1)
-    def _():
-        pl_, dl, kl = times(left_of([(edge[n, 0], edge[n, 1]) for n in range(3)]), 3, last)
-        put(out, 0, pl_)
-        put(out, 1, dl, -1)
-        put(out, 2, kl)
-
-
-def density_of(res):
+def inner_kernel(stay, go, got, out):
+    x, z, y, c = place()
+
+    def work(last, own):
+        lp = wide_rows(lambda h, part: last[h, part].reshape(512, 256))
+        prod = dot(left_of([lp]), own[0].reshape(1024, 256))
+        out[...] = (own[1].reshape(1024, 256).astype(F32) - prod).astype(BF)
+
+    @pl.when(c == 0)
+    def _():
+        work(got, stay)
+
+    @pl.when(c == 1)
+    def _():
+        work(go, got)
+
+
+def last_kernel(
+    edge, edge_s, inner, stay, go, got, uk, uks, res, slot0, slot1, slot2, slot3, parts
+):
+    x, z, y, c = place()
     wr, wi = res[0, 0], res[0, 1]
-    return lambda re, im: wr * re.astype(F32) - wi * im.astype(F32)
-
-
-def third_kernel(edge, edge_s, half0, half1, res, prod, dens):
-    x, z, y, c = place()
-    density = density_of(res)
-
-    def work(e, right, half):
-        own = slice(256 * half, 256 * half + 256)
-        left = left_of([(e[n, 0], e[n, 1]) for n in range(3)])
-        prod[...] = dot(left, right[1].reshape(1024, 256))
-        dens[0] = density(e[2, 0, :, own], e[2, 1, :, own])
+
+    def density(re, im):
+        return wr * re.astype(F32) - wi * im.astype(F32)
+
+    def work(e0, e1, last, own, dk, half):
+        cols = slice(256 * half, 256 * half + 256)
+        xp0, d0r, xk0 = [(e1[n, 0], e1[n, 1]) for n in range(3)]
+        kd, dpr = [(e0[n, 0], e0[n, 1]) for n in range(2)]
+        left = left_of([xp0, d0r, xk0])
+        pg, og, kg = pairs_of(dot(left, inner[...]), 3)
+        pe, oe, ke = pairs_of(dot(left, last[half].reshape(1024, 256)), 3)
+        kl, pl_ = pairs_of(dot(left_of([kd, dpr]), own[0].reshape(1024, 256)), 2)
+        xkk = [dk[2, half, i].reshape(128, 256).astype(F32) + kl[i] - kg[i] for i in range(2)]
+        parts[0] = density(*xkk)
+        parts[1] = density(*[-(pl_[i] + pg[i]) for i in range(2)])
+        parts[2] = density(-og[0], -og[1])
+        parts[3] = density(*[-(kd[i][:, cols].astype(F32) + ke[i]) for i in range(2)])
+        parts[4] = density(xk0[0][:, cols], xk0[1][:, cols])
 
         @pl.when(y < 2)
         def _():
-            dens[1] = density(e[1, 0, :, own], e[1, 1, :, own])
+            parts[5] = density(d0r[0][:, cols], d0r[1][:, cols])
+            parts[6] = density(*[dpr[i][:, cols].astype(F32) - pe[i] for i in range(2)])
 
         @pl.when(y >= 2)
         def _():
-            dens[1] = density(e[0, 0, :, own], e[0, 1, :, own])
-
-    @pl.when(c == 0)
-    def _():
-        work(edge_s, half0, 0)
-
-    @pl.when(c == 1)
-    def _():
-        work(edge, half1, 1)
-
-
-def last_kernel(
-    edge, edge_s, more, more_s, half0, half1, prod, dens, uk, uks, res,
-    slot0, slot1, slot2, slot3, parts,
-):
-    x, z, y, c = place()
-    density = density_of(res)
-
-    def work(e0, e1, right, dk, half):
-        own = slice(256 * half, 256 * half + 256)
-        xpp = [e0[1, i].astype(F32) - e1[0, i].astype(F32) for i in range(2)]
-        xkp = [-(e0[0, i].astype(F32) + e1[2, i].astype(F32)) for i in range(2)]
-        left = left_of(
-            [
-                tuple(v.astype(BF) for v in xpp),
-                (e1[1, 0], e1[1, 1]),
-                tuple(v.astype(BF) for v in xkp),
-            ]
-        )
-        pk, ok, kk = pairs_of(prod[...] + dot(left, right[0].reshape(1024, 256)), 3)
-        parts[0] = density(
-            dk[2, half, 0].reshape(128, 256).astype(F32) - kk[0],
-            dk[2, half, 1].reshape(128, 256).astype(F32) - kk[1],
-        )
-        parts[1] = density(-pk[0], -pk[1])
-        parts[2] = density(-ok[0], -ok[1])
-        parts[3] = density(xkp[0][:, own], xkp[1][:, own])
-        parts[4] = dens[0]
-        parts[5] = dens[1]
-
-        @pl.when(y < 2)
-        def _():
-            parts[6] = density(xpp[0][:, own], xpp[1][:, own])
-
-        @pl.when(y >= 2)
-        def _():
-            parts[6] = density(e1[1, 0, :, own], e1[1, 1, :, own])
-
-    @pl.when(c == 0)
-    def _():
-        work(edge, more_s, half0, uk, 0)
-
-    @pl.when(c == 1)
-    def _():
-        work(edge_s, more, half1, uks, 1)
+            parts[5] = density(xp0[0][:, cols], xp0[1][:, cols])
+            parts[6] = density(-oe[0], -oe[1])
+
+    @pl.when(c == 0)
+    def _():
+        work(edge, edge_s, got, stay, uk, 0)
+
+    @pl.when(c == 1)
+    def _():
+        work(edge_s, edge, go, got, uks, 1)
 
     for d, out in enumerate((slot0, slot1, slot2, slot3)):
         at = pl.multiple_of(32 * lax.rem((x ^ d) + y, 4), 32)
@@ -411,7 +388,7 @@
     came[2] = lax.ppermute(far, grid, ring_other(2))
     uks = lax.ppermute(uk, "col", SWAP)
     blocks = (far, came[3], came[2], came[1])
-    half0, half1 = call(
+    stay, go = call(
         split_kernel,
         [shape(2, 2, 4, 4, 32, 256)] * 2,
         [hbm()] * 5,
@@ -419,43 +396,34 @@
         [pltpu.SemaphoreType.DMA((8,))],
         nbytes=4 << 20,
     )(*blocks, uks)
-    half1 = lax.ppermute(half1, "col", SWAP)
-    edge, last = call(
+    got = lax.ppermute(go, "col", SWAP)
+    edge = call(
         first_kernel,
-        [shape(3, 2, 128, 512), shape(2, 2, 4, 4, 32, 256)],
+        [shape(3, 2, 128, 512)],
         [hbm()] * 4 + [vm()] * 2 + [hbm()],
-        [vm(), hbm()],
+        [vm()],
         [pltpu.VMEM((2, 2, 2, 4, 4, 32, 256), BF), pltpu.SemaphoreType.DMA((8,))],
         flops=805306368,
         nbytes=4 << 20,
-    )(*blocks, uk, uks, half0)
+    )(*blocks, uk, uks, stay)[0]
     edge_s = lax.ppermute(edge, "col", SWAP)
-    more = call(
-        next_kernel,
-        [shape(3, 2, 128, 512)],
-        [vm(), vm(), hbm()],
+    inner = call(
+        inner_kernel,
+        [shape(1024, 256)],
+        [vm()] * 3,
         [vm()],
-        flops=805306368,
-        nbytes=2 << 20,
-    )(edge, last, half1)[0]
-    more_s = lax.ppermute(more, "col", SWAP)
-    prod, dens = call(
-        third_kernel,
-        [shape(768, 256, dtype=F32), shape(2, 128, 256, dtype=F32)],
-        [vm()] * 4 + [sm()],
-        [vm()] * 2,
-        flops=402653184,
-        nbytes=2 << 20,
-    )(edge, edge_s, half0, half1, residues)
+        flops=536870912,
+        nbytes=3 << 20,
+    )(stay, go, got)[0]
     slots = call(
         last_kernel,
         [shape(7, 32, 256)] * 4,
-        [vm()] * 10 + [sm()],
+        [vm()] * 8 + [sm()],
         [vm()] * 4,
         [pltpu.VMEM((7, 128, 256), F32)],
-        flops=402653184,
-        nbytes=4 << 20,
-    )(edge, edge_s, more, more_s, half0, half1, prod, dens, uk, uks, residues)
+        flops=1073741824,
+        nbytes=4 << 20,
+    )(edge, edge_s, inner, stay, go, got, uk, uks, residues)
     at_x = [slots[0]] + [lax.ppermute(slots[d], "pole", pairs_x(d)) for d in (2, 3, 1)]
     total = call(sum_kernel, [shape(7, 32, 256)], [vm()] * 4, [vm()], nbytes=1 << 20)(*at_x)[0]
     sent = {d: lax.ppermute(total, ("pole", "row"), spread(d)) for d in (0, 1, 3, 2)}

time: 74.8 us -> 73.6 us (0.984)
  starting transfers between devices: 30.5 us -> 29.2 us
    ppermute x2 -> x1, starting transfers between devices: 1.28 us -> 0.09 us  [body(): got = lax.ppermute(go, 'col', SWAP)]
    pallas_call x4 -> x3, Pallas kernels: 3.02 us -> 3.28 us  [the longest x1 1.94 us: body(): call(last_kernel, [shape(7, 32, 256)] * 4, [vm()] * 8 + [sm()], [vm()] *...]
  transfers between devices with their start and end apart: 20 -> 19, of which waited for: 13 -> 12; matrix products, arithmetic and copies ran while one was open for 0% -> 0% of each run, Pallas kernels for 5% -> 4%
where the time goes in v4:
time: 73.6 us; the launch traced here: 73.5 us
  waiting for transfers between devices  36.4 us (49%)
  starting transfers between devices  29.2 us (40%)
  Pallas kernels  7.73 us (11%)
    ppermute x2, waiting for transfers between devices, body(): came = {d: lax.ppermute(near, grid, ring_other(d)) for d in (1, 3)}  16.2 us
    ppermute x4, starting transfers between devices, body(): lax.ppermute(total, ('pole', 'row'), spread(d))  11.3 us
    ppermute x3, waiting for transfers between devices, body(): came = {d: lax.ppermute(bufs[d], grid, ring_both(d)) for d in (1, 3, 2)}  8.66 us
    ppermute x3, starting transfers between devices, body(): came = {d: lax.ppermute(bufs[d], grid, ring_both(d)) for d in (1, 3, 2)}  5.3 us
    ppermute x3, starting transfers between devices, body(): lax.ppermute(slots[d], 'pole', pairs_x(d))  4.79 us
    ppermute x4, waiting for transfers between devices, body(): lax.ppermute(total, ('pole', 'row'), spread(d))  4.57 us
    ppermute x2, starting transfers between devices, body(): came = {d: lax.ppermute(near, grid, ring_other(d)) for d in (1, 3)}  4.19 us
    ppermute x3, waiting for transfers between devices, body(): lax.ppermute(slots[d], 'pole', pairs_x(d))  3.8 us
  transfers between devices with their start and end apart: 19, of which 12 were waited for; matrix products, arithmetic and copies ran while one was open for 0% of the time, Pallas kernels for 4%

profile of v4, /device:TPU:4, one launch (start us, length us, event | category | flops | bytes accessed | tf_op | source)
XLA Modules:
  0.0 73.5 jit_solution(2983837776386649515)
XLA Ops:
  0.5 1.9 %shard_map.64 = (bf16[6,2,2,32,256]{4,3,2,1,0:T(8,128)(2,1)S(1)}, bf16[6,2,2,32,256]{4,3,2,1,0:T(8,128)(2,1)S(1)}, bf16[6,2,2,32,256]{4,3,2,1,0:T(8,128)(2,1)S(1...) custom-call(bf16[10,2,32,256]{3,2,1,0:T(8,128)(2,1)} %bitcast.4, ...), custom_call_target="tpu_custom_call" | custom-call | bytes 4194304 | tf_op jit(solution)/shard_map/pallas_call | solution.py:357
  3.3 3.3 %collective-permute-start.3 = (bf16[6,2,2,32,256]{4,3,2,1,0:T(8,128)(2,1)S(1)}, bf16[6,2,2,32,256]{4,3,2,1,0:T(8,128)(2,1)S(1)}, u32[]{:S(2)}, u32[]{:S(2)}) collective-permute-start(bf16[6,2,2,32,256]{4,3,2,1,0:T(8,128)(2,1)S(1)} %get-tuple-element.31), channel_id=1, source_target_pairs={{0,4},{1,17},{2,6},{3,19},{4,0},{5,21},{6,2},{7,23},{8,12},{9,25},... | collective-permute-start | bytes 1179656 | tf_op jit(solution)/shard_map/ppermute | solution.py:378
  6.6 1.1 %collective-permute-start.4 = (bf16[6,2,2,32,256]{4,3,2,1,0:T(8,128)(2,1)S(1)}, bf16[6,2,2,32,256]{4,3,2,1,0:T(8,128)(2,1)S(1)}, u32[]{:S(2)}, u32[]{:S(2)}) collective-permute-start(bf16[6,2,2,32,256]{4,3,2,1,0:T(8,128)(2,1)S(1)} %get-tuple-element.32), channel_id=1, source_target_pairs={{0,6},{1,25},{2,0},{3,27},{4,2},{5,29},{6,4},{7,31},{8,14},{9,1},{... | collective-permute-start | bytes 1179656 | tf_op jit(solution)/shard_map/ppermute | solution.py:378
  7.7 1.0 %collective-permute-start.5 = (bf16[6,2,2,32,256]{4,3,2,1,0:T(8,128)(2,1)S(1)}, bf16[6,2,2,32,256]{4,3,2,1,0:T(8,128)(2,1)S(1)}, u32[]{:S(2)}, u32[]{:S(2)}) collective-permute-start(bf16[6,2,2,32,256]{4,3,2,1,0:T(8,128)(2,1)S(1)} %get-tuple-element.33), channel_id=1, source_target_pairs={{0,2},{1,9},{2,4},{3,11},{4,6},{5,13},{6,0},{7,15},{8,10},{9,17},{... | collective-permute-start | bytes 1179656 | tf_op jit(solution)/shard_map/ppermute | solution.py:378
  8.6 4.1 %collective-permute-done.3.b2 = bf16[6,2,2,32,256]{4,3,2,1,0:T(8,128)(2,1)S(1)} collective-permute-done((bf16[6,2,2,32,256]{4,3,2,1,0:T(8,128)(2,1)S(1)}, bf16[6,2,2,32,256]{4,3,2,1,0:T(8,128)(2,1)S(1)}, u32[]{:S(2)}, u32[]{:S(2)}) %collective-permute-start.3) | collective-permute-done | bytes 393248 | tf_op jit(solution)/shard_map/ppermute | solution.py:378
  12.7 4.6 %collective-permute-done.4.b3 = bf16[6,2,2,32,256]{4,3,2,1,0:T(8,128)(2,1)S(1)} collective-permute-done((bf16[6,2,2,32,256]{4,3,2,1,0:T(8,128)(2,1)S(1)}, bf16[6,2,2,32,256]{4,3,2,1,0:T(8,128)(2,1)S(1)}, u32[]{:S(2)}, u32[]{:S(2)}) %collective-permute-start.4) | collective-permute-done | bytes 393248 | tf_op jit(solution)/shard_map/ppermute | solution.py:378
  17.8 2.0 %collective-permute-start.8 = (bf16[3,2,2,4,32,256]{5,4,3,2,1,0:T(8,128)(2,1)S(1)}, bf16[3,2,2,4,32,256]{5,4,3,2,1,0:T(8,128)(2,1)S(1)}, u32[]{:S(2)}, u32[]{:S(2)}) collective-permute-start(bf16[3,2,2,4,32,256]{5,4,3,2,1,0:T(8,128)(2,1)S(1)} %get-tuple-element.35), channel_id=1, source_target_pairs={{0,8},{1,3},{2,10},{3,5},{4,12},{5,7},{6,14},{7,1},{8,16},{9,11},{... | collective-permute-start | bytes 2359304 | tf_op jit(solution)/shard_map/ppermute | solution.py:387
  19.8 2.2 %collective-permute-start.6 = (bf16[3,2,2,4,32,256]{5,4,3,2,1,0:T(8,128)(2,1)S(1)}, bf16[3,2,2,4,32,256]{5,4,3,2,1,0:T(8,128)(2,1)S(1)}, u32[]{:S(2)}, u32[]{:S(2)}) collective-permute-start(bf16[3,2,2,4,32,256]{5,4,3,2,1,0:T(8,128)(2,1)S(1)} %get-tuple-element.35), channel_id=1, source_target_pairs={{0,24},{1,7},{2,26},{3,1},{4,28},{5,3},{6,30},{7,5},{8,0},{9,15},{... | collective-permute-start | bytes 2359304 | tf_op jit(solution)/shard_map/ppermute | solution.py:387
  22.0 1.8 %collective-permute-start.7 = (bf16[3,2,2,4,32,256]{5,4,3,2,1,0:T(8,128)(2,1)S(1)}, bf16[3,2,2,4,32,256]{5,4,3,2,1,0:T(8,128)(2,1)S(1)}, u32[]{:S(2)}, u32[]{:S(2)}) collective-permute-start(bf16[3,2,2,4,32,256]{5,4,3,2,1,0:T(8,128)(2,1)S(1)} %get-tuple-element.34.r0), channel_id=1, source_target_pairs={{0,16},{1,5},{2,18},{3,7},{4,20},{5,1},{6,22},{7,3},{8,24},{9,13},... | collective-permute-start | bytes 2359304 | tf_op jit(solution)/shard_map/ppermute | solution.py:388
  23.8 8.1 %collective-permute-done.8.r1 = bf16[3,2,2,4,32,256]{5,4,3,2,1,0:T(8,128)(2,1)S(1)} collective-permute-done((bf16[3,2,2,4,32,256]{5,4,3,2,1,0:T(8,128)(2,1)S(1)}, bf16[3,2,2,4,32,256]{5,4,3,2,1,0:T(8,128)(2,1)S(1)}, u32[]{:S(2)}, u32[]{:S(2)}) %collective-permute-start.8) | collective-permute-done | bytes 786464 | tf_op jit(solution)/shard_map/ppermute | solution.py:387
  31.9 8.1 %collective-permute-done.6.r3 = bf16[3,2,2,4,32,256]{5,4,3,2,1,0:T(8,128)(2,1)S(1)} collective-permute-done((bf16[3,2,2,4,32,256]{5,4,3,2,1,0:T(8,128)(2,1)S(1)}, bf16[3,2,2,4,32,256]{5,4,3,2,1,0:T(8,128)(2,1)S(1)}, u32[]{:S(2)}, u32[]{:S(2)}) %collective-permute-start.6) | collective-permute-done | bytes 786464 | tf_op jit(solution)/shard_map/ppermute | solution.py:387
  40.0 1.8 %collective-permute-done.7.r2 = bf16[3,2,2,4,32,256]{5,4,3,2,1,0:T(8,128)(2,1)S(1)} collective-permute-done((bf16[3,2,2,4,32,256]{5,4,3,2,1,0:T(8,128)(2,1)S(1)}, bf16[3,2,2,4,32,256]{5,4,3,2,1,0:T(8,128)(2,1)S(1)}, u32[]{:S(2)}, u32[]{:S(2)}) %collective-permute-start.7) | collective-permute-done | bytes 786464 | tf_op jit(solution)/shard_map/ppermute | solution.py:388
  42.8 1.3 %collective-permute-start.10 = (bf16[3,2,128,512]{3,2,1,0:T(8,128)(2,1)S(1)}, bf16[3,2,128,512]{3,2,1,0:T(8,128)(2,1)S(1)}, u32[]{:S(2)}, u32[]{:S(2)}) collective-permute-start(bf16[3,2,128,512]{3,2,1,0:T(8,128)(2,1)S(1)} %shard_map.68.edge), channel_id=1, source_target_pairs={{0,1},{1,0},{2,3},{3,2},{4,5},{5,4},{6,7},{7,6},{8,9},{9,8},{10,11... | collective-permute-start | bytes 2359304 | tf_op jit(solution)/shard_map/ppermute | solution.py:409
  46.0 1.9 %shard_map.70 = (bf16[7,32,256]{2,1,0:T(8,128)(2,1)S(1)}, bf16[7,32,256]{2,1,0:T(8,128)(2,1)S(1)}, bf16[7,32,256]{2,1,0:T(8,128)(2,1)S(1)}, bf16[7,32,256]{2,1,0:T(8,128)(2,1)S(1)}) custom-call(bf16[3,2,128,512]{3,2,1,0:T(8,128)(2,1)S(1)} %shard_map.68.edge, bf16[3,2,128,512]{3,2,1,0:T(8,128)(2,1)S(1)} %collective-permute-done.10.edge_s, ...), custom_call_target="tpu_custom_call" | custom-call | flops 1073741824 | bytes 4194304 | tf_op jit(solution)/shard_map/pallas_call | solution.py:418
  48.5 2.2 %collective-permute-start.13 = (bf16[7,32,256]{2,1,0:T(8,128)(2,1)S(1)}, bf16[7,32,256]{2,1,0:T(8,128)(2,1)S(1)}, u32[]{:S(2)}, u32[]{:S(2)}) collective-permute-start(bf16[7,32,256]{2,1,0:T(8,128)(2,1)S(1)} %get-tuple-element.41), channel_id=1, source_target_pairs={{0,96},{32,64},{64,32},{96,0},{1,97},{33,65},{65,33},{97,1},{2,98}... | collective-permute-start | bytes 344072 | tf_op jit(solution)/shard_map/ppermute | solution.py:427
  50.7 2.0 %collective-permute-start.14 = (bf16[7,32,256]{2,1,0:T(8,128)(2,1)S(1)}, bf16[7,32,256]{2,1,0:T(8,128)(2,1)S(1)}, u32[]{:S(2)}, u32[]{:S(2)}) collective-permute-start(bf16[7,32,256]{2,1,0:T(8,128)(2,1)S(1)} %get-tuple-element.42), channel_id=1, source_target_pairs={{0,32},{32,0},{64,96},{96,64},{1,33},{33,1},{65,97},{97,65},{2,34}... | collective-permute-start | bytes 344072 | tf_op jit(solution)/shard_map/ppermute | solution.py:427
  52.7 2.8 %collective-permute-done.12.a1 = bf16[7,32,256]{2,1,0:T(8,128)(2,1)S(1)} collective-permute-done((bf16[7,32,256]{2,1,0:T(8,128)(2,1)S(1)}, bf16[7,32,256]{2,1,0:T(8,128)(2,1)S(1)}, u32[]{:S(2)}, u32[]{:S(2)}) %collective-permute-start.12) | collective-permute-done | bytes 114720 | tf_op jit(solution)/shard_map/ppermute | solution.py:427
  55.5 1.0 %collective-permute-done.13.a2 = bf16[7,32,256]{2,1,0:T(8,128)(2,1)S(1)} collective-permute-done((bf16[7,32,256]{2,1,0:T(8,128)(2,1)S(1)}, bf16[7,32,256]{2,1,0:T(8,128)(2,1)S(1)}, u32[]{:S(2)}, u32[]{:S(2)}) %collective-permute-start.13) | collective-permute-done | bytes 114720 | tf_op jit(solution)/shard_map/ppermute | solution.py:427
  56.6 3.8 %collective-permute-start.18 = (bf16[7,32,256]{2,1,0:T(8,128)(2,1)S(1)}, bf16[7,32,256]{2,1,0:T(8,128)(2,1)S(1)}, u32[]{:S(2)}, u32[]{:S(2)}) collective-permute-start(bf16[7,32,256]{2,1,0:T(8,128)(2,1)S(1)} %shard_map.71), channel_id=1, source_target_pairs={{0,64},{2,66},{4,68},{6,70},{8,72},{10,74},{12,76},{14,78},{16,80}... | collective-permute-start | bytes 344072 | tf_op jit(solution)/shard_map/ppermute | solution.py:429
  60.3 2.8 %collective-permute-start.17 = (bf16[7,32,256]{2,1,0:T(8,128)(2,1)S(1)}, bf16[7,32,256]{2,1,0:T(8,128)(2,1)S(1)}, u32[]{:S(2)}, u32[]{:S(2)}) collective-permute-start(bf16[7,32,256]{2,1,0:T(8,128)(2,1)S(1)} %shard_map.71), channel_id=1, source_target_pairs={{0,96},{2,98},{4,100},{6,102},{8,104},{10,106},{12,108},{14,110},{... | collective-permute-start | bytes 344072 | tf_op jit(solution)/shard_map/ppermute | solution.py:429
  64.0 3.9 %collective-permute-start.15 = (bf16[7,32,256]{2,1,0:T(8,128)(2,1)S(1)}, bf16[7,32,256]{2,1,0:T(8,128)(2,1)S(1)}, u32[]{:S(2)}, u32[]{:S(2)}) collective-permute-start(bf16[7,32,256]{2,1,0:T(8,128)(2,1)S(1)} %shard_map.71), channel_id=1, source_target_pairs={{0,0},{2,2},{4,4},{6,6},{8,8},{10,10},{12,12},{14,14},{16,16},{18,... | collective-permute-start | bytes 344072 | tf_op jit(solution)/shard_map/ppermute | solution.py:429
  67.9 2.5 %collective-permute-done.16.g1 = bf16[7,32,256]{2,1,0:T(8,128)(2,1)S(1)} collective-permute-done((bf16[7,32,256]{2,1,0:T(8,128)(2,1)S(1)}, bf16[7,32,256]{2,1,0:T(8,128)(2,1)S(1)}, u32[]{:S(2)}, u32[]{:S(2)}) %collective-permute-start.16) | collective-permute-done | bytes 114720 | tf_op jit(solution)/shard_map/ppermute | solution.py:429
  70.4 2.0 %collective-permute-done.15.g0 = bf16[7,32,256]{2,1,0:T(8,128)(2,1)S(1)} collective-permute-done((bf16[7,32,256]{2,1,0:T(8,128)(2,1)S(1)}, bf16[7,32,256]{2,1,0:T(8,128)(2,1)S(1)}, u32[]{:S(2)}, u32[]{:S(2)}) %collective-permute-start.15) | collective-permute-done | bytes 114720 | tf_op jit(solution)/shard_map/ppermute | solution.py:429
  72.5 1.0 %shard_map.72 = f32[27,32,256]{2,1,0:T(8,128)} custom-call(bf16[7,32,256]{2,1,0:T(8,128)(2,1)S(1)} %collective-permute-done.15.g0, bf16[7,32,256]{2,1,0:T(8,128)(2,1)S(1)} %collective-permute-done.16.g1, bf16[7,32,256]{2,1,0:T(8,128)(2,1)S(1)} %collective-permute-done.17.g3, bf16[7,32,256]{2,1,0:T(8,128)(2,1)S(1)} %collective-permute-done.18.g2), custom_call_target="tpu_custom_call" | custom-call | bytes 2097152 | tf_op jit(solution)/shard_map/pallas_call | solution.py:431
  (25 shorter events, 6.3 us)
Async XLA Ops:
  0.0 2.6 %collective-permute-start = (bf16[10,2,32,256]{3,2,1,0:T(8,128)(2,1)}, bf16[10,2,32,256]{3,2,1,0:T(8,128)(2,1)S(1)}, u32[]{:S(2)}, u32[]{:S(2)}) collective-permute-start(bf16[10,2,32,256]{3,2,1,0:T(8,128)(2,1)} %bitcast.3), channel_id=1, source_target_pairs={{0,1},{1,0},{2,3},{3,2},{4,5},{5,4},{6,7},{7,6},{8,9},{9,8},{10,11... | collective-permute-start | bytes 983048 | tf_op jit(solution)/shard_map/ppermute | solution.py:355
  0.0 2.6 %collective-permute-start.1 = (bf16[10,2,32,256]{3,2,1,0:T(8,128)(2,1)}, bf16[10,2,32,256]{3,2,1,0:T(8,128)(2,1)S(1)}, u32[]{:S(2)}, u32[]{:S(2)}) collective-permute-start(bf16[10,2,32,256]{3,2,1,0:T(8,128)(2,1)} %bitcast.5), channel_id=1, source_target_pairs={{0,1},{1,0},{2,3},{3,2},{4,5},{5,4},{6,7},{7,6},{8,9},{9,8},{10,11... | collective-permute-start | bytes 983048 | tf_op jit(solution)/shard_map/ppermute | solution.py:355
  0.5 2.1 %collective-permute-start.2 = (bf16[7,2,32,256]{3,2,1,0:T(8,128)(2,1)}, bf16[7,2,32,256]{3,2,1,0:T(8,128)(2,1)S(1)}, u32[]{:S(2)}, u32[]{:S(2)}) collective-permute-start(bf16[7,2,32,256]{3,2,1,0:T(8,128)(2,1)} %bitcast.7), channel_id=1, source_target_pairs={{0,1},{1,0},{2,3},{3,2},{4,5},{5,4},{6,7},{7,6},{8,9},{9,8},{10,11... | collective-permute-start | bytes 688136 | tf_op jit(solution)/shard_map/ppermute | solution.py:355
  3.3 9.4 %collective-permute-start.3 = (bf16[6,2,2,32,256]{4,3,2,1,0:T(8,128)(2,1)S(1)}, bf16[6,2,2,32,256]{4,3,2,1,0:T(8,128)(2,1)S(1)}, u32[]{:S(2)}, u32[]{:S(2)}) collective-permute-start(bf16[6,2,2,32,256]{4,3,2,1,0:T(8,128)(2,1)S(1)} %get-tuple-element.31), channel_id=1, source_target_pairs={{0,4},{1,17},{2,6},{3,19},{4,0},{5,21},{6,2},{7,23},{8,12},{9,25},... | collective-permute-start | bytes 1179656 | tf_op jit(solution)/shard_map/ppermute | solution.py:378
  6.6 10.7 %collective-permute-start.4 = (bf16[6,2,2,32,256]{4,3,2,1,0:T(8,128)(2,1)S(1)}, bf16[6,2,2,32,256]{4,3,2,1,0:T(8,128)(2,1)S(1)}, u32[]{:S(2)}, u32[]{:S(2)}) collective-permute-start(bf16[6,2,2,32,256]{4,3,2,1,0:T(8,128)(2,1)S(1)} %get-tuple-element.32), channel_id=1, source_target_pairs={{0,6},{1,25},{2,0},{3,27},{4,2},{5,29},{6,4},{7,31},{8,14},{9,1},{... | collective-permute-start | bytes 1179656 | tf_op jit(solution)/shard_map/ppermute | solution.py:378
  7.7 9.6 %collective-permute-start.5 = (bf16[6,2,2,32,256]{4,3,2,1,0:T(8,128)(2,1)S(1)}, bf16[6,2,2,32,256]{4,3,2,1,0:T(8,128)(2,1)S(1)}, u32[]{:S(2)}, u32[]{:S(2)}) collective-permute-start(bf16[6,2,2,32,256]{4,3,2,1,0:T(8,128)(2,1)S(1)} %get-tuple-element.33), channel_id=1, source_target_pairs={{0,2},{1,9},{2,4},{3,11},{4,6},{5,13},{6,0},{7,15},{8,10},{9,17},{... | collective-permute-start | bytes 1179656 | tf_op jit(solution)/shard_map/ppermute | solution.py:378
  17.8 14.1 %collective-permute-start.8 = (bf16[3,2,2,4,32,256]{5,4,3,2,1,0:T(8,128)(2,1)S(1)}, bf16[3,2,2,4,32,256]{5,4,3,2,1,0:T(8,128)(2,1)S(1)}, u32[]{:S(2)}, u32[]{:S(2)}) collective-permute-start(bf16[3,2,2,4,32,256]{5,4,3,2,1,0:T(8,128)(2,1)S(1)} %get-tuple-element.35), channel_id=1, source_target_pairs={{0,8},{1,3},{2,10},{3,5},{4,12},{5,7},{6,14},{7,1},{8,16},{9,11},{... | collective-permute-start | bytes 2359304 | tf_op jit(solution)/shard_map/ppermute | solution.py:387
  19.8 20.2 %collective-permute-start.6 = (bf16[3,2,2,4,32,256]{5,4,3,2,1,0:T(8,128)(2,1)S(1)}, bf16[3,2,2,4,32,256]{5,4,3,2,1,0:T(8,128)(2,1)S(1)}, u32[]{:S(2)}, u32[]{:S(2)}) collective-permute-start(bf16[3,2,2,4,32,256]{5,4,3,2,1,0:T(8,128)(2,1)S(1)} %get-tuple-element.35), channel_id=1, source_target_pairs={{0,24},{1,7},{2,26},{3,1},{4,28},{5,3},{6,30},{7,5},{8,0},{9,15},{... | collective-permute-start | bytes 2359304 | tf_op jit(solution)/shard_map/ppermute | solution.py:387
  22.0 19.8 %collective-permute-start.7 = (bf16[3,2,2,4,32,256]{5,4,3,2,1,0:T(8,128)(2,1)S(1)}, bf16[3,2,2,4,32,256]{5,4,3,2,1,0:T(8,128)(2,1)S(1)}, u32[]{:S(2)}, u32[]{:S(2)}) collective-permute-start(bf16[3,2,2,4,32,256]{5,4,3,2,1,0:T(8,128)(2,1)S(1)} %get-tuple-element.34.r0), channel_id=1, source_target_pairs={{0,16},{1,5},{2,18},{3,7},{4,20},{5,1},{6,22},{7,3},{8,24},{9,13},... | collective-permute-start | bytes 2359304 | tf_op jit(solution)/shard_map/ppermute | solution.py:388
  23.8 18.0 %collective-permute-start.9 = (bf16[3,2,2,4,32,256]{5,4,3,2,1,0:T(8,128)(2,1)S(1)}, bf16[3,2,2,4,32,256]{5,4,3,2,1,0:T(8,128)(2,1)S(1)}, u32[]{:S(2)}, u32[]{:S(2)}) collective-permute-start(bf16[3,2,2,4,32,256]{5,4,3,2,1,0:T(8,128)(2,1)S(1)} %get-tuple-element.36.uk), channel_id=1, source_target_pairs={{0,1},{1,0},{2,3},{3,2},{4,5},{5,4},{6,7},{7,6},{8,9},{9,8},{10,11... | collective-permute-start | bytes 2359304 | tf_op jit(solution)/shard_map/ppermute | solution.py:389
  42.0 2.7 %collective-permute-start.11 = (bf16[2,2,4,4,32,256]{5,4,3,2,1,0:T(8,128)(2,1)S(1)}, bf16[2,2,4,4,32,256]{5,4,3,2,1,0:T(8,128)(2,1)S(1)}, u32[]{:S(2)}, u32[]{:S(2)}) collective-permute-start(bf16[2,2,4,4,32,256]{5,4,3,2,1,0:T(8,128)(2,1)S(1)} %get-tuple-element.38.go), channel_id=1, source_target_pairs={{0,1},{1,0},{2,3},{3,2},{4,5},{5,4},{6,7},{7,6},{8,9},{9,8},{10,11... | collective-permute-start | bytes 3145736 | tf_op jit(solution)/shard_map/ppermute | solution.py:399
  42.8 3.2 %copy-start = (f32[1,2]{1,0:T(1,128)S(1)}, f32[1,2]{1,0:T(1,128)}, u32[]{:S(2)}) copy-start(f32[1,2]{1,0:T(1,128)} %res.1) | copy-start | bytes 28
  42.8 3.2 %collective-permute-start.10 = (bf16[3,2,128,512]{3,2,1,0:T(8,128)(2,1)S(1)}, bf16[3,2,128,512]{3,2,1,0:T(8,128)(2,1)S(1)}, u32[]{:S(2)}, u32[]{:S(2)}) collective-permute-start(bf16[3,2,128,512]{3,2,1,0:T(8,128)(2,1)S(1)} %shard_map.68.edge), channel_id=1, source_target_pairs={{0,1},{1,0},{2,3},{3,2},{4,5},{5,4},{6,7},{7,6},{8,9},{9,8},{10,11... | collective-permute-start | bytes 2359304 | tf_op jit(solution)/shard_map/ppermute | solution.py:409
  47.9 7.6 %collective-permute-start.12 = (bf16[7,32,256]{2,1,0:T(8,128)(2,1)S(1)}, bf16[7,32,256]{2,1,0:T(8,128)(2,1)S(1)}, u32[]{:S(2)}, u32[]{:S(2)}) collective-permute-start(bf16[7,32,256]{2,1,0:T(8,128)(2,1)S(1)} %get-tuple-element.40), channel_id=1, source_target_pairs={{0,64},{32,96},{64,0},{96,32},{1,65},{33,97},{65,1},{97,33},{2,66}... | collective-permute-start | bytes 344072 | tf_op jit(solution)/shard_map/ppermute | solution.py:427
  48.5 8.0 %collective-permute-start.13 = (bf16[7,32,256]{2,1,0:T(8,128)(2,1)S(1)}, bf16[7,32,256]{2,1,0:T(8,128)(2,1)S(1)}, u32[]{:S(2)}, u32[]{:S(2)}) collective-permute-start(bf16[7,32,256]{2,1,0:T(8,128)(2,1)S(1)} %get-tuple-element.41), channel_id=1, source_target_pairs={{0,96},{32,64},{64,32},{96,0},{1,97},{33,65},{65,33},{97,1},{2,98}... | collective-permute-start | bytes 344072 | tf_op jit(solution)/shard_map/ppermute | solution.py:427
  50.7 5.8 %collective-permute-start.14 = (bf16[7,32,256]{2,1,0:T(8,128)(2,1)S(1)}, bf16[7,32,256]{2,1,0:T(8,128)(2,1)S(1)}, u32[]{:S(2)}, u32[]{:S(2)}) collective-permute-start(bf16[7,32,256]{2,1,0:T(8,128)(2,1)S(1)} %get-tuple-element.42), channel_id=1, source_target_pairs={{0,32},{32,0},{64,96},{96,64},{1,33},{33,1},{65,97},{97,65},{2,34}... | collective-permute-start | bytes 344072 | tf_op jit(solution)/shard_map/ppermute | solution.py:427
  56.6 11.3 %collective-permute-start.18 = (bf16[7,32,256]{2,1,0:T(8,128)(2,1)S(1)}, bf16[7,32,256]{2,1,0:T(8,128)(2,1)S(1)}, u32[]{:S(2)}, u32[]{:S(2)}) collective-permute-start(bf16[7,32,256]{2,1,0:T(8,128)(2,1)S(1)} %shard_map.71), channel_id=1, source_target_pairs={{0,64},{2,66},{4,68},{6,70},{8,72},{10,74},{12,76},{14,78},{16,80}... | collective-permute-start | bytes 344072 | tf_op jit(solution)/shard_map/ppermute | solution.py:429
  60.3 7.6 %collective-permute-start.17 = (bf16[7,32,256]{2,1,0:T(8,128)(2,1)S(1)}, bf16[7,32,256]{2,1,0:T(8,128)(2,1)S(1)}, u32[]{:S(2)}, u32[]{:S(2)}) collective-permute-start(bf16[7,32,256]{2,1,0:T(8,128)(2,1)S(1)} %shard_map.71), channel_id=1, source_target_pairs={{0,96},{2,98},{4,100},{6,102},{8,104},{10,106},{12,108},{14,110},{... | collective-permute-start | bytes 344072 | tf_op jit(solution)/shard_map/ppermute | solution.py:429
  63.1 7.3 %collective-permute-start.16 = (bf16[7,32,256]{2,1,0:T(8,128)(2,1)S(1)}, bf16[7,32,256]{2,1,0:T(8,128)(2,1)S(1)}, u32[]{:S(2)}, u32[]{:S(2)}) collective-permute-start(bf16[7,32,256]{2,1,0:T(8,128)(2,1)S(1)} %shard_map.71), channel_id=1, source_target_pairs={{0,32},{2,34},{4,36},{6,38},{8,40},{10,42},{12,44},{14,46},{16,48}... | collective-permute-start | bytes 344072 | tf_op jit(solution)/shard_map/ppermute | solution.py:429
  64.0 8.5 %collective-permute-start.15 = (bf16[7,32,256]{2,1,0:T(8,128)(2,1)S(1)}, bf16[7,32,256]{2,1,0:T(8,128)(2,1)S(1)}, u32[]{:S(2)}, u32[]{:S(2)}) collective-permute-start(bf16[7,32,256]{2,1,0:T(8,128)(2,1)S(1)} %shard_map.71), channel_id=1, source_target_pairs={{0,0},{2,2},{4,4},{6,6},{8,8},{10,10},{12,12},{14,14},{16,16},{18,... | collective-permute-start | bytes 344072 | tf_op jit(solution)/shard_map/ppermute | solution.py:429

commit v5 on v4

--- a/solution.py
+++ b/solution.py
@@ -34,6 +34,15 @@
     return [(x, x ^ step) for x in range(4)]
 
 
+def pairs_xy(step):
+    return [
+        (x * 16 + z * 4 + y, (x ^ (4 - step)) * 16 + z * 4 + (y ^ step))
+        for x in range(4)
+        for z in range(4)
+        for y in range(4)
+    ]
+
+
 SWAP = [(0, 1), (1, 0)]
 
 
@@ -42,8 +51,12 @@
     return lax.axis_index("pole"), lax.div(row, 4), lax.rem(row, 4), lax.axis_index("col")
 
 
-def node_of(y):
-    return 3 + 2 * lax.rem(y, 2) + lax.div(y, 2)
+def index_of(x, y):
+    return x ^ lax.rem(8 - y, 4)
+
+
+def node_of(m):
+    return 3 + 2 * lax.rem(m, 2) + lax.div(m, 2)
 
 
 def vm():
@@ -92,7 +105,7 @@
     def _():
         h = 0 if own else 1
         for d, out in enumerate(outs):
-            k = node_of(lax.rem(y + d, 4))
+            k = node_of(index_of(x, lax.rem(y + d, 4)))
             p = lax.div(k - 1, 2)
             at = 2 * (k - 3) + 2
             out[0, h] = dia[p] * mask(p, p, 1, h)
@@ -138,7 +151,7 @@
 
 def merge_kernel(b0, b2, b3, b1, near, far, uk, sems):
     x, z, y, c = place()
-    p = lax.rem(y, 2)
+    p = lax.rem(index_of(x, y), 2)
 
     @pl.when(c == 0)
     def _():
@@ -292,12 +305,12 @@
         parts[3] = density(*[-(kd[i][:, cols].astype(F32) + ke[i]) for i in range(2)])
         parts[4] = density(xk0[0][:, cols], xk0[1][:, cols])
 
-        @pl.when(y < 2)
+        @pl.when(index_of(x, y) < 2)
         def _():
             parts[5] = density(d0r[0][:, cols], d0r[1][:, cols])
             parts[6] = density(*[dpr[i][:, cols].astype(F32) - pe[i] for i in range(2)])
 
-        @pl.when(y >= 2)
+        @pl.when(index_of(x, y) >= 2)
         def _():
             parts[5] = density(xp0[0][:, cols], xp0[1][:, cols])
             parts[6] = density(-oe[0], -oe[1])
@@ -311,7 +324,7 @@
         work(edge_s, edge, go, got, uks, 1)
 
     for d, out in enumerate((slot0, slot1, slot2, slot3)):
-        at = pl.multiple_of(32 * lax.rem((x ^ d) + y, 4), 32)
+        at = pl.multiple_of(32 * (y ^ d), 32)
         for b in range(7):
             out[b] = parts[b, pl.ds(at, 32), :].astype(BF)
 
@@ -321,19 +334,10 @@
     out[...] = (total + (a2[...].astype(F32) + a3[...].astype(F32))).astype(BF)
 
 
-def spread(step):
-    return [
-        (x * 16 + z * 4 + y, ((x + step) % 4) * 16 + z * 4 + (x + y) % 4)
-        for x in range(4)
-        for z in range(4)
-        for y in range(4)
-    ]
-
-
 def final_kernel(g0, g1, g3, g2, out):
     x, z, y, c = place()
     for d, g in enumerate((g0, g1, g2, g3)):
-        b = lax.rem(y + 8 - x + d, 4)
+        b = index_of(x ^ d, y)
         k = node_of(b)
         p = 1 + lax.rem(b, 2)
         pair = 2 * (k - 3) + 2
@@ -424,10 +428,9 @@
         flops=1073741824,
         nbytes=4 << 20,
     )(edge, edge_s, inner, stay, go, got, uk, uks, residues)
-    at_x = [slots[0]] + [lax.ppermute(slots[d], "pole", pairs_x(d)) for d in (2, 3, 1)]
+    at_x = [slots[0]] + [lax.ppermute(slots[d], ("pole", "row"), pairs_xy(d)) for d in (2, 3, 1)]
     total = call(sum_kernel, [shape(7, 32, 256)], [vm()] * 4, [vm()], nbytes=1 << 20)(*at_x)[0]
-    sent = {d: lax.ppermute(total, ("pole", "row"), spread(d)) for d in (0, 1, 3, 2)}
-    full = [sent[d] for d in (0, 1, 3, 2)]
+    full = [total] + [lax.ppermute(total, "pole", pairs_x(d)) for d in (1, 3, 2)]
     return call(
         final_kernel, [shape(27, 32, 256, dtype=F32)], [vm()] * 4, [vm()], nbytes=2 << 20
     )(*full)[0]

time: 73.6 us -> 70.8 us (0.962)
  the two profiles are of different devices: /device:TPU:4 before, /device:TPU:0 now
where the time goes in v5:
time: 70.8 us; the launch traced here: 70.7 us
  waiting for transfers between devices  39.5 us (56%)
  starting transfers between devices  23.4 us (33%)
  Pallas kernels  7.74 us (11%)
    ppermute x2, waiting for transfers between devices, body(): came = {d: lax.ppermute(near, grid, ring_other(d)) for d in (1, 3)}  16.2 us
    ppermute x3, waiting for transfers between devices, body(): came = {d: lax.ppermute(bufs[d], grid, ring_both(d)) for d in (1, 3, 2)}  8.66 us
    ppermute x3, waiting for transfers between devices, body(): lax.ppermute(slots[d], ('pole', 'row'), pairs_xy(d))  6.93 us
    ppermute x3, starting transfers between devices, body(): lax.ppermute(slots[d], ('pole', 'row'), pairs_xy(d))  6.62 us
    ppermute x3, starting transfers between devices, body(): came = {d: lax.ppermute(bufs[d], grid, ring_both(d)) for d in (1, 3, 2)}  5.38 us
    ppermute x3, waiting for transfers between devices, body(): lax.ppermute(total, 'pole', pairs_x(d))  4.51 us
    ppermute x2, starting transfers between devices, body(): came = {d: lax.ppermute(near, grid, ring_other(d)) for d in (1, 3)}  4.19 us
    ppermute x3, starting transfers between devices, body(): lax.ppermute(total, 'pole', pairs_x(d))  3.57 us
  transfers between devices with their start and end apart: 18, of which 13 were waited for; matrix products, arithmetic and copies ran while one was open for 0% of the time, Pallas kernels for 5%

profile of v5, /device:TPU:0, one launch (start us, length us, event | category | flops | bytes accessed | tf_op | source)
XLA Modules:
  0.0 70.7 jit_solution(10284722290964065348)
XLA Ops:
  0.5 2.0 %shard_map.64 = (bf16[6,2,2,32,256]{4,3,2,1,0:T(8,128)(2,1)S(1)}, bf16[6,2,2,32,256]{4,3,2,1,0:T(8,128)(2,1)S(1)}, bf16[6,2,2,32,256]{4,3,2,1,0:T(8,128)(2,1)S(1...) custom-call(bf16[10,2,32,256]{3,2,1,0:T(8,128)(2,1)} %bitcast.4, ...), custom_call_target="tpu_custom_call" | custom-call | bytes 4194304 | tf_op jit(solution)/shard_map/pallas_call | solution.py:361
  3.4 3.4 %collective-permute-start.3 = (bf16[6,2,2,32,256]{4,3,2,1,0:T(8,128)(2,1)S(1)}, bf16[6,2,2,32,256]{4,3,2,1,0:T(8,128)(2,1)S(1)}, u32[]{:S(2)}, u32[]{:S(2)}) collective-permute-start(bf16[6,2,2,32,256]{4,3,2,1,0:T(8,128)(2,1)S(1)} %get-tuple-element.31), channel_id=1, source_target_pairs={{0,4},{1,17},{2,6},{3,19},{4,0},{5,21},{6,2},{7,23},{8,12},{9,25},... | collective-permute-start | bytes 1179656 | tf_op jit(solution)/shard_map/ppermute | solution.py:382
  6.7 1.1 %collective-permute-start.4 = (bf16[6,2,2,32,256]{4,3,2,1,0:T(8,128)(2,1)S(1)}, bf16[6,2,2,32,256]{4,3,2,1,0:T(8,128)(2,1)S(1)}, u32[]{:S(2)}, u32[]{:S(2)}) collective-permute-start(bf16[6,2,2,32,256]{4,3,2,1,0:T(8,128)(2,1)S(1)} %get-tuple-element.32), channel_id=1, source_target_pairs={{0,6},{1,25},{2,0},{3,27},{4,2},{5,29},{6,4},{7,31},{8,14},{9,1},{... | collective-permute-start | bytes 1179656 | tf_op jit(solution)/shard_map/ppermute | solution.py:382
  7.8 1.0 %collective-permute-start.5 = (bf16[6,2,2,32,256]{4,3,2,1,0:T(8,128)(2,1)S(1)}, bf16[6,2,2,32,256]{4,3,2,1,0:T(8,128)(2,1)S(1)}, u32[]{:S(2)}, u32[]{:S(2)}) collective-permute-start(bf16[6,2,2,32,256]{4,3,2,1,0:T(8,128)(2,1)S(1)} %get-tuple-element.33), channel_id=1, source_target_pairs={{0,2},{1,9},{2,4},{3,11},{4,6},{5,13},{6,0},{7,15},{8,10},{9,17},{... | collective-permute-start | bytes 1179656 | tf_op jit(solution)/shard_map/ppermute | solution.py:382
  8.7 4.0 %collective-permute-done.3.b2 = bf16[6,2,2,32,256]{4,3,2,1,0:T(8,128)(2,1)S(1)} collective-permute-done((bf16[6,2,2,32,256]{4,3,2,1,0:T(8,128)(2,1)S(1)}, bf16[6,2,2,32,256]{4,3,2,1,0:T(8,128)(2,1)S(1)}, u32[]{:S(2)}, u32[]{:S(2)}) %collective-permute-start.3) | collective-permute-done | bytes 393248 | tf_op jit(solution)/shard_map/ppermute | solution.py:382
  12.7 4.7 %collective-permute-done.4.b3 = bf16[6,2,2,32,256]{4,3,2,1,0:T(8,128)(2,1)S(1)} collective-permute-done((bf16[6,2,2,32,256]{4,3,2,1,0:T(8,128)(2,1)S(1)}, bf16[6,2,2,32,256]{4,3,2,1,0:T(8,128)(2,1)S(1)}, u32[]{:S(2)}, u32[]{:S(2)}) %collective-permute-start.4) | collective-permute-done | bytes 393248 | tf_op jit(solution)/shard_map/ppermute | solution.py:382
  17.9 2.0 %collective-permute-start.8 = (bf16[3,2,2,4,32,256]{5,4,3,2,1,0:T(8,128)(2,1)S(1)}, bf16[3,2,2,4,32,256]{5,4,3,2,1,0:T(8,128)(2,1)S(1)}, u32[]{:S(2)}, u32[]{:S(2)}) collective-permute-start(bf16[3,2,2,4,32,256]{5,4,3,2,1,0:T(8,128)(2,1)S(1)} %get-tuple-element.35), channel_id=1, source_target_pairs={{0,8},{1,3},{2,10},{3,5},{4,12},{5,7},{6,14},{7,1},{8,16},{9,11},{... | collective-permute-start | bytes 2359304 | tf_op jit(solution)/shard_map/ppermute | solution.py:391
  19.9 2.2 %collective-permute-start.6 = (bf16[3,2,2,4,32,256]{5,4,3,2,1,0:T(8,128)(2,1)S(1)}, bf16[3,2,2,4,32,256]{5,4,3,2,1,0:T(8,128)(2,1)S(1)}, u32[]{:S(2)}, u32[]{:S(2)}) collective-permute-start(bf16[3,2,2,4,32,256]{5,4,3,2,1,0:T(8,128)(2,1)S(1)} %get-tuple-element.35), channel_id=1, source_target_pairs={{0,24},{1,7},{2,26},{3,1},{4,28},{5,3},{6,30},{7,5},{8,0},{9,15},{... | collective-permute-start | bytes 2359304 | tf_op jit(solution)/shard_map/ppermute | solution.py:391
  22.1 1.8 %collective-permute-start.7 = (bf16[3,2,2,4,32,256]{5,4,3,2,1,0:T(8,128)(2,1)S(1)}, bf16[3,2,2,4,32,256]{5,4,3,2,1,0:T(8,128)(2,1)S(1)}, u32[]{:S(2)}, u32[]{:S(2)}) collective-permute-start(bf16[3,2,2,4,32,256]{5,4,3,2,1,0:T(8,128)(2,1)S(1)} %get-tuple-element.34.r0), channel_id=1, source_target_pairs={{0,16},{1,5},{2,18},{3,7},{4,20},{5,1},{6,22},{7,3},{8,24},{9,13},... | collective-permute-start | bytes 2359304 | tf_op jit(solution)/shard_map/ppermute | solution.py:392
  23.9 8.1 %collective-permute-done.8.r1 = bf16[3,2,2,4,32,256]{5,4,3,2,1,0:T(8,128)(2,1)S(1)} collective-permute-done((bf16[3,2,2,4,32,256]{5,4,3,2,1,0:T(8,128)(2,1)S(1)}, bf16[3,2,2,4,32,256]{5,4,3,2,1,0:T(8,128)(2,1)S(1)}, u32[]{:S(2)}, u32[]{:S(2)}) %collective-permute-start.8) | collective-permute-done | bytes 786464 | tf_op jit(solution)/shard_map/ppermute | solution.py:391
  32.0 8.1 %collective-permute-done.6.r3 = bf16[3,2,2,4,32,256]{5,4,3,2,1,0:T(8,128)(2,1)S(1)} collective-permute-done((bf16[3,2,2,4,32,256]{5,4,3,2,1,0:T(8,128)(2,1)S(1)}, bf16[3,2,2,4,32,256]{5,4,3,2,1,0:T(8,128)(2,1)S(1)}, u32[]{:S(2)}, u32[]{:S(2)}) %collective-permute-start.6) | collective-permute-done | bytes 786464 | tf_op jit(solution)/shard_map/ppermute | solution.py:391
  40.1 1.8 %collective-permute-done.7.r2 = bf16[3,2,2,4,32,256]{5,4,3,2,1,0:T(8,128)(2,1)S(1)} collective-permute-done((bf16[3,2,2,4,32,256]{5,4,3,2,1,0:T(8,128)(2,1)S(1)}, bf16[3,2,2,4,32,256]{5,4,3,2,1,0:T(8,128)(2,1)S(1)}, u32[]{:S(2)}, u32[]{:S(2)}) %collective-permute-start.7) | collective-permute-done | bytes 786464 | tf_op jit(solution)/shard_map/ppermute | solution.py:392
  42.9 1.3 %collective-permute-start.10 = (bf16[3,2,128,512]{3,2,1,0:T(8,128)(2,1)S(1)}, bf16[3,2,128,512]{3,2,1,0:T(8,128)(2,1)S(1)}, u32[]{:S(2)}, u32[]{:S(2)}) collective-permute-start(bf16[3,2,128,512]{3,2,1,0:T(8,128)(2,1)S(1)} %shard_map.68.edge), channel_id=1, source_target_pairs={{0,1},{1,0},{2,3},{3,2},{4,5},{5,4},{6,7},{7,6},{8,9},{9,8},{10,11... | collective-permute-start | bytes 2359304 | tf_op jit(solution)/shard_map/ppermute | solution.py:413
  46.1 1.9 %shard_map.70 = (bf16[7,32,256]{2,1,0:T(8,128)(2,1)S(1)}, bf16[7,32,256]{2,1,0:T(8,128)(2,1)S(1)}, bf16[7,32,256]{2,1,0:T(8,128)(2,1)S(1)}, bf16[7,32,256]{2,1,0:T(8,128)(2,1)S(1)}) custom-call(bf16[3,2,128,512]{3,2,1,0:T(8,128)(2,1)S(1)} %shard_map.68.edge, bf16[3,2,128,512]{3,2,1,0:T(8,128)(2,1)S(1)} %collective-permute-done.10.edge_s, ...), custom_call_target="tpu_custom_call" | custom-call | flops 1073741824 | bytes 4194304 | tf_op jit(solution)/shard_map/pallas_call | solution.py:422
  48.0 5.4 %collective-permute-start.12 = (bf16[7,32,256]{2,1,0:T(8,128)(2,1)S(1)}, bf16[7,32,256]{2,1,0:T(8,128)(2,1)S(1)}, u32[]{:S(2)}, u32[]{:S(2)}) collective-permute-start(bf16[7,32,256]{2,1,0:T(8,128)(2,1)S(1)} %get-tuple-element.40), channel_id=1, source_target_pairs={{0,68},{2,70},{4,64},{6,66},{8,76},{10,78},{12,72},{14,74},{16,84}... | collective-permute-start | bytes 344072 | tf_op jit(solution)/shard_map/ppermute | solution.py:431
  53.4 1.2 %collective-permute-start.13 = (bf16[7,32,256]{2,1,0:T(8,128)(2,1)S(1)}, bf16[7,32,256]{2,1,0:T(8,128)(2,1)S(1)}, u32[]{:S(2)}, u32[]{:S(2)}) collective-permute-start(bf16[7,32,256]{2,1,0:T(8,128)(2,1)S(1)} %get-tuple-element.41), channel_id=1, source_target_pairs={{0,38},{2,36},{4,34},{6,32},{8,46},{10,44},{12,42},{14,40},{16,54}... | collective-permute-start | bytes 344072 | tf_op jit(solution)/shard_map/ppermute | solution.py:431
  54.6 2.8 %collective-permute-done.12.a1 = bf16[7,32,256]{2,1,0:T(8,128)(2,1)S(1)} collective-permute-done((bf16[7,32,256]{2,1,0:T(8,128)(2,1)S(1)}, bf16[7,32,256]{2,1,0:T(8,128)(2,1)S(1)}, u32[]{:S(2)}, u32[]{:S(2)}) %collective-permute-start.12) | collective-permute-done | bytes 114720 | tf_op jit(solution)/shard_map/ppermute | solution.py:431
  57.4 3.2 %collective-permute-done.13.a2 = bf16[7,32,256]{2,1,0:T(8,128)(2,1)S(1)} collective-permute-done((bf16[7,32,256]{2,1,0:T(8,128)(2,1)S(1)}, bf16[7,32,256]{2,1,0:T(8,128)(2,1)S(1)}, u32[]{:S(2)}, u32[]{:S(2)}) %collective-permute-start.13) | collective-permute-done | bytes 114720 | tf_op jit(solution)/shard_map/ppermute | solution.py:431
  60.6 1.0 %collective-permute-done.14.a3 = bf16[7,32,256]{2,1,0:T(8,128)(2,1)S(1)} collective-permute-done((bf16[7,32,256]{2,1,0:T(8,128)(2,1)S(1)}, bf16[7,32,256]{2,1,0:T(8,128)(2,1)S(1)}, u32[]{:S(2)}, u32[]{:S(2)}) %collective-permute-start.14) | collective-permute-done | bytes 114720 | tf_op jit(solution)/shard_map/ppermute | solution.py:431
  61.6 1.4 %collective-permute-start.17 = (bf16[7,32,256]{2,1,0:T(8,128)(2,1)S(1)}, bf16[7,32,256]{2,1,0:T(8,128)(2,1)S(1)}, u32[]{:S(2)}, u32[]{:S(2)}) collective-permute-start(bf16[7,32,256]{2,1,0:T(8,128)(2,1)S(1)} %shard_map.71.g0), channel_id=1, source_target_pairs={{0,64},{32,96},{64,0},{96,32},{1,65},{33,97},{65,1},{97,33},{2,66}... | collective-permute-start | bytes 344072 | tf_op jit(solution)/shard_map/ppermute | solution.py:433
  63.0 1.7 %collective-permute-start.16 = (bf16[7,32,256]{2,1,0:T(8,128)(2,1)S(1)}, bf16[7,32,256]{2,1,0:T(8,128)(2,1)S(1)}, u32[]{:S(2)}, u32[]{:S(2)}) collective-permute-start(bf16[7,32,256]{2,1,0:T(8,128)(2,1)S(1)} %shard_map.71.g0), channel_id=1, source_target_pairs={{0,96},{32,64},{64,32},{96,0},{1,97},{33,65},{65,33},{97,1},{2,98}... | collective-permute-start | bytes 344072 | tf_op jit(solution)/shard_map/ppermute | solution.py:433
  65.2 3.7 %collective-permute-done.17.g2 = bf16[7,32,256]{2,1,0:T(8,128)(2,1)S(1)} collective-permute-done((bf16[7,32,256]{2,1,0:T(8,128)(2,1)S(1)}, bf16[7,32,256]{2,1,0:T(8,128)(2,1)S(1)}, u32[]{:S(2)}, u32[]{:S(2)}) %collective-permute-start.17) | collective-permute-done | bytes 114720 | tf_op jit(solution)/shard_map/ppermute | solution.py:433
  68.9 0.8 %collective-permute-done.16.g3 = bf16[7,32,256]{2,1,0:T(8,128)(2,1)S(1)} collective-permute-done((bf16[7,32,256]{2,1,0:T(8,128)(2,1)S(1)}, bf16[7,32,256]{2,1,0:T(8,128)(2,1)S(1)}, u32[]{:S(2)}, u32[]{:S(2)}) %collective-permute-start.16) | collective-permute-done | bytes 114720 | tf_op jit(solution)/shard_map/ppermute | solution.py:433
  69.7 1.0 %shard_map.72 = f32[27,32,256]{2,1,0:T(8,128)} custom-call(bf16[7,32,256]{2,1,0:T(8,128)(2,1)S(1)} %shard_map.71.g0, bf16[7,32,256]{2,1,0:T(8,128)(2,1)S(1)} %collective-permute-done.15.g1, bf16[7,32,256]{2,1,0:T(8,128)(2,1)S(1)} %collective-permute-done.16.g3, bf16[7,32,256]{2,1,0:T(8,128)(2,1)S(1)} %collective-permute-done.17.g2), custom_call_target="tpu_custom_call" | custom-call | bytes 2097152 | tf_op jit(solution)/shard_map/pallas_call | solution.py:434
  (23 shorter events, 5.3 us)
Async XLA Ops:
  0.0 2.6 %collective-permute-start = (bf16[10,2,32,256]{3,2,1,0:T(8,128)(2,1)}, bf16[10,2,32,256]{3,2,1,0:T(8,128)(2,1)S(1)}, u32[]{:S(2)}, u32[]{:S(2)}) collective-permute-start(bf16[10,2,32,256]{3,2,1,0:T(8,128)(2,1)} %bitcast.3), channel_id=1, source_target_pairs={{0,1},{1,0},{2,3},{3,2},{4,5},{5,4},{6,7},{7,6},{8,9},{9,8},{10,11... | collective-permute-start | bytes 983048 | tf_op jit(solution)/shard_map/ppermute | solution.py:359
  0.0 2.6 %collective-permute-start.1 = (bf16[10,2,32,256]{3,2,1,0:T(8,128)(2,1)}, bf16[10,2,32,256]{3,2,1,0:T(8,128)(2,1)S(1)}, u32[]{:S(2)}, u32[]{:S(2)}) collective-permute-start(bf16[10,2,32,256]{3,2,1,0:T(8,128)(2,1)} %bitcast.5), channel_id=1, source_target_pairs={{0,1},{1,0},{2,3},{3,2},{4,5},{5,4},{6,7},{7,6},{8,9},{9,8},{10,11... | collective-permute-start | bytes 983048 | tf_op jit(solution)/shard_map/ppermute | solution.py:359
  0.5 2.1 %collective-permute-start.2 = (bf16[7,2,32,256]{3,2,1,0:T(8,128)(2,1)}, bf16[7,2,32,256]{3,2,1,0:T(8,128)(2,1)S(1)}, u32[]{:S(2)}, u32[]{:S(2)}) collective-permute-start(bf16[7,2,32,256]{3,2,1,0:T(8,128)(2,1)} %bitcast.7), channel_id=1, source_target_pairs={{0,1},{1,0},{2,3},{3,2},{4,5},{5,4},{6,7},{7,6},{8,9},{9,8},{10,11... | collective-permute-start | bytes 688136 | tf_op jit(solution)/shard_map/ppermute | solution.py:359
  3.4 9.4 %collective-permute-start.3 = (bf16[6,2,2,32,256]{4,3,2,1,0:T(8,128)(2,1)S(1)}, bf16[6,2,2,32,256]{4,3,2,1,0:T(8,128)(2,1)S(1)}, u32[]{:S(2)}, u32[]{:S(2)}) collective-permute-start(bf16[6,2,2,32,256]{4,3,2,1,0:T(8,128)(2,1)S(1)} %get-tuple-element.31), channel_id=1, source_target_pairs={{0,4},{1,17},{2,6},{3,19},{4,0},{5,21},{6,2},{7,23},{8,12},{9,25},... | collective-permute-start | bytes 1179656 | tf_op jit(solution)/shard_map/ppermute | solution.py:382
  6.7 10.7 %collective-permute-start.4 = (bf16[6,2,2,32,256]{4,3,2,1,0:T(8,128)(2,1)S(1)}, bf16[6,2,2,32,256]{4,3,2,1,0:T(8,128)(2,1)S(1)}, u32[]{:S(2)}, u32[]{:S(2)}) collective-permute-start(bf16[6,2,2,32,256]{4,3,2,1,0:T(8,128)(2,1)S(1)} %get-tuple-element.32), channel_id=1, source_target_pairs={{0,6},{1,25},{2,0},{3,27},{4,2},{5,29},{6,4},{7,31},{8,14},{9,1},{... | collective-permute-start | bytes 1179656 | tf_op jit(solution)/shard_map/ppermute | solution.py:382
  7.8 9.6 %collective-permute-start.5 = (bf16[6,2,2,32,256]{4,3,2,1,0:T(8,128)(2,1)S(1)}, bf16[6,2,2,32,256]{4,3,2,1,0:T(8,128)(2,1)S(1)}, u32[]{:S(2)}, u32[]{:S(2)}) collective-permute-start(bf16[6,2,2,32,256]{4,3,2,1,0:T(8,128)(2,1)S(1)} %get-tuple-element.33), channel_id=1, source_target_pairs={{0,2},{1,9},{2,4},{3,11},{4,6},{5,13},{6,0},{7,15},{8,10},{9,17},{... | collective-permute-start | bytes 1179656 | tf_op jit(solution)/shard_map/ppermute | solution.py:382
  17.9 14.1 %collective-permute-start.8 = (bf16[3,2,2,4,32,256]{5,4,3,2,1,0:T(8,128)(2,1)S(1)}, bf16[3,2,2,4,32,256]{5,4,3,2,1,0:T(8,128)(2,1)S(1)}, u32[]{:S(2)}, u32[]{:S(2)}) collective-permute-start(bf16[3,2,2,4,32,256]{5,4,3,2,1,0:T(8,128)(2,1)S(1)} %get-tuple-element.35), channel_id=1, source_target_pairs={{0,8},{1,3},{2,10},{3,5},{4,12},{5,7},{6,14},{7,1},{8,16},{9,11},{... | collective-permute-start | bytes 2359304 | tf_op jit(solution)/shard_map/ppermute | solution.py:391
  19.9 20.2 %collective-permute-start.6 = (bf16[3,2,2,4,32,256]{5,4,3,2,1,0:T(8,128)(2,1)S(1)}, bf16[3,2,2,4,32,256]{5,4,3,2,1,0:T(8,128)(2,1)S(1)}, u32[]{:S(2)}, u32[]{:S(2)}) collective-permute-start(bf16[3,2,2,4,32,256]{5,4,3,2,1,0:T(8,128)(2,1)S(1)} %get-tuple-element.35), channel_id=1, source_target_pairs={{0,24},{1,7},{2,26},{3,1},{4,28},{5,3},{6,30},{7,5},{8,0},{9,15},{... | collective-permute-start | bytes 2359304 | tf_op jit(solution)/shard_map/ppermute | solution.py:391
  22.1 19.8 %collective-permute-start.7 = (bf16[3,2,2,4,32,256]{5,4,3,2,1,0:T(8,128)(2,1)S(1)}, bf16[3,2,2,4,32,256]{5,4,3,2,1,0:T(8,128)(2,1)S(1)}, u32[]{:S(2)}, u32[]{:S(2)}) collective-permute-start(bf16[3,2,2,4,32,256]{5,4,3,2,1,0:T(8,128)(2,1)S(1)} %get-tuple-element.34.r0), channel_id=1, source_target_pairs={{0,16},{1,5},{2,18},{3,7},{4,20},{5,1},{6,22},{7,3},{8,24},{9,13},... | collective-permute-start | bytes 2359304 | tf_op jit(solution)/shard_map/ppermute | solution.py:392
  23.9 18.0 %collective-permute-start.9 = (bf16[3,2,2,4,32,256]{5,4,3,2,1,0:T(8,128)(2,1)S(1)}, bf16[3,2,2,4,32,256]{5,4,3,2,1,0:T(8,128)(2,1)S(1)}, u32[]{:S(2)}, u32[]{:S(2)}) collective-permute-start(bf16[3,2,2,4,32,256]{5,4,3,2,1,0:T(8,128)(2,1)S(1)} %get-tuple-element.36.uk), channel_id=1, source_target_pairs={{0,1},{1,0},{2,3},{3,2},{4,5},{5,4},{6,7},{7,6},{8,9},{9,8},{10,11... | collective-permute-start | bytes 2359304 | tf_op jit(solution)/shard_map/ppermute | solution.py:393
  42.1 2.7 %collective-permute-start.11 = (bf16[2,2,4,4,32,256]{5,4,3,2,1,0:T(8,128)(2,1)S(1)}, bf16[2,2,4,4,32,256]{5,4,3,2,1,0:T(8,128)(2,1)S(1)}, u32[]{:S(2)}, u32[]{:S(2)}) collective-permute-start(bf16[2,2,4,4,32,256]{5,4,3,2,1,0:T(8,128)(2,1)S(1)} %get-tuple-element.38.go), channel_id=1, source_target_pairs={{0,1},{1,0},{2,3},{3,2},{4,5},{5,4},{6,7},{7,6},{8,9},{9,8},{10,11... | collective-permute-start | bytes 3145736 | tf_op jit(solution)/shard_map/ppermute | solution.py:403
  42.8 3.2 %copy-start = (f32[1,2]{1,0:T(1,128)S(1)}, f32[1,2]{1,0:T(1,128)}, u32[]{:S(2)}) copy-start(f32[1,2]{1,0:T(1,128)} %res.1) | copy-start | bytes 28
  42.9 3.2 %collective-permute-start.10 = (bf16[3,2,128,512]{3,2,1,0:T(8,128)(2,1)S(1)}, bf16[3,2,128,512]{3,2,1,0:T(8,128)(2,1)S(1)}, u32[]{:S(2)}, u32[]{:S(2)}) collective-permute-start(bf16[3,2,128,512]{3,2,1,0:T(8,128)(2,1)S(1)} %shard_map.68.edge), channel_id=1, source_target_pairs={{0,1},{1,0},{2,3},{3,2},{4,5},{5,4},{6,7},{7,6},{8,9},{9,8},{10,11... | collective-permute-start | bytes 2359304 | tf_op jit(solution)/shard_map/ppermute | solution.py:413
  48.0 9.4 %collective-permute-start.12 = (bf16[7,32,256]{2,1,0:T(8,128)(2,1)S(1)}, bf16[7,32,256]{2,1,0:T(8,128)(2,1)S(1)}, u32[]{:S(2)}, u32[]{:S(2)}) collective-permute-start(bf16[7,32,256]{2,1,0:T(8,128)(2,1)S(1)} %get-tuple-element.40), channel_id=1, source_target_pairs={{0,68},{2,70},{4,64},{6,66},{8,76},{10,78},{12,72},{14,74},{16,84}... | collective-permute-start | bytes 344072 | tf_op jit(solution)/shard_map/ppermute | solution.py:431
  53.4 7.2 %collective-permute-start.13 = (bf16[7,32,256]{2,1,0:T(8,128)(2,1)S(1)}, bf16[7,32,256]{2,1,0:T(8,128)(2,1)S(1)}, u32[]{:S(2)}, u32[]{:S(2)}) collective-permute-start(bf16[7,32,256]{2,1,0:T(8,128)(2,1)S(1)} %get-tuple-element.41), channel_id=1, source_target_pairs={{0,38},{2,36},{4,34},{6,32},{8,46},{10,44},{12,42},{14,40},{16,54}... | collective-permute-start | bytes 344072 | tf_op jit(solution)/shard_map/ppermute | solution.py:431
  54.6 7.0 %collective-permute-start.14 = (bf16[7,32,256]{2,1,0:T(8,128)(2,1)S(1)}, bf16[7,32,256]{2,1,0:T(8,128)(2,1)S(1)}, u32[]{:S(2)}, u32[]{:S(2)}) collective-permute-start(bf16[7,32,256]{2,1,0:T(8,128)(2,1)S(1)} %get-tuple-element.42), channel_id=1, source_target_pairs={{0,98},{2,96},{4,102},{6,100},{8,106},{10,104},{12,110},{14,108},{... | collective-permute-start | bytes 344072 | tf_op jit(solution)/shard_map/ppermute | solution.py:431
  61.6 7.3 %collective-permute-start.17 = (bf16[7,32,256]{2,1,0:T(8,128)(2,1)S(1)}, bf16[7,32,256]{2,1,0:T(8,128)(2,1)S(1)}, u32[]{:S(2)}, u32[]{:S(2)}) collective-permute-start(bf16[7,32,256]{2,1,0:T(8,128)(2,1)S(1)} %shard_map.71.g0), channel_id=1, source_target_pairs={{0,64},{32,96},{64,0},{96,32},{1,65},{33,97},{65,1},{97,33},{2,66}... | collective-permute-start | bytes 344072 | tf_op jit(solution)/shard_map/ppermute | solution.py:433
  63.0 6.7 %collective-permute-start.16 = (bf16[7,32,256]{2,1,0:T(8,128)(2,1)S(1)}, bf16[7,32,256]{2,1,0:T(8,128)(2,1)S(1)}, u32[]{:S(2)}, u32[]{:S(2)}) collective-permute-start(bf16[7,32,256]{2,1,0:T(8,128)(2,1)S(1)} %shard_map.71.g0), channel_id=1, source_target_pairs={{0,96},{32,64},{64,32},{96,0},{1,97},{33,65},{65,33},{97,1},{2,98}... | collective-permute-start | bytes 344072 | tf_op jit(solution)/shard_map/ppermute | solution.py:433
  64.7 5.0 %collective-permute-start.15 = (bf16[7,32,256]{2,1,0:T(8,128)(2,1)S(1)}, bf16[7,32,256]{2,1,0:T(8,128)(2,1)S(1)}, u32[]{:S(2)}, u32[]{:S(2)}) collective-permute-start(bf16[7,32,256]{2,1,0:T(8,128)(2,1)S(1)} %shard_map.71.g0), channel_id=1, source_target_pairs={{0,32},{32,0},{64,96},{96,64},{1,33},{33,1},{65,97},{97,65},{2,34}... | collective-permute-start | bytes 344072 | tf_op jit(solution)/shard_map/ppermute | solution.py:433

commit v6 on v5

--- a/solution.py
+++ b/solution.py
@@ -193,26 +193,6 @@
     ]
 
 
-def split_kernel(r0, r3, r2, r1, after, stay, go, sems):
-    x, z, y, c = place()
-
-    @pl.when(c == 0)
-    def _():
-        copies = []
-        for d, buf in enumerate((r0, r1, r2, r3)):
-            at = lax.rem(z + 4 - d, 4)
-            copies.append((buf.at[pl.ds(1, 2), 0], stay.at[:, :, at]))
-            copies.append((buf.at[pl.ds(1, 2), 1], go.at[:, :, at]))
-        run_copies(copies, sems)
-
-    @pl.when(c == 1)
-    def _():
-        copies = []
-        for d, buf in enumerate((r0, r1, r2, r3)):
-            copies.append((buf.at[2], go.at[:, :, :, lax.rem(y + 4 - d, 4)]))
-        run_copies(copies, sems)
-
-
 def wide_rows(get):
     return tuple(jnp.concatenate([get(0, part), get(1, part)], axis=1) for part in range(2))
 
@@ -230,7 +210,7 @@
         out[slot, i] = (pair[i] if sign > 0 else -pair[i]).astype(BF)
 
 
-def first_kernel(r0, r3, r2, r1, uk, uks, after, out, right, sems):
+def first_kernel(r0, r3, r2, r1, uks, out, stay, go, lead, right, sems):
     x, z, y, c = place()
 
     def rows_of(block):
@@ -240,19 +220,19 @@
     def _():
         copies = []
         for d, buf in enumerate((r0, r1, r2, r3)):
-            copies.append((buf.at[0], right.at[0, :, :, lax.rem(z + 4 - d, 4)]))
+            at = lax.rem(z + 4 - d, 4)
+            copies.append((buf.at[pl.ds(1, 2), 0], stay.at[:, :, at]))
+            copies.append((buf.at[pl.ds(1, 2), 1], go.at[:, :, at]))
+            copies.append((buf.at[0], lead.at[:, :, at]))
         run_copies(copies, sems)
-        ukp = wide_rows(lambda h, part: uk[0, h, part].reshape(128, 256))
-        (kd,) = times(left_of([ukp]), 1, right[0])
-        put(out, 0, kd)
-        put(out, 1, rows_of(0))
 
     @pl.when(c == 1)
     def _():
         copies = []
         for d, buf in enumerate((r0, r1, r2, r3)):
-            at = lax.rem(y + 4 - d, 4)
-            copies.append((buf.at[pl.ds(0, 2)], right.at[:, :, :, :, at]))
+            copies.append((buf.at[pl.ds(0, 2)], right.at[:, :, :, :, lax.rem(y + 4 - d, 4)]))
+        for d, buf in enumerate((r0, r1, r2, r3)):
+            copies.append((buf.at[2], go.at[:, :, :, lax.rem(y + 4 - d, 4)]))
         run_copies(copies, sems)
         ukp = wide_rows(lambda h, part: uks[0, h, part].reshape(128, 256))
         uk0 = wide_rows(lambda h, part: uks[1, h, part].reshape(128, 256))
@@ -264,6 +244,17 @@
         put(out, 2, xk0, -1)
 
 
+def next_kernel(edge, lead, uk, after, out):
+    x, z, y, c = place()
+
+    @pl.when(c == 0)
+    def _():
+        ukp = wide_rows(lambda h, part: uk[0, h, part].reshape(128, 256))
+        (kd,) = times(left_of([ukp]), 1, lead)
+        put(out, 0, kd)
+        put(out, 1, wide_rows(lambda h, part: lead[h, part, z].reshape(128, 256)))
+
+
 def inner_kernel(stay, go, got, out):
     x, z, y, c = place()
 
@@ -288,7 +279,7 @@
     wr, wi = res[0, 0], res[0, 1]
 
     def density(re, im):
-        return wr * re.astype(F32) - wi * im.astype(F32)
+        return (wr * re.astype(F32) - wi * im.astype(F32)).astype(BF)
 
     def work(e0, e1, last, own, dk, half):
         cols = slice(256 * half, 256 * half + 256)
@@ -326,7 +317,7 @@
     for d, out in enumerate((slot0, slot1, slot2, slot3)):
         at = pl.multiple_of(32 * (y ^ d), 32)
         for b in range(7):
-            out[b] = parts[b, pl.ds(at, 32), :].astype(BF)
+            out[b] = parts[b, pl.ds(at, 32), :]
 
 
 def sum_kernel(a0, a1, a2, a3, out):
@@ -392,24 +383,25 @@
     came[2] = lax.ppermute(far, grid, ring_other(2))
     uks = lax.ppermute(uk, "col", SWAP)
     blocks = (far, came[3], came[2], came[1])
-    stay, go = call(
-        split_kernel,
-        [shape(2, 2, 4, 4, 32, 256)] * 2,
-        [hbm()] * 5,
-        [hbm()] * 2,
-        [pltpu.SemaphoreType.DMA((8,))],
+    edge, stay, go, lead = call(
+        first_kernel,
+        [shape(3, 2, 128, 512)] + [shape(2, 2, 4, 4, 32, 256)] * 3,
+        [hbm()] * 4 + [vm()],
+        [vm()] + [hbm()] * 3,
+        [pltpu.VMEM((2, 2, 2, 4, 4, 32, 256), BF), pltpu.SemaphoreType.DMA((12,))],
+        flops=805306368,
         nbytes=4 << 20,
     )(*blocks, uks)
     got = lax.ppermute(go, "col", SWAP)
     edge = call(
-        first_kernel,
+        next_kernel,
         [shape(3, 2, 128, 512)],
-        [hbm()] * 4 + [vm()] * 2 + [hbm()],
+        [hbm()] + [vm()] * 2 + [hbm()],
         [vm()],
-        [pltpu.VMEM((2, 2, 2, 4, 4, 32, 256), BF), pltpu.SemaphoreType.DMA((8,))],
-        flops=805306368,
-        nbytes=4 << 20,
-    )(*blocks, uk, uks, stay)[0]
+        flops=268435456,
+        nbytes=2 << 20,
+        aliases={0: 0},
+    )(edge, lead, uk, stay)[0]
     edge_s = lax.ppermute(edge, "col", SWAP)
     inner = call(
         inner_kernel,
@@ -424,7 +416,7 @@
         [shape(7, 32, 256)] * 4,
         [vm()] * 8 + [sm()],
         [vm()] * 4,
-        [pltpu.VMEM((7, 128, 256), F32)],
+        [pltpu.VMEM((7, 128, 256), BF)],
         flops=1073741824,
         nbytes=4 << 20,
     )(edge, edge_s, inner, stay, go, got, uk, uks, residues)

time: 70.8 us -> 70.1 us (level)
    ppermute x2, waiting for transfers between devices: 16.2 us -> 9.38 us  [body(): came = {d: lax.ppermute(near, grid, ring_other(d)) for d in (1, 3)}]
    ppermute x1, waiting for transfers between devices: 1.8 us -> 6.83 us  [body(): came[2] = lax.ppermute(far, grid, ring_other(2))]
    ppermute x1, starting transfers between devices: 1.78 us -> 3.96 us  [body(): came[2] = lax.ppermute(far, grid, ring_other(2))]
    ppermute x1, waiting for transfers between devices: 0.71 us -> 2.09 us  [body(): got = lax.ppermute(go, 'col', SWAP)]
    ppermute x1, starting transfers between devices: 1.28 us -> 0.09 us  [body(): edge_s = lax.ppermute(edge, 'col', SWAP)]
    ppermute x2, starting transfers between devices: 4.19 us -> 3.24 us  [body(): came = {d: lax.ppermute(near, grid, ring_other(d)) for d in (1, 3)}]
  transfers between devices with their start and end apart: 18 -> 18, of which waited for: 13 -> 13; matrix products, arithmetic and copies ran while one was open for 0% -> 0% of each run, Pallas kernels for 5% -> 4%
where the time goes in v6:
time: 70.1 us; the launch traced here: 70 us
  waiting for transfers between devices  38.8 us (55%)
  starting transfers between devices  23.4 us (33%)
  Pallas kernels  7.66 us (11%)
    ppermute x2, waiting for transfers between devices, body(): came = {d: lax.ppermute(near, grid, ring_other(d)) for d in (1, 3)}  9.38 us
    ppermute x3, waiting for transfers between devices, body(): came = {d: lax.ppermute(bufs[d], grid, ring_both(d)) for d in (1, 3, 2)}  8.66 us
    ppermute x3, waiting for transfers between devices, body(): lax.ppermute(slots[d], ('pole', 'row'), pairs_xy(d))  6.88 us
    ppermute x1, waiting for transfers between devices, body(): came[2] = lax.ppermute(far, grid, ring_other(2))  6.83 us
    ppermute x3, starting transfers between devices, body(): lax.ppermute(slots[d], ('pole', 'row'), pairs_xy(d))  6.61 us
    ppermute x3, starting transfers between devices, body(): came = {d: lax.ppermute(bufs[d], grid, ring_both(d)) for d in (1, 3, 2)}  5.38 us
    ppermute x3, waiting for transfers between devices, body(): lax.ppermute(total, 'pole', pairs_x(d))  4.42 us
    ppermute x1, starting transfers between devices, body(): came[2] = lax.ppermute(far, grid, ring_other(2))  3.96 us
  transfers between devices with their start and end apart: 18, of which 13 were waited for; matrix products, arithmetic and copies ran while one was open for 0% of the time, Pallas kernels for 4%

profile of v6, /device:TPU:0, one launch (start us, length us, event | category | flops | bytes accessed | tf_op | source)
XLA Modules:
  0.0 70.0 jit_solution(1332494968222786707)
XLA Ops:
  0.5 2.0 %shard_map.64 = (bf16[6,2,2,32,256]{4,3,2,1,0:T(8,128)(2,1)S(1)}, bf16[6,2,2,32,256]{4,3,2,1,0:T(8,128)(2,1)S(1)}, bf16[6,2,2,32,256]{4,3,2,1,0:T(8,128)(2,1)S(1...) custom-call(bf16[10,2,32,256]{3,2,1,0:T(8,128)(2,1)} %bitcast.4, ...), custom_call_target="tpu_custom_call" | custom-call | bytes 4194304 | tf_op jit(solution)/shard_map/pallas_call | solution.py:352
  3.4 3.4 %collective-permute-start.3 = (bf16[6,2,2,32,256]{4,3,2,1,0:T(8,128)(2,1)S(1)}, bf16[6,2,2,32,256]{4,3,2,1,0:T(8,128)(2,1)S(1)}, u32[]{:S(2)}, u32[]{:S(2)}) collective-permute-start(bf16[6,2,2,32,256]{4,3,2,1,0:T(8,128)(2,1)S(1)} %get-tuple-element.33), channel_id=1, source_target_pairs={{0,4},{1,17},{2,6},{3,19},{4,0},{5,21},{6,2},{7,23},{8,12},{9,25},... | collective-permute-start | bytes 1179656 | tf_op jit(solution)/shard_map/ppermute | solution.py:373
  6.7 1.1 %collective-permute-start.4 = (bf16[6,2,2,32,256]{4,3,2,1,0:T(8,128)(2,1)S(1)}, bf16[6,2,2,32,256]{4,3,2,1,0:T(8,128)(2,1)S(1)}, u32[]{:S(2)}, u32[]{:S(2)}) collective-permute-start(bf16[6,2,2,32,256]{4,3,2,1,0:T(8,128)(2,1)S(1)} %get-tuple-element.34), channel_id=1, source_target_pairs={{0,6},{1,25},{2,0},{3,27},{4,2},{5,29},{6,4},{7,31},{8,14},{9,1},{... | collective-permute-start | bytes 1179656 | tf_op jit(solution)/shard_map/ppermute | solution.py:373
  7.8 1.0 %collective-permute-start.5 = (bf16[6,2,2,32,256]{4,3,2,1,0:T(8,128)(2,1)S(1)}, bf16[6,2,2,32,256]{4,3,2,1,0:T(8,128)(2,1)S(1)}, u32[]{:S(2)}, u32[]{:S(2)}) collective-permute-start(bf16[6,2,2,32,256]{4,3,2,1,0:T(8,128)(2,1)S(1)} %get-tuple-element.35), channel_id=1, source_target_pairs={{0,2},{1,9},{2,4},{3,11},{4,6},{5,13},{6,0},{7,15},{8,10},{9,17},{... | collective-permute-start | bytes 1179656 | tf_op jit(solution)/shard_map/ppermute | solution.py:373
  8.7 4.0 %collective-permute-done.3.b2 = bf16[6,2,2,32,256]{4,3,2,1,0:T(8,128)(2,1)S(1)} collective-permute-done((bf16[6,2,2,32,256]{4,3,2,1,0:T(8,128)(2,1)S(1)}, bf16[6,2,2,32,256]{4,3,2,1,0:T(8,128)(2,1)S(1)}, u32[]{:S(2)}, u32[]{:S(2)}) %collective-permute-start.3) | collective-permute-done | bytes 393248 | tf_op jit(solution)/shard_map/ppermute | solution.py:373
  12.7 4.7 %collective-permute-done.4.b3 = bf16[6,2,2,32,256]{4,3,2,1,0:T(8,128)(2,1)S(1)} collective-permute-done((bf16[6,2,2,32,256]{4,3,2,1,0:T(8,128)(2,1)S(1)}, bf16[6,2,2,32,256]{4,3,2,1,0:T(8,128)(2,1)S(1)}, u32[]{:S(2)}, u32[]{:S(2)}) %collective-permute-start.4) | collective-permute-done | bytes 393248 | tf_op jit(solution)/shard_map/ppermute | solution.py:373
  17.9 4.0 %collective-permute-start.7 = (bf16[3,2,2,4,32,256]{5,4,3,2,1,0:T(8,128)(2,1)S(1)}, bf16[3,2,2,4,32,256]{5,4,3,2,1,0:T(8,128)(2,1)S(1)}, u32[]{:S(2)}, u32[]{:S(2)}) collective-permute-start(bf16[3,2,2,4,32,256]{5,4,3,2,1,0:T(8,128)(2,1)S(1)} %get-tuple-element.36.r0), channel_id=1, source_target_pairs={{0,16},{1,5},{2,18},{3,7},{4,20},{5,1},{6,22},{7,3},{8,24},{9,13},... | collective-permute-start | bytes 2359304 | tf_op jit(solution)/shard_map/ppermute | solution.py:383
  21.9 1.0 %collective-permute-start.8 = (bf16[3,2,2,4,32,256]{5,4,3,2,1,0:T(8,128)(2,1)S(1)}, bf16[3,2,2,4,32,256]{5,4,3,2,1,0:T(8,128)(2,1)S(1)}, u32[]{:S(2)}, u32[]{:S(2)}) collective-permute-start(bf16[3,2,2,4,32,256]{5,4,3,2,1,0:T(8,128)(2,1)S(1)} %get-tuple-element.37), channel_id=1, source_target_pairs={{0,8},{1,3},{2,10},{3,5},{4,12},{5,7},{6,14},{7,1},{8,16},{9,11},{... | collective-permute-start | bytes 2359304 | tf_op jit(solution)/shard_map/ppermute | solution.py:382
  22.9 2.2 %collective-permute-start.6 = (bf16[3,2,2,4,32,256]{5,4,3,2,1,0:T(8,128)(2,1)S(1)}, bf16[3,2,2,4,32,256]{5,4,3,2,1,0:T(8,128)(2,1)S(1)}, u32[]{:S(2)}, u32[]{:S(2)}) collective-permute-start(bf16[3,2,2,4,32,256]{5,4,3,2,1,0:T(8,128)(2,1)S(1)} %get-tuple-element.37), channel_id=1, source_target_pairs={{0,24},{1,7},{2,26},{3,1},{4,28},{5,3},{6,30},{7,5},{8,0},{9,15},{... | collective-permute-start | bytes 2359304 | tf_op jit(solution)/shard_map/ppermute | solution.py:382
  25.1 6.8 %collective-permute-done.7.r2 = bf16[3,2,2,4,32,256]{5,4,3,2,1,0:T(8,128)(2,1)S(1)} collective-permute-done((bf16[3,2,2,4,32,256]{5,4,3,2,1,0:T(8,128)(2,1)S(1)}, bf16[3,2,2,4,32,256]{5,4,3,2,1,0:T(8,128)(2,1)S(1)}, u32[]{:S(2)}, u32[]{:S(2)}) %collective-permute-start.7) | collective-permute-done | bytes 786464 | tf_op jit(solution)/shard_map/ppermute | solution.py:383
  31.9 8.3 %collective-permute-done.8.r1 = bf16[3,2,2,4,32,256]{5,4,3,2,1,0:T(8,128)(2,1)S(1)} collective-permute-done((bf16[3,2,2,4,32,256]{5,4,3,2,1,0:T(8,128)(2,1)S(1)}, bf16[3,2,2,4,32,256]{5,4,3,2,1,0:T(8,128)(2,1)S(1)}, u32[]{:S(2)}, u32[]{:S(2)}) %collective-permute-start.8) | collective-permute-done | bytes 786464 | tf_op jit(solution)/shard_map/ppermute | solution.py:382
  40.3 1.1 %collective-permute-done.6.r3 = bf16[3,2,2,4,32,256]{5,4,3,2,1,0:T(8,128)(2,1)S(1)} collective-permute-done((bf16[3,2,2,4,32,256]{5,4,3,2,1,0:T(8,128)(2,1)S(1)}, bf16[3,2,2,4,32,256]{5,4,3,2,1,0:T(8,128)(2,1)S(1)}, u32[]{:S(2)}, u32[]{:S(2)}) %collective-permute-start.6) | collective-permute-done | bytes 786464 | tf_op jit(solution)/shard_map/ppermute | solution.py:382
  42.3 2.1 %collective-permute-done.11.got = bf16[2,2,4,4,32,256]{5,4,3,2,1,0:T(8,128)(2,1)S(1)} collective-permute-done((bf16[2,2,4,4,32,256]{5,4,3,2,1,0:T(8,128)(2,1)S(1)}, bf16[2,2,4,4,32,256]{5,4,3,2,1,0:T(8,128)(2,1)S(1)}, u32[]{:S(2)}, u32[]{:S(2)}) %collective-permute-start.11) | collective-permute-done | bytes 1048608 | tf_op jit(solution)/shard_map/ppermute | solution.py:395
  44.4 0.7 %shard_map.69.inner = bf16[1024,256]{1,0:T(8,128)(2,1)S(1)} custom-call(bf16[2,2,4,4,32,256]{5,4,3,2,1,0:T(8,128)(2,1)S(1)} %get-tuple-element.41.after.stay, bf16[2,2,4,4,32,256]{5,4,3,2,1,0:T(8,128)(2,1)S(1)} %get-tuple-element.42.go, bf16[2,2,4,4,32,256]{5,4,3,2,1,0:T(8,128)(2,1)S(1)} %collective-permute-done.11.got), custom_call_target="tpu_custom_call" | custom-call | flops 536870912 | bytes 3145728 | tf_op jit(solution)/shard_map/pallas_call | solution.py:406
  45.5 1.9 %shard_map.70 = (bf16[7,32,256]{2,1,0:T(8,128)(2,1)S(1)}, bf16[7,32,256]{2,1,0:T(8,128)(2,1)S(1)}, bf16[7,32,256]{2,1,0:T(8,128)(2,1)S(1)}, bf16[7,32,256]{2,1,0:T(8,128)(2,1)S(1)}) custom-call(bf16[3,2,128,512]{3,2,1,0:T(8,128)(2,1)S(1)} %shard_map.68.edge, bf16[3,2,128,512]{3,2,1,0:T(8,128)(2,1)S(1)} %collective-permute-done.10.edge_s, ...), custom_call_target="tpu_custom_call" | custom-call | flops 1073741824 | bytes 4194304 | tf_op jit(solution)/shard_map/pallas_call | solution.py:414
  47.5 5.3 %collective-permute-start.12 = (bf16[7,32,256]{2,1,0:T(8,128)(2,1)S(1)}, bf16[7,32,256]{2,1,0:T(8,128)(2,1)S(1)}, u32[]{:S(2)}, u32[]{:S(2)}) collective-permute-start(bf16[7,32,256]{2,1,0:T(8,128)(2,1)S(1)} %get-tuple-element.44), channel_id=1, source_target_pairs={{0,68},{2,70},{4,64},{6,66},{8,76},{10,78},{12,72},{14,74},{16,84}... | collective-permute-start | bytes 344072 | tf_op jit(solution)/shard_map/ppermute | solution.py:423
  52.8 1.2 %collective-permute-start.13 = (bf16[7,32,256]{2,1,0:T(8,128)(2,1)S(1)}, bf16[7,32,256]{2,1,0:T(8,128)(2,1)S(1)}, u32[]{:S(2)}, u32[]{:S(2)}) collective-permute-start(bf16[7,32,256]{2,1,0:T(8,128)(2,1)S(1)} %get-tuple-element.45), channel_id=1, source_target_pairs={{0,38},{2,36},{4,34},{6,32},{8,46},{10,44},{12,42},{14,40},{16,54}... | collective-permute-start | bytes 344072 | tf_op jit(solution)/shard_map/ppermute | solution.py:423
  54.1 2.6 %collective-permute-done.12.a1 = bf16[7,32,256]{2,1,0:T(8,128)(2,1)S(1)} collective-permute-done((bf16[7,32,256]{2,1,0:T(8,128)(2,1)S(1)}, bf16[7,32,256]{2,1,0:T(8,128)(2,1)S(1)}, u32[]{:S(2)}, u32[]{:S(2)}) %collective-permute-start.12) | collective-permute-done | bytes 114720 | tf_op jit(solution)/shard_map/ppermute | solution.py:423
  56.7 3.2 %collective-permute-done.13.a2 = bf16[7,32,256]{2,1,0:T(8,128)(2,1)S(1)} collective-permute-done((bf16[7,32,256]{2,1,0:T(8,128)(2,1)S(1)}, bf16[7,32,256]{2,1,0:T(8,128)(2,1)S(1)}, u32[]{:S(2)}, u32[]{:S(2)}) %collective-permute-start.13) | collective-permute-done | bytes 114720 | tf_op jit(solution)/shard_map/ppermute | solution.py:423
  59.8 1.1 %collective-permute-done.14.a3 = bf16[7,32,256]{2,1,0:T(8,128)(2,1)S(1)} collective-permute-done((bf16[7,32,256]{2,1,0:T(8,128)(2,1)S(1)}, bf16[7,32,256]{2,1,0:T(8,128)(2,1)S(1)}, u32[]{:S(2)}, u32[]{:S(2)}) %collective-permute-start.14) | collective-permute-done | bytes 114720 | tf_op jit(solution)/shard_map/ppermute | solution.py:423
  61.0 1.4 %collective-permute-start.17 = (bf16[7,32,256]{2,1,0:T(8,128)(2,1)S(1)}, bf16[7,32,256]{2,1,0:T(8,128)(2,1)S(1)}, u32[]{:S(2)}, u32[]{:S(2)}) collective-permute-start(bf16[7,32,256]{2,1,0:T(8,128)(2,1)S(1)} %shard_map.71.g0), channel_id=1, source_target_pairs={{0,64},{32,96},{64,0},{96,32},{1,65},{33,97},{65,1},{97,33},{2,66}... | collective-permute-start | bytes 344072 | tf_op jit(solution)/shard_map/ppermute | solution.py:425
  62.4 1.6 %collective-permute-start.16 = (bf16[7,32,256]{2,1,0:T(8,128)(2,1)S(1)}, bf16[7,32,256]{2,1,0:T(8,128)(2,1)S(1)}, u32[]{:S(2)}, u32[]{:S(2)}) collective-permute-start(bf16[7,32,256]{2,1,0:T(8,128)(2,1)S(1)} %shard_map.71.g0), channel_id=1, source_target_pairs={{0,96},{32,64},{64,32},{96,0},{1,97},{33,65},{65,33},{97,1},{2,98}... | collective-permute-start | bytes 344072 | tf_op jit(solution)/shard_map/ppermute | solution.py:425
  64.6 3.8 %collective-permute-done.17.g2 = bf16[7,32,256]{2,1,0:T(8,128)(2,1)S(1)} collective-permute-done((bf16[7,32,256]{2,1,0:T(8,128)(2,1)S(1)}, bf16[7,32,256]{2,1,0:T(8,128)(2,1)S(1)}, u32[]{:S(2)}, u32[]{:S(2)}) %collective-permute-start.17) | collective-permute-done | bytes 114720 | tf_op jit(solution)/shard_map/ppermute | solution.py:425
  69.0 1.0 %shard_map.72 = f32[27,32,256]{2,1,0:T(8,128)} custom-call(bf16[7,32,256]{2,1,0:T(8,128)(2,1)S(1)} %shard_map.71.g0, bf16[7,32,256]{2,1,0:T(8,128)(2,1)S(1)} %collective-permute-done.15.g1, bf16[7,32,256]{2,1,0:T(8,128)(2,1)S(1)} %collective-permute-done.16.g3, bf16[7,32,256]{2,1,0:T(8,128)(2,1)S(1)} %collective-permute-done.17.g2), custom_call_target="tpu_custom_call" | custom-call | bytes 2097152 | tf_op jit(solution)/shard_map/pallas_call | solution.py:426
  (23 shorter events, 4.5 us)
Async XLA Ops:
  0.0 2.6 %collective-permute-start = (bf16[10,2,32,256]{3,2,1,0:T(8,128)(2,1)}, bf16[10,2,32,256]{3,2,1,0:T(8,128)(2,1)S(1)}, u32[]{:S(2)}, u32[]{:S(2)}) collective-permute-start(bf16[10,2,32,256]{3,2,1,0:T(8,128)(2,1)} %bitcast.3), channel_id=1, source_target_pairs={{0,1},{1,0},{2,3},{3,2},{4,5},{5,4},{6,7},{7,6},{8,9},{9,8},{10,11... | collective-permute-start | bytes 983048 | tf_op jit(solution)/shard_map/ppermute | solution.py:350
  0.0 2.6 %collective-permute-start.1 = (bf16[10,2,32,256]{3,2,1,0:T(8,128)(2,1)}, bf16[10,2,32,256]{3,2,1,0:T(8,128)(2,1)S(1)}, u32[]{:S(2)}, u32[]{:S(2)}) collective-permute-start(bf16[10,2,32,256]{3,2,1,0:T(8,128)(2,1)} %bitcast.5), channel_id=1, source_target_pairs={{0,1},{1,0},{2,3},{3,2},{4,5},{5,4},{6,7},{7,6},{8,9},{9,8},{10,11... | collective-permute-start | bytes 983048 | tf_op jit(solution)/shard_map/ppermute | solution.py:350
  0.5 2.1 %collective-permute-start.2 = (bf16[7,2,32,256]{3,2,1,0:T(8,128)(2,1)}, bf16[7,2,32,256]{3,2,1,0:T(8,128)(2,1)S(1)}, u32[]{:S(2)}, u32[]{:S(2)}) collective-permute-start(bf16[7,2,32,256]{3,2,1,0:T(8,128)(2,1)} %bitcast.7), channel_id=1, source_target_pairs={{0,1},{1,0},{2,3},{3,2},{4,5},{5,4},{6,7},{7,6},{8,9},{9,8},{10,11... | collective-permute-start | bytes 688136 | tf_op jit(solution)/shard_map/ppermute | solution.py:350
  3.4 9.4 %collective-permute-start.3 = (bf16[6,2,2,32,256]{4,3,2,1,0:T(8,128)(2,1)S(1)}, bf16[6,2,2,32,256]{4,3,2,1,0:T(8,128)(2,1)S(1)}, u32[]{:S(2)}, u32[]{:S(2)}) collective-permute-start(bf16[6,2,2,32,256]{4,3,2,1,0:T(8,128)(2,1)S(1)} %get-tuple-element.33), channel_id=1, source_target_pairs={{0,4},{1,17},{2,6},{3,19},{4,0},{5,21},{6,2},{7,23},{8,12},{9,25},... | collective-permute-start | bytes 1179656 | tf_op jit(solution)/shard_map/ppermute | solution.py:373
  6.7 10.7 %collective-permute-start.4 = (bf16[6,2,2,32,256]{4,3,2,1,0:T(8,128)(2,1)S(1)}, bf16[6,2,2,32,256]{4,3,2,1,0:T(8,128)(2,1)S(1)}, u32[]{:S(2)}, u32[]{:S(2)}) collective-permute-start(bf16[6,2,2,32,256]{4,3,2,1,0:T(8,128)(2,1)S(1)} %get-tuple-element.34), channel_id=1, source_target_pairs={{0,6},{1,25},{2,0},{3,27},{4,2},{5,29},{6,4},{7,31},{8,14},{9,1},{... | collective-permute-start | bytes 1179656 | tf_op jit(solution)/shard_map/ppermute | solution.py:373
  7.8 9.6 %collective-permute-start.5 = (bf16[6,2,2,32,256]{4,3,2,1,0:T(8,128)(2,1)S(1)}, bf16[6,2,2,32,256]{4,3,2,1,0:T(8,128)(2,1)S(1)}, u32[]{:S(2)}, u32[]{:S(2)}) collective-permute-start(bf16[6,2,2,32,256]{4,3,2,1,0:T(8,128)(2,1)S(1)} %get-tuple-element.35), channel_id=1, source_target_pairs={{0,2},{1,9},{2,4},{3,11},{4,6},{5,13},{6,0},{7,15},{8,10},{9,17},{... | collective-permute-start | bytes 1179656 | tf_op jit(solution)/shard_map/ppermute | solution.py:373
  17.9 14.0 %collective-permute-start.7 = (bf16[3,2,2,4,32,256]{5,4,3,2,1,0:T(8,128)(2,1)S(1)}, bf16[3,2,2,4,32,256]{5,4,3,2,1,0:T(8,128)(2,1)S(1)}, u32[]{:S(2)}, u32[]{:S(2)}) collective-permute-start(bf16[3,2,2,4,32,256]{5,4,3,2,1,0:T(8,128)(2,1)S(1)} %get-tuple-element.36.r0), channel_id=1, source_target_pairs={{0,16},{1,5},{2,18},{3,7},{4,20},{5,1},{6,22},{7,3},{8,24},{9,13},... | collective-permute-start | bytes 2359304 | tf_op jit(solution)/shard_map/ppermute | solution.py:383
  21.9 18.4 %collective-permute-start.8 = (bf16[3,2,2,4,32,256]{5,4,3,2,1,0:T(8,128)(2,1)S(1)}, bf16[3,2,2,4,32,256]{5,4,3,2,1,0:T(8,128)(2,1)S(1)}, u32[]{:S(2)}, u32[]{:S(2)}) collective-permute-start(bf16[3,2,2,4,32,256]{5,4,3,2,1,0:T(8,128)(2,1)S(1)} %get-tuple-element.37), channel_id=1, source_target_pairs={{0,8},{1,3},{2,10},{3,5},{4,12},{5,7},{6,14},{7,1},{8,16},{9,11},{... | collective-permute-start | bytes 2359304 | tf_op jit(solution)/shard_map/ppermute | solution.py:382
  22.9 18.4 %collective-permute-start.6 = (bf16[3,2,2,4,32,256]{5,4,3,2,1,0:T(8,128)(2,1)S(1)}, bf16[3,2,2,4,32,256]{5,4,3,2,1,0:T(8,128)(2,1)S(1)}, u32[]{:S(2)}, u32[]{:S(2)}) collective-permute-start(bf16[3,2,2,4,32,256]{5,4,3,2,1,0:T(8,128)(2,1)S(1)} %get-tuple-element.37), channel_id=1, source_target_pairs={{0,24},{1,7},{2,26},{3,1},{4,28},{5,3},{6,30},{7,5},{8,0},{9,15},{... | collective-permute-start | bytes 2359304 | tf_op jit(solution)/shard_map/ppermute | solution.py:382
  25.1 16.2 %collective-permute-start.9 = (bf16[3,2,2,4,32,256]{5,4,3,2,1,0:T(8,128)(2,1)S(1)}, bf16[3,2,2,4,32,256]{5,4,3,2,1,0:T(8,128)(2,1)S(1)}, u32[]{:S(2)}, u32[]{:S(2)}) collective-permute-start(bf16[3,2,2,4,32,256]{5,4,3,2,1,0:T(8,128)(2,1)S(1)} %get-tuple-element.38.uk), channel_id=1, source_target_pairs={{0,1},{1,0},{2,3},{3,2},{4,5},{5,4},{6,7},{7,6},{8,9},{9,8},{10,11... | collective-permute-start | bytes 2359304 | tf_op jit(solution)/shard_map/ppermute | solution.py:384
  41.7 2.7 %collective-permute-start.11 = (bf16[2,2,4,4,32,256]{5,4,3,2,1,0:T(8,128)(2,1)S(1)}, bf16[2,2,4,4,32,256]{5,4,3,2,1,0:T(8,128)(2,1)S(1)}, u32[]{:S(2)}, u32[]{:S(2)}) collective-permute-start(bf16[2,2,4,4,32,256]{5,4,3,2,1,0:T(8,128)(2,1)S(1)} %get-tuple-element.42.go), channel_id=1, source_target_pairs={{0,1},{1,0},{2,3},{3,2},{4,5},{5,4},{6,7},{7,6},{8,9},{9,8},{10,11... | collective-permute-start | bytes 3145736 | tf_op jit(solution)/shard_map/ppermute | solution.py:395
  42.2 3.3 %copy-start = (f32[1,2]{1,0:T(1,128)S(1)}, f32[1,2]{1,0:T(1,128)}, u32[]{:S(2)}) copy-start(f32[1,2]{1,0:T(1,128)} %res.1) | copy-start | bytes 28
  42.2 3.3 %collective-permute-start.10 = (bf16[3,2,128,512]{3,2,1,0:T(8,128)(2,1)S(1)}, bf16[3,2,128,512]{3,2,1,0:T(8,128)(2,1)S(1)}, u32[]{:S(2)}, u32[]{:S(2)}) collective-permute-start(bf16[3,2,128,512]{3,2,1,0:T(8,128)(2,1)S(1)} %shard_map.68.edge), channel_id=1, source_target_pairs={{0,1},{1,0},{2,3},{3,2},{4,5},{5,4},{6,7},{7,6},{8,9},{9,8},{10,11... | collective-permute-start | bytes 2359304 | tf_op jit(solution)/shard_map/ppermute | solution.py:405
  47.5 9.2 %collective-permute-start.12 = (bf16[7,32,256]{2,1,0:T(8,128)(2,1)S(1)}, bf16[7,32,256]{2,1,0:T(8,128)(2,1)S(1)}, u32[]{:S(2)}, u32[]{:S(2)}) collective-permute-start(bf16[7,32,256]{2,1,0:T(8,128)(2,1)S(1)} %get-tuple-element.44), channel_id=1, source_target_pairs={{0,68},{2,70},{4,64},{6,66},{8,76},{10,78},{12,72},{14,74},{16,84}... | collective-permute-start | bytes 344072 | tf_op jit(solution)/shard_map/ppermute | solution.py:423
  52.8 7.0 %collective-permute-start.13 = (bf16[7,32,256]{2,1,0:T(8,128)(2,1)S(1)}, bf16[7,32,256]{2,1,0:T(8,128)(2,1)S(1)}, u32[]{:S(2)}, u32[]{:S(2)}) collective-permute-start(bf16[7,32,256]{2,1,0:T(8,128)(2,1)S(1)} %get-tuple-element.45), channel_id=1, source_target_pairs={{0,38},{2,36},{4,34},{6,32},{8,46},{10,44},{12,42},{14,40},{16,54}... | collective-permute-start | bytes 344072 | tf_op jit(solution)/shard_map/ppermute | solution.py:423
  54.1 6.9 %collective-permute-start.14 = (bf16[7,32,256]{2,1,0:T(8,128)(2,1)S(1)}, bf16[7,32,256]{2,1,0:T(8,128)(2,1)S(1)}, u32[]{:S(2)}, u32[]{:S(2)}) collective-permute-start(bf16[7,32,256]{2,1,0:T(8,128)(2,1)S(1)} %get-tuple-element.46), channel_id=1, source_target_pairs={{0,98},{2,96},{4,102},{6,100},{8,106},{10,104},{12,110},{14,108},{... | collective-permute-start | bytes 344072 | tf_op jit(solution)/shard_map/ppermute | solution.py:423
  61.0 7.4 %collective-permute-start.17 = (bf16[7,32,256]{2,1,0:T(8,128)(2,1)S(1)}, bf16[7,32,256]{2,1,0:T(8,128)(2,1)S(1)}, u32[]{:S(2)}, u32[]{:S(2)}) collective-permute-start(bf16[7,32,256]{2,1,0:T(8,128)(2,1)S(1)} %shard_map.71.g0), channel_id=1, source_target_pairs={{0,64},{32,96},{64,0},{96,32},{1,65},{33,97},{65,1},{97,33},{2,66}... | collective-permute-start | bytes 344072 | tf_op jit(solution)/shard_map/ppermute | solution.py:425
  62.4 6.6 %collective-permute-start.16 = (bf16[7,32,256]{2,1,0:T(8,128)(2,1)S(1)}, bf16[7,32,256]{2,1,0:T(8,128)(2,1)S(1)}, u32[]{:S(2)}, u32[]{:S(2)}) collective-permute-start(bf16[7,32,256]{2,1,0:T(8,128)(2,1)S(1)} %shard_map.71.g0), channel_id=1, source_target_pairs={{0,96},{32,64},{64,32},{96,0},{1,97},{33,65},{65,33},{97,1},{2,98}... | collective-permute-start | bytes 344072 | tf_op jit(solution)/shard_map/ppermute | solution.py:425
  64.0 5.0 %collective-permute-start.15 = (bf16[7,32,256]{2,1,0:T(8,128)(2,1)S(1)}, bf16[7,32,256]{2,1,0:T(8,128)(2,1)S(1)}, u32[]{:S(2)}, u32[]{:S(2)}) collective-permute-start(bf16[7,32,256]{2,1,0:T(8,128)(2,1)S(1)} %shard_map.71.g0), channel_id=1, source_target_pairs={{0,32},{32,0},{64,96},{96,64},{1,33},{33,1},{65,97},{97,65},{2,34}... | collective-permute-start | bytes 344072 | tf_op jit(solution)/shard_map/ppermute | solution.py:425

commit v7 on v6

--- a/solution.py
+++ b/solution.py
@@ -113,7 +113,6 @@
             out[2, h] = low[at + 1] * mask(0, k, pattern[at + 1], h)
             out[3, h] = up[at] * mask(k, p, pattern[at], h)
             out[4, h] = up[at + 1] * mask(k, 0, pattern[at + 1], h)
-            out[5, h] = dia[k] * mask(k, k, 1, h)
 
     @pl.when(c == 1)
     def _():
@@ -127,14 +126,27 @@
                 out[t, h] = tiles[t]
 
 
-def pack_own_kernel(
-    low_in, up_in, dia_in, widths_in, pattern_in, o0, o1, o2, o3, widths, pattern, low, up, dia, sems
-):
+def pack_own_kernel(low_in, up_in, dia_in, widths_in, pattern_in, res_in, *refs):
+    outs, parts, (widths, pattern, low, up, dia, res, sems) = refs[:4], refs[4:8], refs[8:]
     run_copies(
-        [(low_in, low), (up_in, up), (dia_in, dia), (widths_in, widths), (pattern_in, pattern)],
+        [
+            (low_in, low),
+            (up_in, up),
+            (dia_in, dia),
+            (widths_in, widths),
+            (pattern_in, pattern),
+            (res_in, res),
+        ],
         sems,
     )
-    pack(low, up, dia, widths, pattern, (o0, o1, o2, o3), True)
+    pack(low, up, dia, widths, pattern, outs, True)
+    x, z, y, c = place()
+    rows = (32 * (4 * z + y)) + lax.broadcasted_iota(jnp.int32, (32, 256), 0)
+    cols = (256 * c) + lax.broadcasted_iota(jnp.int32, (32, 256), 1)
+    for d, part in enumerate(parts):
+        k = node_of(index_of(x ^ d, y))
+        dens = res[0, 0] * dia[k, 0].astype(F32) - res[0, 1] * dia[k, 1].astype(F32)
+        part[...] = jnp.where((rows < widths[k]) & (cols < widths[k]), dens, 0.0).astype(BF)
 
 
 def pack_other_kernel(low, up, dia, widths, pattern, i0, i1, i2, i3, *outs):
@@ -160,7 +172,7 @@
             at = lax.rem(y + 4 - d, 4)
             copies.append((buf.at[pl.ds(0, 3)], near.at[:, :, :, at]))
             copies.append((buf.at[pl.ds(0, 3)], far.at[:, :, :, at]))
-            copies.append((buf.at[pl.ds(3, 3)], uk.at[:, :, :, at]))
+            copies.append((buf.at[pl.ds(3, 2)], uk.at[:, :, :, at]))
         run_copies(copies, sems)
 
     @pl.when(c == 1)
@@ -210,7 +222,7 @@
         out[slot, i] = (pair[i] if sign > 0 else -pair[i]).astype(BF)
 
 
-def first_kernel(r0, r3, r2, r1, uks, out, stay, go, lead, right, sems):
+def first_kernel(r0, r3, r2, r1, uks, p2, p3, p1, out, stay, go, lead, right, sems):
     x, z, y, c = place()
 
     def rows_of(block):
@@ -273,7 +285,7 @@
 
 
 def last_kernel(
-    edge, edge_s, inner, stay, go, got, uk, uks, res, slot0, slot1, slot2, slot3, parts
+    edge, edge_s, inner, stay, go, got, res, slot0, slot1, slot2, slot3, parts
 ):
     x, z, y, c = place()
     wr, wi = res[0, 0], res[0, 1]
@@ -281,7 +293,7 @@
     def density(re, im):
         return (wr * re.astype(F32) - wi * im.astype(F32)).astype(BF)
 
-    def work(e0, e1, last, own, dk, half):
+    def work(e0, e1, last, own, half):
         cols = slice(256 * half, 256 * half + 256)
         xp0, d0r, xk0 = [(e1[n, 0], e1[n, 1]) for n in range(3)]
         kd, dpr = [(e0[n, 0], e0[n, 1]) for n in range(2)]
@@ -289,8 +301,7 @@
         pg, og, kg = pairs_of(dot(left, inner[...]), 3)
         pe, oe, ke = pairs_of(dot(left, last[half].reshape(1024, 256)), 3)
         kl, pl_ = pairs_of(dot(left_of([kd, dpr]), own[0].reshape(1024, 256)), 2)
-        xkk = [dk[2, half, i].reshape(128, 256).astype(F32) + kl[i] - kg[i] for i in range(2)]
-        parts[0] = density(*xkk)
+        parts[0] = density(*[kl[i] - kg[i] for i in range(2)])
         parts[1] = density(*[-(pl_[i] + pg[i]) for i in range(2)])
         parts[2] = density(-og[0], -og[1])
         parts[3] = density(*[-(kd[i][:, cols].astype(F32) + ke[i]) for i in range(2)])
@@ -308,11 +319,11 @@
 
     @pl.when(c == 0)
     def _():
-        work(edge, edge_s, got, stay, uk, 0)
+        work(edge, edge_s, got, stay, 0)
 
     @pl.when(c == 1)
     def _():
-        work(edge_s, edge, go, got, uks, 1)
+        work(edge_s, edge, go, got, 1)
 
     for d, out in enumerate((slot0, slot1, slot2, slot3)):
         at = pl.multiple_of(32 * (y ^ d), 32)
@@ -320,9 +331,12 @@
             out[b] = parts[b, pl.ds(at, 32), :]
 
 
-def sum_kernel(a0, a1, a2, a3, out):
+def sum_kernel(a0, a1, a2, a3, d0, d1, d2, d3, out):
     total = a0[...].astype(F32) + a1[...].astype(F32)
-    out[...] = (total + (a2[...].astype(F32) + a3[...].astype(F32))).astype(BF)
+    total = total + (a2[...].astype(F32) + a3[...].astype(F32))
+    diag = d0[...].astype(F32) + d1[...].astype(F32) + d2[...].astype(F32) + d3[...].astype(F32)
+    out[0] = (total[0] + diag).astype(BF)
+    out[1:] = total[1:].astype(BF)
 
 
 def final_kernel(g0, g1, g3, g2, out):
@@ -351,29 +365,34 @@
     grid = ("row", "col")
     *bufs, widths, pattern = call(
         pack_own_kernel,
-        [shape(6, 2, 2, 32, 256)] * 4 + [shape(7, dtype=jnp.int32), shape(10, dtype=jnp.int32)],
-        [in_hbm()] * 5,
-        [vm()] * 4 + [sm()] * 2,
+        [shape(5, 2, 2, 32, 256)] * 4
+        + [shape(32, 256)] * 4
+        + [shape(7, dtype=jnp.int32), shape(10, dtype=jnp.int32)],
+        [in_hbm()] * 6,
+        [vm()] * 8 + [sm()] * 2,
         [
             pltpu.VMEM((10, 2, 32, 256), BF),
             pltpu.VMEM((10, 2, 32, 256), BF),
             pltpu.VMEM((7, 2, 32, 256), BF),
-            pltpu.SemaphoreType.DMA((5,)),
+            pltpu.SMEM((1, 2), F32),
+            pltpu.SemaphoreType.DMA((6,)),
         ],
         nbytes=4 << 20,
-    )(*[pltpu.with_memory_space_constraint(a, pltpu.HBM) for a in (*mine, widths, pattern)])
+    )(*[pltpu.with_memory_space_constraint(a, pltpu.HBM) for a in (*mine, widths, pattern, residues)])
+    bufs, parts = bufs[:4], bufs[4:]
     bufs = call(
         pack_other_kernel,
-        [shape(6, 2, 2, 32, 256)] * 4,
+        [shape(5, 2, 2, 32, 256)] * 4,
         [vm()] * 3 + [sm()] * 2 + [hbm()] * 4,
         [vm()] * 4,
         nbytes=4 << 20,
         aliases={5: 0, 6: 1, 7: 2, 8: 3},
     )(*swapped, widths, pattern, *bufs)
     came = {d: lax.ppermute(bufs[d], grid, ring_both(d)) for d in (1, 3, 2)}
+    parts = [parts[0]] + [lax.ppermute(parts[d], "pole", pairs_x(d)) for d in (2, 3, 1)]
     near, far, uk = call(
         merge_kernel,
-        [shape(3, 2, 2, 4, 32, 256)] * 3,
+        [shape(3, 2, 2, 4, 32, 256)] * 2 + [shape(2, 2, 2, 4, 32, 256)],
         [hbm()] * 4,
         [hbm()] * 3,
         [pltpu.SemaphoreType.DMA((16,))],
@@ -386,12 +405,12 @@
     edge, stay, go, lead = call(
         first_kernel,
         [shape(3, 2, 128, 512)] + [shape(2, 2, 4, 4, 32, 256)] * 3,
-        [hbm()] * 4 + [vm()],
+        [hbm()] * 4 + [vm()] + [hbm()] * 3,
         [vm()] + [hbm()] * 3,
         [pltpu.VMEM((2, 2, 2, 4, 4, 32, 256), BF), pltpu.SemaphoreType.DMA((12,))],
         flops=805306368,
         nbytes=4 << 20,
-    )(*blocks, uks)
+    )(*blocks, uks, *parts[1:])
     got = lax.ppermute(go, "col", SWAP)
     edge = call(
         next_kernel,
@@ -414,14 +433,16 @@
     slots = call(
         last_kernel,
         [shape(7, 32, 256)] * 4,
-        [vm()] * 8 + [sm()],
+        [vm()] * 6 + [sm()],
         [vm()] * 4,
         [pltpu.VMEM((7, 128, 256), BF)],
         flops=1073741824,
         nbytes=4 << 20,
-    )(edge, edge_s, inner, stay, go, got, uk, uks, residues)
+    )(edge, edge_s, inner, stay, go, got, residues)
     at_x = [slots[0]] + [lax.ppermute(slots[d], ("pole", "row"), pairs_xy(d)) for d in (2, 3, 1)]
-    total = call(sum_kernel, [shape(7, 32, 256)], [vm()] * 4, [vm()], nbytes=1 << 20)(*at_x)[0]
+    total = call(sum_kernel, [shape(7, 32, 256)], [vm()] * 8, [vm()], nbytes=1 << 20)(
+        *at_x, *parts
+    )[0]
     full = [total] + [lax.ppermute(total, "pole", pairs_x(d)) for d in (1, 3, 2)]
     return call(
         final_kernel, [shape(27, 32, 256, dtype=F32)], [vm()] * 4, [vm()], nbytes=2 << 20

time: 70.1 us -> 68.7 us (0.980)
  waiting for transfers between devices: 38.8 us -> 31.4 us
  starting transfers between devices: 23.4 us -> 29.4 us
    ppermute x0 -> x3, waiting for transfers between devices: none -> 7.87 us  [body(): lax.ppermute(parts[d], 'pole', pairs_x(d))]
    ppermute x2, waiting for transfers between devices: 9.38 us -> 2.27 us  [body(): came = {d: lax.ppermute(near, grid, ring_other(d)) for d in (1, 3)}]
    ppermute x1, waiting for transfers between devices: 6.83 us -> 0.01 us  [body(): came[2] = lax.ppermute(far, grid, ring_other(2))]
    ppermute x0 -> x3, starting transfers between devices: none -> 6.06 us  [body(): lax.ppermute(parts[d], 'pole', pairs_x(d))]
    ppermute x3, waiting for transfers between devices: 8.66 us -> 7.31 us  [body(): came = {d: lax.ppermute(bufs[d], grid, ring_both(d)) for d in (1, 3, 2)}]
  transfers between devices with their start and end apart: 18 -> 21, of which waited for: 13 -> 16; matrix products, arithmetic and copies ran while one was open for 0% -> 0% of each run, Pallas kernels for 4% -> 5%
where the time goes in v7:
time: 68.7 us; the launch traced here: 68.6 us
  waiting for transfers between devices  31.4 us (46%)
  starting transfers between devices  29.4 us (43%)
  Pallas kernels  7.64 us (11%)
    ppermute x3, waiting for transfers between devices, body(): lax.ppermute(parts[d], 'pole', pairs_x(d))  7.87 us
    ppermute x3, waiting for transfers between devices, body(): came = {d: lax.ppermute(bufs[d], grid, ring_both(d)) for d in (1, 3, 2)}  7.31 us
    ppermute x3, waiting for transfers between devices, body(): lax.ppermute(slots[d], ('pole', 'row'), pairs_xy(d))  6.88 us
    ppermute x3, starting transfers between devices, body(): lax.ppermute(slots[d], ('pole', 'row'), pairs_xy(d))  6.55 us
    ppermute x3, starting transfers between devices, body(): lax.ppermute(parts[d], 'pole', pairs_x(d))  6.06 us
    ppermute x3, starting transfers between devices, body(): came = {d: lax.ppermute(bufs[d], grid, ring_both(d)) for d in (1, 3, 2)}  5.38 us
    ppermute x3, waiting for transfers between devices, body(): lax.ppermute(total, 'pole', pairs_x(d))  4.42 us
    ppermute x1, starting transfers between devices, body(): came[2] = lax.ppermute(far, grid, ring_other(2))  3.96 us
  transfers between devices with their start and end apart: 21, of which 16 were waited for; matrix products, arithmetic and copies ran while one was open for 0% of the time, Pallas kernels for 5%

profile of v7, /device:TPU:0, one launch (start us, length us, event | category | flops | bytes accessed | tf_op | source)
XLA Modules:
  0.0 68.6 jit_solution(2516087675681715820)
XLA Ops:
  0.5 2.0 %shard_map.64 = (bf16[5,2,2,32,256]{4,3,2,1,0:T(8,128)(2,1)S(1)}, bf16[5,2,2,32,256]{4,3,2,1,0:T(8,128)(2,1)S(1)}, bf16[5,2,2,32,256]{4,3,2,1,0:T(8,128)(2,1)S(1...) custom-call(bf16[10,2,32,256]{3,2,1,0:T(8,128)(2,1)} %bitcast.4, ...), custom_call_target="tpu_custom_call" | custom-call | bytes 4194304 | tf_op jit(solution)/shard_map/pallas_call | solution.py:366
  3.3 3.4 %collective-permute-start.3 = (bf16[5,2,2,32,256]{4,3,2,1,0:T(8,128)(2,1)S(1)}, bf16[5,2,2,32,256]{4,3,2,1,0:T(8,128)(2,1)S(1)}, u32[]{:S(2)}, u32[]{:S(2)}) collective-permute-start(bf16[5,2,2,32,256]{4,3,2,1,0:T(8,128)(2,1)S(1)} %get-tuple-element.37), channel_id=1, source_target_pairs={{0,4},{1,17},{2,6},{3,19},{4,0},{5,21},{6,2},{7,23},{8,12},{9,25},... | collective-permute-start | bytes 983048 | tf_op jit(solution)/shard_map/ppermute | solution.py:391
  6.7 1.1 %collective-permute-start.4 = (bf16[5,2,2,32,256]{4,3,2,1,0:T(8,128)(2,1)S(1)}, bf16[5,2,2,32,256]{4,3,2,1,0:T(8,128)(2,1)S(1)}, u32[]{:S(2)}, u32[]{:S(2)}) collective-permute-start(bf16[5,2,2,32,256]{4,3,2,1,0:T(8,128)(2,1)S(1)} %get-tuple-element.38), channel_id=1, source_target_pairs={{0,6},{1,25},{2,0},{3,27},{4,2},{5,29},{6,4},{7,31},{8,14},{9,1},{... | collective-permute-start | bytes 983048 | tf_op jit(solution)/shard_map/ppermute | solution.py:391
  8.7 3.3 %collective-permute-done.3.b2 = bf16[5,2,2,32,256]{4,3,2,1,0:T(8,128)(2,1)S(1)} collective-permute-done((bf16[5,2,2,32,256]{4,3,2,1,0:T(8,128)(2,1)S(1)}, bf16[5,2,2,32,256]{4,3,2,1,0:T(8,128)(2,1)S(1)}, u32[]{:S(2)}, u32[]{:S(2)}) %collective-permute-start.3) | collective-permute-done | bytes 327712 | tf_op jit(solution)/shard_map/ppermute | solution.py:391
  12.0 4.0 %collective-permute-done.4.b3 = bf16[5,2,2,32,256]{4,3,2,1,0:T(8,128)(2,1)S(1)} collective-permute-done((bf16[5,2,2,32,256]{4,3,2,1,0:T(8,128)(2,1)S(1)}, bf16[5,2,2,32,256]{4,3,2,1,0:T(8,128)(2,1)S(1)}, u32[]{:S(2)}, u32[]{:S(2)}) %collective-permute-start.4) | collective-permute-done | bytes 327712 | tf_op jit(solution)/shard_map/ppermute | solution.py:391
  16.5 4.0 %collective-permute-start.7 = (bf16[3,2,2,4,32,256]{5,4,3,2,1,0:T(8,128)(2,1)S(1)}, bf16[3,2,2,4,32,256]{5,4,3,2,1,0:T(8,128)(2,1)S(1)}, u32[]{:S(2)}, u32[]{:S(2)}) collective-permute-start(bf16[3,2,2,4,32,256]{5,4,3,2,1,0:T(8,128)(2,1)S(1)} %get-tuple-element.40.r0), channel_id=1, source_target_pairs={{0,16},{1,5},{2,18},{3,7},{4,20},{5,1},{6,22},{7,3},{8,24},{9,13},... | collective-permute-start | bytes 2359304 | tf_op jit(solution)/shard_map/ppermute | solution.py:402
  21.5 2.2 %collective-permute-start.6 = (bf16[3,2,2,4,32,256]{5,4,3,2,1,0:T(8,128)(2,1)S(1)}, bf16[3,2,2,4,32,256]{5,4,3,2,1,0:T(8,128)(2,1)S(1)}, u32[]{:S(2)}, u32[]{:S(2)}) collective-permute-start(bf16[3,2,2,4,32,256]{5,4,3,2,1,0:T(8,128)(2,1)S(1)} %get-tuple-element.41), channel_id=1, source_target_pairs={{0,24},{1,7},{2,26},{3,1},{4,28},{5,3},{6,30},{7,5},{8,0},{9,15},{... | collective-permute-start | bytes 2359304 | tf_op jit(solution)/shard_map/ppermute | solution.py:401
  23.7 3.0 %collective-permute-start.10 = (bf16[32,256]{1,0:T(8,128)(2,1)S(1)}, bf16[32,256]{1,0:T(8,128)(2,1)S(1)}, u32[]{:S(2)}, u32[]{:S(2)}) collective-permute-start(bf16[32,256]{1,0:T(8,128)(2,1)S(1)} %get-tuple-element.43), channel_id=1, source_target_pairs={{0,64},{32,96},{64,0},{96,32},{1,65},{33,97},{65,1},{97,33},{2,66}... | collective-permute-start | bytes 49160 | tf_op jit(solution)/shard_map/ppermute | solution.py:392
  26.7 2.2 %collective-permute-done.10.p2.d1 = bf16[32,256]{1,0:T(8,128)(2,1)S(1)} collective-permute-done((bf16[32,256]{1,0:T(8,128)(2,1)S(1)}, bf16[32,256]{1,0:T(8,128)(2,1)S(1)}, u32[]{:S(2)}, u32[]{:S(2)}) %collective-permute-start.10) | collective-permute-done | bytes 16416 | tf_op jit(solution)/shard_map/ppermute | solution.py:392
  29.0 2.8 %collective-permute-start.11 = (bf16[32,256]{1,0:T(8,128)(2,1)S(1)}, bf16[32,256]{1,0:T(8,128)(2,1)S(1)}, u32[]{:S(2)}, u32[]{:S(2)}) collective-permute-start(bf16[32,256]{1,0:T(8,128)(2,1)S(1)} %get-tuple-element.44), channel_id=1, source_target_pairs={{0,96},{32,64},{64,32},{96,0},{1,97},{33,65},{65,33},{97,1},{2,98}... | collective-permute-start | bytes 49160 | tf_op jit(solution)/shard_map/ppermute | solution.py:392
  31.7 2.2 %collective-permute-done.11.p3.d2 = bf16[32,256]{1,0:T(8,128)(2,1)S(1)} collective-permute-done((bf16[32,256]{1,0:T(8,128)(2,1)S(1)}, bf16[32,256]{1,0:T(8,128)(2,1)S(1)}, u32[]{:S(2)}, u32[]{:S(2)}) %collective-permute-start.11) | collective-permute-done | bytes 16416 | tf_op jit(solution)/shard_map/ppermute | solution.py:392
  34.2 3.5 %collective-permute-done.12.p1.d3 = bf16[32,256]{1,0:T(8,128)(2,1)S(1)} collective-permute-done((bf16[32,256]{1,0:T(8,128)(2,1)S(1)}, bf16[32,256]{1,0:T(8,128)(2,1)S(1)}, u32[]{:S(2)}, u32[]{:S(2)}) %collective-permute-start.12) | collective-permute-done | bytes 16416 | tf_op jit(solution)/shard_map/ppermute | solution.py:392
  37.7 1.2 %collective-permute-done.8.r1 = bf16[3,2,2,4,32,256]{5,4,3,2,1,0:T(8,128)(2,1)S(1)} collective-permute-done((bf16[3,2,2,4,32,256]{5,4,3,2,1,0:T(8,128)(2,1)S(1)}, bf16[3,2,2,4,32,256]{5,4,3,2,1,0:T(8,128)(2,1)S(1)}, u32[]{:S(2)}, u32[]{:S(2)}) %collective-permute-start.8) | collective-permute-done | bytes 786464 | tf_op jit(solution)/shard_map/ppermute | solution.py:401
  38.9 1.1 %collective-permute-done.6.r3 = bf16[3,2,2,4,32,256]{5,4,3,2,1,0:T(8,128)(2,1)S(1)} collective-permute-done((bf16[3,2,2,4,32,256]{5,4,3,2,1,0:T(8,128)(2,1)S(1)}, bf16[3,2,2,4,32,256]{5,4,3,2,1,0:T(8,128)(2,1)S(1)}, u32[]{:S(2)}, u32[]{:S(2)}) %collective-permute-start.6) | collective-permute-done | bytes 786464 | tf_op jit(solution)/shard_map/ppermute | solution.py:401
  40.9 2.1 %collective-permute-done.14.got = bf16[2,2,4,4,32,256]{5,4,3,2,1,0:T(8,128)(2,1)S(1)} collective-permute-done((bf16[2,2,4,4,32,256]{5,4,3,2,1,0:T(8,128)(2,1)S(1)}, bf16[2,2,4,4,32,256]{5,4,3,2,1,0:T(8,128)(2,1)S(1)}, u32[]{:S(2)}, u32[]{:S(2)}) %collective-permute-start.14) | collective-permute-done | bytes 1048608 | tf_op jit(solution)/shard_map/ppermute | solution.py:414
  44.1 1.9 %shard_map.70 = (bf16[7,32,256]{2,1,0:T(8,128)(2,1)S(1)}, bf16[7,32,256]{2,1,0:T(8,128)(2,1)S(1)}, bf16[7,32,256]{2,1,0:T(8,128)(2,1)S(1)}, bf16[7,32,256]{2,1,0:T(8,128)(2,1)S(1)}) custom-call(bf16[3,2,128,512]{3,2,1,0:T(8,128)(2,1)S(1)} %shard_map.68.edge, bf16[3,2,128,512]{3,2,1,0:T(8,128)(2,1)S(1)} %collective-permute-done.13.edge_s, ...), custom_call_target="tpu_custom_call" | custom-call | flops 1073741824 | bytes 4194304 | tf_op jit(solution)/shard_map/pallas_call | solution.py:433
  46.1 5.3 %collective-permute-start.15 = (bf16[7,32,256]{2,1,0:T(8,128)(2,1)S(1)}, bf16[7,32,256]{2,1,0:T(8,128)(2,1)S(1)}, u32[]{:S(2)}, u32[]{:S(2)}) collective-permute-start(bf16[7,32,256]{2,1,0:T(8,128)(2,1)S(1)} %get-tuple-element.51), channel_id=1, source_target_pairs={{0,68},{2,70},{4,64},{6,66},{8,76},{10,78},{12,72},{14,74},{16,84}... | collective-permute-start | bytes 344072 | tf_op jit(solution)/shard_map/ppermute | solution.py:442
  51.4 1.2 %collective-permute-start.16 = (bf16[7,32,256]{2,1,0:T(8,128)(2,1)S(1)}, bf16[7,32,256]{2,1,0:T(8,128)(2,1)S(1)}, u32[]{:S(2)}, u32[]{:S(2)}) collective-permute-start(bf16[7,32,256]{2,1,0:T(8,128)(2,1)S(1)} %get-tuple-element.52), channel_id=1, source_target_pairs={{0,38},{2,36},{4,34},{6,32},{8,46},{10,44},{12,42},{14,40},{16,54}... | collective-permute-start | bytes 344072 | tf_op jit(solution)/shard_map/ppermute | solution.py:442
  52.6 2.6 %collective-permute-done.15.a1 = bf16[7,32,256]{2,1,0:T(8,128)(2,1)S(1)} collective-permute-done((bf16[7,32,256]{2,1,0:T(8,128)(2,1)S(1)}, bf16[7,32,256]{2,1,0:T(8,128)(2,1)S(1)}, u32[]{:S(2)}, u32[]{:S(2)}) %collective-permute-start.15) | collective-permute-done | bytes 114720 | tf_op jit(solution)/shard_map/ppermute | solution.py:442
  55.3 3.1 %collective-permute-done.16.a2 = bf16[7,32,256]{2,1,0:T(8,128)(2,1)S(1)} collective-permute-done((bf16[7,32,256]{2,1,0:T(8,128)(2,1)S(1)}, bf16[7,32,256]{2,1,0:T(8,128)(2,1)S(1)}, u32[]{:S(2)}, u32[]{:S(2)}) %collective-permute-start.16) | collective-permute-done | bytes 114720 | tf_op jit(solution)/shard_map/ppermute | solution.py:442
  58.4 1.1 %collective-permute-done.17.a3 = bf16[7,32,256]{2,1,0:T(8,128)(2,1)S(1)} collective-permute-done((bf16[7,32,256]{2,1,0:T(8,128)(2,1)S(1)}, bf16[7,32,256]{2,1,0:T(8,128)(2,1)S(1)}, u32[]{:S(2)}, u32[]{:S(2)}) %collective-permute-start.17) | collective-permute-done | bytes 114720 | tf_op jit(solution)/shard_map/ppermute | solution.py:442
  59.6 1.4 %collective-permute-start.20 = (bf16[7,32,256]{2,1,0:T(8,128)(2,1)S(1)}, bf16[7,32,256]{2,1,0:T(8,128)(2,1)S(1)}, u32[]{:S(2)}, u32[]{:S(2)}) collective-permute-start(bf16[7,32,256]{2,1,0:T(8,128)(2,1)S(1)} %shard_map.71.g0), channel_id=1, source_target_pairs={{0,64},{32,96},{64,0},{96,32},{1,65},{33,97},{65,1},{97,33},{2,66}... | collective-permute-start | bytes 344072 | tf_op jit(solution)/shard_map/ppermute | solution.py:446
  60.9 1.6 %collective-permute-start.19 = (bf16[7,32,256]{2,1,0:T(8,128)(2,1)S(1)}, bf16[7,32,256]{2,1,0:T(8,128)(2,1)S(1)}, u32[]{:S(2)}, u32[]{:S(2)}) collective-permute-start(bf16[7,32,256]{2,1,0:T(8,128)(2,1)S(1)} %shard_map.71.g0), channel_id=1, source_target_pairs={{0,96},{32,64},{64,32},{96,0},{1,97},{33,65},{65,33},{97,1},{2,98}... | collective-permute-start | bytes 344072 | tf_op jit(solution)/shard_map/ppermute | solution.py:446
  63.2 3.8 %collective-permute-done.20.g2 = bf16[7,32,256]{2,1,0:T(8,128)(2,1)S(1)} collective-permute-done((bf16[7,32,256]{2,1,0:T(8,128)(2,1)S(1)}, bf16[7,32,256]{2,1,0:T(8,128)(2,1)S(1)}, u32[]{:S(2)}, u32[]{:S(2)}) %collective-permute-start.20) | collective-permute-done | bytes 114720 | tf_op jit(solution)/shard_map/ppermute | solution.py:446
  (29 shorter events, 8.5 us)
Async XLA Ops:
  0.0 2.6 %collective-permute-start = (bf16[10,2,32,256]{3,2,1,0:T(8,128)(2,1)}, bf16[10,2,32,256]{3,2,1,0:T(8,128)(2,1)S(1)}, u32[]{:S(2)}, u32[]{:S(2)}) collective-permute-start(bf16[10,2,32,256]{3,2,1,0:T(8,128)(2,1)} %bitcast.3), channel_id=1, source_target_pairs={{0,1},{1,0},{2,3},{3,2},{4,5},{5,4},{6,7},{7,6},{8,9},{9,8},{10,11... | collective-permute-start | bytes 983048 | tf_op jit(solution)/shard_map/ppermute | solution.py:364
  0.0 2.6 %collective-permute-start.1 = (bf16[10,2,32,256]{3,2,1,0:T(8,128)(2,1)}, bf16[10,2,32,256]{3,2,1,0:T(8,128)(2,1)S(1)}, u32[]{:S(2)}, u32[]{:S(2)}) collective-permute-start(bf16[10,2,32,256]{3,2,1,0:T(8,128)(2,1)} %bitcast.5), channel_id=1, source_target_pairs={{0,1},{1,0},{2,3},{3,2},{4,5},{5,4},{6,7},{7,6},{8,9},{9,8},{10,11... | collective-permute-start | bytes 983048 | tf_op jit(solution)/shard_map/ppermute | solution.py:364
  0.5 2.1 %collective-permute-start.2 = (bf16[7,2,32,256]{3,2,1,0:T(8,128)(2,1)}, bf16[7,2,32,256]{3,2,1,0:T(8,128)(2,1)S(1)}, u32[]{:S(2)}, u32[]{:S(2)}) collective-permute-start(bf16[7,2,32,256]{3,2,1,0:T(8,128)(2,1)} %bitcast.7), channel_id=1, source_target_pairs={{0,1},{1,0},{2,3},{3,2},{4,5},{5,4},{6,7},{7,6},{8,9},{9,8},{10,11... | collective-permute-start | bytes 688136 | tf_op jit(solution)/shard_map/ppermute | solution.py:364
  3.3 8.7 %collective-permute-start.3 = (bf16[5,2,2,32,256]{4,3,2,1,0:T(8,128)(2,1)S(1)}, bf16[5,2,2,32,256]{4,3,2,1,0:T(8,128)(2,1)S(1)}, u32[]{:S(2)}, u32[]{:S(2)}) collective-permute-start(bf16[5,2,2,32,256]{4,3,2,1,0:T(8,128)(2,1)S(1)} %get-tuple-element.37), channel_id=1, source_target_pairs={{0,4},{1,17},{2,6},{3,19},{4,0},{5,21},{6,2},{7,23},{8,12},{9,25},... | collective-permute-start | bytes 983048 | tf_op jit(solution)/shard_map/ppermute | solution.py:391
  6.7 9.3 %collective-permute-start.4 = (bf16[5,2,2,32,256]{4,3,2,1,0:T(8,128)(2,1)S(1)}, bf16[5,2,2,32,256]{4,3,2,1,0:T(8,128)(2,1)S(1)}, u32[]{:S(2)}, u32[]{:S(2)}) collective-permute-start(bf16[5,2,2,32,256]{4,3,2,1,0:T(8,128)(2,1)S(1)} %get-tuple-element.38), channel_id=1, source_target_pairs={{0,6},{1,25},{2,0},{3,27},{4,2},{5,29},{6,4},{7,31},{8,14},{9,1},{... | collective-permute-start | bytes 983048 | tf_op jit(solution)/shard_map/ppermute | solution.py:391
  7.7 8.3 %collective-permute-start.5 = (bf16[5,2,2,32,256]{4,3,2,1,0:T(8,128)(2,1)S(1)}, bf16[5,2,2,32,256]{4,3,2,1,0:T(8,128)(2,1)S(1)}, u32[]{:S(2)}, u32[]{:S(2)}) collective-permute-start(bf16[5,2,2,32,256]{4,3,2,1,0:T(8,128)(2,1)S(1)} %get-tuple-element.39), channel_id=1, source_target_pairs={{0,2},{1,9},{2,4},{3,11},{4,6},{5,13},{6,0},{7,15},{8,10},{9,17},{... | collective-permute-start | bytes 983048 | tf_op jit(solution)/shard_map/ppermute | solution.py:391
  16.5 21.1 %collective-permute-start.7 = (bf16[3,2,2,4,32,256]{5,4,3,2,1,0:T(8,128)(2,1)S(1)}, bf16[3,2,2,4,32,256]{5,4,3,2,1,0:T(8,128)(2,1)S(1)}, u32[]{:S(2)}, u32[]{:S(2)}) collective-permute-start(bf16[3,2,2,4,32,256]{5,4,3,2,1,0:T(8,128)(2,1)S(1)} %get-tuple-element.40.r0), channel_id=1, source_target_pairs={{0,16},{1,5},{2,18},{3,7},{4,20},{5,1},{6,22},{7,3},{8,24},{9,13},... | collective-permute-start | bytes 2359304 | tf_op jit(solution)/shard_map/ppermute | solution.py:402
  20.5 18.4 %collective-permute-start.8 = (bf16[3,2,2,4,32,256]{5,4,3,2,1,0:T(8,128)(2,1)S(1)}, bf16[3,2,2,4,32,256]{5,4,3,2,1,0:T(8,128)(2,1)S(1)}, u32[]{:S(2)}, u32[]{:S(2)}) collective-permute-start(bf16[3,2,2,4,32,256]{5,4,3,2,1,0:T(8,128)(2,1)S(1)} %get-tuple-element.41), channel_id=1, source_target_pairs={{0,8},{1,3},{2,10},{3,5},{4,12},{5,7},{6,14},{7,1},{8,16},{9,11},{... | collective-permute-start | bytes 2359304 | tf_op jit(solution)/shard_map/ppermute | solution.py:401
  21.5 18.4 %collective-permute-start.6 = (bf16[3,2,2,4,32,256]{5,4,3,2,1,0:T(8,128)(2,1)S(1)}, bf16[3,2,2,4,32,256]{5,4,3,2,1,0:T(8,128)(2,1)S(1)}, u32[]{:S(2)}, u32[]{:S(2)}) collective-permute-start(bf16[3,2,2,4,32,256]{5,4,3,2,1,0:T(8,128)(2,1)S(1)} %get-tuple-element.41), channel_id=1, source_target_pairs={{0,24},{1,7},{2,26},{3,1},{4,28},{5,3},{6,30},{7,5},{8,0},{9,15},{... | collective-permute-start | bytes 2359304 | tf_op jit(solution)/shard_map/ppermute | solution.py:401
  23.7 13.9 %collective-permute-start.9 = (bf16[2,2,2,4,32,256]{5,4,3,2,1,0:T(8,128)(2,1)S(1)}, bf16[2,2,2,4,32,256]{5,4,3,2,1,0:T(8,128)(2,1)S(1)}, u32[]{:S(2)}, u32[]{:S(2)}) collective-permute-start(bf16[2,2,2,4,32,256]{5,4,3,2,1,0:T(8,128)(2,1)S(1)} %get-tuple-element.42.uk), channel_id=1, source_target_pairs={{0,1},{1,0},{2,3},{3,2},{4,5},{5,4},{6,7},{7,6},{8,9},{9,8},{10,11... | collective-permute-start | bytes 1572872 | tf_op jit(solution)/shard_map/ppermute | solution.py:403
  23.7 5.2 %collective-permute-start.10 = (bf16[32,256]{1,0:T(8,128)(2,1)S(1)}, bf16[32,256]{1,0:T(8,128)(2,1)S(1)}, u32[]{:S(2)}, u32[]{:S(2)}) collective-permute-start(bf16[32,256]{1,0:T(8,128)(2,1)S(1)} %get-tuple-element.43), channel_id=1, source_target_pairs={{0,64},{32,96},{64,0},{96,32},{1,65},{33,97},{65,1},{97,33},{2,66}... | collective-permute-start | bytes 49160 | tf_op jit(solution)/shard_map/ppermute | solution.py:392
  29.0 4.9 %collective-permute-start.11 = (bf16[32,256]{1,0:T(8,128)(2,1)S(1)}, bf16[32,256]{1,0:T(8,128)(2,1)S(1)}, u32[]{:S(2)}, u32[]{:S(2)}) collective-permute-start(bf16[32,256]{1,0:T(8,128)(2,1)S(1)} %get-tuple-element.44), channel_id=1, source_target_pairs={{0,96},{32,64},{64,32},{96,0},{1,97},{33,65},{65,33},{97,1},{2,98}... | collective-permute-start | bytes 49160 | tf_op jit(solution)/shard_map/ppermute | solution.py:392
  33.9 3.7 %collective-permute-start.12 = (bf16[32,256]{1,0:T(8,128)(2,1)S(1)}, bf16[32,256]{1,0:T(8,128)(2,1)S(1)}, u32[]{:S(2)}, u32[]{:S(2)}) collective-permute-start(bf16[32,256]{1,0:T(8,128)(2,1)S(1)} %get-tuple-element.45), channel_id=1, source_target_pairs={{0,32},{32,0},{64,96},{96,64},{1,33},{33,1},{65,97},{97,65},{2,34}... | collective-permute-start | bytes 49160 | tf_op jit(solution)/shard_map/ppermute | solution.py:392
  40.3 2.7 %collective-permute-start.14 = (bf16[2,2,4,4,32,256]{5,4,3,2,1,0:T(8,128)(2,1)S(1)}, bf16[2,2,4,4,32,256]{5,4,3,2,1,0:T(8,128)(2,1)S(1)}, u32[]{:S(2)}, u32[]{:S(2)}) collective-permute-start(bf16[2,2,4,4,32,256]{5,4,3,2,1,0:T(8,128)(2,1)S(1)} %get-tuple-element.49.go), channel_id=1, source_target_pairs={{0,1},{1,0},{2,3},{3,2},{4,5},{5,4},{6,7},{7,6},{8,9},{9,8},{10,11... | collective-permute-start | bytes 3145736 | tf_op jit(solution)/shard_map/ppermute | solution.py:414
  40.8 3.3 %copy-start = (f32[1,2]{1,0:T(1,128)S(1)}, f32[1,2]{1,0:T(1,128)}, u32[]{:S(2)}) copy-start(f32[1,2]{1,0:T(1,128)} %res.1) | copy-start | bytes 28
  40.8 3.3 %collective-permute-start.13 = (bf16[3,2,128,512]{3,2,1,0:T(8,128)(2,1)S(1)}, bf16[3,2,128,512]{3,2,1,0:T(8,128)(2,1)S(1)}, u32[]{:S(2)}, u32[]{:S(2)}) collective-permute-start(bf16[3,2,128,512]{3,2,1,0:T(8,128)(2,1)S(1)} %shard_map.68.edge), channel_id=1, source_target_pairs={{0,1},{1,0},{2,3},{3,2},{4,5},{5,4},{6,7},{7,6},{8,9},{9,8},{10,11... | collective-permute-start | bytes 2359304 | tf_op jit(solution)/shard_map/ppermute | solution.py:424
  46.1 9.2 %collective-permute-start.15 = (bf16[7,32,256]{2,1,0:T(8,128)(2,1)S(1)}, bf16[7,32,256]{2,1,0:T(8,128)(2,1)S(1)}, u32[]{:S(2)}, u32[]{:S(2)}) collective-permute-start(bf16[7,32,256]{2,1,0:T(8,128)(2,1)S(1)} %get-tuple-element.51), channel_id=1, source_target_pairs={{0,68},{2,70},{4,64},{6,66},{8,76},{10,78},{12,72},{14,74},{16,84}... | collective-permute-start | bytes 344072 | tf_op jit(solution)/shard_map/ppermute | solution.py:442
  51.4 7.0 %collective-permute-start.16 = (bf16[7,32,256]{2,1,0:T(8,128)(2,1)S(1)}, bf16[7,32,256]{2,1,0:T(8,128)(2,1)S(1)}, u32[]{:S(2)}, u32[]{:S(2)}) collective-permute-start(bf16[7,32,256]{2,1,0:T(8,128)(2,1)S(1)} %get-tuple-element.52), channel_id=1, source_target_pairs={{0,38},{2,36},{4,34},{6,32},{8,46},{10,44},{12,42},{14,40},{16,54}... | collective-permute-start | bytes 344072 | tf_op jit(solution)/shard_map/ppermute | solution.py:442
  52.6 6.9 %collective-permute-start.17 = (bf16[7,32,256]{2,1,0:T(8,128)(2,1)S(1)}, bf16[7,32,256]{2,1,0:T(8,128)(2,1)S(1)}, u32[]{:S(2)}, u32[]{:S(2)}) collective-permute-start(bf16[7,32,256]{2,1,0:T(8,128)(2,1)S(1)} %get-tuple-element.53), channel_id=1, source_target_pairs={{0,98},{2,96},{4,102},{6,100},{8,106},{10,104},{12,110},{14,108},{... | collective-permute-start | bytes 344072 | tf_op jit(solution)/shard_map/ppermute | solution.py:442
  59.6 7.4 %collective-permute-start.20 = (bf16[7,32,256]{2,1,0:T(8,128)(2,1)S(1)}, bf16[7,32,256]{2,1,0:T(8,128)(2,1)S(1)}, u32[]{:S(2)}, u32[]{:S(2)}) collective-permute-start(bf16[7,32,256]{2,1,0:T(8,128)(2,1)S(1)} %shard_map.71.g0), channel_id=1, source_target_pairs={{0,64},{32,96},{64,0},{96,32},{1,65},{33,97},{65,1},{97,33},{2,66}... | collective-permute-start | bytes 344072 | tf_op jit(solution)/shard_map/ppermute | solution.py:446
  60.9 6.6 %collective-permute-start.19 = (bf16[7,32,256]{2,1,0:T(8,128)(2,1)S(1)}, bf16[7,32,256]{2,1,0:T(8,128)(2,1)S(1)}, u32[]{:S(2)}, u32[]{:S(2)}) collective-permute-start(bf16[7,32,256]{2,1,0:T(8,128)(2,1)S(1)} %shard_map.71.g0), channel_id=1, source_target_pairs={{0,96},{32,64},{64,32},{96,0},{1,97},{33,65},{65,33},{97,1},{2,98}... | collective-permute-start | bytes 344072 | tf_op jit(solution)/shard_map/ppermute | solution.py:446
  62.6 5.0 %collective-permute-start.18 = (bf16[7,32,256]{2,1,0:T(8,128)(2,1)S(1)}, bf16[7,32,256]{2,1,0:T(8,128)(2,1)S(1)}, u32[]{:S(2)}, u32[]{:S(2)}) collective-permute-start(bf16[7,32,256]{2,1,0:T(8,128)(2,1)S(1)} %shard_map.71.g0), channel_id=1, source_target_pairs={{0,32},{32,0},{64,96},{96,64},{1,33},{33,1},{65,97},{97,65},{2,34}... | collective-permute-start | bytes 344072 | tf_op jit(solution)/shard_map/ppermute | solution.py:446

commit v8 on v7

--- a/solution.py
+++ b/solution.py
@@ -127,7 +127,7 @@
 
 
 def pack_own_kernel(low_in, up_in, dia_in, widths_in, pattern_in, res_in, *refs):
-    outs, parts, (widths, pattern, low, up, dia, res, sems) = refs[:4], refs[4:8], refs[8:]
+    outs, parts, (widths, pattern, res, low, up, dia, sems) = refs[:4], refs[4:8], refs[8:]
     run_copies(
         [
             (low_in, low),
@@ -217,13 +217,41 @@
     ]
 
 
-def put(out, slot, pair, sign=1):
+def put(out, pair, sign=1):
     for i in range(2):
-        out[slot, i] = (pair[i] if sign > 0 else -pair[i]).astype(BF)
-
-
-def first_kernel(r0, r3, r2, r1, uks, p2, p3, p1, out, stay, go, lead, right, sems):
-    x, z, y, c = place()
+        out[i] = (pair[i] if sign > 0 else -pair[i]).astype(BF)
+
+
+def early_kernel(r0, r2, p2, p3, p1, go, sems):
+    x, z, y, c = place()
+    part_of_last(((0, r0), (2, r2)), go, sems)
+
+
+def part_of_last(given, go, sems):
+    x, z, y, c = place()
+
+    @pl.when(c == 0)
+    def _():
+        copies = []
+        for d, buf in given:
+            at = lax.div(lax.rem(z + 4 - d, 4), 2)
+            copies.append((buf.at[pl.ds(1, 2), 1], go.at[:, :, at]))
+        run_copies(copies, sems)
+
+    @pl.when(c == 1)
+    def _():
+        copies = []
+        for d, buf in given:
+            at = lax.div(lax.rem(y + 4 - d, 4), 2)
+            copies.append((buf.at[2], go.at[:, :, at]))
+        run_copies(copies, sems)
+
+
+def first_kernel(
+    r0, r3, r2, r1, uks, before, out0, out1, out2, stay, go, lead, right, sems
+):
+    x, z, y, c = place()
+    part_of_last(((1, r1), (3, r3)), go, sems)
 
     def rows_of(block):
         return wide_rows(lambda h, part: right[block, h, part, z].reshape(128, 256))
@@ -234,7 +262,6 @@
         for d, buf in enumerate((r0, r1, r2, r3)):
             at = lax.rem(z + 4 - d, 4)
             copies.append((buf.at[pl.ds(1, 2), 0], stay.at[:, :, at]))
-            copies.append((buf.at[pl.ds(1, 2), 1], go.at[:, :, at]))
             copies.append((buf.at[0], lead.at[:, :, at]))
         run_copies(copies, sems)
 
@@ -242,32 +269,32 @@
     def _():
         copies = []
         for d, buf in enumerate((r0, r1, r2, r3)):
-            copies.append((buf.at[pl.ds(0, 2)], right.at[:, :, :, :, lax.rem(y + 4 - d, 4)]))
-        for d, buf in enumerate((r0, r1, r2, r3)):
-            copies.append((buf.at[2], go.at[:, :, :, lax.rem(y + 4 - d, 4)]))
+            at = lax.rem(y + 4 - d, 4)
+            copies.append((buf.at[pl.ds(0, 2)], right.at[:, :, :, :, at]))
+            copies.append((buf.at[2], stay.at[:, :, :, at]))
         run_copies(copies, sems)
         ukp = wide_rows(lambda h, part: uks[0, h, part].reshape(128, 256))
         uk0 = wide_rows(lambda h, part: uks[1, h, part].reshape(128, 256))
         (kv,) = times(left_of([ukp]), 1, right[1])
         v = tuple((uk0[i].astype(F32) - kv[i]).astype(BF) for i in range(2))
         xk0, xp0 = times(left_of([v, rows_of(1)]), 2, right[0])
-        put(out, 0, xp0, -1)
-        put(out, 1, rows_of(0))
-        put(out, 2, xk0, -1)
-
-
-def next_kernel(edge, lead, uk, after, out):
+        put(out0, xp0, -1)
+        put(out1, rows_of(0))
+        put(out2, xk0, -1)
+
+
+def next_kernel(edge0, edge1, lead, uk, after, out0, out1):
     x, z, y, c = place()
 
     @pl.when(c == 0)
     def _():
         ukp = wide_rows(lambda h, part: uk[0, h, part].reshape(128, 256))
         (kd,) = times(left_of([ukp]), 1, lead)
-        put(out, 0, kd)
-        put(out, 1, wide_rows(lambda h, part: lead[h, part, z].reshape(128, 256)))
-
-
-def inner_kernel(stay, go, got, out):
+        put(out0, kd)
+        put(out1, wide_rows(lambda h, part: lead[h, part, z].reshape(128, 256)))
+
+
+def inner_kernel(edge0, edge1, edge2, stay, got_a, got_b, out, early, other, sems):
     x, z, y, c = place()
 
     def work(last, own):
@@ -277,30 +304,50 @@
 
     @pl.when(c == 0)
     def _():
-        work(got, stay)
+        copies = []
+        for buf, low in ((got_a, lax.rem(y, 2)), (got_b, 1 - lax.rem(y, 2))):
+            for n in range(2):
+                copies.append((buf.at[:, :, n], other.at[:, :, :, 2 * n + low]))
+        run_copies(copies, sems)
+        work(other, stay)
+        left = left_of([(e[0], e[1]) for e in (edge0, edge1)])
+        early[0:512] = dot(left, stay[0].reshape(1024, 256))
 
     @pl.when(c == 1)
     def _():
-        work(go, got)
+        copies = []
+        for buf, low in ((got_a, lax.rem(z, 2)), (got_b, 1 - lax.rem(z, 2))):
+            for n in range(2):
+                copies.append((buf.at[:, :, n], other.at[:, :, 2 * n + low]))
+        run_copies(copies, sems)
+        work(stay, other)
+        left = left_of([(e[0], e[1]) for e in (edge0, edge1, edge2)])
+        early[...] = dot(left, stay[1].reshape(1024, 256))
 
 
 def last_kernel(
-    edge, edge_s, inner, stay, go, got, res, slot0, slot1, slot2, slot3, parts
+    edge0, edge1, edge2, swap0, swap1, swap2, inner, early, got, res,
+    slot0, slot1, slot2, slot3, parts,
 ):
+    edge, edge_s = (edge0, edge1, edge2), (swap0, swap1, swap2)
     x, z, y, c = place()
     wr, wi = res[0, 0], res[0, 1]
 
     def density(re, im):
         return (wr * re.astype(F32) - wi * im.astype(F32)).astype(BF)
 
-    def work(e0, e1, last, own, half):
+    def work(e0, e1, half):
         cols = slice(256 * half, 256 * half + 256)
-        xp0, d0r, xk0 = [(e1[n, 0], e1[n, 1]) for n in range(3)]
-        kd, dpr = [(e0[n, 0], e0[n, 1]) for n in range(2)]
+        xp0, d0r, xk0 = [(e1[n][0], e1[n][1]) for n in range(3)]
+        kd, dpr = [(e0[n][0], e0[n][1]) for n in range(2)]
         left = left_of([xp0, d0r, xk0])
         pg, og, kg = pairs_of(dot(left, inner[...]), 3)
-        pe, oe, ke = pairs_of(dot(left, last[half].reshape(1024, 256)), 3)
-        kl, pl_ = pairs_of(dot(left_of([kd, dpr]), own[0].reshape(1024, 256)), 2)
+        if half == 0:
+            pe, oe, ke = pairs_of(dot(left, got[0].reshape(1024, 256)), 3)
+            kl, pl_ = pairs_of(early[0:512], 2)
+        else:
+            pe, oe, ke = pairs_of(early[...], 3)
+            kl, pl_ = pairs_of(dot(left_of([kd, dpr]), got[0].reshape(1024, 256)), 2)
         parts[0] = density(*[kl[i] - kg[i] for i in range(2)])
         parts[1] = density(*[-(pl_[i] + pg[i]) for i in range(2)])
         parts[2] = density(-og[0], -og[1])
@@ -319,11 +366,11 @@
 
     @pl.when(c == 0)
     def _():
-        work(edge, edge_s, got, stay, 0)
+        work(edge, edge_s, 0)
 
     @pl.when(c == 1)
     def _():
-        work(edge_s, edge, go, got, 1)
+        work(edge_s, edge, 1)
 
     for d, out in enumerate((slot0, slot1, slot2, slot3)):
         at = pl.multiple_of(32 * (y ^ d), 32)
@@ -363,18 +410,17 @@
     mine = (lower_factor[0], upper_factor[0], diag_inverse[0])
     swapped = [lax.ppermute(a, "col", SWAP) for a in mine]
     grid = ("row", "col")
-    *bufs, widths, pattern = call(
+    *bufs, widths, pattern, weights = call(
         pack_own_kernel,
         [shape(5, 2, 2, 32, 256)] * 4
         + [shape(32, 256)] * 4
-        + [shape(7, dtype=jnp.int32), shape(10, dtype=jnp.int32)],
+        + [shape(7, dtype=jnp.int32), shape(10, dtype=jnp.int32), shape(1, 2, dtype=F32)],
         [in_hbm()] * 6,
-        [vm()] * 8 + [sm()] * 2,
+        [vm()] * 8 + [sm()] * 3,
         [
             pltpu.VMEM((10, 2, 32, 256), BF),
             pltpu.VMEM((10, 2, 32, 256), BF),
             pltpu.VMEM((7, 2, 32, 256), BF),
-            pltpu.SMEM((1, 2), F32),
             pltpu.SemaphoreType.DMA((6,)),
         ],
         nbytes=4 << 20,
@@ -402,43 +448,56 @@
     came[2] = lax.ppermute(far, grid, ring_other(2))
     uks = lax.ppermute(uk, "col", SWAP)
     blocks = (far, came[3], came[2], came[1])
-    edge, stay, go, lead = call(
+    half = shape(2, 2, 2, 4, 32, 256)
+    go = call(
+        early_kernel,
+        [half],
+        [hbm()] * 5,
+        [hbm()],
+        [pltpu.SemaphoreType.DMA((2,))],
+        nbytes=1 << 20,
+    )(far, came[2], *parts[1:])[0]
+    got_early = lax.ppermute(go, "col", SWAP)
+    whole = shape(2, 2, 4, 4, 32, 256)
+    slab = shape(2, 128, 512)
+    *edge, stay, go, lead = call(
         first_kernel,
-        [shape(3, 2, 128, 512)] + [shape(2, 2, 4, 4, 32, 256)] * 3,
-        [hbm()] * 4 + [vm()] + [hbm()] * 3,
-        [vm()] + [hbm()] * 3,
-        [pltpu.VMEM((2, 2, 2, 4, 4, 32, 256), BF), pltpu.SemaphoreType.DMA((12,))],
+        [slab] * 3 + [whole, half, whole],
+        [hbm()] * 4 + [vm()] + [hbm()],
+        [vm()] * 3 + [hbm()] * 3,
+        [pltpu.VMEM((2, 2, 2, 4, 4, 32, 256), BF), pltpu.SemaphoreType.DMA((8,))],
         flops=805306368,
         nbytes=4 << 20,
-    )(*blocks, uks, *parts[1:])
+    )(*blocks, uks, got_early)
     got = lax.ppermute(go, "col", SWAP)
-    edge = call(
+    edge[:2] = call(
         next_kernel,
-        [shape(3, 2, 128, 512)],
-        [hbm()] + [vm()] * 2 + [hbm()],
-        [vm()],
+        [slab] * 2,
+        [hbm()] * 2 + [vm()] * 2 + [hbm()],
+        [vm()] * 2,
         flops=268435456,
         nbytes=2 << 20,
-        aliases={0: 0},
-    )(edge, lead, uk, stay)[0]
-    edge_s = lax.ppermute(edge, "col", SWAP)
-    inner = call(
+        aliases={0: 0, 1: 1},
+    )(*edge[:2], lead, uk, stay)
+    edge_s = [lax.ppermute(e, "col", SWAP) for e in edge]
+    inner, early, other = call(
         inner_kernel,
-        [shape(1024, 256)],
+        [shape(1024, 256), shape(768, 256, dtype=F32), whole],
+        [vm()] * 4 + [hbm()] * 2,
         [vm()] * 3,
-        [vm()],
-        flops=536870912,
-        nbytes=3 << 20,
-    )(stay, go, got)[0]
+        [pltpu.SemaphoreType.DMA((4,))],
+        flops=939524096,
+        nbytes=4 << 20,
+    )(*edge, stay, got_early, got)
     slots = call(
         last_kernel,
         [shape(7, 32, 256)] * 4,
-        [vm()] * 6 + [sm()],
+        [vm()] * 9 + [sm()],
         [vm()] * 4,
         [pltpu.VMEM((7, 128, 256), BF)],
-        flops=1073741824,
+        flops=805306368,
         nbytes=4 << 20,
-    )(edge, edge_s, inner, stay, go, got, residues)
+    )(*edge, *edge_s, inner, early, other, weights)
     at_x = [slots[0]] + [lax.ppermute(slots[d], ("pole", "row"), pairs_xy(d)) for d in (2, 3, 1)]
     total = call(sum_kernel, [shape(7, 32, 256)], [vm()] * 8, [vm()], nbytes=1 << 20)(
         *at_x, *parts

time: 68.7 us -> 67.6 us (0.984)
  waiting for transfers between devices: 31.4 us -> 29.9 us
    ppermute x3, waiting for transfers between devices: 7.87 us -> 3.34 us  [body(): lax.ppermute(parts[d], 'pole', pairs_x(d))]
    ppermute x2, waiting for transfers between devices: 2.27 us -> 6.33 us  [body(): came = {d: lax.ppermute(near, grid, ring_other(d)) for d in (1, 3)}]
    ppermute x1, waiting for transfers between devices: 2.09 us -> 0.76 us  [body(): got = lax.ppermute(go, 'col', SWAP)]
    ppermute x1, waiting for transfers between devices: 0.01 us -> 0.73 us  [body(): uks = lax.ppermute(uk, 'col', SWAP)]
    pallas_call x4 -> x5, Pallas kernels: 3.44 us -> 3.55 us  [the longest x1 1.66 us: body(): call(last_kernel, [shape(7, 32, 256)] * 4, [vm()] * 9 + [sm()], [vm()] *...]
  transfers between devices with their start and end apart: 21 -> 24, of which waited for: 16 -> 16; matrix products, arithmetic and copies ran while one was open for 0% -> 0% of each run, Pallas kernels for 5% -> 5%
where the time goes in v8:
time: 67.6 us; the launch traced here: 67.5 us
  waiting for transfers between devices  29.9 us (44%)
  starting transfers between devices  29.7 us (44%)
  Pallas kernels  7.76 us (11%)
    ppermute x3, waiting for transfers between devices, body(): came = {d: lax.ppermute(bufs[d], grid, ring_both(d)) for d in (1, 3, 2)}  7.31 us
    ppermute x3, waiting for transfers between devices, body(): lax.ppermute(slots[d], ('pole', 'row'), pairs_xy(d))  6.88 us
    ppermute x3, starting transfers between devices, body(): lax.ppermute(slots[d], ('pole', 'row'), pairs_xy(d))  6.55 us
    ppermute x2, waiting for transfers between devices, body(): came = {d: lax.ppermute(near, grid, ring_other(d)) for d in (1, 3)}  6.33 us
    ppermute x3, starting transfers between devices, body(): lax.ppermute(parts[d], 'pole', pairs_x(d))  5.64 us
    ppermute x3, starting transfers between devices, body(): came = {d: lax.ppermute(bufs[d], grid, ring_both(d)) for d in (1, 3, 2)}  5.38 us
    ppermute x3, waiting for transfers between devices, body(): lax.ppermute(total, 'pole', pairs_x(d))  4.42 us
    ppermute x1, starting transfers between devices, body(): came[2] = lax.ppermute(far, grid, ring_other(2))  3.96 us
  transfers between devices with their start and end apart: 24, of which 16 were waited for; matrix products, arithmetic and copies ran while one was open for 0% of the time, Pallas kernels for 5%

profile of v8, /device:TPU:0, one launch (start us, length us, event | category | flops | bytes accessed | tf_op | source)
XLA Modules:
  0.0 67.5 jit_solution(866767275557033436)
XLA Ops:
  0.5 2.0 %shard_map.64 = (bf16[5,2,2,32,256]{4,3,2,1,0:T(8,128)(2,1)S(1)}, bf16[5,2,2,32,256]{4,3,2,1,0:T(8,128)(2,1)S(1)}, bf16[5,2,2,32,256]{4,3,2,1,0:T(8,128)(2,1)S(1...) custom-call(bf16[10,2,32,256]{3,2,1,0:T(8,128)(2,1)} %bitcast.4, ...), custom_call_target="tpu_custom_call" | custom-call | bytes 4194304 | tf_op jit(solution)/shard_map/pallas_call | solution.py:413
  3.3 3.4 %collective-permute-start.3 = (bf16[5,2,2,32,256]{4,3,2,1,0:T(8,128)(2,1)S(1)}, bf16[5,2,2,32,256]{4,3,2,1,0:T(8,128)(2,1)S(1)}, u32[]{:S(2)}, u32[]{:S(2)}) collective-permute-start(bf16[5,2,2,32,256]{4,3,2,1,0:T(8,128)(2,1)S(1)} %get-tuple-element.45), channel_id=1, source_target_pairs={{0,4},{1,17},{2,6},{3,19},{4,0},{5,21},{6,2},{7,23},{8,12},{9,25},... | collective-permute-start | bytes 983048 | tf_op jit(solution)/shard_map/ppermute | solution.py:437
  6.7 1.1 %collective-permute-start.4 = (bf16[5,2,2,32,256]{4,3,2,1,0:T(8,128)(2,1)S(1)}, bf16[5,2,2,32,256]{4,3,2,1,0:T(8,128)(2,1)S(1)}, u32[]{:S(2)}, u32[]{:S(2)}) collective-permute-start(bf16[5,2,2,32,256]{4,3,2,1,0:T(8,128)(2,1)S(1)} %get-tuple-element.46), channel_id=1, source_target_pairs={{0,6},{1,25},{2,0},{3,27},{4,2},{5,29},{6,4},{7,31},{8,14},{9,1},{... | collective-permute-start | bytes 983048 | tf_op jit(solution)/shard_map/ppermute | solution.py:437
  8.7 3.3 %collective-permute-done.3.b2 = bf16[5,2,2,32,256]{4,3,2,1,0:T(8,128)(2,1)S(1)} collective-permute-done((bf16[5,2,2,32,256]{4,3,2,1,0:T(8,128)(2,1)S(1)}, bf16[5,2,2,32,256]{4,3,2,1,0:T(8,128)(2,1)S(1)}, u32[]{:S(2)}, u32[]{:S(2)}) %collective-permute-start.3) | collective-permute-done | bytes 327712 | tf_op jit(solution)/shard_map/ppermute | solution.py:437
  12.0 4.0 %collective-permute-done.4.b3 = bf16[5,2,2,32,256]{4,3,2,1,0:T(8,128)(2,1)S(1)} collective-permute-done((bf16[5,2,2,32,256]{4,3,2,1,0:T(8,128)(2,1)S(1)}, bf16[5,2,2,32,256]{4,3,2,1,0:T(8,128)(2,1)S(1)}, u32[]{:S(2)}, u32[]{:S(2)}) %collective-permute-start.4) | collective-permute-done | bytes 327712 | tf_op jit(solution)/shard_map/ppermute | solution.py:437
  16.5 4.0 %collective-permute-start.7 = (bf16[3,2,2,4,32,256]{5,4,3,2,1,0:T(8,128)(2,1)S(1)}, bf16[3,2,2,4,32,256]{5,4,3,2,1,0:T(8,128)(2,1)S(1)}, u32[]{:S(2)}, u32[]{:S(2)}) collective-permute-start(bf16[3,2,2,4,32,256]{5,4,3,2,1,0:T(8,128)(2,1)S(1)} %get-tuple-element.48.r0), channel_id=1, source_target_pairs={{0,16},{1,5},{2,18},{3,7},{4,20},{5,1},{6,22},{7,3},{8,24},{9,13},... | collective-permute-start | bytes 2359304 | tf_op jit(solution)/shard_map/ppermute | solution.py:448
  21.5 2.2 %collective-permute-start.6 = (bf16[3,2,2,4,32,256]{5,4,3,2,1,0:T(8,128)(2,1)S(1)}, bf16[3,2,2,4,32,256]{5,4,3,2,1,0:T(8,128)(2,1)S(1)}, u32[]{:S(2)}, u32[]{:S(2)}) collective-permute-start(bf16[3,2,2,4,32,256]{5,4,3,2,1,0:T(8,128)(2,1)S(1)} %get-tuple-element.49), channel_id=1, source_target_pairs={{0,24},{1,7},{2,26},{3,1},{4,28},{5,3},{6,30},{7,5},{8,0},{9,15},{... | collective-permute-start | bytes 2359304 | tf_op jit(solution)/shard_map/ppermute | solution.py:447
  23.7 3.0 %collective-permute-start.10 = (bf16[32,256]{1,0:T(8,128)(2,1)S(1)}, bf16[32,256]{1,0:T(8,128)(2,1)S(1)}, u32[]{:S(2)}, u32[]{:S(2)}) collective-permute-start(bf16[32,256]{1,0:T(8,128)(2,1)S(1)} %get-tuple-element.51), channel_id=1, source_target_pairs={{0,64},{32,96},{64,0},{96,32},{1,65},{33,97},{65,1},{97,33},{2,66}... | collective-permute-start | bytes 49160 | tf_op jit(solution)/shard_map/ppermute | solution.py:438
  26.7 1.1 %collective-permute-start.11 = (bf16[32,256]{1,0:T(8,128)(2,1)S(1)}, bf16[32,256]{1,0:T(8,128)(2,1)S(1)}, u32[]{:S(2)}, u32[]{:S(2)}) collective-permute-start(bf16[32,256]{1,0:T(8,128)(2,1)S(1)} %get-tuple-element.52), channel_id=1, source_target_pairs={{0,96},{32,64},{64,32},{96,0},{1,97},{33,65},{65,33},{97,1},{2,98}... | collective-permute-start | bytes 49160 | tf_op jit(solution)/shard_map/ppermute | solution.py:438
  27.9 1.1 %collective-permute-done.10.p2.d1 = bf16[32,256]{1,0:T(8,128)(2,1)S(1)} collective-permute-done((bf16[32,256]{1,0:T(8,128)(2,1)S(1)}, bf16[32,256]{1,0:T(8,128)(2,1)S(1)}, u32[]{:S(2)}, u32[]{:S(2)}) %collective-permute-start.10) | collective-permute-done | bytes 16416 | tf_op jit(solution)/shard_map/ppermute | solution.py:438
  29.0 1.5 %collective-permute-start.12 = (bf16[32,256]{1,0:T(8,128)(2,1)S(1)}, bf16[32,256]{1,0:T(8,128)(2,1)S(1)}, u32[]{:S(2)}, u32[]{:S(2)}) collective-permute-start(bf16[32,256]{1,0:T(8,128)(2,1)S(1)} %get-tuple-element.53), channel_id=1, source_target_pairs={{0,32},{32,0},{64,96},{96,64},{1,33},{33,1},{65,97},{97,65},{2,34}... | collective-permute-start | bytes 49160 | tf_op jit(solution)/shard_map/ppermute | solution.py:438
  30.4 1.2 %collective-permute-done.11.p3.d2 = bf16[32,256]{1,0:T(8,128)(2,1)S(1)} collective-permute-done((bf16[32,256]{1,0:T(8,128)(2,1)S(1)}, bf16[32,256]{1,0:T(8,128)(2,1)S(1)}, u32[]{:S(2)}, u32[]{:S(2)}) %collective-permute-start.11) | collective-permute-done | bytes 16416 | tf_op jit(solution)/shard_map/ppermute | solution.py:438
  33.6 5.3 %collective-permute-done.8.r1 = bf16[3,2,2,4,32,256]{5,4,3,2,1,0:T(8,128)(2,1)S(1)} collective-permute-done((bf16[3,2,2,4,32,256]{5,4,3,2,1,0:T(8,128)(2,1)S(1)}, bf16[3,2,2,4,32,256]{5,4,3,2,1,0:T(8,128)(2,1)S(1)}, u32[]{:S(2)}, u32[]{:S(2)}) %collective-permute-start.8) | collective-permute-done | bytes 786464 | tf_op jit(solution)/shard_map/ppermute | solution.py:447
  38.9 1.1 %collective-permute-done.6.r3 = bf16[3,2,2,4,32,256]{5,4,3,2,1,0:T(8,128)(2,1)S(1)} collective-permute-done((bf16[3,2,2,4,32,256]{5,4,3,2,1,0:T(8,128)(2,1)S(1)}, bf16[3,2,2,4,32,256]{5,4,3,2,1,0:T(8,128)(2,1)S(1)}, u32[]{:S(2)}, u32[]{:S(2)}) %collective-permute-start.6) | collective-permute-done | bytes 786464 | tf_op jit(solution)/shard_map/ppermute | solution.py:447
  42.2 1.1 %shard_map.70 = (bf16[1024,256]{1,0:T(8,128)(2,1)S(1)}, f32[768,256]{1,0:T(8,128)S(1)}, bf16[2,2,4,4,32,256]{5,4,3,2,1,0:T(8,128)(2,1)S(1)}) custom-call(bf16[2,128,512]{2,1,0:T(8,128)(2,1)S(1)} %get-tuple-element.58.edge0, bf16[2,128,512]{2,1,0:T(8,128)(2,1)S(1)} %get-tuple-element.59.edge1, bf16[2,128,512]{2,1,0:T(8,128)(2,1)S(1)} %get-tuple-element.60.edge2, ...), custom_call_target="tpu_custom_call" | custom-call | flops 939524096 | bytes 4194304 | tf_op jit(solution)/shard_map/pallas_call | solution.py:483
  43.3 1.7 %shard_map.71 = (bf16[7,32,256]{2,1,0:T(8,128)(2,1)S(1)}, bf16[7,32,256]{2,1,0:T(8,128)(2,1)S(1)}, bf16[7,32,256]{2,1,0:T(8,128)(2,1)S(1)}, bf16[7,32,256]{2,1,0:T(8,128)(2,1)S(1)}) custom-call(bf16[2,128,512]{2,1,0:T(8,128)(2,1)S(1)} %get-tuple-element.58.edge0, bf16[2,128,512]{2,1,0:T(8,128)(2,1)S(1)} %get-tuple-element.59.edge1, ...), custom_call_target="tpu_custom_call" | custom-call | flops 805306368 | bytes 4194304 | tf_op jit(solution)/shard_map/pallas_call | solution.py:492
  45.0 5.3 %collective-permute-start.18 = (bf16[7,32,256]{2,1,0:T(8,128)(2,1)S(1)}, bf16[7,32,256]{2,1,0:T(8,128)(2,1)S(1)}, u32[]{:S(2)}, u32[]{:S(2)}) collective-permute-start(bf16[7,32,256]{2,1,0:T(8,128)(2,1)S(1)} %get-tuple-element.67), channel_id=1, source_target_pairs={{0,68},{2,70},{4,64},{6,66},{8,76},{10,78},{12,72},{14,74},{16,84}... | collective-permute-start | bytes 344072 | tf_op jit(solution)/shard_map/ppermute | solution.py:501
  50.3 1.2 %collective-permute-start.19 = (bf16[7,32,256]{2,1,0:T(8,128)(2,1)S(1)}, bf16[7,32,256]{2,1,0:T(8,128)(2,1)S(1)}, u32[]{:S(2)}, u32[]{:S(2)}) collective-permute-start(bf16[7,32,256]{2,1,0:T(8,128)(2,1)S(1)} %get-tuple-element.68), channel_id=1, source_target_pairs={{0,38},{2,36},{4,34},{6,32},{8,46},{10,44},{12,42},{14,40},{16,54}... | collective-permute-start | bytes 344072 | tf_op jit(solution)/shard_map/ppermute | solution.py:501
  51.6 2.6 %collective-permute-done.18.a1 = bf16[7,32,256]{2,1,0:T(8,128)(2,1)S(1)} collective-permute-done((bf16[7,32,256]{2,1,0:T(8,128)(2,1)S(1)}, bf16[7,32,256]{2,1,0:T(8,128)(2,1)S(1)}, u32[]{:S(2)}, u32[]{:S(2)}) %collective-permute-start.18) | collective-permute-done | bytes 114720 | tf_op jit(solution)/shard_map/ppermute | solution.py:501
  54.2 3.1 %collective-permute-done.19.a2 = bf16[7,32,256]{2,1,0:T(8,128)(2,1)S(1)} collective-permute-done((bf16[7,32,256]{2,1,0:T(8,128)(2,1)S(1)}, bf16[7,32,256]{2,1,0:T(8,128)(2,1)S(1)}, u32[]{:S(2)}, u32[]{:S(2)}) %collective-permute-start.19) | collective-permute-done | bytes 114720 | tf_op jit(solution)/shard_map/ppermute | solution.py:501
  57.3 1.1 %collective-permute-done.20.a3 = bf16[7,32,256]{2,1,0:T(8,128)(2,1)S(1)} collective-permute-done((bf16[7,32,256]{2,1,0:T(8,128)(2,1)S(1)}, bf16[7,32,256]{2,1,0:T(8,128)(2,1)S(1)}, u32[]{:S(2)}, u32[]{:S(2)}) %collective-permute-start.20) | collective-permute-done | bytes 114720 | tf_op jit(solution)/shard_map/ppermute | solution.py:501
  58.5 1.4 %collective-permute-start.23 = (bf16[7,32,256]{2,1,0:T(8,128)(2,1)S(1)}, bf16[7,32,256]{2,1,0:T(8,128)(2,1)S(1)}, u32[]{:S(2)}, u32[]{:S(2)}) collective-permute-start(bf16[7,32,256]{2,1,0:T(8,128)(2,1)S(1)} %shard_map.72.g0), channel_id=1, source_target_pairs={{0,64},{32,96},{64,0},{96,32},{1,65},{33,97},{65,1},{97,33},{2,66}... | collective-permute-start | bytes 344072 | tf_op jit(solution)/shard_map/ppermute | solution.py:505
  59.9 1.6 %collective-permute-start.22 = (bf16[7,32,256]{2,1,0:T(8,128)(2,1)S(1)}, bf16[7,32,256]{2,1,0:T(8,128)(2,1)S(1)}, u32[]{:S(2)}, u32[]{:S(2)}) collective-permute-start(bf16[7,32,256]{2,1,0:T(8,128)(2,1)S(1)} %shard_map.72.g0), channel_id=1, source_target_pairs={{0,96},{32,64},{64,32},{96,0},{1,97},{33,65},{65,33},{97,1},{2,98}... | collective-permute-start | bytes 344072 | tf_op jit(solution)/shard_map/ppermute | solution.py:505
  62.1 3.8 %collective-permute-done.23.g2 = bf16[7,32,256]{2,1,0:T(8,128)(2,1)S(1)} collective-permute-done((bf16[7,32,256]{2,1,0:T(8,128)(2,1)S(1)}, bf16[7,32,256]{2,1,0:T(8,128)(2,1)S(1)}, u32[]{:S(2)}, u32[]{:S(2)}) %collective-permute-start.23) | collective-permute-done | bytes 114720 | tf_op jit(solution)/shard_map/ppermute | solution.py:505
  (34 shorter events, 10.3 us)
Async XLA Ops:
  0.0 2.6 %collective-permute-start = (bf16[10,2,32,256]{3,2,1,0:T(8,128)(2,1)}, bf16[10,2,32,256]{3,2,1,0:T(8,128)(2,1)S(1)}, u32[]{:S(2)}, u32[]{:S(2)}) collective-permute-start(bf16[10,2,32,256]{3,2,1,0:T(8,128)(2,1)} %bitcast.3), channel_id=1, source_target_pairs={{0,1},{1,0},{2,3},{3,2},{4,5},{5,4},{6,7},{7,6},{8,9},{9,8},{10,11... | collective-permute-start | bytes 983048 | tf_op jit(solution)/shard_map/ppermute | solution.py:411
  0.0 2.6 %collective-permute-start.1 = (bf16[10,2,32,256]{3,2,1,0:T(8,128)(2,1)}, bf16[10,2,32,256]{3,2,1,0:T(8,128)(2,1)S(1)}, u32[]{:S(2)}, u32[]{:S(2)}) collective-permute-start(bf16[10,2,32,256]{3,2,1,0:T(8,128)(2,1)} %bitcast.5), channel_id=1, source_target_pairs={{0,1},{1,0},{2,3},{3,2},{4,5},{5,4},{6,7},{7,6},{8,9},{9,8},{10,11... | collective-permute-start | bytes 983048 | tf_op jit(solution)/shard_map/ppermute | solution.py:411
  0.5 2.1 %collective-permute-start.2 = (bf16[7,2,32,256]{3,2,1,0:T(8,128)(2,1)}, bf16[7,2,32,256]{3,2,1,0:T(8,128)(2,1)S(1)}, u32[]{:S(2)}, u32[]{:S(2)}) collective-permute-start(bf16[7,2,32,256]{3,2,1,0:T(8,128)(2,1)} %bitcast.7), channel_id=1, source_target_pairs={{0,1},{1,0},{2,3},{3,2},{4,5},{5,4},{6,7},{7,6},{8,9},{9,8},{10,11... | collective-permute-start | bytes 688136 | tf_op jit(solution)/shard_map/ppermute | solution.py:411
  3.3 8.7 %collective-permute-start.3 = (bf16[5,2,2,32,256]{4,3,2,1,0:T(8,128)(2,1)S(1)}, bf16[5,2,2,32,256]{4,3,2,1,0:T(8,128)(2,1)S(1)}, u32[]{:S(2)}, u32[]{:S(2)}) collective-permute-start(bf16[5,2,2,32,256]{4,3,2,1,0:T(8,128)(2,1)S(1)} %get-tuple-element.45), channel_id=1, source_target_pairs={{0,4},{1,17},{2,6},{3,19},{4,0},{5,21},{6,2},{7,23},{8,12},{9,25},... | collective-permute-start | bytes 983048 | tf_op jit(solution)/shard_map/ppermute | solution.py:437
  6.7 9.3 %collective-permute-start.4 = (bf16[5,2,2,32,256]{4,3,2,1,0:T(8,128)(2,1)S(1)}, bf16[5,2,2,32,256]{4,3,2,1,0:T(8,128)(2,1)S(1)}, u32[]{:S(2)}, u32[]{:S(2)}) collective-permute-start(bf16[5,2,2,32,256]{4,3,2,1,0:T(8,128)(2,1)S(1)} %get-tuple-element.46), channel_id=1, source_target_pairs={{0,6},{1,25},{2,0},{3,27},{4,2},{5,29},{6,4},{7,31},{8,14},{9,1},{... | collective-permute-start | bytes 983048 | tf_op jit(solution)/shard_map/ppermute | solution.py:437
  7.7 8.3 %collective-permute-start.5 = (bf16[5,2,2,32,256]{4,3,2,1,0:T(8,128)(2,1)S(1)}, bf16[5,2,2,32,256]{4,3,2,1,0:T(8,128)(2,1)S(1)}, u32[]{:S(2)}, u32[]{:S(2)}) collective-permute-start(bf16[5,2,2,32,256]{4,3,2,1,0:T(8,128)(2,1)S(1)} %get-tuple-element.47), channel_id=1, source_target_pairs={{0,2},{1,9},{2,4},{3,11},{4,6},{5,13},{6,0},{7,15},{8,10},{9,17},{... | collective-permute-start | bytes 983048 | tf_op jit(solution)/shard_map/ppermute | solution.py:437
  16.5 16.2 %collective-permute-start.7 = (bf16[3,2,2,4,32,256]{5,4,3,2,1,0:T(8,128)(2,1)S(1)}, bf16[3,2,2,4,32,256]{5,4,3,2,1,0:T(8,128)(2,1)S(1)}, u32[]{:S(2)}, u32[]{:S(2)}) collective-permute-start(bf16[3,2,2,4,32,256]{5,4,3,2,1,0:T(8,128)(2,1)S(1)} %get-tuple-element.48.r0), channel_id=1, source_target_pairs={{0,16},{1,5},{2,18},{3,7},{4,20},{5,1},{6,22},{7,3},{8,24},{9,13},... | collective-permute-start | bytes 2359304 | tf_op jit(solution)/shard_map/ppermute | solution.py:448
  20.5 18.4 %collective-permute-start.8 = (bf16[3,2,2,4,32,256]{5,4,3,2,1,0:T(8,128)(2,1)S(1)}, bf16[3,2,2,4,32,256]{5,4,3,2,1,0:T(8,128)(2,1)S(1)}, u32[]{:S(2)}, u32[]{:S(2)}) collective-permute-start(bf16[3,2,2,4,32,256]{5,4,3,2,1,0:T(8,128)(2,1)S(1)} %get-tuple-element.49), channel_id=1, source_target_pairs={{0,8},{1,3},{2,10},{3,5},{4,12},{5,7},{6,14},{7,1},{8,16},{9,11},{... | collective-permute-start | bytes 2359304 | tf_op jit(solution)/shard_map/ppermute | solution.py:447
  21.5 18.4 %collective-permute-start.6 = (bf16[3,2,2,4,32,256]{5,4,3,2,1,0:T(8,128)(2,1)S(1)}, bf16[3,2,2,4,32,256]{5,4,3,2,1,0:T(8,128)(2,1)S(1)}, u32[]{:S(2)}, u32[]{:S(2)}) collective-permute-start(bf16[3,2,2,4,32,256]{5,4,3,2,1,0:T(8,128)(2,1)S(1)} %get-tuple-element.49), channel_id=1, source_target_pairs={{0,24},{1,7},{2,26},{3,1},{4,28},{5,3},{6,30},{7,5},{8,0},{9,15},{... | collective-permute-start | bytes 2359304 | tf_op jit(solution)/shard_map/ppermute | solution.py:447
  23.7 5.3 %collective-permute-start.10 = (bf16[32,256]{1,0:T(8,128)(2,1)S(1)}, bf16[32,256]{1,0:T(8,128)(2,1)S(1)}, u32[]{:S(2)}, u32[]{:S(2)}) collective-permute-start(bf16[32,256]{1,0:T(8,128)(2,1)S(1)} %get-tuple-element.51), channel_id=1, source_target_pairs={{0,64},{32,96},{64,0},{96,32},{1,65},{33,97},{65,1},{97,33},{2,66}... | collective-permute-start | bytes 49160 | tf_op jit(solution)/shard_map/ppermute | solution.py:438
  26.7 4.9 %collective-permute-start.11 = (bf16[32,256]{1,0:T(8,128)(2,1)S(1)}, bf16[32,256]{1,0:T(8,128)(2,1)S(1)}, u32[]{:S(2)}, u32[]{:S(2)}) collective-permute-start(bf16[32,256]{1,0:T(8,128)(2,1)S(1)} %get-tuple-element.52), channel_id=1, source_target_pairs={{0,96},{32,64},{64,32},{96,0},{1,97},{33,65},{65,33},{97,1},{2,98}... | collective-permute-start | bytes 49160 | tf_op jit(solution)/shard_map/ppermute | solution.py:438
  29.0 3.7 %collective-permute-start.12 = (bf16[32,256]{1,0:T(8,128)(2,1)S(1)}, bf16[32,256]{1,0:T(8,128)(2,1)S(1)}, u32[]{:S(2)}, u32[]{:S(2)}) collective-permute-start(bf16[32,256]{1,0:T(8,128)(2,1)S(1)} %get-tuple-element.53), channel_id=1, source_target_pairs={{0,32},{32,0},{64,96},{96,64},{1,33},{33,1},{65,97},{97,65},{2,34}... | collective-permute-start | bytes 49160 | tf_op jit(solution)/shard_map/ppermute | solution.py:438
  31.7 1.9 %collective-permute-start.9 = (bf16[2,2,2,4,32,256]{5,4,3,2,1,0:T(8,128)(2,1)S(1)}, bf16[2,2,2,4,32,256]{5,4,3,2,1,0:T(8,128)(2,1)S(1)}, u32[]{:S(2)}, u32[]{:S(2)}) collective-permute-start(bf16[2,2,2,4,32,256]{5,4,3,2,1,0:T(8,128)(2,1)S(1)} %get-tuple-element.50.uk), channel_id=1, source_target_pairs={{0,1},{1,0},{2,3},{3,2},{4,5},{5,4},{6,7},{7,6},{8,9},{9,8},{10,11... | collective-permute-start | bytes 1572872 | tf_op jit(solution)/shard_map/ppermute | solution.py:449
  32.8 7.2 %collective-permute-start.13 = (bf16[2,2,2,4,32,256]{5,4,3,2,1,0:T(8,128)(2,1)S(1)}, bf16[2,2,2,4,32,256]{5,4,3,2,1,0:T(8,128)(2,1)S(1)}, u32[]{:S(2)}, u32[]{:S(2)}) collective-permute-start(bf16[2,2,2,4,32,256]{5,4,3,2,1,0:T(8,128)(2,1)S(1)} %shard_map.67), channel_id=1, source_target_pairs={{0,1},{1,0},{2,3},{3,2},{4,5},{5,4},{6,7},{7,6},{8,9},{9,8},{10,11... | collective-permute-start | bytes 1572872 | tf_op jit(solution)/shard_map/ppermute | solution.py:460
  40.2 2.0 %collective-permute-start.17 = (bf16[2,2,2,4,32,256]{5,4,3,2,1,0:T(8,128)(2,1)S(1)}, bf16[2,2,2,4,32,256]{5,4,3,2,1,0:T(8,128)(2,1)S(1)}, u32[]{:S(2)}, u32[]{:S(2)}) collective-permute-start(bf16[2,2,2,4,32,256]{5,4,3,2,1,0:T(8,128)(2,1)S(1)} %get-tuple-element.61), channel_id=1, source_target_pairs={{0,1},{1,0},{2,3},{3,2},{4,5},{5,4},{6,7},{7,6},{8,9},{9,8},{10,11... | collective-permute-start | bytes 1572872 | tf_op jit(solution)/shard_map/ppermute | solution.py:472
  40.8 2.5 %collective-permute-start.14 = (bf16[2,128,512]{2,1,0:T(8,128)(2,1)S(1)}, bf16[2,128,512]{2,1,0:T(8,128)(2,1)S(1)}, u32[]{:S(2)}, u32[]{:S(2)}) collective-permute-start(bf16[2,128,512]{2,1,0:T(8,128)(2,1)S(1)} %get-tuple-element.58.edge0), channel_id=1, source_target_pairs={{0,1},{1,0},{2,3},{3,2},{4,5},{5,4},{6,7},{7,6},{8,9},{9,8},{10,11... | collective-permute-start | bytes 786440 | tf_op jit(solution)/shard_map/ppermute | solution.py:482
  40.9 2.5 %collective-permute-start.15 = (bf16[2,128,512]{2,1,0:T(8,128)(2,1)S(1)}, bf16[2,128,512]{2,1,0:T(8,128)(2,1)S(1)}, u32[]{:S(2)}, u32[]{:S(2)}) collective-permute-start(bf16[2,128,512]{2,1,0:T(8,128)(2,1)S(1)} %get-tuple-element.59.edge1), channel_id=1, source_target_pairs={{0,1},{1,0},{2,3},{3,2},{4,5},{5,4},{6,7},{7,6},{8,9},{9,8},{10,11... | collective-permute-start | bytes 786440 | tf_op jit(solution)/shard_map/ppermute | solution.py:482
  41.4 2.0 %collective-permute-start.16 = (bf16[2,128,512]{2,1,0:T(8,128)(2,1)S(1)}, bf16[2,128,512]{2,1,0:T(8,128)(2,1)S(1)}, u32[]{:S(2)}, u32[]{:S(2)}) collective-permute-start(bf16[2,128,512]{2,1,0:T(8,128)(2,1)S(1)} %get-tuple-element.60.edge2), channel_id=1, source_target_pairs={{0,1},{1,0},{2,3},{3,2},{4,5},{5,4},{6,7},{7,6},{8,9},{9,8},{10,11... | collective-permute-start | bytes 786440 | tf_op jit(solution)/shard_map/ppermute | solution.py:482
  45.0 9.2 %collective-permute-start.18 = (bf16[7,32,256]{2,1,0:T(8,128)(2,1)S(1)}, bf16[7,32,256]{2,1,0:T(8,128)(2,1)S(1)}, u32[]{:S(2)}, u32[]{:S(2)}) collective-permute-start(bf16[7,32,256]{2,1,0:T(8,128)(2,1)S(1)} %get-tuple-element.67), channel_id=1, source_target_pairs={{0,68},{2,70},{4,64},{6,66},{8,76},{10,78},{12,72},{14,74},{16,84}... | collective-permute-start | bytes 344072 | tf_op jit(solution)/shard_map/ppermute | solution.py:501
  50.3 7.0 %collective-permute-start.19 = (bf16[7,32,256]{2,1,0:T(8,128)(2,1)S(1)}, bf16[7,32,256]{2,1,0:T(8,128)(2,1)S(1)}, u32[]{:S(2)}, u32[]{:S(2)}) collective-permute-start(bf16[7,32,256]{2,1,0:T(8,128)(2,1)S(1)} %get-tuple-element.68), channel_id=1, source_target_pairs={{0,38},{2,36},{4,34},{6,32},{8,46},{10,44},{12,42},{14,40},{16,54}... | collective-permute-start | bytes 344072 | tf_op jit(solution)/shard_map/ppermute | solution.py:501
  51.6 6.9 %collective-permute-start.20 = (bf16[7,32,256]{2,1,0:T(8,128)(2,1)S(1)}, bf16[7,32,256]{2,1,0:T(8,128)(2,1)S(1)}, u32[]{:S(2)}, u32[]{:S(2)}) collective-permute-start(bf16[7,32,256]{2,1,0:T(8,128)(2,1)S(1)} %get-tuple-element.69), channel_id=1, source_target_pairs={{0,98},{2,96},{4,102},{6,100},{8,106},{10,104},{12,110},{14,108},{... | collective-permute-start | bytes 344072 | tf_op jit(solution)/shard_map/ppermute | solution.py:501
  58.5 7.4 %collective-permute-start.23 = (bf16[7,32,256]{2,1,0:T(8,128)(2,1)S(1)}, bf16[7,32,256]{2,1,0:T(8,128)(2,1)S(1)}, u32[]{:S(2)}, u32[]{:S(2)}) collective-permute-start(bf16[7,32,256]{2,1,0:T(8,128)(2,1)S(1)} %shard_map.72.g0), channel_id=1, source_target_pairs={{0,64},{32,96},{64,0},{96,32},{1,65},{33,97},{65,1},{97,33},{2,66}... | collective-permute-start | bytes 344072 | tf_op jit(solution)/shard_map/ppermute | solution.py:505
  59.9 6.6 %collective-permute-start.22 = (bf16[7,32,256]{2,1,0:T(8,128)(2,1)S(1)}, bf16[7,32,256]{2,1,0:T(8,128)(2,1)S(1)}, u32[]{:S(2)}, u32[]{:S(2)}) collective-permute-start(bf16[7,32,256]{2,1,0:T(8,128)(2,1)S(1)} %shard_map.72.g0), channel_id=1, source_target_pairs={{0,96},{32,64},{64,32},{96,0},{1,97},{33,65},{65,33},{97,1},{2,98}... | collective-permute-start | bytes 344072 | tf_op jit(solution)/shard_map/ppermute | solution.py:505
  61.5 5.0 %collective-permute-start.21 = (bf16[7,32,256]{2,1,0:T(8,128)(2,1)S(1)}, bf16[7,32,256]{2,1,0:T(8,128)(2,1)S(1)}, u32[]{:S(2)}, u32[]{:S(2)}) collective-permute-start(bf16[7,32,256]{2,1,0:T(8,128)(2,1)S(1)} %shard_map.72.g0), channel_id=1, source_target_pairs={{0,32},{32,0},{64,96},{96,64},{1,33},{33,1},{65,97},{97,65},{2,34}... | collective-permute-start | bytes 344072 | tf_op jit(solution)/shard_map/ppermute | solution.py:505

commit v9 on v8

--- a/solution.py
+++ b/solution.py
@@ -149,7 +149,15 @@
         part[...] = jnp.where((rows < widths[k]) & (cols < widths[k]), dens, 0.0).astype(BF)
 
 
-def pack_other_kernel(low, up, dia, widths, pattern, i0, i1, i2, i3, *outs):
+def pack_other_kernel(low, up, dia, widths, pattern, *refs):
+    given, outs = refs[:4], refs[4:]
+    for half in range(2):
+
+        @pl.when(lax.axis_index("col") == half)
+        def _():
+            for before, out in zip(given, outs):
+                out[:, half] = before[:, half]
+
     pack(low, up, dia, widths, pattern, outs, False)
 
 
@@ -292,6 +300,11 @@
         (kd,) = times(left_of([ukp]), 1, lead)
         put(out0, kd)
         put(out1, wide_rows(lambda h, part: lead[h, part, z].reshape(128, 256)))
+
+    @pl.when(c == 1)
+    def _():
+        out0[...] = edge0[...]
+        out1[...] = edge1[...]
 
 
 def inner_kernel(edge0, edge1, edge2, stay, got_a, got_b, out, early, other, sems):
@@ -429,7 +442,7 @@
     bufs = call(
         pack_other_kernel,
         [shape(5, 2, 2, 32, 256)] * 4,
-        [vm()] * 3 + [sm()] * 2 + [hbm()] * 4,
+        [vm()] * 3 + [sm()] * 2 + [vm()] * 4,
         [vm()] * 4,
         nbytes=4 << 20,
         aliases={5: 0, 6: 1, 7: 2, 8: 3},
@@ -473,7 +486,7 @@
     edge[:2] = call(
         next_kernel,
         [slab] * 2,
-        [hbm()] * 2 + [vm()] * 2 + [hbm()],
+        [vm()] * 4 + [hbm()],
         [vm()] * 2,
         flops=268435456,
         nbytes=2 << 20,

time: 67.6 us -> 67.7 us (level)
  no operation moved by 1% of the time
where the time goes in v9:
time: 67.7 us; the launch traced here: 67.6 us
  waiting for transfers between devices  29.9 us (44%)
  starting transfers between devices  29.7 us (44%)
  Pallas kernels  7.84 us (12%)
    ppermute x3, waiting for transfers between devices, body(): came = {d: lax.ppermute(bufs[d], grid, ring_both(d)) for d in (1, 3, 2)}  7.31 us
    ppermute x3, waiting for transfers between devices, body(): lax.ppermute(slots[d], ('pole', 'row'), pairs_xy(d))  6.88 us
    ppermute x3, starting transfers between devices, body(): lax.ppermute(slots[d], ('pole', 'row'), pairs_xy(d))  6.54 us
    ppermute x2, waiting for transfers between devices, body(): came = {d: lax.ppermute(near, grid, ring_other(d)) for d in (1, 3)}  6.33 us
    ppermute x3, starting transfers between devices, body(): lax.ppermute(parts[d], 'pole', pairs_x(d))  5.64 us
    ppermute x3, starting transfers between devices, body(): came = {d: lax.ppermute(bufs[d], grid, ring_both(d)) for d in (1, 3, 2)}  5.38 us
    ppermute x3, waiting for transfers between devices, body(): lax.ppermute(total, 'pole', pairs_x(d))  4.41 us
    ppermute x1, starting transfers between devices, body(): came[2] = lax.ppermute(far, grid, ring_other(2))  3.96 us
  transfers between devices with their start and end apart: 24, of which 16 were waited for; matrix products, arithmetic and copies ran while one was open for 0% of the time, Pallas kernels for 5%

profile of v9, /device:TPU:0, one launch (start us, length us, event | category | flops | bytes accessed | tf_op | source)
XLA Modules:
  0.0 67.6 jit_solution(4545712747050132224)
XLA Ops:
  0.5 2.0 %shard_map.64 = (bf16[5,2,2,32,256]{4,3,2,1,0:T(8,128)(2,1)S(1)}, bf16[5,2,2,32,256]{4,3,2,1,0:T(8,128)(2,1)S(1)}, bf16[5,2,2,32,256]{4,3,2,1,0:T(8,128)(2,1)S(1...) custom-call(bf16[10,2,32,256]{3,2,1,0:T(8,128)(2,1)} %bitcast.4, ...), custom_call_target="tpu_custom_call" | custom-call | bytes 4194304 | tf_op jit(solution)/shard_map/pallas_call | solution.py:426
  3.4 3.4 %collective-permute-start.3 = (bf16[5,2,2,32,256]{4,3,2,1,0:T(8,128)(2,1)S(1)}, bf16[5,2,2,32,256]{4,3,2,1,0:T(8,128)(2,1)S(1)}, u32[]{:S(2)}, u32[]{:S(2)}) collective-permute-start(bf16[5,2,2,32,256]{4,3,2,1,0:T(8,128)(2,1)S(1)} %get-tuple-element.45), channel_id=1, source_target_pairs={{0,4},{1,17},{2,6},{3,19},{4,0},{5,21},{6,2},{7,23},{8,12},{9,25},... | collective-permute-start | bytes 983048 | tf_op jit(solution)/shard_map/ppermute | solution.py:450
  6.8 1.1 %collective-permute-start.4 = (bf16[5,2,2,32,256]{4,3,2,1,0:T(8,128)(2,1)S(1)}, bf16[5,2,2,32,256]{4,3,2,1,0:T(8,128)(2,1)S(1)}, u32[]{:S(2)}, u32[]{:S(2)}) collective-permute-start(bf16[5,2,2,32,256]{4,3,2,1,0:T(8,128)(2,1)S(1)} %get-tuple-element.46), channel_id=1, source_target_pairs={{0,6},{1,25},{2,0},{3,27},{4,2},{5,29},{6,4},{7,31},{8,14},{9,1},{... | collective-permute-start | bytes 983048 | tf_op jit(solution)/shard_map/ppermute | solution.py:450
  8.8 3.3 %collective-permute-done.3.b2 = bf16[5,2,2,32,256]{4,3,2,1,0:T(8,128)(2,1)S(1)} collective-permute-done((bf16[5,2,2,32,256]{4,3,2,1,0:T(8,128)(2,1)S(1)}, bf16[5,2,2,32,256]{4,3,2,1,0:T(8,128)(2,1)S(1)}, u32[]{:S(2)}, u32[]{:S(2)}) %collective-permute-start.3) | collective-permute-done | bytes 327712 | tf_op jit(solution)/shard_map/ppermute | solution.py:450
  12.1 4.0 %collective-permute-done.4.b3 = bf16[5,2,2,32,256]{4,3,2,1,0:T(8,128)(2,1)S(1)} collective-permute-done((bf16[5,2,2,32,256]{4,3,2,1,0:T(8,128)(2,1)S(1)}, bf16[5,2,2,32,256]{4,3,2,1,0:T(8,128)(2,1)S(1)}, u32[]{:S(2)}, u32[]{:S(2)}) %collective-permute-start.4) | collective-permute-done | bytes 327712 | tf_op jit(solution)/shard_map/ppermute | solution.py:450
  16.6 4.0 %collective-permute-start.7 = (bf16[3,2,2,4,32,256]{5,4,3,2,1,0:T(8,128)(2,1)S(1)}, bf16[3,2,2,4,32,256]{5,4,3,2,1,0:T(8,128)(2,1)S(1)}, u32[]{:S(2)}, u32[]{:S(2)}) collective-permute-start(bf16[3,2,2,4,32,256]{5,4,3,2,1,0:T(8,128)(2,1)S(1)} %get-tuple-element.48.r0), channel_id=1, source_target_pairs={{0,16},{1,5},{2,18},{3,7},{4,20},{5,1},{6,22},{7,3},{8,24},{9,13},... | collective-permute-start | bytes 2359304 | tf_op jit(solution)/shard_map/ppermute | solution.py:461
  21.6 2.2 %collective-permute-start.6 = (bf16[3,2,2,4,32,256]{5,4,3,2,1,0:T(8,128)(2,1)S(1)}, bf16[3,2,2,4,32,256]{5,4,3,2,1,0:T(8,128)(2,1)S(1)}, u32[]{:S(2)}, u32[]{:S(2)}) collective-permute-start(bf16[3,2,2,4,32,256]{5,4,3,2,1,0:T(8,128)(2,1)S(1)} %get-tuple-element.49), channel_id=1, source_target_pairs={{0,24},{1,7},{2,26},{3,1},{4,28},{5,3},{6,30},{7,5},{8,0},{9,15},{... | collective-permute-start | bytes 2359304 | tf_op jit(solution)/shard_map/ppermute | solution.py:460
  23.8 3.0 %collective-permute-start.10 = (bf16[32,256]{1,0:T(8,128)(2,1)S(1)}, bf16[32,256]{1,0:T(8,128)(2,1)S(1)}, u32[]{:S(2)}, u32[]{:S(2)}) collective-permute-start(bf16[32,256]{1,0:T(8,128)(2,1)S(1)} %get-tuple-element.51), channel_id=1, source_target_pairs={{0,64},{32,96},{64,0},{96,32},{1,65},{33,97},{65,1},{97,33},{2,66}... | collective-permute-start | bytes 49160 | tf_op jit(solution)/shard_map/ppermute | solution.py:451
  26.8 1.1 %collective-permute-start.11 = (bf16[32,256]{1,0:T(8,128)(2,1)S(1)}, bf16[32,256]{1,0:T(8,128)(2,1)S(1)}, u32[]{:S(2)}, u32[]{:S(2)}) collective-permute-start(bf16[32,256]{1,0:T(8,128)(2,1)S(1)} %get-tuple-element.52), channel_id=1, source_target_pairs={{0,96},{32,64},{64,32},{96,0},{1,97},{33,65},{65,33},{97,1},{2,98}... | collective-permute-start | bytes 49160 | tf_op jit(solution)/shard_map/ppermute | solution.py:451
  27.9 1.1 %collective-permute-done.10.p2.d1 = bf16[32,256]{1,0:T(8,128)(2,1)S(1)} collective-permute-done((bf16[32,256]{1,0:T(8,128)(2,1)S(1)}, bf16[32,256]{1,0:T(8,128)(2,1)S(1)}, u32[]{:S(2)}, u32[]{:S(2)}) %collective-permute-start.10) | collective-permute-done | bytes 16416 | tf_op jit(solution)/shard_map/ppermute | solution.py:451
  29.0 1.5 %collective-permute-start.12 = (bf16[32,256]{1,0:T(8,128)(2,1)S(1)}, bf16[32,256]{1,0:T(8,128)(2,1)S(1)}, u32[]{:S(2)}, u32[]{:S(2)}) collective-permute-start(bf16[32,256]{1,0:T(8,128)(2,1)S(1)} %get-tuple-element.53), channel_id=1, source_target_pairs={{0,32},{32,0},{64,96},{96,64},{1,33},{33,1},{65,97},{97,65},{2,34}... | collective-permute-start | bytes 49160 | tf_op jit(solution)/shard_map/ppermute | solution.py:451
  30.5 1.2 %collective-permute-done.11.p3.d2 = bf16[32,256]{1,0:T(8,128)(2,1)S(1)} collective-permute-done((bf16[32,256]{1,0:T(8,128)(2,1)S(1)}, bf16[32,256]{1,0:T(8,128)(2,1)S(1)}, u32[]{:S(2)}, u32[]{:S(2)}) %collective-permute-start.11) | collective-permute-done | bytes 16416 | tf_op jit(solution)/shard_map/ppermute | solution.py:451
  33.7 5.3 %collective-permute-done.8.r1 = bf16[3,2,2,4,32,256]{5,4,3,2,1,0:T(8,128)(2,1)S(1)} collective-permute-done((bf16[3,2,2,4,32,256]{5,4,3,2,1,0:T(8,128)(2,1)S(1)}, bf16[3,2,2,4,32,256]{5,4,3,2,1,0:T(8,128)(2,1)S(1)}, u32[]{:S(2)}, u32[]{:S(2)}) %collective-permute-start.8) | collective-permute-done | bytes 786464 | tf_op jit(solution)/shard_map/ppermute | solution.py:460
  38.9 1.1 %collective-permute-done.6.r3 = bf16[3,2,2,4,32,256]{5,4,3,2,1,0:T(8,128)(2,1)S(1)} collective-permute-done((bf16[3,2,2,4,32,256]{5,4,3,2,1,0:T(8,128)(2,1)S(1)}, bf16[3,2,2,4,32,256]{5,4,3,2,1,0:T(8,128)(2,1)S(1)}, u32[]{:S(2)}, u32[]{:S(2)}) %collective-permute-start.6) | collective-permute-done | bytes 786464 | tf_op jit(solution)/shard_map/ppermute | solution.py:460
  42.3 1.1 %shard_map.70 = (bf16[1024,256]{1,0:T(8,128)(2,1)S(1)}, f32[768,256]{1,0:T(8,128)S(1)}, bf16[2,2,4,4,32,256]{5,4,3,2,1,0:T(8,128)(2,1)S(1)}) custom-call(bf16[2,128,512]{2,1,0:T(8,128)(2,1)S(1)} %get-tuple-element.58.edge0, bf16[2,128,512]{2,1,0:T(8,128)(2,1)S(1)} %get-tuple-element.59.edge1, bf16[2,128,512]{2,1,0:T(8,128)(2,1)S(1)} %get-tuple-element.60.edge2, ...), custom_call_target="tpu_custom_call" | custom-call | flops 939524096 | bytes 4194304 | tf_op jit(solution)/shard_map/pallas_call | solution.py:496
  43.4 1.7 %shard_map.71 = (bf16[7,32,256]{2,1,0:T(8,128)(2,1)S(1)}, bf16[7,32,256]{2,1,0:T(8,128)(2,1)S(1)}, bf16[7,32,256]{2,1,0:T(8,128)(2,1)S(1)}, bf16[7,32,256]{2,1,0:T(8,128)(2,1)S(1)}) custom-call(bf16[2,128,512]{2,1,0:T(8,128)(2,1)S(1)} %get-tuple-element.58.edge0, bf16[2,128,512]{2,1,0:T(8,128)(2,1)S(1)} %get-tuple-element.59.edge1, ...), custom_call_target="tpu_custom_call" | custom-call | flops 805306368 | bytes 4194304 | tf_op jit(solution)/shard_map/pallas_call | solution.py:505
  45.1 5.3 %collective-permute-start.18 = (bf16[7,32,256]{2,1,0:T(8,128)(2,1)S(1)}, bf16[7,32,256]{2,1,0:T(8,128)(2,1)S(1)}, u32[]{:S(2)}, u32[]{:S(2)}) collective-permute-start(bf16[7,32,256]{2,1,0:T(8,128)(2,1)S(1)} %get-tuple-element.67), channel_id=1, source_target_pairs={{0,68},{2,70},{4,64},{6,66},{8,76},{10,78},{12,72},{14,74},{16,84}... | collective-permute-start | bytes 344072 | tf_op jit(solution)/shard_map/ppermute | solution.py:514
  50.4 1.2 %collective-permute-start.19 = (bf16[7,32,256]{2,1,0:T(8,128)(2,1)S(1)}, bf16[7,32,256]{2,1,0:T(8,128)(2,1)S(1)}, u32[]{:S(2)}, u32[]{:S(2)}) collective-permute-start(bf16[7,32,256]{2,1,0:T(8,128)(2,1)S(1)} %get-tuple-element.68), channel_id=1, source_target_pairs={{0,38},{2,36},{4,34},{6,32},{8,46},{10,44},{12,42},{14,40},{16,54}... | collective-permute-start | bytes 344072 | tf_op jit(solution)/shard_map/ppermute | solution.py:514
  51.6 2.6 %collective-permute-done.18.a1 = bf16[7,32,256]{2,1,0:T(8,128)(2,1)S(1)} collective-permute-done((bf16[7,32,256]{2,1,0:T(8,128)(2,1)S(1)}, bf16[7,32,256]{2,1,0:T(8,128)(2,1)S(1)}, u32[]{:S(2)}, u32[]{:S(2)}) %collective-permute-start.18) | collective-permute-done | bytes 114720 | tf_op jit(solution)/shard_map/ppermute | solution.py:514
  54.3 3.1 %collective-permute-done.19.a2 = bf16[7,32,256]{2,1,0:T(8,128)(2,1)S(1)} collective-permute-done((bf16[7,32,256]{2,1,0:T(8,128)(2,1)S(1)}, bf16[7,32,256]{2,1,0:T(8,128)(2,1)S(1)}, u32[]{:S(2)}, u32[]{:S(2)}) %collective-permute-start.19) | collective-permute-done | bytes 114720 | tf_op jit(solution)/shard_map/ppermute | solution.py:514
  57.4 1.1 %collective-permute-done.20.a3 = bf16[7,32,256]{2,1,0:T(8,128)(2,1)S(1)} collective-permute-done((bf16[7,32,256]{2,1,0:T(8,128)(2,1)S(1)}, bf16[7,32,256]{2,1,0:T(8,128)(2,1)S(1)}, u32[]{:S(2)}, u32[]{:S(2)}) %collective-permute-start.20) | collective-permute-done | bytes 114720 | tf_op jit(solution)/shard_map/ppermute | solution.py:514
  58.6 1.4 %collective-permute-start.23 = (bf16[7,32,256]{2,1,0:T(8,128)(2,1)S(1)}, bf16[7,32,256]{2,1,0:T(8,128)(2,1)S(1)}, u32[]{:S(2)}, u32[]{:S(2)}) collective-permute-start(bf16[7,32,256]{2,1,0:T(8,128)(2,1)S(1)} %shard_map.72.g0), channel_id=1, source_target_pairs={{0,64},{32,96},{64,0},{96,32},{1,65},{33,97},{65,1},{97,33},{2,66}... | collective-permute-start | bytes 344072 | tf_op jit(solution)/shard_map/ppermute | solution.py:518
  60.0 1.6 %collective-permute-start.22 = (bf16[7,32,256]{2,1,0:T(8,128)(2,1)S(1)}, bf16[7,32,256]{2,1,0:T(8,128)(2,1)S(1)}, u32[]{:S(2)}, u32[]{:S(2)}) collective-permute-start(bf16[7,32,256]{2,1,0:T(8,128)(2,1)S(1)} %shard_map.72.g0), channel_id=1, source_target_pairs={{0,96},{32,64},{64,32},{96,0},{1,97},{33,65},{65,33},{97,1},{2,98}... | collective-permute-start | bytes 344072 | tf_op jit(solution)/shard_map/ppermute | solution.py:518
  62.2 3.8 %collective-permute-done.23.g2 = bf16[7,32,256]{2,1,0:T(8,128)(2,1)S(1)} collective-permute-done((bf16[7,32,256]{2,1,0:T(8,128)(2,1)S(1)}, bf16[7,32,256]{2,1,0:T(8,128)(2,1)S(1)}, u32[]{:S(2)}, u32[]{:S(2)}) %collective-permute-start.23) | collective-permute-done | bytes 114720 | tf_op jit(solution)/shard_map/ppermute | solution.py:518
  (34 shorter events, 10.4 us)
Async XLA Ops:
  0.0 2.6 %collective-permute-start = (bf16[10,2,32,256]{3,2,1,0:T(8,128)(2,1)}, bf16[10,2,32,256]{3,2,1,0:T(8,128)(2,1)S(1)}, u32[]{:S(2)}, u32[]{:S(2)}) collective-permute-start(bf16[10,2,32,256]{3,2,1,0:T(8,128)(2,1)} %bitcast.3), channel_id=1, source_target_pairs={{0,1},{1,0},{2,3},{3,2},{4,5},{5,4},{6,7},{7,6},{8,9},{9,8},{10,11... | collective-permute-start | bytes 983048 | tf_op jit(solution)/shard_map/ppermute | solution.py:424
  0.0 2.6 %collective-permute-start.1 = (bf16[10,2,32,256]{3,2,1,0:T(8,128)(2,1)}, bf16[10,2,32,256]{3,2,1,0:T(8,128)(2,1)S(1)}, u32[]{:S(2)}, u32[]{:S(2)}) collective-permute-start(bf16[10,2,32,256]{3,2,1,0:T(8,128)(2,1)} %bitcast.5), channel_id=1, source_target_pairs={{0,1},{1,0},{2,3},{3,2},{4,5},{5,4},{6,7},{7,6},{8,9},{9,8},{10,11... | collective-permute-start | bytes 983048 | tf_op jit(solution)/shard_map/ppermute | solution.py:424
  0.5 2.1 %collective-permute-start.2 = (bf16[7,2,32,256]{3,2,1,0:T(8,128)(2,1)}, bf16[7,2,32,256]{3,2,1,0:T(8,128)(2,1)S(1)}, u32[]{:S(2)}, u32[]{:S(2)}) collective-permute-start(bf16[7,2,32,256]{3,2,1,0:T(8,128)(2,1)} %bitcast.7), channel_id=1, source_target_pairs={{0,1},{1,0},{2,3},{3,2},{4,5},{5,4},{6,7},{7,6},{8,9},{9,8},{10,11... | collective-permute-start | bytes 688136 | tf_op jit(solution)/shard_map/ppermute | solution.py:424
  3.4 8.7 %collective-permute-start.3 = (bf16[5,2,2,32,256]{4,3,2,1,0:T(8,128)(2,1)S(1)}, bf16[5,2,2,32,256]{4,3,2,1,0:T(8,128)(2,1)S(1)}, u32[]{:S(2)}, u32[]{:S(2)}) collective-permute-start(bf16[5,2,2,32,256]{4,3,2,1,0:T(8,128)(2,1)S(1)} %get-tuple-element.45), channel_id=1, source_target_pairs={{0,4},{1,17},{2,6},{3,19},{4,0},{5,21},{6,2},{7,23},{8,12},{9,25},... | collective-permute-start | bytes 983048 | tf_op jit(solution)/shard_map/ppermute | solution.py:450
  6.8 9.3 %collective-permute-start.4 = (bf16[5,2,2,32,256]{4,3,2,1,0:T(8,128)(2,1)S(1)}, bf16[5,2,2,32,256]{4,3,2,1,0:T(8,128)(2,1)S(1)}, u32[]{:S(2)}, u32[]{:S(2)}) collective-permute-start(bf16[5,2,2,32,256]{4,3,2,1,0:T(8,128)(2,1)S(1)} %get-tuple-element.46), channel_id=1, source_target_pairs={{0,6},{1,25},{2,0},{3,27},{4,2},{5,29},{6,4},{7,31},{8,14},{9,1},{... | collective-permute-start | bytes 983048 | tf_op jit(solution)/shard_map/ppermute | solution.py:450
  7.8 8.3 %collective-permute-start.5 = (bf16[5,2,2,32,256]{4,3,2,1,0:T(8,128)(2,1)S(1)}, bf16[5,2,2,32,256]{4,3,2,1,0:T(8,128)(2,1)S(1)}, u32[]{:S(2)}, u32[]{:S(2)}) collective-permute-start(bf16[5,2,2,32,256]{4,3,2,1,0:T(8,128)(2,1)S(1)} %get-tuple-element.47), channel_id=1, source_target_pairs={{0,2},{1,9},{2,4},{3,11},{4,6},{5,13},{6,0},{7,15},{8,10},{9,17},{... | collective-permute-start | bytes 983048 | tf_op jit(solution)/shard_map/ppermute | solution.py:450
  16.6 16.2 %collective-permute-start.7 = (bf16[3,2,2,4,32,256]{5,4,3,2,1,0:T(8,128)(2,1)S(1)}, bf16[3,2,2,4,32,256]{5,4,3,2,1,0:T(8,128)(2,1)S(1)}, u32[]{:S(2)}, u32[]{:S(2)}) collective-permute-start(bf16[3,2,2,4,32,256]{5,4,3,2,1,0:T(8,128)(2,1)S(1)} %get-tuple-element.48.r0), channel_id=1, source_target_pairs={{0,16},{1,5},{2,18},{3,7},{4,20},{5,1},{6,22},{7,3},{8,24},{9,13},... | collective-permute-start | bytes 2359304 | tf_op jit(solution)/shard_map/ppermute | solution.py:461
  20.5 18.4 %collective-permute-start.8 = (bf16[3,2,2,4,32,256]{5,4,3,2,1,0:T(8,128)(2,1)S(1)}, bf16[3,2,2,4,32,256]{5,4,3,2,1,0:T(8,128)(2,1)S(1)}, u32[]{:S(2)}, u32[]{:S(2)}) collective-permute-start(bf16[3,2,2,4,32,256]{5,4,3,2,1,0:T(8,128)(2,1)S(1)} %get-tuple-element.49), channel_id=1, source_target_pairs={{0,8},{1,3},{2,10},{3,5},{4,12},{5,7},{6,14},{7,1},{8,16},{9,11},{... | collective-permute-start | bytes 2359304 | tf_op jit(solution)/shard_map/ppermute | solution.py:460
  21.6 18.4 %collective-permute-start.6 = (bf16[3,2,2,4,32,256]{5,4,3,2,1,0:T(8,128)(2,1)S(1)}, bf16[3,2,2,4,32,256]{5,4,3,2,1,0:T(8,128)(2,1)S(1)}, u32[]{:S(2)}, u32[]{:S(2)}) collective-permute-start(bf16[3,2,2,4,32,256]{5,4,3,2,1,0:T(8,128)(2,1)S(1)} %get-tuple-element.49), channel_id=1, source_target_pairs={{0,24},{1,7},{2,26},{3,1},{4,28},{5,3},{6,30},{7,5},{8,0},{9,15},{... | collective-permute-start | bytes 2359304 | tf_op jit(solution)/shard_map/ppermute | solution.py:460
  23.8 5.3 %collective-permute-start.10 = (bf16[32,256]{1,0:T(8,128)(2,1)S(1)}, bf16[32,256]{1,0:T(8,128)(2,1)S(1)}, u32[]{:S(2)}, u32[]{:S(2)}) collective-permute-start(bf16[32,256]{1,0:T(8,128)(2,1)S(1)} %get-tuple-element.51), channel_id=1, source_target_pairs={{0,64},{32,96},{64,0},{96,32},{1,65},{33,97},{65,1},{97,33},{2,66}... | collective-permute-start | bytes 49160 | tf_op jit(solution)/shard_map/ppermute | solution.py:451
  26.8 4.9 %collective-permute-start.11 = (bf16[32,256]{1,0:T(8,128)(2,1)S(1)}, bf16[32,256]{1,0:T(8,128)(2,1)S(1)}, u32[]{:S(2)}, u32[]{:S(2)}) collective-permute-start(bf16[32,256]{1,0:T(8,128)(2,1)S(1)} %get-tuple-element.52), channel_id=1, source_target_pairs={{0,96},{32,64},{64,32},{96,0},{1,97},{33,65},{65,33},{97,1},{2,98}... | collective-permute-start | bytes 49160 | tf_op jit(solution)/shard_map/ppermute | solution.py:451
  29.0 3.7 %collective-permute-start.12 = (bf16[32,256]{1,0:T(8,128)(2,1)S(1)}, bf16[32,256]{1,0:T(8,128)(2,1)S(1)}, u32[]{:S(2)}, u32[]{:S(2)}) collective-permute-start(bf16[32,256]{1,0:T(8,128)(2,1)S(1)} %get-tuple-element.53), channel_id=1, source_target_pairs={{0,32},{32,0},{64,96},{96,64},{1,33},{33,1},{65,97},{97,65},{2,34}... | collective-permute-start | bytes 49160 | tf_op jit(solution)/shard_map/ppermute | solution.py:451
  31.8 1.9 %collective-permute-start.9 = (bf16[2,2,2,4,32,256]{5,4,3,2,1,0:T(8,128)(2,1)S(1)}, bf16[2,2,2,4,32,256]{5,4,3,2,1,0:T(8,128)(2,1)S(1)}, u32[]{:S(2)}, u32[]{:S(2)}) collective-permute-start(bf16[2,2,2,4,32,256]{5,4,3,2,1,0:T(8,128)(2,1)S(1)} %get-tuple-element.50.uk), channel_id=1, source_target_pairs={{0,1},{1,0},{2,3},{3,2},{4,5},{5,4},{6,7},{7,6},{8,9},{9,8},{10,11... | collective-permute-start | bytes 1572872 | tf_op jit(solution)/shard_map/ppermute | solution.py:462
  32.8 7.2 %collective-permute-start.13 = (bf16[2,2,2,4,32,256]{5,4,3,2,1,0:T(8,128)(2,1)S(1)}, bf16[2,2,2,4,32,256]{5,4,3,2,1,0:T(8,128)(2,1)S(1)}, u32[]{:S(2)}, u32[]{:S(2)}) collective-permute-start(bf16[2,2,2,4,32,256]{5,4,3,2,1,0:T(8,128)(2,1)S(1)} %shard_map.67), channel_id=1, source_target_pairs={{0,1},{1,0},{2,3},{3,2},{4,5},{5,4},{6,7},{7,6},{8,9},{9,8},{10,11... | collective-permute-start | bytes 1572872 | tf_op jit(solution)/shard_map/ppermute | solution.py:473
  40.3 2.0 %collective-permute-start.17 = (bf16[2,2,2,4,32,256]{5,4,3,2,1,0:T(8,128)(2,1)S(1)}, bf16[2,2,2,4,32,256]{5,4,3,2,1,0:T(8,128)(2,1)S(1)}, u32[]{:S(2)}, u32[]{:S(2)}) collective-permute-start(bf16[2,2,2,4,32,256]{5,4,3,2,1,0:T(8,128)(2,1)S(1)} %get-tuple-element.61), channel_id=1, source_target_pairs={{0,1},{1,0},{2,3},{3,2},{4,5},{5,4},{6,7},{7,6},{8,9},{9,8},{10,11... | collective-permute-start | bytes 1572872 | tf_op jit(solution)/shard_map/ppermute | solution.py:485
  40.8 2.5 %collective-permute-start.14 = (bf16[2,128,512]{2,1,0:T(8,128)(2,1)S(1)}, bf16[2,128,512]{2,1,0:T(8,128)(2,1)S(1)}, u32[]{:S(2)}, u32[]{:S(2)}) collective-permute-start(bf16[2,128,512]{2,1,0:T(8,128)(2,1)S(1)} %get-tuple-element.58.edge0), channel_id=1, source_target_pairs={{0,1},{1,0},{2,3},{3,2},{4,5},{5,4},{6,7},{7,6},{8,9},{9,8},{10,11... | collective-permute-start | bytes 786440 | tf_op jit(solution)/shard_map/ppermute | solution.py:495
  41.0 2.4 %collective-permute-start.15 = (bf16[2,128,512]{2,1,0:T(8,128)(2,1)S(1)}, bf16[2,128,512]{2,1,0:T(8,128)(2,1)S(1)}, u32[]{:S(2)}, u32[]{:S(2)}) collective-permute-start(bf16[2,128,512]{2,1,0:T(8,128)(2,1)S(1)} %get-tuple-element.59.edge1), channel_id=1, source_target_pairs={{0,1},{1,0},{2,3},{3,2},{4,5},{5,4},{6,7},{7,6},{8,9},{9,8},{10,11... | collective-permute-start | bytes 786440 | tf_op jit(solution)/shard_map/ppermute | solution.py:495
  41.4 2.0 %collective-permute-start.16 = (bf16[2,128,512]{2,1,0:T(8,128)(2,1)S(1)}, bf16[2,128,512]{2,1,0:T(8,128)(2,1)S(1)}, u32[]{:S(2)}, u32[]{:S(2)}) collective-permute-start(bf16[2,128,512]{2,1,0:T(8,128)(2,1)S(1)} %get-tuple-element.60.edge2), channel_id=1, source_target_pairs={{0,1},{1,0},{2,3},{3,2},{4,5},{5,4},{6,7},{7,6},{8,9},{9,8},{10,11... | collective-permute-start | bytes 786440 | tf_op jit(solution)/shard_map/ppermute | solution.py:495
  45.1 9.2 %collective-permute-start.18 = (bf16[7,32,256]{2,1,0:T(8,128)(2,1)S(1)}, bf16[7,32,256]{2,1,0:T(8,128)(2,1)S(1)}, u32[]{:S(2)}, u32[]{:S(2)}) collective-permute-start(bf16[7,32,256]{2,1,0:T(8,128)(2,1)S(1)} %get-tuple-element.67), channel_id=1, source_target_pairs={{0,68},{2,70},{4,64},{6,66},{8,76},{10,78},{12,72},{14,74},{16,84}... | collective-permute-start | bytes 344072 | tf_op jit(solution)/shard_map/ppermute | solution.py:514
  50.4 7.0 %collective-permute-start.19 = (bf16[7,32,256]{2,1,0:T(8,128)(2,1)S(1)}, bf16[7,32,256]{2,1,0:T(8,128)(2,1)S(1)}, u32[]{:S(2)}, u32[]{:S(2)}) collective-permute-start(bf16[7,32,256]{2,1,0:T(8,128)(2,1)S(1)} %get-tuple-element.68), channel_id=1, source_target_pairs={{0,38},{2,36},{4,34},{6,32},{8,46},{10,44},{12,42},{14,40},{16,54}... | collective-permute-start | bytes 344072 | tf_op jit(solution)/shard_map/ppermute | solution.py:514
  51.6 6.9 %collective-permute-start.20 = (bf16[7,32,256]{2,1,0:T(8,128)(2,1)S(1)}, bf16[7,32,256]{2,1,0:T(8,128)(2,1)S(1)}, u32[]{:S(2)}, u32[]{:S(2)}) collective-permute-start(bf16[7,32,256]{2,1,0:T(8,128)(2,1)S(1)} %get-tuple-element.69), channel_id=1, source_target_pairs={{0,98},{2,96},{4,102},{6,100},{8,106},{10,104},{12,110},{14,108},{... | collective-permute-start | bytes 344072 | tf_op jit(solution)/shard_map/ppermute | solution.py:514
  58.6 7.4 %collective-permute-start.23 = (bf16[7,32,256]{2,1,0:T(8,128)(2,1)S(1)}, bf16[7,32,256]{2,1,0:T(8,128)(2,1)S(1)}, u32[]{:S(2)}, u32[]{:S(2)}) collective-permute-start(bf16[7,32,256]{2,1,0:T(8,128)(2,1)S(1)} %shard_map.72.g0), channel_id=1, source_target_pairs={{0,64},{32,96},{64,0},{96,32},{1,65},{33,97},{65,1},{97,33},{2,66}... | collective-permute-start | bytes 344072 | tf_op jit(solution)/shard_map/ppermute | solution.py:518
  60.0 6.6 %collective-permute-start.22 = (bf16[7,32,256]{2,1,0:T(8,128)(2,1)S(1)}, bf16[7,32,256]{2,1,0:T(8,128)(2,1)S(1)}, u32[]{:S(2)}, u32[]{:S(2)}) collective-permute-start(bf16[7,32,256]{2,1,0:T(8,128)(2,1)S(1)} %shard_map.72.g0), channel_id=1, source_target_pairs={{0,96},{32,64},{64,32},{96,0},{1,97},{33,65},{65,33},{97,1},{2,98}... | collective-permute-start | bytes 344072 | tf_op jit(solution)/shard_map/ppermute | solution.py:518
  61.6 5.0 %collective-permute-start.21 = (bf16[7,32,256]{2,1,0:T(8,128)(2,1)S(1)}, bf16[7,32,256]{2,1,0:T(8,128)(2,1)S(1)}, u32[]{:S(2)}, u32[]{:S(2)}) collective-permute-start(bf16[7,32,256]{2,1,0:T(8,128)(2,1)S(1)} %shard_map.72.g0), channel_id=1, source_target_pairs={{0,32},{32,0},{64,96},{96,64},{1,33},{33,1},{65,97},{97,65},{2,34}... | collective-permute-start | bytes 344072 | tf_op jit(solution)/shard_map/ppermute | solution.py:518

commit v10 on v9

--- a/solution.py
+++ b/solution.py
@@ -231,42 +231,37 @@
 
 
 def early_kernel(r0, r2, p2, p3, p1, go, sems):
-    x, z, y, c = place()
-    part_of_last(((0, r0), (2, r2)), go, sems)
-
-
-def part_of_last(given, go, sems):
-    x, z, y, c = place()
-
-    @pl.when(c == 0)
-    def _():
-        copies = []
-        for d, buf in given:
-            at = lax.div(lax.rem(z + 4 - d, 4), 2)
-            copies.append((buf.at[pl.ds(1, 2), 1], go.at[:, :, at]))
-        run_copies(copies, sems)
-
-    @pl.when(c == 1)
-    def _():
-        copies = []
-        for d, buf in given:
-            at = lax.div(lax.rem(y + 4 - d, 4), 2)
-            copies.append((buf.at[2], go.at[:, :, at]))
-        run_copies(copies, sems)
+    zero, one = part_of_last(((0, r0), (2, r2)), go)
+    for half, copies in enumerate((zero, one)):
+
+        @pl.when(lax.axis_index("col") == half)
+        def _():
+            run_copies(copies, sems)
+
+
+def part_of_last(given, go):
+    x, z, y, c = place()
+    zero, one = [], []
+    for d, buf in given:
+        at = lax.div(lax.rem(z + 4 - d, 4), 2)
+        zero.append((buf.at[pl.ds(1, 2), 1], go.at[:, :, at]))
+        at = lax.div(lax.rem(y + 4 - d, 4), 2)
+        one.append((buf.at[2], go.at[:, :, at]))
+    return zero, one
 
 
 def first_kernel(
     r0, r3, r2, r1, uks, before, out0, out1, out2, stay, go, lead, right, sems
 ):
     x, z, y, c = place()
-    part_of_last(((1, r1), (3, r3)), go, sems)
+    zero, one = part_of_last(((1, r1), (3, r3)), go)
 
     def rows_of(block):
         return wide_rows(lambda h, part: right[block, h, part, z].reshape(128, 256))
 
     @pl.when(c == 0)
     def _():
-        copies = []
+        copies = list(zero)
         for d, buf in enumerate((r0, r1, r2, r3)):
             at = lax.rem(z + 4 - d, 4)
             copies.append((buf.at[pl.ds(1, 2), 0], stay.at[:, :, at]))
@@ -275,12 +270,18 @@
 
     @pl.when(c == 1)
     def _():
-        copies = []
+        copies, late = [], list(one)
         for d, buf in enumerate((r0, r1, r2, r3)):
             at = lax.rem(y + 4 - d, 4)
             copies.append((buf.at[pl.ds(0, 2)], right.at[:, :, :, :, at]))
-            copies.append((buf.at[2], stay.at[:, :, :, at]))
-        run_copies(copies, sems)
+            late.append((buf.at[2], stay.at[:, :, :, at]))
+        made = [
+            pltpu.make_async_copy(s, t, sems.at[i]) for i, (s, t) in enumerate(copies + late)
+        ]
+        for m in made:
+            m.start()
+        for m in made[: len(copies)]:
+            m.wait()
         ukp = wide_rows(lambda h, part: uks[0, h, part].reshape(128, 256))
         uk0 = wide_rows(lambda h, part: uks[1, h, part].reshape(128, 256))
         (kv,) = times(left_of([ukp]), 1, right[1])
@@ -289,6 +290,8 @@
         put(out0, xp0, -1)
         put(out1, rows_of(0))
         put(out2, xk0, -1)
+        for m in made[len(copies) :]:
+            m.wait()
 
 
 def next_kernel(edge0, edge1, lead, uk, after, out0, out1):
@@ -478,7 +481,7 @@
         [slab] * 3 + [whole, half, whole],
         [hbm()] * 4 + [vm()] + [hbm()],
         [vm()] * 3 + [hbm()] * 3,
-        [pltpu.VMEM((2, 2, 2, 4, 4, 32, 256), BF), pltpu.SemaphoreType.DMA((8,))],
+        [pltpu.VMEM((2, 2, 2, 4, 4, 32, 256), BF), pltpu.SemaphoreType.DMA((10,))],
         flops=805306368,
         nbytes=4 << 20,
     )(*blocks, uks, got_early)

time: 67.7 us -> 67.7 us (level)
  no operation moved by 1% of the time
where the time goes in v10:
time: 67.7 us; the launch traced here: 67.6 us
  waiting for transfers between devices  29.9 us (44%)
  starting transfers between devices  29.7 us (44%)
  Pallas kernels  7.84 us (12%)
    ppermute x3, waiting for transfers between devices, body(): came = {d: lax.ppermute(bufs[d], grid, ring_both(d)) for d in (1, 3, 2)}  7.31 us
    ppermute x3, waiting for transfers between devices, body(): lax.ppermute(slots[d], ('pole', 'row'), pairs_xy(d))  6.88 us
    ppermute x3, starting transfers between devices, body(): lax.ppermute(slots[d], ('pole', 'row'), pairs_xy(d))  6.55 us
    ppermute x2, waiting for transfers between devices, body(): came = {d: lax.ppermute(near, grid, ring_other(d)) for d in (1, 3)}  6.33 us
    ppermute x3, starting transfers between devices, body(): lax.ppermute(parts[d], 'pole', pairs_x(d))  5.64 us
    ppermute x3, starting transfers between devices, body(): came = {d: lax.ppermute(bufs[d], grid, ring_both(d)) for d in (1, 3, 2)}  5.38 us
    ppermute x3, waiting for transfers between devices, body(): lax.ppermute(total, 'pole', pairs_x(d))  4.42 us
    ppermute x1, starting transfers between devices, body(): came[2] = lax.ppermute(far, grid, ring_other(2))  3.96 us
  transfers between devices with their start and end apart: 24, of which 16 were waited for; matrix products, arithmetic and copies ran while one was open for 0% of the time, Pallas kernels for 5%

profile of v10, /device:TPU:0, one launch (start us, length us, event | category | flops | bytes accessed | tf_op | source)
XLA Modules:
  0.0 67.6 jit_solution(12429483980527167956)
XLA Ops:
  0.5 2.0 %shard_map.64 = (bf16[5,2,2,32,256]{4,3,2,1,0:T(8,128)(2,1)S(1)}, bf16[5,2,2,32,256]{4,3,2,1,0:T(8,128)(2,1)S(1)}, bf16[5,2,2,32,256]{4,3,2,1,0:T(8,128)(2,1)S(1...) custom-call(bf16[10,2,32,256]{3,2,1,0:T(8,128)(2,1)} %bitcast.4, ...), custom_call_target="tpu_custom_call" | custom-call | bytes 4194304 | tf_op jit(solution)/shard_map/pallas_call | solution.py:429
  3.4 3.4 %collective-permute-start.3 = (bf16[5,2,2,32,256]{4,3,2,1,0:T(8,128)(2,1)S(1)}, bf16[5,2,2,32,256]{4,3,2,1,0:T(8,128)(2,1)S(1)}, u32[]{:S(2)}, u32[]{:S(2)}) collective-permute-start(bf16[5,2,2,32,256]{4,3,2,1,0:T(8,128)(2,1)S(1)} %get-tuple-element.45), channel_id=1, source_target_pairs={{0,4},{1,17},{2,6},{3,19},{4,0},{5,21},{6,2},{7,23},{8,12},{9,25},... | collective-permute-start | bytes 983048 | tf_op jit(solution)/shard_map/ppermute | solution.py:453
  6.8 1.1 %collective-permute-start.4 = (bf16[5,2,2,32,256]{4,3,2,1,0:T(8,128)(2,1)S(1)}, bf16[5,2,2,32,256]{4,3,2,1,0:T(8,128)(2,1)S(1)}, u32[]{:S(2)}, u32[]{:S(2)}) collective-permute-start(bf16[5,2,2,32,256]{4,3,2,1,0:T(8,128)(2,1)S(1)} %get-tuple-element.46), channel_id=1, source_target_pairs={{0,6},{1,25},{2,0},{3,27},{4,2},{5,29},{6,4},{7,31},{8,14},{9,1},{... | collective-permute-start | bytes 983048 | tf_op jit(solution)/shard_map/ppermute | solution.py:453
  8.8 3.3 %collective-permute-done.3.b2 = bf16[5,2,2,32,256]{4,3,2,1,0:T(8,128)(2,1)S(1)} collective-permute-done((bf16[5,2,2,32,256]{4,3,2,1,0:T(8,128)(2,1)S(1)}, bf16[5,2,2,32,256]{4,3,2,1,0:T(8,128)(2,1)S(1)}, u32[]{:S(2)}, u32[]{:S(2)}) %collective-permute-start.3) | collective-permute-done | bytes 327712 | tf_op jit(solution)/shard_map/ppermute | solution.py:453
  12.1 4.0 %collective-permute-done.4.b3 = bf16[5,2,2,32,256]{4,3,2,1,0:T(8,128)(2,1)S(1)} collective-permute-done((bf16[5,2,2,32,256]{4,3,2,1,0:T(8,128)(2,1)S(1)}, bf16[5,2,2,32,256]{4,3,2,1,0:T(8,128)(2,1)S(1)}, u32[]{:S(2)}, u32[]{:S(2)}) %collective-permute-start.4) | collective-permute-done | bytes 327712 | tf_op jit(solution)/shard_map/ppermute | solution.py:453
  16.6 4.0 %collective-permute-start.7 = (bf16[3,2,2,4,32,256]{5,4,3,2,1,0:T(8,128)(2,1)S(1)}, bf16[3,2,2,4,32,256]{5,4,3,2,1,0:T(8,128)(2,1)S(1)}, u32[]{:S(2)}, u32[]{:S(2)}) collective-permute-start(bf16[3,2,2,4,32,256]{5,4,3,2,1,0:T(8,128)(2,1)S(1)} %get-tuple-element.48.r0), channel_id=1, source_target_pairs={{0,16},{1,5},{2,18},{3,7},{4,20},{5,1},{6,22},{7,3},{8,24},{9,13},... | collective-permute-start | bytes 2359304 | tf_op jit(solution)/shard_map/ppermute | solution.py:464
  21.6 2.2 %collective-permute-start.6 = (bf16[3,2,2,4,32,256]{5,4,3,2,1,0:T(8,128)(2,1)S(1)}, bf16[3,2,2,4,32,256]{5,4,3,2,1,0:T(8,128)(2,1)S(1)}, u32[]{:S(2)}, u32[]{:S(2)}) collective-permute-start(bf16[3,2,2,4,32,256]{5,4,3,2,1,0:T(8,128)(2,1)S(1)} %get-tuple-element.49), channel_id=1, source_target_pairs={{0,24},{1,7},{2,26},{3,1},{4,28},{5,3},{6,30},{7,5},{8,0},{9,15},{... | collective-permute-start | bytes 2359304 | tf_op jit(solution)/shard_map/ppermute | solution.py:463
  23.8 3.0 %collective-permute-start.10 = (bf16[32,256]{1,0:T(8,128)(2,1)S(1)}, bf16[32,256]{1,0:T(8,128)(2,1)S(1)}, u32[]{:S(2)}, u32[]{:S(2)}) collective-permute-start(bf16[32,256]{1,0:T(8,128)(2,1)S(1)} %get-tuple-element.51), channel_id=1, source_target_pairs={{0,64},{32,96},{64,0},{96,32},{1,65},{33,97},{65,1},{97,33},{2,66}... | collective-permute-start | bytes 49160 | tf_op jit(solution)/shard_map/ppermute | solution.py:454
  26.8 1.1 %collective-permute-start.11 = (bf16[32,256]{1,0:T(8,128)(2,1)S(1)}, bf16[32,256]{1,0:T(8,128)(2,1)S(1)}, u32[]{:S(2)}, u32[]{:S(2)}) collective-permute-start(bf16[32,256]{1,0:T(8,128)(2,1)S(1)} %get-tuple-element.52), channel_id=1, source_target_pairs={{0,96},{32,64},{64,32},{96,0},{1,97},{33,65},{65,33},{97,1},{2,98}... | collective-permute-start | bytes 49160 | tf_op jit(solution)/shard_map/ppermute | solution.py:454
  27.9 1.1 %collective-permute-done.10.p2.d1 = bf16[32,256]{1,0:T(8,128)(2,1)S(1)} collective-permute-done((bf16[32,256]{1,0:T(8,128)(2,1)S(1)}, bf16[32,256]{1,0:T(8,128)(2,1)S(1)}, u32[]{:S(2)}, u32[]{:S(2)}) %collective-permute-start.10) | collective-permute-done | bytes 16416 | tf_op jit(solution)/shard_map/ppermute | solution.py:454
  29.0 1.5 %collective-permute-start.12 = (bf16[32,256]{1,0:T(8,128)(2,1)S(1)}, bf16[32,256]{1,0:T(8,128)(2,1)S(1)}, u32[]{:S(2)}, u32[]{:S(2)}) collective-permute-start(bf16[32,256]{1,0:T(8,128)(2,1)S(1)} %get-tuple-element.53), channel_id=1, source_target_pairs={{0,32},{32,0},{64,96},{96,64},{1,33},{33,1},{65,97},{97,65},{2,34}... | collective-permute-start | bytes 49160 | tf_op jit(solution)/shard_map/ppermute | solution.py:454
  30.5 1.2 %collective-permute-done.11.p3.d2 = bf16[32,256]{1,0:T(8,128)(2,1)S(1)} collective-permute-done((bf16[32,256]{1,0:T(8,128)(2,1)S(1)}, bf16[32,256]{1,0:T(8,128)(2,1)S(1)}, u32[]{:S(2)}, u32[]{:S(2)}) %collective-permute-start.11) | collective-permute-done | bytes 16416 | tf_op jit(solution)/shard_map/ppermute | solution.py:454
  33.7 5.3 %collective-permute-done.8.r1 = bf16[3,2,2,4,32,256]{5,4,3,2,1,0:T(8,128)(2,1)S(1)} collective-permute-done((bf16[3,2,2,4,32,256]{5,4,3,2,1,0:T(8,128)(2,1)S(1)}, bf16[3,2,2,4,32,256]{5,4,3,2,1,0:T(8,128)(2,1)S(1)}, u32[]{:S(2)}, u32[]{:S(2)}) %collective-permute-start.8) | collective-permute-done | bytes 786464 | tf_op jit(solution)/shard_map/ppermute | solution.py:463
  38.9 1.1 %collective-permute-done.6.r3 = bf16[3,2,2,4,32,256]{5,4,3,2,1,0:T(8,128)(2,1)S(1)} collective-permute-done((bf16[3,2,2,4,32,256]{5,4,3,2,1,0:T(8,128)(2,1)S(1)}, bf16[3,2,2,4,32,256]{5,4,3,2,1,0:T(8,128)(2,1)S(1)}, u32[]{:S(2)}, u32[]{:S(2)}) %collective-permute-start.6) | collective-permute-done | bytes 786464 | tf_op jit(solution)/shard_map/ppermute | solution.py:463
  42.3 1.1 %shard_map.70 = (bf16[1024,256]{1,0:T(8,128)(2,1)S(1)}, f32[768,256]{1,0:T(8,128)S(1)}, bf16[2,2,4,4,32,256]{5,4,3,2,1,0:T(8,128)(2,1)S(1)}) custom-call(bf16[2,128,512]{2,1,0:T(8,128)(2,1)S(1)} %get-tuple-element.58.edge0, bf16[2,128,512]{2,1,0:T(8,128)(2,1)S(1)} %get-tuple-element.59.edge1, bf16[2,128,512]{2,1,0:T(8,128)(2,1)S(1)} %get-tuple-element.60.edge2, ...), custom_call_target="tpu_custom_call" | custom-call | flops 939524096 | bytes 4194304 | tf_op jit(solution)/shard_map/pallas_call | solution.py:499
  43.4 1.7 %shard_map.71 = (bf16[7,32,256]{2,1,0:T(8,128)(2,1)S(1)}, bf16[7,32,256]{2,1,0:T(8,128)(2,1)S(1)}, bf16[7,32,256]{2,1,0:T(8,128)(2,1)S(1)}, bf16[7,32,256]{2,1,0:T(8,128)(2,1)S(1)}) custom-call(bf16[2,128,512]{2,1,0:T(8,128)(2,1)S(1)} %get-tuple-element.58.edge0, bf16[2,128,512]{2,1,0:T(8,128)(2,1)S(1)} %get-tuple-element.59.edge1, ...), custom_call_target="tpu_custom_call" | custom-call | flops 805306368 | bytes 4194304 | tf_op jit(solution)/shard_map/pallas_call | solution.py:508
  45.1 5.3 %collective-permute-start.18 = (bf16[7,32,256]{2,1,0:T(8,128)(2,1)S(1)}, bf16[7,32,256]{2,1,0:T(8,128)(2,1)S(1)}, u32[]{:S(2)}, u32[]{:S(2)}) collective-permute-start(bf16[7,32,256]{2,1,0:T(8,128)(2,1)S(1)} %get-tuple-element.67), channel_id=1, source_target_pairs={{0,68},{2,70},{4,64},{6,66},{8,76},{10,78},{12,72},{14,74},{16,84}... | collective-permute-start | bytes 344072 | tf_op jit(solution)/shard_map/ppermute | solution.py:517
  50.4 1.2 %collective-permute-start.19 = (bf16[7,32,256]{2,1,0:T(8,128)(2,1)S(1)}, bf16[7,32,256]{2,1,0:T(8,128)(2,1)S(1)}, u32[]{:S(2)}, u32[]{:S(2)}) collective-permute-start(bf16[7,32,256]{2,1,0:T(8,128)(2,1)S(1)} %get-tuple-element.68), channel_id=1, source_target_pairs={{0,38},{2,36},{4,34},{6,32},{8,46},{10,44},{12,42},{14,40},{16,54}... | collective-permute-start | bytes 344072 | tf_op jit(solution)/shard_map/ppermute | solution.py:517
  51.6 2.6 %collective-permute-done.18.a1 = bf16[7,32,256]{2,1,0:T(8,128)(2,1)S(1)} collective-permute-done((bf16[7,32,256]{2,1,0:T(8,128)(2,1)S(1)}, bf16[7,32,256]{2,1,0:T(8,128)(2,1)S(1)}, u32[]{:S(2)}, u32[]{:S(2)}) %collective-permute-start.18) | collective-permute-done | bytes 114720 | tf_op jit(solution)/shard_map/ppermute | solution.py:517
  54.3 3.1 %collective-permute-done.19.a2 = bf16[7,32,256]{2,1,0:T(8,128)(2,1)S(1)} collective-permute-done((bf16[7,32,256]{2,1,0:T(8,128)(2,1)S(1)}, bf16[7,32,256]{2,1,0:T(8,128)(2,1)S(1)}, u32[]{:S(2)}, u32[]{:S(2)}) %collective-permute-start.19) | collective-permute-done | bytes 114720 | tf_op jit(solution)/shard_map/ppermute | solution.py:517
  57.4 1.1 %collective-permute-done.20.a3 = bf16[7,32,256]{2,1,0:T(8,128)(2,1)S(1)} collective-permute-done((bf16[7,32,256]{2,1,0:T(8,128)(2,1)S(1)}, bf16[7,32,256]{2,1,0:T(8,128)(2,1)S(1)}, u32[]{:S(2)}, u32[]{:S(2)}) %collective-permute-start.20) | collective-permute-done | bytes 114720 | tf_op jit(solution)/shard_map/ppermute | solution.py:517
  58.6 1.4 %collective-permute-start.23 = (bf16[7,32,256]{2,1,0:T(8,128)(2,1)S(1)}, bf16[7,32,256]{2,1,0:T(8,128)(2,1)S(1)}, u32[]{:S(2)}, u32[]{:S(2)}) collective-permute-start(bf16[7,32,256]{2,1,0:T(8,128)(2,1)S(1)} %shard_map.72.g0), channel_id=1, source_target_pairs={{0,64},{32,96},{64,0},{96,32},{1,65},{33,97},{65,1},{97,33},{2,66}... | collective-permute-start | bytes 344072 | tf_op jit(solution)/shard_map/ppermute | solution.py:521
  60.0 1.6 %collective-permute-start.22 = (bf16[7,32,256]{2,1,0:T(8,128)(2,1)S(1)}, bf16[7,32,256]{2,1,0:T(8,128)(2,1)S(1)}, u32[]{:S(2)}, u32[]{:S(2)}) collective-permute-start(bf16[7,32,256]{2,1,0:T(8,128)(2,1)S(1)} %shard_map.72.g0), channel_id=1, source_target_pairs={{0,96},{32,64},{64,32},{96,0},{1,97},{33,65},{65,33},{97,1},{2,98}... | collective-permute-start | bytes 344072 | tf_op jit(solution)/shard_map/ppermute | solution.py:521
  62.2 3.8 %collective-permute-done.23.g2 = bf16[7,32,256]{2,1,0:T(8,128)(2,1)S(1)} collective-permute-done((bf16[7,32,256]{2,1,0:T(8,128)(2,1)S(1)}, bf16[7,32,256]{2,1,0:T(8,128)(2,1)S(1)}, u32[]{:S(2)}, u32[]{:S(2)}) %collective-permute-start.23) | collective-permute-done | bytes 114720 | tf_op jit(solution)/shard_map/ppermute | solution.py:521
  (34 shorter events, 10.4 us)
Async XLA Ops:
  0.0 2.6 %collective-permute-start = (bf16[10,2,32,256]{3,2,1,0:T(8,128)(2,1)}, bf16[10,2,32,256]{3,2,1,0:T(8,128)(2,1)S(1)}, u32[]{:S(2)}, u32[]{:S(2)}) collective-permute-start(bf16[10,2,32,256]{3,2,1,0:T(8,128)(2,1)} %bitcast.3), channel_id=1, source_target_pairs={{0,1},{1,0},{2,3},{3,2},{4,5},{5,4},{6,7},{7,6},{8,9},{9,8},{10,11... | collective-permute-start | bytes 983048 | tf_op jit(solution)/shard_map/ppermute | solution.py:427
  0.0 2.6 %collective-permute-start.1 = (bf16[10,2,32,256]{3,2,1,0:T(8,128)(2,1)}, bf16[10,2,32,256]{3,2,1,0:T(8,128)(2,1)S(1)}, u32[]{:S(2)}, u32[]{:S(2)}) collective-permute-start(bf16[10,2,32,256]{3,2,1,0:T(8,128)(2,1)} %bitcast.5), channel_id=1, source_target_pairs={{0,1},{1,0},{2,3},{3,2},{4,5},{5,4},{6,7},{7,6},{8,9},{9,8},{10,11... | collective-permute-start | bytes 983048 | tf_op jit(solution)/shard_map/ppermute | solution.py:427
  0.5 2.1 %collective-permute-start.2 = (bf16[7,2,32,256]{3,2,1,0:T(8,128)(2,1)}, bf16[7,2,32,256]{3,2,1,0:T(8,128)(2,1)S(1)}, u32[]{:S(2)}, u32[]{:S(2)}) collective-permute-start(bf16[7,2,32,256]{3,2,1,0:T(8,128)(2,1)} %bitcast.7), channel_id=1, source_target_pairs={{0,1},{1,0},{2,3},{3,2},{4,5},{5,4},{6,7},{7,6},{8,9},{9,8},{10,11... | collective-permute-start | bytes 688136 | tf_op jit(solution)/shard_map/ppermute | solution.py:427
  3.4 8.7 %collective-permute-start.3 = (bf16[5,2,2,32,256]{4,3,2,1,0:T(8,128)(2,1)S(1)}, bf16[5,2,2,32,256]{4,3,2,1,0:T(8,128)(2,1)S(1)}, u32[]{:S(2)}, u32[]{:S(2)}) collective-permute-start(bf16[5,2,2,32,256]{4,3,2,1,0:T(8,128)(2,1)S(1)} %get-tuple-element.45), channel_id=1, source_target_pairs={{0,4},{1,17},{2,6},{3,19},{4,0},{5,21},{6,2},{7,23},{8,12},{9,25},... | collective-permute-start | bytes 983048 | tf_op jit(solution)/shard_map/ppermute | solution.py:453
  6.8 9.3 %collective-permute-start.4 = (bf16[5,2,2,32,256]{4,3,2,1,0:T(8,128)(2,1)S(1)}, bf16[5,2,2,32,256]{4,3,2,1,0:T(8,128)(2,1)S(1)}, u32[]{:S(2)}, u32[]{:S(2)}) collective-permute-start(bf16[5,2,2,32,256]{4,3,2,1,0:T(8,128)(2,1)S(1)} %get-tuple-element.46), channel_id=1, source_target_pairs={{0,6},{1,25},{2,0},{3,27},{4,2},{5,29},{6,4},{7,31},{8,14},{9,1},{... | collective-permute-start | bytes 983048 | tf_op jit(solution)/shard_map/ppermute | solution.py:453
  7.8 8.3 %collective-permute-start.5 = (bf16[5,2,2,32,256]{4,3,2,1,0:T(8,128)(2,1)S(1)}, bf16[5,2,2,32,256]{4,3,2,1,0:T(8,128)(2,1)S(1)}, u32[]{:S(2)}, u32[]{:S(2)}) collective-permute-start(bf16[5,2,2,32,256]{4,3,2,1,0:T(8,128)(2,1)S(1)} %get-tuple-element.47), channel_id=1, source_target_pairs={{0,2},{1,9},{2,4},{3,11},{4,6},{5,13},{6,0},{7,15},{8,10},{9,17},{... | collective-permute-start | bytes 983048 | tf_op jit(solution)/shard_map/ppermute | solution.py:453
  16.6 16.2 %collective-permute-start.7 = (bf16[3,2,2,4,32,256]{5,4,3,2,1,0:T(8,128)(2,1)S(1)}, bf16[3,2,2,4,32,256]{5,4,3,2,1,0:T(8,128)(2,1)S(1)}, u32[]{:S(2)}, u32[]{:S(2)}) collective-permute-start(bf16[3,2,2,4,32,256]{5,4,3,2,1,0:T(8,128)(2,1)S(1)} %get-tuple-element.48.r0), channel_id=1, source_target_pairs={{0,16},{1,5},{2,18},{3,7},{4,20},{5,1},{6,22},{7,3},{8,24},{9,13},... | collective-permute-start | bytes 2359304 | tf_op jit(solution)/shard_map/ppermute | solution.py:464
  20.5 18.4 %collective-permute-start.8 = (bf16[3,2,2,4,32,256]{5,4,3,2,1,0:T(8,128)(2,1)S(1)}, bf16[3,2,2,4,32,256]{5,4,3,2,1,0:T(8,128)(2,1)S(1)}, u32[]{:S(2)}, u32[]{:S(2)}) collective-permute-start(bf16[3,2,2,4,32,256]{5,4,3,2,1,0:T(8,128)(2,1)S(1)} %get-tuple-element.49), channel_id=1, source_target_pairs={{0,8},{1,3},{2,10},{3,5},{4,12},{5,7},{6,14},{7,1},{8,16},{9,11},{... | collective-permute-start | bytes 2359304 | tf_op jit(solution)/shard_map/ppermute | solution.py:463
  21.6 18.4 %collective-permute-start.6 = (bf16[3,2,2,4,32,256]{5,4,3,2,1,0:T(8,128)(2,1)S(1)}, bf16[3,2,2,4,32,256]{5,4,3,2,1,0:T(8,128)(2,1)S(1)}, u32[]{:S(2)}, u32[]{:S(2)}) collective-permute-start(bf16[3,2,2,4,32,256]{5,4,3,2,1,0:T(8,128)(2,1)S(1)} %get-tuple-element.49), channel_id=1, source_target_pairs={{0,24},{1,7},{2,26},{3,1},{4,28},{5,3},{6,30},{7,5},{8,0},{9,15},{... | collective-permute-start | bytes 2359304 | tf_op jit(solution)/shard_map/ppermute | solution.py:463
  23.8 5.3 %collective-permute-start.10 = (bf16[32,256]{1,0:T(8,128)(2,1)S(1)}, bf16[32,256]{1,0:T(8,128)(2,1)S(1)}, u32[]{:S(2)}, u32[]{:S(2)}) collective-permute-start(bf16[32,256]{1,0:T(8,128)(2,1)S(1)} %get-tuple-element.51), channel_id=1, source_target_pairs={{0,64},{32,96},{64,0},{96,32},{1,65},{33,97},{65,1},{97,33},{2,66}... | collective-permute-start | bytes 49160 | tf_op jit(solution)/shard_map/ppermute | solution.py:454
  26.8 4.9 %collective-permute-start.11 = (bf16[32,256]{1,0:T(8,128)(2,1)S(1)}, bf16[32,256]{1,0:T(8,128)(2,1)S(1)}, u32[]{:S(2)}, u32[]{:S(2)}) collective-permute-start(bf16[32,256]{1,0:T(8,128)(2,1)S(1)} %get-tuple-element.52), channel_id=1, source_target_pairs={{0,96},{32,64},{64,32},{96,0},{1,97},{33,65},{65,33},{97,1},{2,98}... | collective-permute-start | bytes 49160 | tf_op jit(solution)/shard_map/ppermute | solution.py:454
  29.0 3.7 %collective-permute-start.12 = (bf16[32,256]{1,0:T(8,128)(2,1)S(1)}, bf16[32,256]{1,0:T(8,128)(2,1)S(1)}, u32[]{:S(2)}, u32[]{:S(2)}) collective-permute-start(bf16[32,256]{1,0:T(8,128)(2,1)S(1)} %get-tuple-element.53), channel_id=1, source_target_pairs={{0,32},{32,0},{64,96},{96,64},{1,33},{33,1},{65,97},{97,65},{2,34}... | collective-permute-start | bytes 49160 | tf_op jit(solution)/shard_map/ppermute | solution.py:454
  31.8 1.9 %collective-permute-start.9 = (bf16[2,2,2,4,32,256]{5,4,3,2,1,0:T(8,128)(2,1)S(1)}, bf16[2,2,2,4,32,256]{5,4,3,2,1,0:T(8,128)(2,1)S(1)}, u32[]{:S(2)}, u32[]{:S(2)}) collective-permute-start(bf16[2,2,2,4,32,256]{5,4,3,2,1,0:T(8,128)(2,1)S(1)} %get-tuple-element.50.uk), channel_id=1, source_target_pairs={{0,1},{1,0},{2,3},{3,2},{4,5},{5,4},{6,7},{7,6},{8,9},{9,8},{10,11... | collective-permute-start | bytes 1572872 | tf_op jit(solution)/shard_map/ppermute | solution.py:465
  32.8 7.2 %collective-permute-start.13 = (bf16[2,2,2,4,32,256]{5,4,3,2,1,0:T(8,128)(2,1)S(1)}, bf16[2,2,2,4,32,256]{5,4,3,2,1,0:T(8,128)(2,1)S(1)}, u32[]{:S(2)}, u32[]{:S(2)}) collective-permute-start(bf16[2,2,2,4,32,256]{5,4,3,2,1,0:T(8,128)(2,1)S(1)} %shard_map.67), channel_id=1, source_target_pairs={{0,1},{1,0},{2,3},{3,2},{4,5},{5,4},{6,7},{7,6},{8,9},{9,8},{10,11... | collective-permute-start | bytes 1572872 | tf_op jit(solution)/shard_map/ppermute | solution.py:476
  40.3 2.0 %collective-permute-start.17 = (bf16[2,2,2,4,32,256]{5,4,3,2,1,0:T(8,128)(2,1)S(1)}, bf16[2,2,2,4,32,256]{5,4,3,2,1,0:T(8,128)(2,1)S(1)}, u32[]{:S(2)}, u32[]{:S(2)}) collective-permute-start(bf16[2,2,2,4,32,256]{5,4,3,2,1,0:T(8,128)(2,1)S(1)} %get-tuple-element.61), channel_id=1, source_target_pairs={{0,1},{1,0},{2,3},{3,2},{4,5},{5,4},{6,7},{7,6},{8,9},{9,8},{10,11... | collective-permute-start | bytes 1572872 | tf_op jit(solution)/shard_map/ppermute | solution.py:488
  40.8 2.5 %collective-permute-start.14 = (bf16[2,128,512]{2,1,0:T(8,128)(2,1)S(1)}, bf16[2,128,512]{2,1,0:T(8,128)(2,1)S(1)}, u32[]{:S(2)}, u32[]{:S(2)}) collective-permute-start(bf16[2,128,512]{2,1,0:T(8,128)(2,1)S(1)} %get-tuple-element.58.edge0), channel_id=1, source_target_pairs={{0,1},{1,0},{2,3},{3,2},{4,5},{5,4},{6,7},{7,6},{8,9},{9,8},{10,11... | collective-permute-start | bytes 786440 | tf_op jit(solution)/shard_map/ppermute | solution.py:498
  41.0 2.4 %collective-permute-start.15 = (bf16[2,128,512]{2,1,0:T(8,128)(2,1)S(1)}, bf16[2,128,512]{2,1,0:T(8,128)(2,1)S(1)}, u32[]{:S(2)}, u32[]{:S(2)}) collective-permute-start(bf16[2,128,512]{2,1,0:T(8,128)(2,1)S(1)} %get-tuple-element.59.edge1), channel_id=1, source_target_pairs={{0,1},{1,0},{2,3},{3,2},{4,5},{5,4},{6,7},{7,6},{8,9},{9,8},{10,11... | collective-permute-start | bytes 786440 | tf_op jit(solution)/shard_map/ppermute | solution.py:498
  41.4 2.0 %collective-permute-start.16 = (bf16[2,128,512]{2,1,0:T(8,128)(2,1)S(1)}, bf16[2,128,512]{2,1,0:T(8,128)(2,1)S(1)}, u32[]{:S(2)}, u32[]{:S(2)}) collective-permute-start(bf16[2,128,512]{2,1,0:T(8,128)(2,1)S(1)} %get-tuple-element.60.edge2), channel_id=1, source_target_pairs={{0,1},{1,0},{2,3},{3,2},{4,5},{5,4},{6,7},{7,6},{8,9},{9,8},{10,11... | collective-permute-start | bytes 786440 | tf_op jit(solution)/shard_map/ppermute | solution.py:498
  45.1 9.2 %collective-permute-start.18 = (bf16[7,32,256]{2,1,0:T(8,128)(2,1)S(1)}, bf16[7,32,256]{2,1,0:T(8,128)(2,1)S(1)}, u32[]{:S(2)}, u32[]{:S(2)}) collective-permute-start(bf16[7,32,256]{2,1,0:T(8,128)(2,1)S(1)} %get-tuple-element.67), channel_id=1, source_target_pairs={{0,68},{2,70},{4,64},{6,66},{8,76},{10,78},{12,72},{14,74},{16,84}... | collective-permute-start | bytes 344072 | tf_op jit(solution)/shard_map/ppermute | solution.py:517
  50.4 7.0 %collective-permute-start.19 = (bf16[7,32,256]{2,1,0:T(8,128)(2,1)S(1)}, bf16[7,32,256]{2,1,0:T(8,128)(2,1)S(1)}, u32[]{:S(2)}, u32[]{:S(2)}) collective-permute-start(bf16[7,32,256]{2,1,0:T(8,128)(2,1)S(1)} %get-tuple-element.68), channel_id=1, source_target_pairs={{0,38},{2,36},{4,34},{6,32},{8,46},{10,44},{12,42},{14,40},{16,54}... | collective-permute-start | bytes 344072 | tf_op jit(solution)/shard_map/ppermute | solution.py:517
  51.6 6.9 %collective-permute-start.20 = (bf16[7,32,256]{2,1,0:T(8,128)(2,1)S(1)}, bf16[7,32,256]{2,1,0:T(8,128)(2,1)S(1)}, u32[]{:S(2)}, u32[]{:S(2)}) collective-permute-start(bf16[7,32,256]{2,1,0:T(8,128)(2,1)S(1)} %get-tuple-element.69), channel_id=1, source_target_pairs={{0,98},{2,96},{4,102},{6,100},{8,106},{10,104},{12,110},{14,108},{... | collective-permute-start | bytes 344072 | tf_op jit(solution)/shard_map/ppermute | solution.py:517
  58.6 7.4 %collective-permute-start.23 = (bf16[7,32,256]{2,1,0:T(8,128)(2,1)S(1)}, bf16[7,32,256]{2,1,0:T(8,128)(2,1)S(1)}, u32[]{:S(2)}, u32[]{:S(2)}) collective-permute-start(bf16[7,32,256]{2,1,0:T(8,128)(2,1)S(1)} %shard_map.72.g0), channel_id=1, source_target_pairs={{0,64},{32,96},{64,0},{96,32},{1,65},{33,97},{65,1},{97,33},{2,66}... | collective-permute-start | bytes 344072 | tf_op jit(solution)/shard_map/ppermute | solution.py:521
  60.0 6.6 %collective-permute-start.22 = (bf16[7,32,256]{2,1,0:T(8,128)(2,1)S(1)}, bf16[7,32,256]{2,1,0:T(8,128)(2,1)S(1)}, u32[]{:S(2)}, u32[]{:S(2)}) collective-permute-start(bf16[7,32,256]{2,1,0:T(8,128)(2,1)S(1)} %shard_map.72.g0), channel_id=1, source_target_pairs={{0,96},{32,64},{64,32},{96,0},{1,97},{33,65},{65,33},{97,1},{2,98}... | collective-permute-start | bytes 344072 | tf_op jit(solution)/shard_map/ppermute | solution.py:521
  61.6 5.0 %collective-permute-start.21 = (bf16[7,32,256]{2,1,0:T(8,128)(2,1)S(1)}, bf16[7,32,256]{2,1,0:T(8,128)(2,1)S(1)}, u32[]{:S(2)}, u32[]{:S(2)}) collective-permute-start(bf16[7,32,256]{2,1,0:T(8,128)(2,1)S(1)} %shard_map.72.g0), channel_id=1, source_target_pairs={{0,32},{32,0},{64,96},{96,64},{1,33},{33,1},{65,97},{97,65},{2,34}... | collective-permute-start | bytes 344072 | tf_op jit(solution)/shard_map/ppermute | solution.py:521

commit v11 on v9

--- a/solution.py
+++ b/solution.py
@@ -98,7 +98,8 @@
     cols = lax.broadcasted_iota(jnp.int32, (32, 256), 1)
 
     def mask(row_node, col_node, on, half):
-        keep = (rows < widths[row_node]) & (cols + 256 * half < widths[col_node]) & (on != 0)
+        deep = jnp.where(on != 0, widths[row_node], 0)
+        keep = (rows < deep) & (cols < widths[col_node] - 256 * half)
         return jnp.where(keep, 1.0, 0.0).astype(BF)[None]
 
     @pl.when(c == 0)
@@ -108,7 +109,7 @@
             k = node_of(index_of(x, lax.rem(y + d, 4)))
             p = lax.div(k - 1, 2)
             at = 2 * (k - 3) + 2
-            out[0, h] = dia[p] * mask(p, p, 1, h)
+            out[0, h] = dia[p] * mask(p, p, jnp.int32(1), h)
             out[1, h] = low[at] * mask(p, k, pattern[at], h)
             out[2, h] = low[at + 1] * mask(0, k, pattern[at + 1], h)
             out[3, h] = up[at] * mask(k, p, pattern[at], h)
@@ -117,7 +118,7 @@
     @pl.when(c == 1)
     def _():
         h = 1 if own else 0
-        tiles = [dia[0] * mask(0, 0, 1, h)]
+        tiles = [dia[0] * mask(0, 0, jnp.int32(1), h)]
         for i in range(2):
             tiles.append(up[i] * mask(1 + i, 0, pattern[i], h))
             tiles.append(low[i] * mask(0, 1 + i, pattern[i], h))

time: 67.7 us -> 67.7 us (level)
  no operation moved by 1% of the time
where the time goes in v11:
time: 67.7 us; the launch traced here: 67.6 us
  waiting for transfers between devices  29.9 us (44%)
  starting transfers between devices  29.7 us (44%)
  Pallas kernels  7.8 us (12%)
    ppermute x3, waiting for transfers between devices, body(): came = {d: lax.ppermute(bufs[d], grid, ring_both(d)) for d in (1, 3, 2)}  7.31 us
    ppermute x3, waiting for transfers between devices, body(): lax.ppermute(slots[d], ('pole', 'row'), pairs_xy(d))  6.88 us
    ppermute x3, starting transfers between devices, body(): lax.ppermute(slots[d], ('pole', 'row'), pairs_xy(d))  6.54 us
    ppermute x2, waiting for transfers between devices, body(): came = {d: lax.ppermute(near, grid, ring_other(d)) for d in (1, 3)}  6.33 us
    ppermute x3, starting transfers between devices, body(): lax.ppermute(parts[d], 'pole', pairs_x(d))  5.65 us
    ppermute x3, starting transfers between devices, body(): came = {d: lax.ppermute(bufs[d], grid, ring_both(d)) for d in (1, 3, 2)}  5.38 us
    ppermute x3, waiting for transfers between devices, body(): lax.ppermute(total, 'pole', pairs_x(d))  4.42 us
    ppermute x1, starting transfers between devices, body(): came[2] = lax.ppermute(far, grid, ring_other(2))  3.96 us
  transfers between devices with their start and end apart: 24, of which 16 were waited for; matrix products, arithmetic and copies ran while one was open for 0% of the time, Pallas kernels for 5%

profile of v11, /device:TPU:0, one launch (start us, length us, event | category | flops | bytes accessed | tf_op | source)
XLA Modules:
  0.0 67.6 jit_solution(9437200211402045328)
XLA Ops:
  0.5 2.0 %shard_map.64 = (bf16[5,2,2,32,256]{4,3,2,1,0:T(8,128)(2,1)S(1)}, bf16[5,2,2,32,256]{4,3,2,1,0:T(8,128)(2,1)S(1)}, bf16[5,2,2,32,256]{4,3,2,1,0:T(8,128)(2,1)S(1...) custom-call(bf16[10,2,32,256]{3,2,1,0:T(8,128)(2,1)} %bitcast.4, ...), custom_call_target="tpu_custom_call" | custom-call | bytes 4194304 | tf_op jit(solution)/shard_map/pallas_call | solution.py:427
  3.4 3.4 %collective-permute-start.3 = (bf16[5,2,2,32,256]{4,3,2,1,0:T(8,128)(2,1)S(1)}, bf16[5,2,2,32,256]{4,3,2,1,0:T(8,128)(2,1)S(1)}, u32[]{:S(2)}, u32[]{:S(2)}) collective-permute-start(bf16[5,2,2,32,256]{4,3,2,1,0:T(8,128)(2,1)S(1)} %get-tuple-element.45), channel_id=1, source_target_pairs={{0,4},{1,17},{2,6},{3,19},{4,0},{5,21},{6,2},{7,23},{8,12},{9,25},... | collective-permute-start | bytes 983048 | tf_op jit(solution)/shard_map/ppermute | solution.py:451
  6.7 1.1 %collective-permute-start.4 = (bf16[5,2,2,32,256]{4,3,2,1,0:T(8,128)(2,1)S(1)}, bf16[5,2,2,32,256]{4,3,2,1,0:T(8,128)(2,1)S(1)}, u32[]{:S(2)}, u32[]{:S(2)}) collective-permute-start(bf16[5,2,2,32,256]{4,3,2,1,0:T(8,128)(2,1)S(1)} %get-tuple-element.46), channel_id=1, source_target_pairs={{0,6},{1,25},{2,0},{3,27},{4,2},{5,29},{6,4},{7,31},{8,14},{9,1},{... | collective-permute-start | bytes 983048 | tf_op jit(solution)/shard_map/ppermute | solution.py:451
  8.8 3.3 %collective-permute-done.3.b2 = bf16[5,2,2,32,256]{4,3,2,1,0:T(8,128)(2,1)S(1)} collective-permute-done((bf16[5,2,2,32,256]{4,3,2,1,0:T(8,128)(2,1)S(1)}, bf16[5,2,2,32,256]{4,3,2,1,0:T(8,128)(2,1)S(1)}, u32[]{:S(2)}, u32[]{:S(2)}) %collective-permute-start.3) | collective-permute-done | bytes 327712 | tf_op jit(solution)/shard_map/ppermute | solution.py:451
  12.0 4.0 %collective-permute-done.4.b3 = bf16[5,2,2,32,256]{4,3,2,1,0:T(8,128)(2,1)S(1)} collective-permute-done((bf16[5,2,2,32,256]{4,3,2,1,0:T(8,128)(2,1)S(1)}, bf16[5,2,2,32,256]{4,3,2,1,0:T(8,128)(2,1)S(1)}, u32[]{:S(2)}, u32[]{:S(2)}) %collective-permute-start.4) | collective-permute-done | bytes 327712 | tf_op jit(solution)/shard_map/ppermute | solution.py:451
  16.6 4.0 %collective-permute-start.7 = (bf16[3,2,2,4,32,256]{5,4,3,2,1,0:T(8,128)(2,1)S(1)}, bf16[3,2,2,4,32,256]{5,4,3,2,1,0:T(8,128)(2,1)S(1)}, u32[]{:S(2)}, u32[]{:S(2)}) collective-permute-start(bf16[3,2,2,4,32,256]{5,4,3,2,1,0:T(8,128)(2,1)S(1)} %get-tuple-element.48.r0), channel_id=1, source_target_pairs={{0,16},{1,5},{2,18},{3,7},{4,20},{5,1},{6,22},{7,3},{8,24},{9,13},... | collective-permute-start | bytes 2359304 | tf_op jit(solution)/shard_map/ppermute | solution.py:462
  21.5 2.2 %collective-permute-start.6 = (bf16[3,2,2,4,32,256]{5,4,3,2,1,0:T(8,128)(2,1)S(1)}, bf16[3,2,2,4,32,256]{5,4,3,2,1,0:T(8,128)(2,1)S(1)}, u32[]{:S(2)}, u32[]{:S(2)}) collective-permute-start(bf16[3,2,2,4,32,256]{5,4,3,2,1,0:T(8,128)(2,1)S(1)} %get-tuple-element.49), channel_id=1, source_target_pairs={{0,24},{1,7},{2,26},{3,1},{4,28},{5,3},{6,30},{7,5},{8,0},{9,15},{... | collective-permute-start | bytes 2359304 | tf_op jit(solution)/shard_map/ppermute | solution.py:461
  23.8 3.0 %collective-permute-start.10 = (bf16[32,256]{1,0:T(8,128)(2,1)S(1)}, bf16[32,256]{1,0:T(8,128)(2,1)S(1)}, u32[]{:S(2)}, u32[]{:S(2)}) collective-permute-start(bf16[32,256]{1,0:T(8,128)(2,1)S(1)} %get-tuple-element.51), channel_id=1, source_target_pairs={{0,64},{32,96},{64,0},{96,32},{1,65},{33,97},{65,1},{97,33},{2,66}... | collective-permute-start | bytes 49160 | tf_op jit(solution)/shard_map/ppermute | solution.py:452
  26.8 1.1 %collective-permute-start.11 = (bf16[32,256]{1,0:T(8,128)(2,1)S(1)}, bf16[32,256]{1,0:T(8,128)(2,1)S(1)}, u32[]{:S(2)}, u32[]{:S(2)}) collective-permute-start(bf16[32,256]{1,0:T(8,128)(2,1)S(1)} %get-tuple-element.52), channel_id=1, source_target_pairs={{0,96},{32,64},{64,32},{96,0},{1,97},{33,65},{65,33},{97,1},{2,98}... | collective-permute-start | bytes 49160 | tf_op jit(solution)/shard_map/ppermute | solution.py:452
  27.9 1.1 %collective-permute-done.10.p2.d1 = bf16[32,256]{1,0:T(8,128)(2,1)S(1)} collective-permute-done((bf16[32,256]{1,0:T(8,128)(2,1)S(1)}, bf16[32,256]{1,0:T(8,128)(2,1)S(1)}, u32[]{:S(2)}, u32[]{:S(2)}) %collective-permute-start.10) | collective-permute-done | bytes 16416 | tf_op jit(solution)/shard_map/ppermute | solution.py:452
  29.0 1.5 %collective-permute-start.12 = (bf16[32,256]{1,0:T(8,128)(2,1)S(1)}, bf16[32,256]{1,0:T(8,128)(2,1)S(1)}, u32[]{:S(2)}, u32[]{:S(2)}) collective-permute-start(bf16[32,256]{1,0:T(8,128)(2,1)S(1)} %get-tuple-element.53), channel_id=1, source_target_pairs={{0,32},{32,0},{64,96},{96,64},{1,33},{33,1},{65,97},{97,65},{2,34}... | collective-permute-start | bytes 49160 | tf_op jit(solution)/shard_map/ppermute | solution.py:452
  30.5 1.2 %collective-permute-done.11.p3.d2 = bf16[32,256]{1,0:T(8,128)(2,1)S(1)} collective-permute-done((bf16[32,256]{1,0:T(8,128)(2,1)S(1)}, bf16[32,256]{1,0:T(8,128)(2,1)S(1)}, u32[]{:S(2)}, u32[]{:S(2)}) %collective-permute-start.11) | collective-permute-done | bytes 16416 | tf_op jit(solution)/shard_map/ppermute | solution.py:452
  33.6 5.3 %collective-permute-done.8.r1 = bf16[3,2,2,4,32,256]{5,4,3,2,1,0:T(8,128)(2,1)S(1)} collective-permute-done((bf16[3,2,2,4,32,256]{5,4,3,2,1,0:T(8,128)(2,1)S(1)}, bf16[3,2,2,4,32,256]{5,4,3,2,1,0:T(8,128)(2,1)S(1)}, u32[]{:S(2)}, u32[]{:S(2)}) %collective-permute-start.8) | collective-permute-done | bytes 786464 | tf_op jit(solution)/shard_map/ppermute | solution.py:461
  38.9 1.1 %collective-permute-done.6.r3 = bf16[3,2,2,4,32,256]{5,4,3,2,1,0:T(8,128)(2,1)S(1)} collective-permute-done((bf16[3,2,2,4,32,256]{5,4,3,2,1,0:T(8,128)(2,1)S(1)}, bf16[3,2,2,4,32,256]{5,4,3,2,1,0:T(8,128)(2,1)S(1)}, u32[]{:S(2)}, u32[]{:S(2)}) %collective-permute-start.6) | collective-permute-done | bytes 786464 | tf_op jit(solution)/shard_map/ppermute | solution.py:461
  42.3 1.1 %shard_map.70 = (bf16[1024,256]{1,0:T(8,128)(2,1)S(1)}, f32[768,256]{1,0:T(8,128)S(1)}, bf16[2,2,4,4,32,256]{5,4,3,2,1,0:T(8,128)(2,1)S(1)}) custom-call(bf16[2,128,512]{2,1,0:T(8,128)(2,1)S(1)} %get-tuple-element.58.edge0, bf16[2,128,512]{2,1,0:T(8,128)(2,1)S(1)} %get-tuple-element.59.edge1, bf16[2,128,512]{2,1,0:T(8,128)(2,1)S(1)} %get-tuple-element.60.edge2, ...), custom_call_target="tpu_custom_call" | custom-call | flops 939524096 | bytes 4194304 | tf_op jit(solution)/shard_map/pallas_call | solution.py:497
  43.4 1.7 %shard_map.71 = (bf16[7,32,256]{2,1,0:T(8,128)(2,1)S(1)}, bf16[7,32,256]{2,1,0:T(8,128)(2,1)S(1)}, bf16[7,32,256]{2,1,0:T(8,128)(2,1)S(1)}, bf16[7,32,256]{2,1,0:T(8,128)(2,1)S(1)}) custom-call(bf16[2,128,512]{2,1,0:T(8,128)(2,1)S(1)} %get-tuple-element.58.edge0, bf16[2,128,512]{2,1,0:T(8,128)(2,1)S(1)} %get-tuple-element.59.edge1, ...), custom_call_target="tpu_custom_call" | custom-call | flops 805306368 | bytes 4194304 | tf_op jit(solution)/shard_map/pallas_call | solution.py:506
  45.1 5.3 %collective-permute-start.18 = (bf16[7,32,256]{2,1,0:T(8,128)(2,1)S(1)}, bf16[7,32,256]{2,1,0:T(8,128)(2,1)S(1)}, u32[]{:S(2)}, u32[]{:S(2)}) collective-permute-start(bf16[7,32,256]{2,1,0:T(8,128)(2,1)S(1)} %get-tuple-element.67), channel_id=1, source_target_pairs={{0,68},{2,70},{4,64},{6,66},{8,76},{10,78},{12,72},{14,74},{16,84}... | collective-permute-start | bytes 344072 | tf_op jit(solution)/shard_map/ppermute | solution.py:515
  50.4 1.2 %collective-permute-start.19 = (bf16[7,32,256]{2,1,0:T(8,128)(2,1)S(1)}, bf16[7,32,256]{2,1,0:T(8,128)(2,1)S(1)}, u32[]{:S(2)}, u32[]{:S(2)}) collective-permute-start(bf16[7,32,256]{2,1,0:T(8,128)(2,1)S(1)} %get-tuple-element.68), channel_id=1, source_target_pairs={{0,38},{2,36},{4,34},{6,32},{8,46},{10,44},{12,42},{14,40},{16,54}... | collective-permute-start | bytes 344072 | tf_op jit(solution)/shard_map/ppermute | solution.py:515
  51.6 2.6 %collective-permute-done.18.a1 = bf16[7,32,256]{2,1,0:T(8,128)(2,1)S(1)} collective-permute-done((bf16[7,32,256]{2,1,0:T(8,128)(2,1)S(1)}, bf16[7,32,256]{2,1,0:T(8,128)(2,1)S(1)}, u32[]{:S(2)}, u32[]{:S(2)}) %collective-permute-start.18) | collective-permute-done | bytes 114720 | tf_op jit(solution)/shard_map/ppermute | solution.py:515
  54.2 3.1 %collective-permute-done.19.a2 = bf16[7,32,256]{2,1,0:T(8,128)(2,1)S(1)} collective-permute-done((bf16[7,32,256]{2,1,0:T(8,128)(2,1)S(1)}, bf16[7,32,256]{2,1,0:T(8,128)(2,1)S(1)}, u32[]{:S(2)}, u32[]{:S(2)}) %collective-permute-start.19) | collective-permute-done | bytes 114720 | tf_op jit(solution)/shard_map/ppermute | solution.py:515
  57.4 1.1 %collective-permute-done.20.a3 = bf16[7,32,256]{2,1,0:T(8,128)(2,1)S(1)} collective-permute-done((bf16[7,32,256]{2,1,0:T(8,128)(2,1)S(1)}, bf16[7,32,256]{2,1,0:T(8,128)(2,1)S(1)}, u32[]{:S(2)}, u32[]{:S(2)}) %collective-permute-start.20) | collective-permute-done | bytes 114720 | tf_op jit(solution)/shard_map/ppermute | solution.py:515
  58.6 1.4 %collective-permute-start.23 = (bf16[7,32,256]{2,1,0:T(8,128)(2,1)S(1)}, bf16[7,32,256]{2,1,0:T(8,128)(2,1)S(1)}, u32[]{:S(2)}, u32[]{:S(2)}) collective-permute-start(bf16[7,32,256]{2,1,0:T(8,128)(2,1)S(1)} %shard_map.72.g0), channel_id=1, source_target_pairs={{0,64},{32,96},{64,0},{96,32},{1,65},{33,97},{65,1},{97,33},{2,66}... | collective-permute-start | bytes 344072 | tf_op jit(solution)/shard_map/ppermute | solution.py:519
  59.9 1.6 %collective-permute-start.22 = (bf16[7,32,256]{2,1,0:T(8,128)(2,1)S(1)}, bf16[7,32,256]{2,1,0:T(8,128)(2,1)S(1)}, u32[]{:S(2)}, u32[]{:S(2)}) collective-permute-start(bf16[7,32,256]{2,1,0:T(8,128)(2,1)S(1)} %shard_map.72.g0), channel_id=1, source_target_pairs={{0,96},{32,64},{64,32},{96,0},{1,97},{33,65},{65,33},{97,1},{2,98}... | collective-permute-start | bytes 344072 | tf_op jit(solution)/shard_map/ppermute | solution.py:519
  62.1 3.8 %collective-permute-done.23.g2 = bf16[7,32,256]{2,1,0:T(8,128)(2,1)S(1)} collective-permute-done((bf16[7,32,256]{2,1,0:T(8,128)(2,1)S(1)}, bf16[7,32,256]{2,1,0:T(8,128)(2,1)S(1)}, u32[]{:S(2)}, u32[]{:S(2)}) %collective-permute-start.23) | collective-permute-done | bytes 114720 | tf_op jit(solution)/shard_map/ppermute | solution.py:519
  (34 shorter events, 10.4 us)
Async XLA Ops:
  0.0 2.6 %collective-permute-start = (bf16[10,2,32,256]{3,2,1,0:T(8,128)(2,1)}, bf16[10,2,32,256]{3,2,1,0:T(8,128)(2,1)S(1)}, u32[]{:S(2)}, u32[]{:S(2)}) collective-permute-start(bf16[10,2,32,256]{3,2,1,0:T(8,128)(2,1)} %bitcast.3), channel_id=1, source_target_pairs={{0,1},{1,0},{2,3},{3,2},{4,5},{5,4},{6,7},{7,6},{8,9},{9,8},{10,11... | collective-permute-start | bytes 983048 | tf_op jit(solution)/shard_map/ppermute | solution.py:425
  0.0 2.6 %collective-permute-start.1 = (bf16[10,2,32,256]{3,2,1,0:T(8,128)(2,1)}, bf16[10,2,32,256]{3,2,1,0:T(8,128)(2,1)S(1)}, u32[]{:S(2)}, u32[]{:S(2)}) collective-permute-start(bf16[10,2,32,256]{3,2,1,0:T(8,128)(2,1)} %bitcast.5), channel_id=1, source_target_pairs={{0,1},{1,0},{2,3},{3,2},{4,5},{5,4},{6,7},{7,6},{8,9},{9,8},{10,11... | collective-permute-start | bytes 983048 | tf_op jit(solution)/shard_map/ppermute | solution.py:425
  0.5 2.1 %collective-permute-start.2 = (bf16[7,2,32,256]{3,2,1,0:T(8,128)(2,1)}, bf16[7,2,32,256]{3,2,1,0:T(8,128)(2,1)S(1)}, u32[]{:S(2)}, u32[]{:S(2)}) collective-permute-start(bf16[7,2,32,256]{3,2,1,0:T(8,128)(2,1)} %bitcast.7), channel_id=1, source_target_pairs={{0,1},{1,0},{2,3},{3,2},{4,5},{5,4},{6,7},{7,6},{8,9},{9,8},{10,11... | collective-permute-start | bytes 688136 | tf_op jit(solution)/shard_map/ppermute | solution.py:425
  3.4 8.7 %collective-permute-start.3 = (bf16[5,2,2,32,256]{4,3,2,1,0:T(8,128)(2,1)S(1)}, bf16[5,2,2,32,256]{4,3,2,1,0:T(8,128)(2,1)S(1)}, u32[]{:S(2)}, u32[]{:S(2)}) collective-permute-start(bf16[5,2,2,32,256]{4,3,2,1,0:T(8,128)(2,1)S(1)} %get-tuple-element.45), channel_id=1, source_target_pairs={{0,4},{1,17},{2,6},{3,19},{4,0},{5,21},{6,2},{7,23},{8,12},{9,25},... | collective-permute-start | bytes 983048 | tf_op jit(solution)/shard_map/ppermute | solution.py:451
  6.7 9.3 %collective-permute-start.4 = (bf16[5,2,2,32,256]{4,3,2,1,0:T(8,128)(2,1)S(1)}, bf16[5,2,2,32,256]{4,3,2,1,0:T(8,128)(2,1)S(1)}, u32[]{:S(2)}, u32[]{:S(2)}) collective-permute-start(bf16[5,2,2,32,256]{4,3,2,1,0:T(8,128)(2,1)S(1)} %get-tuple-element.46), channel_id=1, source_target_pairs={{0,6},{1,25},{2,0},{3,27},{4,2},{5,29},{6,4},{7,31},{8,14},{9,1},{... | collective-permute-start | bytes 983048 | tf_op jit(solution)/shard_map/ppermute | solution.py:451
  7.8 8.3 %collective-permute-start.5 = (bf16[5,2,2,32,256]{4,3,2,1,0:T(8,128)(2,1)S(1)}, bf16[5,2,2,32,256]{4,3,2,1,0:T(8,128)(2,1)S(1)}, u32[]{:S(2)}, u32[]{:S(2)}) collective-permute-start(bf16[5,2,2,32,256]{4,3,2,1,0:T(8,128)(2,1)S(1)} %get-tuple-element.47), channel_id=1, source_target_pairs={{0,2},{1,9},{2,4},{3,11},{4,6},{5,13},{6,0},{7,15},{8,10},{9,17},{... | collective-permute-start | bytes 983048 | tf_op jit(solution)/shard_map/ppermute | solution.py:451
  16.6 16.2 %collective-permute-start.7 = (bf16[3,2,2,4,32,256]{5,4,3,2,1,0:T(8,128)(2,1)S(1)}, bf16[3,2,2,4,32,256]{5,4,3,2,1,0:T(8,128)(2,1)S(1)}, u32[]{:S(2)}, u32[]{:S(2)}) collective-permute-start(bf16[3,2,2,4,32,256]{5,4,3,2,1,0:T(8,128)(2,1)S(1)} %get-tuple-element.48.r0), channel_id=1, source_target_pairs={{0,16},{1,5},{2,18},{3,7},{4,20},{5,1},{6,22},{7,3},{8,24},{9,13},... | collective-permute-start | bytes 2359304 | tf_op jit(solution)/shard_map/ppermute | solution.py:462
  20.5 18.4 %collective-permute-start.8 = (bf16[3,2,2,4,32,256]{5,4,3,2,1,0:T(8,128)(2,1)S(1)}, bf16[3,2,2,4,32,256]{5,4,3,2,1,0:T(8,128)(2,1)S(1)}, u32[]{:S(2)}, u32[]{:S(2)}) collective-permute-start(bf16[3,2,2,4,32,256]{5,4,3,2,1,0:T(8,128)(2,1)S(1)} %get-tuple-element.49), channel_id=1, source_target_pairs={{0,8},{1,3},{2,10},{3,5},{4,12},{5,7},{6,14},{7,1},{8,16},{9,11},{... | collective-permute-start | bytes 2359304 | tf_op jit(solution)/shard_map/ppermute | solution.py:461
  21.5 18.4 %collective-permute-start.6 = (bf16[3,2,2,4,32,256]{5,4,3,2,1,0:T(8,128)(2,1)S(1)}, bf16[3,2,2,4,32,256]{5,4,3,2,1,0:T(8,128)(2,1)S(1)}, u32[]{:S(2)}, u32[]{:S(2)}) collective-permute-start(bf16[3,2,2,4,32,256]{5,4,3,2,1,0:T(8,128)(2,1)S(1)} %get-tuple-element.49), channel_id=1, source_target_pairs={{0,24},{1,7},{2,26},{3,1},{4,28},{5,3},{6,30},{7,5},{8,0},{9,15},{... | collective-permute-start | bytes 2359304 | tf_op jit(solution)/shard_map/ppermute | solution.py:461
  23.8 5.2 %collective-permute-start.10 = (bf16[32,256]{1,0:T(8,128)(2,1)S(1)}, bf16[32,256]{1,0:T(8,128)(2,1)S(1)}, u32[]{:S(2)}, u32[]{:S(2)}) collective-permute-start(bf16[32,256]{1,0:T(8,128)(2,1)S(1)} %get-tuple-element.51), channel_id=1, source_target_pairs={{0,64},{32,96},{64,0},{96,32},{1,65},{33,97},{65,1},{97,33},{2,66}... | collective-permute-start | bytes 49160 | tf_op jit(solution)/shard_map/ppermute | solution.py:452
  26.8 4.9 %collective-permute-start.11 = (bf16[32,256]{1,0:T(8,128)(2,1)S(1)}, bf16[32,256]{1,0:T(8,128)(2,1)S(1)}, u32[]{:S(2)}, u32[]{:S(2)}) collective-permute-start(bf16[32,256]{1,0:T(8,128)(2,1)S(1)} %get-tuple-element.52), channel_id=1, source_target_pairs={{0,96},{32,64},{64,32},{96,0},{1,97},{33,65},{65,33},{97,1},{2,98}... | collective-permute-start | bytes 49160 | tf_op jit(solution)/shard_map/ppermute | solution.py:452
  29.0 3.7 %collective-permute-start.12 = (bf16[32,256]{1,0:T(8,128)(2,1)S(1)}, bf16[32,256]{1,0:T(8,128)(2,1)S(1)}, u32[]{:S(2)}, u32[]{:S(2)}) collective-permute-start(bf16[32,256]{1,0:T(8,128)(2,1)S(1)} %get-tuple-element.53), channel_id=1, source_target_pairs={{0,32},{32,0},{64,96},{96,64},{1,33},{33,1},{65,97},{97,65},{2,34}... | collective-permute-start | bytes 49160 | tf_op jit(solution)/shard_map/ppermute | solution.py:452
  31.7 1.9 %collective-permute-start.9 = (bf16[2,2,2,4,32,256]{5,4,3,2,1,0:T(8,128)(2,1)S(1)}, bf16[2,2,2,4,32,256]{5,4,3,2,1,0:T(8,128)(2,1)S(1)}, u32[]{:S(2)}, u32[]{:S(2)}) collective-permute-start(bf16[2,2,2,4,32,256]{5,4,3,2,1,0:T(8,128)(2,1)S(1)} %get-tuple-element.50.uk), channel_id=1, source_target_pairs={{0,1},{1,0},{2,3},{3,2},{4,5},{5,4},{6,7},{7,6},{8,9},{9,8},{10,11... | collective-permute-start | bytes 1572872 | tf_op jit(solution)/shard_map/ppermute | solution.py:463
  32.8 7.2 %collective-permute-start.13 = (bf16[2,2,2,4,32,256]{5,4,3,2,1,0:T(8,128)(2,1)S(1)}, bf16[2,2,2,4,32,256]{5,4,3,2,1,0:T(8,128)(2,1)S(1)}, u32[]{:S(2)}, u32[]{:S(2)}) collective-permute-start(bf16[2,2,2,4,32,256]{5,4,3,2,1,0:T(8,128)(2,1)S(1)} %shard_map.67), channel_id=1, source_target_pairs={{0,1},{1,0},{2,3},{3,2},{4,5},{5,4},{6,7},{7,6},{8,9},{9,8},{10,11... | collective-permute-start | bytes 1572872 | tf_op jit(solution)/shard_map/ppermute | solution.py:474
  40.3 2.0 %collective-permute-start.17 = (bf16[2,2,2,4,32,256]{5,4,3,2,1,0:T(8,128)(2,1)S(1)}, bf16[2,2,2,4,32,256]{5,4,3,2,1,0:T(8,128)(2,1)S(1)}, u32[]{:S(2)}, u32[]{:S(2)}) collective-permute-start(bf16[2,2,2,4,32,256]{5,4,3,2,1,0:T(8,128)(2,1)S(1)} %get-tuple-element.61), channel_id=1, source_target_pairs={{0,1},{1,0},{2,3},{3,2},{4,5},{5,4},{6,7},{7,6},{8,9},{9,8},{10,11... | collective-permute-start | bytes 1572872 | tf_op jit(solution)/shard_map/ppermute | solution.py:486
  40.8 2.5 %collective-permute-start.14 = (bf16[2,128,512]{2,1,0:T(8,128)(2,1)S(1)}, bf16[2,128,512]{2,1,0:T(8,128)(2,1)S(1)}, u32[]{:S(2)}, u32[]{:S(2)}) collective-permute-start(bf16[2,128,512]{2,1,0:T(8,128)(2,1)S(1)} %get-tuple-element.58.edge0), channel_id=1, source_target_pairs={{0,1},{1,0},{2,3},{3,2},{4,5},{5,4},{6,7},{7,6},{8,9},{9,8},{10,11... | collective-permute-start | bytes 786440 | tf_op jit(solution)/shard_map/ppermute | solution.py:496
  41.0 2.4 %collective-permute-start.15 = (bf16[2,128,512]{2,1,0:T(8,128)(2,1)S(1)}, bf16[2,128,512]{2,1,0:T(8,128)(2,1)S(1)}, u32[]{:S(2)}, u32[]{:S(2)}) collective-permute-start(bf16[2,128,512]{2,1,0:T(8,128)(2,1)S(1)} %get-tuple-element.59.edge1), channel_id=1, source_target_pairs={{0,1},{1,0},{2,3},{3,2},{4,5},{5,4},{6,7},{7,6},{8,9},{9,8},{10,11... | collective-permute-start | bytes 786440 | tf_op jit(solution)/shard_map/ppermute | solution.py:496
  41.4 2.0 %collective-permute-start.16 = (bf16[2,128,512]{2,1,0:T(8,128)(2,1)S(1)}, bf16[2,128,512]{2,1,0:T(8,128)(2,1)S(1)}, u32[]{:S(2)}, u32[]{:S(2)}) collective-permute-start(bf16[2,128,512]{2,1,0:T(8,128)(2,1)S(1)} %get-tuple-element.60.edge2), channel_id=1, source_target_pairs={{0,1},{1,0},{2,3},{3,2},{4,5},{5,4},{6,7},{7,6},{8,9},{9,8},{10,11... | collective-permute-start | bytes 786440 | tf_op jit(solution)/shard_map/ppermute | solution.py:496
  45.1 9.2 %collective-permute-start.18 = (bf16[7,32,256]{2,1,0:T(8,128)(2,1)S(1)}, bf16[7,32,256]{2,1,0:T(8,128)(2,1)S(1)}, u32[]{:S(2)}, u32[]{:S(2)}) collective-permute-start(bf16[7,32,256]{2,1,0:T(8,128)(2,1)S(1)} %get-tuple-element.67), channel_id=1, source_target_pairs={{0,68},{2,70},{4,64},{6,66},{8,76},{10,78},{12,72},{14,74},{16,84}... | collective-permute-start | bytes 344072 | tf_op jit(solution)/shard_map/ppermute | solution.py:515
  50.4 7.0 %collective-permute-start.19 = (bf16[7,32,256]{2,1,0:T(8,128)(2,1)S(1)}, bf16[7,32,256]{2,1,0:T(8,128)(2,1)S(1)}, u32[]{:S(2)}, u32[]{:S(2)}) collective-permute-start(bf16[7,32,256]{2,1,0:T(8,128)(2,1)S(1)} %get-tuple-element.68), channel_id=1, source_target_pairs={{0,38},{2,36},{4,34},{6,32},{8,46},{10,44},{12,42},{14,40},{16,54}... | collective-permute-start | bytes 344072 | tf_op jit(solution)/shard_map/ppermute | solution.py:515
  51.6 6.9 %collective-permute-start.20 = (bf16[7,32,256]{2,1,0:T(8,128)(2,1)S(1)}, bf16[7,32,256]{2,1,0:T(8,128)(2,1)S(1)}, u32[]{:S(2)}, u32[]{:S(2)}) collective-permute-start(bf16[7,32,256]{2,1,0:T(8,128)(2,1)S(1)} %get-tuple-element.69), channel_id=1, source_target_pairs={{0,98},{2,96},{4,102},{6,100},{8,106},{10,104},{12,110},{14,108},{... | collective-permute-start | bytes 344072 | tf_op jit(solution)/shard_map/ppermute | solution.py:515
  58.6 7.4 %collective-permute-start.23 = (bf16[7,32,256]{2,1,0:T(8,128)(2,1)S(1)}, bf16[7,32,256]{2,1,0:T(8,128)(2,1)S(1)}, u32[]{:S(2)}, u32[]{:S(2)}) collective-permute-start(bf16[7,32,256]{2,1,0:T(8,128)(2,1)S(1)} %shard_map.72.g0), channel_id=1, source_target_pairs={{0,64},{32,96},{64,0},{96,32},{1,65},{33,97},{65,1},{97,33},{2,66}... | collective-permute-start | bytes 344072 | tf_op jit(solution)/shard_map/ppermute | solution.py:519
  59.9 6.6 %collective-permute-start.22 = (bf16[7,32,256]{2,1,0:T(8,128)(2,1)S(1)}, bf16[7,32,256]{2,1,0:T(8,128)(2,1)S(1)}, u32[]{:S(2)}, u32[]{:S(2)}) collective-permute-start(bf16[7,32,256]{2,1,0:T(8,128)(2,1)S(1)} %shard_map.72.g0), channel_id=1, source_target_pairs={{0,96},{32,64},{64,32},{96,0},{1,97},{33,65},{65,33},{97,1},{2,98}... | collective-permute-start | bytes 344072 | tf_op jit(solution)/shard_map/ppermute | solution.py:519
  61.6 5.0 %collective-permute-start.21 = (bf16[7,32,256]{2,1,0:T(8,128)(2,1)S(1)}, bf16[7,32,256]{2,1,0:T(8,128)(2,1)S(1)}, u32[]{:S(2)}, u32[]{:S(2)}) collective-permute-start(bf16[7,32,256]{2,1,0:T(8,128)(2,1)S(1)} %shard_map.72.g0), channel_id=1, source_target_pairs={{0,32},{32,0},{64,96},{96,64},{1,33},{33,1},{65,97},{97,65},{2,34}... | collective-permute-start | bytes 344072 | tf_op jit(solution)/shard_map/ppermute | solution.py:519
